TPU v7x, 32 devices: a whole 2x2x4 slice. The times are simulated.
32 devices in a mesh: lon: 8 (over y, x, core), rad: 4 (over z).
Axes of the slice: x: 2, y: 2, z: 4, core: 2. Of those that a mesh axis runs over, the one named last changes fastest.
Arguments:
- state: float32 [5, 32, 48, 1024], P(None, 'rad', None, 'lon'), may hold values from -6 to 6
- outer_rows: float32 [5, 32, 4, 1024], P(None, 'rad', None, 'lon'), may hold values from -6 to 6
- kappa: float32 [32], P('rad'), may hold values from 5e-05 to 0.0005
Outputs:
- increment: float32 [5, 32, 48, 1024], P(None, 'rad', None, 'lon')
All inputs are finite; a program needn't handle non-finite values.
Results may differ from a plain program's by a relative error of at most 0.00002.
Values sent between devices are 32-bit elements; how exact they have to be, the bound alone decides.
No kernel may reach another device: no remote copies, remote signals or barrier semaphores. Data moves between devices by JAX's collectives and lax.ppermute only.
A program may use at most 128 MiB of HBM per device.

v0:
```python
import math

import jax
import jax.numpy as jnp
from jax import lax
from jax.sharding import PartitionSpec as P

first_coeffs = (0.8, -0.2, 4.0 / 105.0, -1.0 / 280.0)
second_coeffs = (-205.0 / 72.0, 1.6, -0.2, 8.0 / 315.0, -1.0 / 560.0)
time_step = 0.002
gamma_less_one = 0.4
radial_ratio = 3.0


def with_halo(block, sides, width, periodic):
    for axis, dim in sides:
        count = lax.axis_size(axis)
        forward = [(i, i + 1) for i in range(count - 1)]
        if periodic:
            forward.append((count - 1, 0))
        backward = [(target, source) for source, target in forward]
        low = lax.ppermute(
            lax.slice_in_dim(block, block.shape[dim] - width, None, axis=dim), axis, forward
        )
        high = lax.ppermute(lax.slice_in_dim(block, 0, width, axis=dim), axis, backward)
        block = jnp.concatenate([low, block, high], axis=dim)
    return block


def passed_along(array, axis, by):
    peers = lax.axis_size(axis)
    return lax.ppermute(array, axis, [(i, (i + by) % peers) for i in range(peers)])


def window(padded, offset, length, axis):
    return lax.slice_in_dim(padded, offset, offset + length, axis=axis)


def first_derivative(padded, length, axis):
    total = first_coeffs[0] * (window(padded, 5, length, axis) - window(padded, 3, length, axis))
    for reach in range(2, 5):
        total = total + first_coeffs[reach - 1] * (
            window(padded, 4 + reach, length, axis) - window(padded, 4 - reach, length, axis)
        )
    return total


def second_derivative(padded, length, axis):
    total = second_coeffs[0] * window(padded, 4, length, axis)
    for reach in range(1, 5):
        total = total + second_coeffs[reach] * (
            window(padded, 4 + reach, length, axis) + window(padded, 4 - reach, length, axis)
        )
    return total


def geometry(rows, nlon):
    index = jnp.arange(rows, dtype=jnp.float32)
    spacing = 2.0 * math.pi / nlon
    theta = (index + 0.5) * spacing
    metric = 1.0 / jnp.sin(theta)
    return (metric[:, None], (jnp.cos(theta) * metric)[:, None])


def tendency(center, pad_lon, pad_row, pad_level, kappa_col, metric, curvature):
    levels, rows, width = (center.shape[1], center.shape[2], center.shape[3])
    slope_lon = metric * first_derivative(pad_lon, width, 3)
    slope_row = first_derivative(pad_row, rows, 2)
    slope_level = radial_ratio * first_derivative(pad_level, levels, 1)
    wind_lon = center[1]
    wind_row = center[2]
    wind_level = center[3]
    temper = center[4]
    carried = wind_lon * slope_lon + wind_row * slope_row + wind_level * slope_level
    spread = slope_lon[1] + slope_row[2] + slope_level[3] + curvature * wind_row
    laplace = (
        metric * metric * second_derivative(pad_lon[4], width, 2)
        + second_derivative(pad_row[4], rows, 1)
        + radial_ratio * radial_ratio * second_derivative(pad_level[4], levels, 0)
    )
    return jnp.stack(
        [
            -carried[0] - spread,
            -carried[1] - temper * slope_lon[0] - slope_lon[4],
            -carried[2] - temper * slope_row[0] - slope_row[4],
            -carried[3] - temper * slope_level[0] - slope_level[4],
            -carried[4] - gamma_less_one * temper * spread + kappa_col * laplace,
        ]
    )


def neighbours(center, outer_rows):
    flip_signs = jnp.array([1.0, -1.0, -1.0, 1.0, 1.0], dtype=jnp.float32).reshape(5, 1, 1, 1)
    pad_lon = with_halo(center, (("lon", 3),), 4, True)
    across = passed_along(center[:, :, :4, :], "lon", lax.axis_size("lon") // 2)
    pad_row = jnp.concatenate([across[:, :, ::-1, :] * flip_signs, center, outer_rows], axis=2)
    return (pad_lon, pad_row)


def on_device(state, outer_rows, kappa):
    levels = state.shape[1]
    metric, curvature = geometry(state.shape[2], state.shape[3] * lax.axis_size("lon"))
    kappa_col = kappa.reshape(levels, 1, 1)
    current = state
    rates = []
    for turn in range(2):
        pad_lon, pad_row = neighbours(current, outer_rows)
        pad_level = with_halo(current, (("rad", 1),), 4, False)
        rate = tendency(current, pad_lon, pad_row, pad_level, kappa_col, metric, curvature)
        rates.append(rate)
        current = current + time_step * rate
    first, second = (rates[0], rates[1])
    return 0.5 * time_step * (first + second)


def solution(mesh):
    placed = (P(None, "rad", None, "lon"), P(None, "rad", None, "lon"), P("rad"))
    return jax.shard_map(
        on_device,
        mesh=mesh,
        in_specs=placed,
        out_specs=P(None, "rad", None, "lon"),
        check_vma=False,
    )
```

profile of v0, /device:TPU:0, one launch (start us, length us, event | category | flops | bytes accessed | tf_op | source)
XLA Modules:
  0.0 184.0 jit_solution(7828236091452626316)
XLA Ops:
  0.0 2.2 %fusion.185 = (f32[5,4,48,128]{3,2,1,0:T(8,128)}, f32[5,4,48,128]{3,2,1,0:T(8,128)}) fusion(f32[5,8,48,128]{3,2,1,0:T(8,128)} %param.5), kind=kLoop, calls=%fused_computation.322 | loop fusion | bytes 1966080 | tf_op jit(solution)/shard_map/slice | solution.py:23
  2.2 5.7 %collective-permute-start.4 = (f32[5,4,48,128]{3,2,1,0:T(8,128)}, f32[5,4,48,128]{3,2,1,0:T(8,128)}, u32[]{:S(2)}, u32[]{:S(2)}) collective-permute-start(f32[5,4,48,128]{3,2,1,0:T(8,128)} %get-tuple-element.46), channel_id=1, source_target_pairs={{0,1},{1,2},{2,3},{4,5},{5,6},{6,7},{8,9},{9,10},{10,11},{12,13},{... | collective-permute-start | bytes 1474568 | tf_op jit(solution)/shard_map/ppermute | solution.py:22
  7.9 1.3 collective-permute-start.3
  9.2 2.2 %copy.167 = f32[5,8,48,128]{2,1,3,0:T(8,128)S(1)} copy(f32[5,8,48,128]{3,2,1,0:T(8,128)} %param.5) | data formatting | bytes 1966080 | tf_op args[0]
  11.6 2.6 %collective-permute-start = (f32[5,8,48,4]{2,1,3,0:T(8,128)S(1)}, f32[5,8,48,4]{2,1,3,0:T(8,128)S(1)}, u32[]{:S(2)}, u32[]{:S(2)}) collective-permute-start(f32[5,8,48,4]{2,1,3,0:T(8,128)S(1)} %get-tuple-element.24), channel_id=1, source_target_pairs={{4,0},{8,4},{12,8},{16,12},{20,16},{24,20},{28,24},{0,28},{5,1},{9... | collective-permute-start | bytes 92168 | tf_op jit(solution)/shard_map/ppermute | solution.py:25
  14.2 0.9 slice.569
  15.2 1.6 collective-permute-start.2
  16.8 1.0 slice_bitcast_fusion.2
  17.8 0.9 slice_bitcast_fusion.3
  18.9 1.0 copy.165
  19.9 2.3 %copy.172 = f32[5,8,4,128]{2,1,3,0:T(8,128)} copy(f32[5,8,4,128]{3,2,1,0:T(4,128)S(1)} %copy-done.17) | data formatting | bytes 163840 | tf_op args[1]
  22.2 0.9 fusion.78
  23.2 2.3 %copy.174 = f32[5,8,4,128]{2,1,3,0:T(8,128)} copy(f32[5,8,4,128]{3,1,2,0:T(8,128)S(1)} %reverse_multiply_fusion.1) | data formatting | bytes 163840 | tf_op jit(solution)/shard_map/mul | solution.py:96
  25.5 2.4 %fusion.149 = (f32[8,56,128]{1,0,2:T(8,128)S(1)}, f32[1,8,56,128]{2,1,3,0:T(8,128)}) fusion(f32[5,8,48,128]{2,1,3,0:T(8,128)S(1)} %copy.167, f32[5,8,4,128]{2,1,3,0:T(8,128)} %copy.174, f32[5,8,4,128]{2,1,3,0:T(8,128)} %copy.172), kind=kLoop, calls=%fused_computation.258 | loop fusion | flops 114688 | bytes 1605632 | tf_op jit(solution)/shard_map/squeeze | solution.py:78
  27.9 1.1 constant_dynamic-update-slice_fusion.3
  29.2 1.1 constant_dynamic-update-slice_fusion
  30.3 2.0 %fusion.184 = (f32[5,8,48,128]{3,2,1,0:T(8,128)}, f32[5,8,48,128]{3,2,1,0:T(8,128)}, f32[5,8,48,128]{3,2,1,0:T(8,128)}, f32[5,8,48,128]{3,2,1,0:T(8,128)}) fusion(f32[5,12,48,128]{3,2,1,0:T(8,128)S(1)} %constant_dynamic-update-slice_fusion), kind=kLoop, calls=%fused_computation.321 | loop fusion | bytes 7864320 | tf_op jit(solution)/shard_map/slice | solution.py:36
  32.3 0.8 fusion.182
  33.1 2.0 %fusion.183 = (f32[5,8,48,128]{3,2,1,0:T(8,128)}, f32[5,8,48,128]{3,2,1,0:T(8,128)}, f32[5,8,48,128]{3,2,1,0:T(8,128)}, f32[5,8,48,128]{3,2,1,0:T(8,128)}) fusion(f32[5,12,48,128]{3,2,1,0:T(8,128)S(1)} %get-tuple-element.44), kind=kLoop, calls=%fused_computation.320 | loop fusion | bytes 7864320 | tf_op jit(solution)/shard_map/slice | solution.py:36
  35.1 1.0 fusion.181
  36.1 3.2 %copy.216 = f32[5,8,48,128]{2,1,3,0:T(8,128)} copy(f32[5,8,48,128]{3,2,1,0:T(8,128)} %get-tuple-element.41) | data formatting | bytes 1966080
  39.2 3.0 %copy.217 = f32[5,8,48,128]{2,1,3,0:T(8,128)} copy(f32[5,8,48,128]{3,2,1,0:T(8,128)} %get-tuple-element.37) | data formatting | bytes 1966080
  42.3 3.1 %copy.214 = f32[5,8,48,128]{2,1,3,0:T(8,128)} copy(f32[5,8,48,128]{3,2,1,0:T(8,128)} %get-tuple-element.42) | data formatting | bytes 1966080
  45.4 3.0 %copy.215 = f32[5,8,48,128]{2,1,3,0:T(8,128)} copy(f32[5,8,48,128]{3,2,1,0:T(8,128)} %get-tuple-element.38) | data formatting | bytes 1966080
  48.4 3.0 %copy.212 = f32[5,8,48,128]{2,1,3,0:T(8,128)} copy(f32[5,8,48,128]{3,2,1,0:T(8,128)} %get-tuple-element.43) | data formatting | bytes 1966080
  51.4 3.1 %copy.213 = f32[5,8,48,128]{2,1,3,0:T(8,128)} copy(f32[5,8,48,128]{3,2,1,0:T(8,128)} %get-tuple-element.39) | data formatting | bytes 1966080
  54.5 3.1 %copy.210 = f32[5,8,48,128]{2,1,3,0:T(8,128)} copy(f32[5,8,48,128]{3,2,1,0:T(8,128)} %get-tuple-element.40) | data formatting | bytes 1966080
  57.6 3.0 %copy.211 = f32[5,8,48,128]{2,1,3,0:T(8,128)} copy(f32[5,8,48,128]{3,2,1,0:T(8,128)} %get-tuple-element.36) | data formatting | bytes 1966080
  60.6 10.6 %broadcast_multiply_fusion.1 = (f32[5,8,48,128]{2,1,3,0:T(8,128)}, f32[5,8,48,128]{2,1,3,0:T(8,128)}) fusion(f32[5,8,48,128]{2,1,3,0:T(8,128)} %copy.216, f32[5,8,48,128]{2,1,3,0:T(8,128)} %copy.217, f32[5,8,48,128]{2,1,3,0:T(8,128)} %copy.214, f32[5,8,48,128]{2,1,3,0:T(8,128)} %copy.215, f32[5,8,48,128]{2,1,3,0:T(8,128)} %copy.212, ...), kind=kLoop, calls=%fused_computation.147 | loop fusion | flops 2949120 | bytes 9830400 | tf_op jit(solution)/shard_map/mul | solution.py:69
  71.3 15.5 %multiply_add_fusion.2 = (f32[5,8,48,128]{2,1,3,0:T(8,128)S(1)}, f32[5,8,48,128]{2,1,3,0:T(8,128)S(1)}, f32[5,8,48,128]{2,1,3,0:T(8,128)}) fusion(f32[5,8,48,128]{2,1,3,0:T(8,128)} %get-tuple-element.13, f32[8,48,128]{1,0,2:T(8,128)} %get-tuple-element.27, f32[8,48,128]{1,0,2:T(8,128)} %get-tuple-element.26, f32[8,48,128]{1,0,2:T(8,128)} %copy.165, ...), kind=kLoop, calls=%fused_computation.142 | loop fusion | flops 10813440 | bytes 5730496 | tf_op jit(solution)/shard_map/add | solution.py:74
  86.8 2.5 %fusion.168 = f32[5,8,48,128]{2,1,3,0:T(8,128)} fusion(f32[5,8,48,128]{2,1,3,0:T(8,128)S(1)} %get-tuple-element.14, f32[5,8,48,128]{2,1,3,0:T(8,128)S(1)} %copy.167, f32[48]{0:T(128)S(1)} %get-tuple-element.48, f32[5,8,48,128]{2,1,3,0:T(8,128)S(1)} %copy-done.9, f32[5,8,48,128]{2,1,3,0:T(8,128)} %get-tuple-element.16, ...), kind=kLoop, calls=%fused_computation.295 | loop fusion | flops 294911 | bytes 1507520
  89.3 0.9 fusion.165
  90.2 2.1 %fusion.163 = f32[5,8,48,128]{2,1,3,0:T(8,128)} fusion(f32[5,8,48,128]{2,1,3,0:T(8,128)} %fusion.165, f32[5,8,48,128]{2,1,3,0:T(8,128)} %get-tuple-element.16, f32[5,8,48,128]{2,1,3,0:T(8,128)S(1)} %get-tuple-element.14, f32[5,8,48,128]{2,1,3,0:T(8,128)S(1)} %copy.167), kind=kLoop, calls=%fused_computation.282 | loop fusion | flops 196608 | bytes 1966080
  92.3 0.9 fusion.161
  93.2 1.9 %copy.224 = f32[1,8,48,128]{2,1,3,0:T(8,128)} copy(f32[1,8,48,128]{3,2,1,0:T(8,128)} %get-tuple-element.35) | data formatting | bytes 393216
  95.2 2.0 %copy.225 = f32[1,8,48,128]{2,1,3,0:T(8,128)} copy(f32[1,8,48,128]{3,2,1,0:T(8,128)} %get-tuple-element.31) | data formatting | bytes 393216
  97.1 1.9 %copy.222 = f32[1,8,48,128]{2,1,3,0:T(8,128)} copy(f32[1,8,48,128]{3,2,1,0:T(8,128)} %get-tuple-element.33) | data formatting | bytes 393216
  99.1 1.9 %copy.223 = f32[1,8,48,128]{2,1,3,0:T(8,128)} copy(f32[1,8,48,128]{3,2,1,0:T(8,128)} %get-tuple-element.29) | data formatting | bytes 393216
  101.0 1.0 copy.220
  102.0 1.9 %copy.221 = f32[1,8,48,128]{2,1,3,0:T(8,128)} copy(f32[1,8,48,128]{3,2,1,0:T(8,128)} %get-tuple-element.30) | data formatting | bytes 393216
  103.9 1.0 copy.218
  104.9 2.0 %copy.219 = f32[1,8,48,128]{2,1,3,0:T(8,128)} copy(f32[1,8,48,128]{3,2,1,0:T(8,128)} %get-tuple-element.28) | data formatting | bytes 393216
  106.9 6.5 %fusion.141 = f32[5,8,48,128]{2,1,3,0:T(8,128)} fusion(f32[5,8,48,128]{2,1,3,0:T(8,128)} %fusion.161, f32[8,56,128]{1,0,2:T(8,128)S(1)} %get-tuple-element.10, f32[8,48,136]{1,0,2:T(8,128)} %fusion.78, f32[5,8,48,128]{2,1,3,0:T(8,128)} %copy-done.7, f32[1,8,48,128]{2,1,3,0:T(8,128)} %copy.224, f32[1,8,48,128]{2,1,3,0:T(8,128)} %copy.225, ...), kind=kLoop, calls=%fused_computation.245 | loop fusion | flops 2605056 | bytes 13697440 | tf_op jit(solution)/shard_map/stack | solution.py:81
  113.5 2.8 %multiply_add_fusion.1 = f32[5,8,48,128]{2,1,3,0:T(8,128)S(1)} fusion(f32[5,8,48,128]{2,1,3,0:T(8,128)} %copy-done, f32[5,8,48,128]{2,1,3,0:T(8,128)} %fusion.141), kind=kLoop, calls=%fused_computation.141 | loop fusion | flops 491520 | bytes 2949120 | tf_op jit(solution)/shard_map/add | solution.py:111
  116.3 1.9 %fusion.179 = (f32[5,4,48,128]{2,1,3,0:T(4,128)}, f32[5,4,48,128]{2,1,3,0:T(4,128)}) fusion(f32[5,8,48,128]{2,1,3,0:T(8,128)S(1)} %multiply_add_fusion.1), kind=kLoop, calls=%fused_computation.316 | loop fusion | bytes 1966080 | tf_op jit(solution)/shard_map/slice | solution.py:25
  118.3 2.6 %collective-permute-start.5 = (f32[5,8,48,4]{2,1,3,0:T(8,128)S(1)}, f32[5,8,48,4]{2,1,3,0:T(8,128)S(1)}, u32[]{:S(2)}, u32[]{:S(2)}) collective-permute-start(f32[5,8,48,4]{2,1,3,0:T(8,128)S(1)} %get-tuple-element.17), channel_id=1, source_target_pairs={{4,0},{8,4},{12,8},{16,12},{20,16},{24,20},{28,24},{0,28},{5,1},{9... | collective-permute-start | bytes 92168 | tf_op jit(solution)/shard_map/ppermute | solution.py:25
  120.9 1.2 slice_bitcast_fusion
  122.1 2.5 %copy.204 = f32[5,4,48,128]{3,2,1,0:T(8,128)} copy(f32[5,4,48,128]{2,1,3,0:T(4,128)} %get-tuple-element.23) | data formatting | bytes 983040 | tf_op jit(solution)/shard_map/slice | solution.py:23
  124.6 5.4 %collective-permute-start.9 = (f32[5,4,48,128]{3,2,1,0:T(8,128)}, f32[5,4,48,128]{3,2,1,0:T(8,128)}, u32[]{:S(2)}, u32[]{:S(2)}) collective-permute-start(f32[5,4,48,128]{3,2,1,0:T(8,128)} %copy.204), channel_id=1, source_target_pairs={{0,1},{1,2},{2,3},{4,5},{5,6},{6,7},{8,9},{9,10},{10,11},{12,13},{... | collective-permute-start | bytes 1474568 | tf_op jit(solution)/shard_map/ppermute | solution.py:22
  129.9 2.5 %copy.202 = f32[5,4,48,128]{3,2,1,0:T(8,128)} copy(f32[5,4,48,128]{2,1,3,0:T(4,128)} %get-tuple-element.22) | data formatting | bytes 983040 | tf_op jit(solution)/shard_map/slice | solution.py:25
  132.5 1.5 collective-permute-start.8
  135.3 0.8 fusion.77
  136.2 3.1 %collective-permute-done.7 = f32[5,8,4,128]{3,1,2,0:T(8,128)S(1)} collective-permute-done((f32[5,8,4,128]{3,1,2,0:T(8,128)S(1)}, f32[5,8,4,128]{3,1,2,0:T(8,128)S(1)}, u32[]{:S(2)}, u32[]{:S(2)}) %collective-permute-start.7) | collective-permute-done | bytes 81952 | tf_op jit(solution)/shard_map/ppermute | solution.py:32
  139.3 2.3 %copy.201 = f32[5,8,4,128]{2,1,3,0:T(8,128)} copy(f32[5,8,4,128]{3,1,2,0:T(8,128)S(1)} %reverse_multiply_fusion) | data formatting | bytes 163840 | tf_op jit(solution)/shard_map/mul | solution.py:96
  141.7 1.4 fusion.113
  143.1 2.5 %copy.205 = f32[5,4,48,128]{2,1,3,0:T(4,128)} copy(f32[5,4,48,128]{3,2,1,0:T(8,128)} %collective-permute-done.9) | data formatting | bytes 983040 | tf_op jit(solution)/shard_map/ppermute | solution.py:22
  145.6 2.6 %copy.203 = f32[5,4,48,128]{2,1,3,0:T(4,128)} copy(f32[5,4,48,128]{3,2,1,0:T(8,128)} %collective-permute-done.8) | data formatting | bytes 983040 | tf_op jit(solution)/shard_map/ppermute | solution.py:25
  148.2 10.5 %broadcast_multiply_fusion = (f32[5,8,48,128]{2,1,3,0:T(8,128)}, f32[5,8,48,128]{2,1,3,0:T(8,128)}) fusion(f32[5,8,48,128]{2,1,3,0:T(8,128)S(1)} %multiply_add_fusion.1, f32[5,4,48,128]{2,1,3,0:T(4,128)} %copy.205, f32[5,4,48,128]{2,1,3,0:T(4,128)} %copy.203), kind=kLoop, calls=%fused_computation.146 | loop fusion | flops 4915200 | bytes 3932160 | tf_op jit(solution)/shard_map/mul | solution.py:69
  158.7 13.3 %multiply_add_fusion = (f32[5,8,48,128]{2,1,3,0:T(8,128)S(1)}, f32[5,8,48,128]{2,1,3,0:T(8,128)}, f32[5,8,48,128]{2,1,3,0:T(8,128)}) fusion(f32[5,8,48,128]{2,1,3,0:T(8,128)} %get-tuple-element.6, f32[8,48,128]{1,0,2:T(8,128)S(1)} %copy-done.13, f32[8,48,128]{1,0,2:T(8,128)S(1)} %copy-done.14, f32[8,48,128]{1,0,2:T(8,128)S(1)} %copy-done.12, ...), kind=kLoop, calls=%fused_computation.140 | loop fusion | flops 10813440 | bytes 5730496 | tf_op jit(solution)/shard_map/add | solution.py:74
  172.0 1.6 fusion.132
  174.3 1.4 fusion.127
  177.2 2.8 %fusion.105 = f32[5,8,48,128]{2,1,3,0:T(8,128)S(1)} fusion(f32[5,8,48,128]{2,1,3,0:T(8,128)S(1)} %fusion.125, f32[8,56,128]{1,0,2:T(8,128)S(1)} %fusion.113, f32[8,48,136]{1,0,2:T(8,128)S(1)} %copy-done.1, f32[5,8,48,128]{2,1,3,0:T(8,128)S(1)} %get-tuple-element.7, f32[5,8,48,128]{2,1,3,0:T(8,128)S(1)} %multiply_add_fusion.1, ...), kind=kLoop, calls=%fused_computation.183 | loop fusion | flops 2998272 | bytes 18023936 | tf_op jit(solution)/shard_map/stack | solution.py:81
  180.1 2.0 %add_multiply_fusion = f32[5,8,48,128]{2,1,3,0:T(8,128)S(1)} fusion(f32[5,8,48,128]{2,1,3,0:T(8,128)} %fusion.141, f32[5,8,48,128]{2,1,3,0:T(8,128)S(1)} %fusion.105), kind=kLoop, calls=%fused_computation.139 | loop fusion | flops 491520 | bytes 2949120 | tf_op jit(solution)/shard_map/mul | solution.py:113
  182.1 1.9 %copy.208 = f32[5,8,48,128]{3,2,1,0:T(8,128)} copy(f32[5,8,48,128]{2,1,3,0:T(8,128)S(1)} %add_multiply_fusion) | data formatting | bytes 1966080 | tf_op jit(solution)/shard_map/mul | solution.py:113
  (67 shorter events, 4.1 us)
Async XLA Ops:
  2.2 25.7 %collective-permute-start.4 = (f32[5,4,48,128]{3,2,1,0:T(8,128)}, f32[5,4,48,128]{3,2,1,0:T(8,128)}, u32[]{:S(2)}, u32[]{:S(2)}) collective-permute-start(f32[5,4,48,128]{3,2,1,0:T(8,128)} %get-tuple-element.46), channel_id=1, source_target_pairs={{0,1},{1,2},{2,3},{4,5},{5,6},{6,7},{8,9},{9,10},{10,11},{12,13},{... | collective-permute-start | bytes 1474568 | tf_op jit(solution)/shard_map/ppermute | solution.py:22
  7.9 21.2 %collective-permute-start.3 = (f32[5,4,48,128]{3,2,1,0:T(8,128)}, f32[5,4,48,128]{3,2,1,0:T(8,128)}, u32[]{:S(2)}, u32[]{:S(2)}) collective-permute-start(f32[5,4,48,128]{3,2,1,0:T(8,128)} %get-tuple-element.47), channel_id=1, source_target_pairs={{1,0},{2,1},{3,2},{5,4},{6,5},{7,6},{9,8},{10,9},{11,10},{13,12},{... | collective-permute-start | bytes 1474568 | tf_op jit(solution)/shard_map/ppermute | solution.py:25
  11.5 95.4 %copy-start = (f32[5,8,48,128]{2,1,3,0:T(8,128)}, f32[5,8,48,128]{2,1,3,0:T(8,128)S(1)}, u32[]{:S(2)}) copy-start(f32[5,8,48,128]{2,1,3,0:T(8,128)S(1)} %copy.167) | copy-start | bytes 2949124
  11.5 8.4 %copy-start.17 = (f32[5,8,4,128]{3,2,1,0:T(4,128)S(1)}, f32[5,8,4,128]{3,2,1,0:T(4,128)}, u32[]{:S(2)}) copy-start(f32[5,8,4,128]{3,2,1,0:T(4,128)} %param.6) | copy-start | bytes 245764
  11.5 10.7 %collective-permute-start.1 = (f32[5,8,48,4]{2,1,3,0:T(8,128)S(1)}, f32[5,8,48,4]{2,1,3,0:T(8,128)S(1)}, u32[]{:S(2)}, u32[]{:S(2)}) collective-permute-start(f32[5,8,48,4]{2,1,3,0:T(8,128)S(1)} %get-tuple-element.25), channel_id=1, source_target_pairs={{0,4},{4,8},{8,12},{12,16},{16,20},{20,24},{24,28},{28,0},{1,5},{5... | collective-permute-start | bytes 92168 | tf_op jit(solution)/shard_map/ppermute | solution.py:22
  11.6 10.6 %collective-permute-start = (f32[5,8,48,4]{2,1,3,0:T(8,128)S(1)}, f32[5,8,48,4]{2,1,3,0:T(8,128)S(1)}, u32[]{:S(2)}, u32[]{:S(2)}) collective-permute-start(f32[5,8,48,4]{2,1,3,0:T(8,128)S(1)} %get-tuple-element.24), channel_id=1, source_target_pairs={{4,0},{8,4},{12,8},{16,12},{20,16},{24,20},{28,24},{0,28},{5,1},{9... | collective-permute-start | bytes 92168 | tf_op jit(solution)/shard_map/ppermute | solution.py:25
  15.2 7.9 %collective-permute-start.2 = (f32[5,8,4,128]{3,1,2,0:T(8,128)S(1)}, f32[5,8,4,128]{3,1,2,0:T(8,128)S(1)}, u32[]{:S(2)}, u32[]{:S(2)}) collective-permute-start(f32[5,8,4,128]{3,1,2,0:T(8,128)S(1)} %copy.209), channel_id=1, source_target_pairs={{0,16},{4,20},{8,24},{12,28},{16,0},{20,4},{24,8},{28,12},{1,17},{... | collective-permute-start | bytes 245768 | tf_op jit(solution)/shard_map/ppermute | solution.py:32
  18.8 52.4 %copy-start.20 = (f32[48]{0:T(128)}, f32[48]{0:T(128)S(1)}, u32[]{:S(2)}) copy-start(f32[48]{0:T(128)S(1)} %sine_divide_fusion) | copy-start | bytes 580
  19.9 3.2 %copy-start.19 = (f32[5]{0:T(128)S(1)}, f32[5]{0:T(128)}, u32[]{:S(2)}) copy-start(f32[5]{0:T(128)} %constant.16.clone) | copy-start | bytes 64
  22.2 1.0 copy-start.15
  22.2 1.0 copy-start.16
  25.5 3.5 %copy-start.6 = (f32[5,8,48,128]{3,2,1,0:T(8,128)S(1)}, f32[5,8,48,128]{3,2,1,0:T(8,128)}, u32[]{:S(2)}) copy-start(f32[5,8,48,128]{3,2,1,0:T(8,128)} %param.5) | copy-start | bytes 2949124
  71.3 15.5 %copy-start.9 = (f32[5,8,48,128]{2,1,3,0:T(8,128)S(1)}, f32[5,8,48,128]{2,1,3,0:T(8,128)}, u32[]{:S(2)}) copy-start(f32[5,8,48,128]{2,1,3,0:T(8,128)} %get-tuple-element.12) | copy-start | bytes 2949124
  86.8 3.4 %copy-start.11 = (f32[5,8,48,128]{2,1,3,0:T(8,128)}, f32[5,8,48,128]{2,1,3,0:T(8,128)S(1)}, u32[]{:S(2)}) copy-start(f32[5,8,48,128]{2,1,3,0:T(8,128)S(1)} %get-tuple-element.15) | copy-start | bytes 2949124
  86.8 5.5 %copy-start.7 = (f32[5,8,48,128]{2,1,3,0:T(8,128)}, f32[5,8,48,128]{2,1,3,0:T(8,128)S(1)}, u32[]{:S(2)}) copy-start(f32[5,8,48,128]{2,1,3,0:T(8,128)S(1)} %get-tuple-element.14) | copy-start | bytes 2949124
  95.2 11.8 %copy-start.18 = (f32[8]{0:T(128)S(1)}, f32[8]{0:T(128)}, u32[]{:S(2)}) copy-start(f32[8]{0:T(128)} %param.7) | copy-start | bytes 100
  118.2 17.1 %collective-permute-start.6 = (f32[5,8,48,4]{2,1,3,0:T(8,128)S(1)}, f32[5,8,48,4]{2,1,3,0:T(8,128)S(1)}, u32[]{:S(2)}, u32[]{:S(2)}) collective-permute-start(f32[5,8,48,4]{2,1,3,0:T(8,128)S(1)} %get-tuple-element.18), channel_id=1, source_target_pairs={{0,4},{4,8},{8,12},{12,16},{16,20},{20,24},{24,28},{28,0},{1,5},{5... | collective-permute-start | bytes 92168 | tf_op jit(solution)/shard_map/ppermute | solution.py:22
  118.3 17.1 %collective-permute-start.5 = (f32[5,8,48,4]{2,1,3,0:T(8,128)S(1)}, f32[5,8,48,4]{2,1,3,0:T(8,128)S(1)}, u32[]{:S(2)}, u32[]{:S(2)}) collective-permute-start(f32[5,8,48,4]{2,1,3,0:T(8,128)S(1)} %get-tuple-element.17), channel_id=1, source_target_pairs={{4,0},{8,4},{12,8},{16,12},{20,16},{24,20},{28,24},{0,28},{5,1},{9... | collective-permute-start | bytes 92168 | tf_op jit(solution)/shard_map/ppermute | solution.py:25
  124.6 18.5 %collective-permute-start.9 = (f32[5,4,48,128]{3,2,1,0:T(8,128)}, f32[5,4,48,128]{3,2,1,0:T(8,128)}, u32[]{:S(2)}, u32[]{:S(2)}) collective-permute-start(f32[5,4,48,128]{3,2,1,0:T(8,128)} %copy.204), channel_id=1, source_target_pairs={{0,1},{1,2},{2,3},{4,5},{5,6},{6,7},{8,9},{9,10},{10,11},{12,13},{... | collective-permute-start | bytes 1474568 | tf_op jit(solution)/shard_map/ppermute | solution.py:22
  132.5 13.1 %collective-permute-start.8 = (f32[5,4,48,128]{3,2,1,0:T(8,128)}, f32[5,4,48,128]{3,2,1,0:T(8,128)}, u32[]{:S(2)}, u32[]{:S(2)}) collective-permute-start(f32[5,4,48,128]{3,2,1,0:T(8,128)} %copy.202), channel_id=1, source_target_pairs={{1,0},{2,1},{3,2},{5,4},{6,5},{7,6},{9,8},{10,9},{11,10},{13,12},{... | collective-permute-start | bytes 1474568 | tf_op jit(solution)/shard_map/ppermute | solution.py:25
  134.8 4.5 %collective-permute-start.7 = (f32[5,8,4,128]{3,1,2,0:T(8,128)S(1)}, f32[5,8,4,128]{3,1,2,0:T(8,128)S(1)}, u32[]{:S(2)}, u32[]{:S(2)}) collective-permute-start(f32[5,8,4,128]{3,1,2,0:T(8,128)S(1)} %copy.200), channel_id=1, source_target_pairs={{0,16},{4,20},{8,24},{12,28},{16,0},{20,4},{24,8},{28,12},{1,17},{... | collective-permute-start | bytes 245768 | tf_op jit(solution)/shard_map/ppermute | solution.py:32
  148.1 10.5 %copy-start.2 = (f32[5,8,4,128]{2,1,3,0:T(8,128)S(1)}, f32[5,8,4,128]{2,1,3,0:T(8,128)}, u32[]{:S(2)}) copy-start(f32[5,8,4,128]{2,1,3,0:T(8,128)} %copy.172) | copy-start | bytes 245764
  148.2 10.5 %copy-start.3 = (f32[5,8,4,128]{2,1,3,0:T(8,128)S(1)}, f32[5,8,4,128]{2,1,3,0:T(8,128)}, u32[]{:S(2)}) copy-start(f32[5,8,4,128]{2,1,3,0:T(8,128)} %copy.201) | copy-start | bytes 245764
  148.2 10.5 %copy-start.12 = (f32[8,48,128]{1,0,2:T(8,128)S(1)}, f32[8,48,128]{1,0,2:T(8,128)}, u32[]{:S(2)}) copy-start(f32[8,48,128]{1,0,2:T(8,128)} %get-tuple-element.19) | copy-start | bytes 589828
  148.2 10.5 %copy-start.13 = (f32[8,48,128]{1,0,2:T(8,128)S(1)}, f32[8,48,128]{1,0,2:T(8,128)}, u32[]{:S(2)}) copy-start(f32[8,48,128]{1,0,2:T(8,128)} %get-tuple-element.20) | copy-start | bytes 589828
  148.2 10.5 %copy-start.14 = (f32[8,48,128]{1,0,2:T(8,128)S(1)}, f32[8,48,128]{1,0,2:T(8,128)}, u32[]{:S(2)}) copy-start(f32[8,48,128]{1,0,2:T(8,128)} %get-tuple-element.21) | copy-start | bytes 589828
  148.2 10.5 %copy-start.21 = (f32[48]{0:T(128)S(1)}, f32[48]{0:T(128)}, u32[]{:S(2)}) copy-start(f32[48]{0:T(128)} %copy-done.20) | copy-start | bytes 580
  172.0 2.2 %copy-start.10 = (f32[5,8,48,128]{2,1,3,0:T(8,128)S(1)}, f32[5,8,48,128]{2,1,3,0:T(8,128)}, u32[]{:S(2)}) copy-start(f32[5,8,48,128]{2,1,3,0:T(8,128)} %get-tuple-element.8) | copy-start | bytes 2949124
  174.2 2.1 %copy-start.8 = (f32[5,8,48,128]{2,1,3,0:T(8,128)S(1)}, f32[5,8,48,128]{2,1,3,0:T(8,128)}, u32[]{:S(2)}) copy-start(f32[5,8,48,128]{2,1,3,0:T(8,128)} %get-tuple-element.5) | copy-start | bytes 2949124
  174.3 2.1 %copy-start.1 = (f32[8,48,136]{1,0,2:T(8,128)S(1)}, f32[8,48,136]{1,0,2:T(8,128)}, u32[]{:S(2)}) copy-start(f32[8,48,136]{1,0,2:T(8,128)} %fusion.77) | copy-start | bytes 626692
  174.3 2.5 %copy-start.4 = (f32[5,4,48,128]{2,1,3,0:T(4,128)S(1)}, f32[5,4,48,128]{2,1,3,0:T(4,128)}, u32[]{:S(2)}) copy-start(f32[5,4,48,128]{2,1,3,0:T(4,128)} %copy.205) | copy-start | bytes 1474564
  174.3 2.9 %copy-start.5 = (f32[5,4,48,128]{2,1,3,0:T(4,128)S(1)}, f32[5,4,48,128]{2,1,3,0:T(4,128)}, u32[]{:S(2)}) copy-start(f32[5,4,48,128]{2,1,3,0:T(4,128)} %copy.203) | copy-start | bytes 1474564
where the time goes:
time: 185 us; the launch traced here: 184 us
  other arithmetic  81.8 us (44%)
  local copies, waits for them, and re-layouts  77.3 us (42%)
  starting transfers between devices  21.4 us (12%)
  waiting for transfers between devices  3.11 us (2%)
    unnamed x64, local copies, waits for them, and re-layouts  45.8 us
    add x2, other arithmetic, tendency(): wind_lon * slope_lon + wind_row * slope_row + wind_level * slope_level  28.8 us
    mul x2, other arithmetic, tendency(): slope_level = radial_ratio * first_derivative(pad_level, levels, 1)  21.1 us
    ppermute x4, starting transfers between devices, with_halo(): lax.ppermute(lax.slice_in_dim(block, block.shape[dim] - width, None, axis...  11.2 us
    unnamed x8, other arithmetic  9.68 us
    another operation x2, other arithmetic, tendency(): jnp.stack([-carried[0] - spread, -carried[1] - temper * slope_lon[0] - sl...  9.36 us
    ppermute x4, starting transfers between devices, with_halo(): lax.ppermute(lax.slice_in_dim(block, 0, width, axis=dim), axis, backward)  8.04 us
    slice x4, local copies, waits for them, and re-layouts, window(): return lax.slice_in_dim(padded, offset, offset + length, axis=axis)  5.82 us
  transfers between devices with their start and end apart: 10, of which 1 were waited for; matrix products, arithmetic and copies ran while one was open for 16% of the time, Pallas kernels for 0%

commit v1 on v0

v1 whole, which is shorter than its diff:
```python
import functools
import math

import jax
import jax.numpy as jnp
import numpy as np
from jax import lax
from jax.experimental import pallas as pl
from jax.experimental.pallas import tpu as pltpu
from jax.sharding import PartitionSpec as P

first_coeffs = (0.8, -0.2, 4.0 / 105.0, -1.0 / 280.0)
second_coeffs = (-205.0 / 72.0, 1.6, -0.2, 8.0 / 315.0, -1.0 / 560.0)
time_step = 0.002
gamma_less_one = 0.4
radial_ratio = 3.0
FIELDS = 5
REACH = 4
TILE = 8
LANES = 128
GROUPS = LANES // (2 * REACH)
signs = (1.0, -1.0, -1.0, 1.0, 1.0)
first_whole = (672.0, -168.0, 32.0, -3.0)
second_whole = (8064.0, -1008.0, 128.0, -9.0)

level_first = tuple(radial_ratio * c for c in first_coeffs)
level_second = tuple(radial_ratio * radial_ratio * c for c in second_coeffs)

VMEM = pl.BlockSpec(memory_space=pltpu.VMEM)
SMEM = pl.BlockSpec(memory_space=pltpu.SMEM)
ANY = pl.BlockSpec(memory_space=pl.ANY)


def held(x):
    return pltpu.with_memory_space_constraint(x, pltpu.VMEM)


def in_vmem(*shape):
    return pltpu.VMEM(shape, jnp.float32)


def stencil_matrix(width):
    matrix = np.zeros((2 * width, 2 * width), np.float32)
    for out in range(width):
        for k in range(1, REACH + 1):
            for sign in (1, -1):
                at = out + sign * k
                if 0 <= at < width:
                    row = at
                elif at < 0:
                    row = width + REACH + at
                else:
                    row = width + REACH + (at - width)
                matrix[row, out] = sign * first_whole[k - 1]
                matrix[row, width + out] = second_whole[k - 1]
    return jnp.asarray(matrix, jnp.bfloat16)


def geometry(rows, nlon, width):
    theta = (np.arange(rows) + 0.5) * (2.0 * math.pi / nlon)
    metric = 1.0 / np.sin(theta)
    table = np.stack([metric / 840.0, metric * metric / 5040.0, np.cos(theta) * metric])
    return jnp.asarray(np.broadcast_to(table[:, :, None], (3, rows, width)), jnp.float32)


def packed(tiles, lane):
    total = None
    for g, tile in enumerate(tiles):
        moved = pltpu.roll(tile, (REACH + 2 * REACH * g) % LANES, 1)
        if total is None:
            total = moved
        else:
            total = jnp.where(lane >= 2 * REACH * g, moved, total)
    return total


def across_level(center_wind, center_temper, halo, kappa, above):
    out = [[None] * REACH for _ in range(FIELDS)]
    for a in range(REACH):
        slopes = []
        for f in range(FIELDS):
            total = None
            for b in range(REACH):
                k = b + REACH - a if above else a + REACH - b
                if 1 <= k <= REACH:
                    c = level_first[k - 1] if above else -level_first[k - 1]
                    term = c * halo[f][b]
                    total = term if total is None else total + term
            slopes.append(total)
        curve = None
        for b in range(REACH):
            k = b + REACH - a if above else a + REACH - b
            if 1 <= k <= REACH:
                term = level_second[k] * halo[4][b]
                curve = term if curve is None else curve + term
        wind, temper = center_wind[a], center_temper[a]
        out[0][a] = -wind * slopes[0] - slopes[3]
        out[1][a] = -wind * slopes[1]
        out[2][a] = -wind * slopes[2]
        out[3][a] = -wind * slopes[3] - temper * slopes[0] - slopes[4]
        out[4][a] = -wind * slopes[4] - (gamma_less_one * temper) * slopes[3] + kappa[a] * curve
    return out


def edges_kernel(levels, rows, state, outer, kappa, padded, low, high, edge, polar, sems, outer_sem):
    block = REACH * rows
    copies = []
    for f in range(FIELDS):
        copies.append(pltpu.make_async_copy(state.at[f], padded.at[f, :, pl.ds(TILE, rows)], sems.at[f]))
        copies[-1].start()
    last = pltpu.make_async_copy(outer, padded.at[:, :, pl.ds(TILE + rows, REACH)], outer_sem)
    last.start()
    for i in range(REACH):
        low[pl.ds(FIELDS * block + i, 1), :] = jnp.full((1, LANES), kappa[i], jnp.float32)
        high[pl.ds(FIELDS * block + i, 1), :] = jnp.full((1, LANES), kappa[levels - REACH + i], jnp.float32)
    low[pl.ds(FIELDS * block + REACH, REACH), :] = jnp.ones((REACH, LANES), jnp.float32)
    high[pl.ds(FIELDS * block + REACH, REACH), :] = jnp.ones((REACH, LANES), jnp.float32)
    lane = lax.broadcasted_iota(jnp.int32, (TILE, LANES), 1)
    for f in range(FIELDS):
        copies[f].wait()
        for l in range(REACH):
            low[pl.ds(f * block + l * rows, rows), :] = padded[f, l, pl.ds(TILE, rows), :]
            high[pl.ds(f * block + l * rows, rows), :] = padded[f, levels - REACH + l, pl.ds(TILE, rows), :]
        pack_edges(f, levels, rows, padded, edge, polar, lane)
    last.wait()


def pack_edges(f, levels, rows, padded, edge, polar, lane):
    per = GROUPS // levels
    for j in range(rows // TILE // per):
        tiles = [
            padded[f, l, pl.ds(TILE + (j * per + u) * TILE, TILE), :]
            for u in range(per)
            for l in range(levels)
        ]
        at = (f * (rows // TILE // per) + j) * TILE
        edge[pl.ds(at, TILE), :] = packed(tiles, lane)
    for l in range(levels):
        for i in range(REACH):
            row = padded[f, l, pl.ds(TILE + REACH - 1 - i, 1), :]
            polar[pl.ds((f * levels + l) * REACH + i, 1), :] = signs[f] * row


def longitude_slopes(levels, rows, padded, left, right, matrix, dlon, elon):
    lane = lax.broadcasted_iota(jnp.int32, (TILE, LANES), 1)
    from_left = (lane % (2 * REACH)) < REACH
    per = GROUPS // levels
    packs = rows // TILE // per
    for f in range(FIELDS):
        halos = [[None] * (rows // TILE) for _ in range(levels)]
        for j in range(packs):
            at = pl.ds((f * packs + j) * TILE, TILE)
            both = jnp.where(from_left, left[at, :], right[at, :])
            for u in range(per):
                for l in range(levels):
                    g = u * levels + l
                    halos[l][j * per + u] = pltpu.roll(both, (LANES - 2 * REACH * g) % LANES, 1)
        x = padded[f, :, pl.ds(TILE, rows), :].reshape(levels * rows, LANES)
        h = jnp.concatenate([halos[l][t] for l in range(levels) for t in range(rows // TILE)], axis=0)
        x = jnp.concatenate([x, h], axis=1)
        width = 2 * LANES if f == 4 else LANES
        m = matrix[:, pl.ds(0, width)]
        total = None
        for piece in range(3):
            part = x.astype(jnp.bfloat16)
            if piece < 2:
                x = x - part.astype(jnp.float32)
            term = jnp.dot(part, m, preferred_element_type=jnp.float32)
            total = term if total is None else total + term
        dlon[f] = total[:, :LANES].reshape(levels, rows, LANES)
        if f == 4:
            elon[...] = total[:, LANES:].reshape(levels, rows, LANES)


def interior(levels, rows, padded, dlon, elon, geo, kappa, store):
    def body(t, carry):
        r0 = pl.multiple_of(t * TILE, TILE)
        here = pl.ds(r0, TILE)
        metric = geo[0, here, :]
        metric2 = geo[1, here, :]
        curvature = geo[2, here, :]
        center = [[padded[f, l, pl.ds(r0 + TILE, TILE), :] for l in range(levels)] for f in range(FIELDS)]
        out = [[None] * levels for _ in range(FIELDS)]
        for l in range(levels):
            wlon, wrow, wlev, temper = (center[f][l] for f in (1, 2, 3, 4))
            slon, srow, slev = [], [], []
            for f in range(FIELDS):
                slon.append(metric * dlon[f, l, here, :])
                total = None
                for k in range(1, REACH + 1):
                    ahead = padded[f, l, pl.ds(r0 + TILE + k, TILE), :]
                    behind = padded[f, l, pl.ds(r0 + TILE - k, TILE), :]
                    term = first_coeffs[k - 1] * (ahead - behind)
                    total = term if total is None else total + term
                    if f == 4:
                        curve = second_coeffs[k] * (ahead + behind)
                        bend = curve if k == 1 else bend + curve
                srow.append(total)
                total = None
                for k in range(1, REACH + 1):
                    up = center[f][l + k] if l + k < levels else None
                    down = center[f][l - k] if l - k >= 0 else None
                    if up is not None and down is not None:
                        term = level_first[k - 1] * (up - down)
                    elif up is not None:
                        term = level_first[k - 1] * up
                    elif down is not None:
                        term = -level_first[k - 1] * down
                    else:
                        continue
                    total = term if total is None else total + term
                slev.append(total)
            lift = None
            for k in range(1, REACH + 1):
                near = [center[4][l + s * k] for s in (1, -1) if 0 <= l + s * k < levels]
                if near:
                    term = level_second[k] * (near[0] + near[1] if len(near) == 2 else near[0])
                    lift = term if lift is None else lift + term
            middle = second_coeffs[0]
            laplace = metric2 * (elon[l, here, :] + (5040.0 * middle) * temper) + bend
            laplace = laplace + (middle + level_second[0]) * temper + lift
            carried = [wlon * slon[f] + wrow * srow[f] + wlev * slev[f] for f in range(FIELDS)]
            spread = slon[1] + srow[2] + slev[3] + curvature * wrow
            out[0][l] = -carried[0] - spread
            out[1][l] = -carried[1] - temper * slon[0] - slon[4]
            out[2][l] = -carried[2] - temper * srow[0] - srow[4]
            out[3][l] = -carried[3] - temper * slev[0] - slev[4]
            out[4][l] = -carried[4] - (gamma_less_one * temper) * spread + kappa[l] * laplace
            for f in range(FIELDS):
                store(f, l, r0, center[f][l], out[f][l])
        return carry

    lax.fori_loop(0, rows // TILE, body, 0)


def fill_polar(levels, padded, polar):
    for f in range(FIELDS):
        for l in range(levels):
            padded[f, l, pl.ds(TILE - REACH, REACH), :] = polar[pl.ds((f * levels + l) * REACH, REACH), :]


def first_kernel(levels, rows, given, polar, left, right, matrix, geo, kappa, padded, rate, low, high, dlon, elon):
    fill_polar(levels, padded, polar)
    longitude_slopes(levels, rows, padded, left, right, matrix, dlon, elon)

    def store(f, l, r0, value, tendency):
        rate[f, l, pl.ds(r0, TILE), :] = tendency
        ahead = value + time_step * tendency
        if l < REACH:
            low[pl.ds((f * REACH + l) * rows + r0, TILE), :] = ahead
        if l >= levels - REACH:
            high[pl.ds((f * REACH + l - levels + REACH) * rows + r0, TILE), :] = ahead

    interior(levels, rows, padded, dlon, elon, geo, kappa, store)


def halo_tile(ref, rows, r0):
    return [
        [ref[pl.ds((f * REACH + b) * rows + r0, TILE), :] for b in range(REACH)] for f in range(FIELDS)
    ]


def section_kernel(levels, rows, padded, rate, below, above, kappa, full, ahead, edge, polar):
    def body(t, carry):
        r0 = pl.multiple_of(t * TILE, TILE)
        for halo_ref, at, up in ((below, 0, False), (above, levels - REACH, True)):
            halo = halo_tile(halo_ref, rows, r0)
            center = [
                [padded[f, at + a, pl.ds(r0 + TILE, TILE), :] for a in range(REACH)] for f in range(FIELDS)
            ]
            extra = across_level(center[3], center[4], halo, [kappa[at + a] for a in range(REACH)], up)
            for f in range(FIELDS):
                for a in range(REACH):
                    total = rate[f, at + a, pl.ds(r0, TILE), :] + extra[f][a]
                    full[f, at + a, pl.ds(r0, TILE), :] = total
                    ahead[f, at + a, pl.ds(r0 + TILE, TILE), :] = center[f][a] + time_step * total
        return carry

    lax.fori_loop(0, rows // TILE, body, 0)
    lane = lax.broadcasted_iota(jnp.int32, (TILE, LANES), 1)
    for f in range(FIELDS):
        pack_edges(f, levels, rows, ahead, edge, polar, lane)
        for l in range(levels):
            ahead[f, l, pl.ds(rows + TILE, REACH), :] = padded[f, l, pl.ds(rows + TILE, REACH), :]


def second_kernel(
    levels, rows, given, polar, left, right, matrix, geo, kappa, full, start, below, above,
    padded, both, low, high, dlon, elon,
):
    fill_polar(levels, padded, polar)
    longitude_slopes(levels, rows, padded, left, right, matrix, dlon, elon)

    def store(f, l, r0, value, tendency):
        at = pl.ds(r0, TILE)
        both[f, l, at, :] = (0.5 * time_step) * (full[f, l, at, :] + tendency)

    interior(levels, rows, padded, dlon, elon, geo, kappa, store)
    tail = FIELDS * REACH * rows

    def body(t, carry):
        r0 = pl.multiple_of(t * TILE, TILE)
        for halo_ref, out, at, up in ((below, low, 0, True), (above, high, levels - REACH, False)):
            beyond = halo_tile(halo_ref, rows, r0)
            mine = [
                [start[f, at + a, pl.ds(r0 + TILE, TILE), :] for a in range(REACH)] for f in range(FIELDS)
            ]
            kappas = [halo_ref[pl.ds(tail + a, 1), :] for a in range(REACH)]
            there = time_step * halo_ref[pl.ds(tail + REACH, 1), :]
            extra = across_level(beyond[3], beyond[4], mine, kappas, up)
            for f in range(FIELDS):
                for a in range(REACH):
                    out[pl.ds((f * REACH + a) * rows + r0, TILE), :] = there * extra[f][a]
        return carry

    lax.fori_loop(0, rows // TILE, body, 0)


def last_kernel(levels, rows, padded, both, below, above, low, high, kappa, out):
    def body(t, carry):
        r0 = pl.multiple_of(t * TILE, TILE)
        for halo_ref, more_ref, at, up in ((below, low, 0, False), (above, high, levels - REACH, True)):
            halo = halo_tile(halo_ref, rows, r0)
            more = halo_tile(more_ref, rows, r0)
            halo = [[halo[f][b] + more[f][b] for b in range(REACH)] for f in range(FIELDS)]
            wind = [padded[3, at + a, pl.ds(r0 + TILE, TILE), :] for a in range(REACH)]
            temper = [padded[4, at + a, pl.ds(r0 + TILE, TILE), :] for a in range(REACH)]
            extra = across_level(wind, temper, halo, [kappa[at + a] for a in range(REACH)], up)
            for f in range(FIELDS):
                for a in range(REACH):
                    old = both[f, at + a, pl.ds(r0, TILE), :]
                    out[f, at + a, pl.ds(r0, TILE), :] = old + (0.5 * time_step) * extra[f][a]
        return carry

    lax.fori_loop(0, rows // TILE, body, 0)


def on_device(state, outer_rows, kappa):
    levels, rows, width = state.shape[1:]
    ring, depth = lax.axis_size("lon"), lax.axis_size("rad")
    assert width == LANES and levels >= 2 * REACH and GROUPS % levels == 0
    assert rows % (TILE * (GROUPS // levels)) == 0
    matrix = stencil_matrix(width)
    geo = geometry(rows, width * ring, width)
    halo_rows = FIELDS * REACH * rows
    packs = FIELDS * levels * rows // GROUPS
    pad_shape = (FIELDS, levels, rows + 2 * TILE, width)
    full_shape = (FIELDS, levels, rows, width)

    def call(kernel, out_shape, in_specs, args, scratch=(), aliases=None, flops=0, name=None):
        args = [held(a) if s is VMEM else a for s, a in zip(in_specs, args)]
        return pl.pallas_call(
            functools.partial(kernel, levels, rows),
            out_shape=out_shape,
            in_specs=list(in_specs),
            out_specs=jax.tree.map(lambda _: VMEM, out_shape),
            scratch_shapes=list(scratch),
            input_output_aliases=aliases or {},
            cost_estimate=pl.CostEstimate(flops=flops, bytes_accessed=0, transcendentals=0),
            compiler_params=pltpu.CompilerParams(vmem_limit_bytes=16 * 2**20),
            name=name,
        )(*args)

    east = [(i, (i + 1) % ring) for i in range(ring)]
    west = [(b, a) for a, b in east]
    half = [(i, (i + ring // 2) % ring) for i in range(ring)]
    up = [(i, i + 1) for i in range(depth - 1)]
    down = [(b, a) for a, b in up]

    def around(edge, polar):
        left = lax.ppermute(edge, "lon", east)
        right = lax.ppermute(edge, "lon", west)
        return left, right, lax.ppermute(polar, "lon", half)

    padded, low, high, edge, polar = call(
        edges_kernel,
        [
            in_vmem(*pad_shape),
            in_vmem(halo_rows + TILE, width),
            in_vmem(halo_rows + TILE, width),
            in_vmem(packs, width),
            in_vmem(FIELDS * levels * REACH, width),
        ],
        (ANY, ANY, SMEM),
        (state, outer_rows, kappa),
        scratch=(pltpu.SemaphoreType.DMA((FIELDS,)), pltpu.SemaphoreType.DMA),
        name="edges",
    )
    below = lax.ppermute(high, "rad", up)
    above = lax.ppermute(low, "rad", down)
    left, right, beyond = around(edge, polar)
    lon_scratch = (in_vmem(*full_shape), in_vmem(*full_shape[1:]))
    padded, rate, low2, high2 = call(
        first_kernel,
        [in_vmem(*pad_shape), in_vmem(*full_shape), in_vmem(halo_rows, width), in_vmem(halo_rows, width)],
        (VMEM,) * 6 + (SMEM,),
        (padded, beyond, left, right, matrix, geo, kappa),
        scratch=lon_scratch,
        aliases={0: 0},
        name="first",
    )
    below2 = lax.ppermute(high2, "rad", up)
    above2 = lax.ppermute(low2, "rad", down)
    full, ahead, edge, polar = call(
        section_kernel,
        [
            in_vmem(*full_shape),
            in_vmem(*pad_shape),
            in_vmem(packs, width),
            in_vmem(FIELDS * levels * REACH, width),
        ],
        (VMEM,) * 4 + (SMEM,),
        (padded, rate, below, above, kappa),
        name="section",
    )
    left, right, beyond = around(edge, polar)
    ahead, both, low, high = call(
        second_kernel,
        [in_vmem(*pad_shape), in_vmem(*full_shape), in_vmem(halo_rows, width), in_vmem(halo_rows, width)],
        (VMEM,) * 6 + (SMEM,) + (VMEM,) * 4,
        (ahead, beyond, left, right, matrix, geo, kappa, full, padded, below, above),
        scratch=lon_scratch,
        aliases={0: 0},
        name="second",
    )
    return call(
        last_kernel,
        jax.ShapeDtypeStruct(full_shape, jnp.float32),
        (VMEM,) * 6 + (SMEM,),
        (ahead, both, below2, above2, low, high, kappa),
        name="last",
    )


def solution(mesh):
    placed = (P(None, "rad", None, "lon"), P(None, "rad", None, "lon"), P("rad"))
    return jax.shard_map(
        on_device,
        mesh=mesh,
        in_specs=placed,
        out_specs=P(None, "rad", None, "lon"),
        check_vma=False,
    )
```

time: 185 us -> 42.2 us (0.23)
  other arithmetic: 81.8 us -> 0 us
  local copies, waits for them, and re-layouts: 77.3 us -> 4.54 us
  Pallas kernels: 0 us -> 11 us
  waiting for transfers between devices: 3.11 us -> 10.2 us
  starting transfers between devices: 21.4 us -> 16 us
    unnamed x64 -> x12, local copies, waits for them, and re-layouts: 45.8 us -> 4.54 us
    add x3 -> x0, other arithmetic: 31.6 us -> none  [the longest x2 28.8 us: tendency(): wind_lon * slope_lon + wind_row * slope_row + wind_level * slope_level]
    mul x8 -> x0, other arithmetic: 25.6 us -> none  [the longest x2 21.1 us: tendency(): slope_level = radial_ratio * first_derivative(pad_level, levels, 1)]
    slice x12 -> x0, local copies, waits for them, and re-layouts: 16.7 us -> none  [the longest x4 5.82 us: window(): return lax.slice_in_dim(padded, offset, offset + length, axis=axis)]
    pallas_call x0 -> x5, Pallas kernels: none -> 11 us  [call(): pl.pallas_call(functools.partial(kernel, levels, rows), out_shape=out_sha...]
    unnamed x8 -> x0, other arithmetic: 9.68 us -> none
    another operation x2 -> x0, other arithmetic: 9.36 us -> none  [tendency(): jnp.stack([-carried[0] - spread, -carried[1] - temper * slope_lon[0] - sl...]
    mul x5 -> x0, local copies, waits for them, and re-layouts: 8.52 us -> none  [the longest x2 4.67 us: neighbours(): across[:, :, ::-1, :] * flip_signs]
  transfers between devices with their start and end apart: 10 -> 10, of which waited for: 1 -> 5; matrix products, arithmetic and copies ran while one was open for 16% -> 0% of each run, Pallas kernels for 0% -> 18%
where the time goes in v1:
time: 42.2 us; the launch traced here: 41.9 us
  starting transfers between devices  16 us (38%)
  Pallas kernels  11 us (26%)
  waiting for transfers between devices  10.2 us (24%)
  local copies, waits for them, and re-layouts  4.54 us (11%)
    pallas_call x5, Pallas kernels, call(): pl.pallas_call(functools.partial(kernel, levels, rows), out_shape=out_sha...  11 us
    ppermute x1, starting transfers between devices, on_device(): below = lax.ppermute(high, 'rad', up)  4.96 us
    ppermute x2, waiting for transfers between devices, around(): left = lax.ppermute(edge, 'lon', east)  4.91 us
    unnamed x12, local copies, waits for them, and re-layouts  4.54 us
    ppermute x1, starting transfers between devices, on_device(): below2 = lax.ppermute(high2, 'rad', up)  4.3 us
    ppermute x2, waiting for transfers between devices, around(): right = lax.ppermute(edge, 'lon', west)  3.47 us
    ppermute x2, starting transfers between devices, around(): return (left, right, lax.ppermute(polar, 'lon', half))  3.18 us
    ppermute x1, waiting for transfers between devices, on_device(): above2 = lax.ppermute(low2, 'rad', down)  1.79 us
  transfers between devices with their start and end apart: 10, of which 5 were waited for; matrix products, arithmetic and copies ran while one was open for 0% of the time, Pallas kernels for 18%

profile of v1, /device:TPU:0, one launch (start us, length us, event | category | flops | bytes accessed | tf_op | source)
XLA Modules:
  0.0 41.9 jit_solution(16639807719574007614)
XLA Ops:
  0.0 0.0 copy-start
  0.0 1.2 %copy-done = f32[5,8,48,128]{3,2,1,0:T(8,128)S(1)} copy-done((f32[5,8,48,128]{3,2,1,0:T(8,128)S(1)}, f32[5,8,48,128]{3,2,1,0:T(8,128)}, u32[]{:S(2)}) %copy-start) | copy-done | bytes 983064
  1.2 0.0 copy-start.4
  1.2 0.9 %copy-done.4 = f32[5,8,4,128]{3,2,1,0:T(4,128)S(1)} copy-done((f32[5,8,4,128]{3,2,1,0:T(4,128)S(1)}, f32[5,8,4,128]{3,2,1,0:T(4,128)}, u32[]{:S(2)}) %copy-start.4) | copy-done | bytes 81944
  2.1 0.0 copy-start.5
  2.1 0.7 %copy-done.5 = f32[8]{0:T(128)S(1)} copy-done((f32[8]{0:T(128)S(1)}, f32[8]{0:T(128)}, u32[]{:S(2)}) %copy-start.5) | copy-done | bytes 56
  2.7 1.4 %edges.1 = (f32[5,8,64,128]{3,2,1,0:T(8,128)S(1)}, f32[968,128]{1,0:T(8,128)S(1)}, f32[968,128]{1,0:T(8,128)S(1)}, f32[120,128]{1,0:T(8,128)S(1)}, f32[160,128]{1,0:T(8,128)S(1)}) custom-call(f32[5,8,48,128]{3,2,1,0:T(8,128)S(1)} %copy-done, f32[5,8,4,128]{3,2,1,0:T(4,128)S(1)} %copy-done.4, f32[8]{0:T(128)S(1)} %copy-done.5), custom_call_target="tpu_custom_call" | custom-call | tf_op jit(solution)/shard_map/edges/pallas_call | solution.py:352
  4.2 5.0 %collective-permute-start.3 = (f32[968,128]{1,0:T(8,128)S(1)}, f32[968,128]{1,0:T(8,128)S(1)}, u32[]{:S(2)}, u32[]{:S(2)}) collective-permute-start(f32[968,128]{1,0:T(8,128)S(1)} %get-tuple-element.27), channel_id=1, source_target_pairs={{0,1},{1,2},{2,3},{4,5},{5,6},{6,7},{8,9},{9,10},{10,11},{12,13},{... | collective-permute-start | bytes 1486856 | tf_op jit(solution)/shard_map/ppermute | solution.py:389
  9.1 1.3 %collective-permute-start.4 = (f32[968,128]{1,0:T(8,128)S(1)}, f32[968,128]{1,0:T(8,128)S(1)}, u32[]{:S(2)}, u32[]{:S(2)}) collective-permute-start(f32[968,128]{1,0:T(8,128)S(1)} %get-tuple-element.28), channel_id=1, source_target_pairs={{1,0},{2,1},{3,2},{5,4},{6,5},{7,6},{9,8},{10,9},{11,10},{13,12},{... | collective-permute-start | bytes 1486856 | tf_op jit(solution)/shard_map/ppermute | solution.py:390
  10.4 1.6 %collective-permute-start = (f32[160,128]{1,0:T(8,128)S(1)}, f32[160,128]{1,0:T(8,128)S(1)}, u32[]{:S(2)}, u32[]{:S(2)}) collective-permute-start(f32[160,128]{1,0:T(8,128)S(1)} %get-tuple-element.23), channel_id=1, source_target_pairs={{0,16},{4,20},{8,24},{12,28},{16,0},{20,4},{24,8},{28,12},{1,17},{... | collective-permute-start | bytes 245768 | tf_op jit(solution)/shard_map/ppermute | solution.py:373
  12.0 0.3 collective-permute-start.2
  12.3 0.2 collective-permute-start.1
  12.5 1.7 %collective-permute-done.2.right = f32[120,128]{1,0:T(8,128)S(1)} collective-permute-done((f32[120,128]{1,0:T(8,128)S(1)}, f32[120,128]{1,0:T(8,128)S(1)}, u32[]{:S(2)}, u32[]{:S(2)}) %collective-permute-start.2) | collective-permute-done | bytes 61472 | tf_op jit(solution)/shard_map/ppermute | solution.py:372
  14.2 2.7 %collective-permute-done.1.left = f32[120,128]{1,0:T(8,128)S(1)} collective-permute-done((f32[120,128]{1,0:T(8,128)S(1)}, f32[120,128]{1,0:T(8,128)S(1)}, u32[]{:S(2)}, u32[]{:S(2)}) %collective-permute-start.1) | collective-permute-done | bytes 61472 | tf_op jit(solution)/shard_map/ppermute | solution.py:371
  16.9 0.0 collective-permute-done.polar
  16.9 0.0 copy-start.1
  16.9 0.9 %copy-done.1 = bf16[256,256]{1,0:T(8,128)(2,1)S(1)} copy-done((bf16[256,256]{1,0:T(8,128)(2,1)S(1)}, bf16[256,256]{1,0:T(8,128)(2,1)}, u32[]{:S(2)}) %copy-start.1) | copy-done | bytes 131096
  17.8 0.0 copy-start.2
  17.8 0.9 %copy-done.2 = f32[3,48,128]{2,1,0:T(8,128)S(1)} copy-done((f32[3,48,128]{2,1,0:T(8,128)S(1)}, f32[3,48,128]{2,1,0:T(8,128)}, u32[]{:S(2)}) %copy-start.2) | copy-done | bytes 73752
  18.7 3.0 %first.1 = (f32[5,8,64,128]{3,2,1,0:T(8,128)S(1)}, f32[5,8,48,128]{3,2,1,0:T(8,128)S(1)}, f32[960,128]{1,0:T(8,128)S(1)}, f32[960,128]{1,0:T(8,128)S(1)}) custom-call(f32[5,8,64,128]{3,2,1,0:T(8,128)S(1)} %get-tuple-element.22.given, f32[160,128]{1,0:T(8,128)S(1)} %collective-permute-done.polar, ...), custom_call_target="tpu_custom_call", output_to_operand_aliasing={{0}: (0, {})} | custom-call | tf_op jit(solution)/shard_map/first/pallas_call | solution.py:352
  21.7 4.3 %collective-permute-start.8 = (f32[960,128]{1,0:T(8,128)S(1)}, f32[960,128]{1,0:T(8,128)S(1)}, u32[]{:S(2)}, u32[]{:S(2)}) collective-permute-start(f32[960,128]{1,0:T(8,128)S(1)} %get-tuple-element.35), channel_id=1, source_target_pairs={{0,1},{1,2},{2,3},{4,5},{5,6},{6,7},{8,9},{9,10},{10,11},{12,13},{... | collective-permute-start | bytes 1474568 | tf_op jit(solution)/shard_map/ppermute | solution.py:402
  26.0 1.3 %collective-permute-start.9 = (f32[960,128]{1,0:T(8,128)S(1)}, f32[960,128]{1,0:T(8,128)S(1)}, u32[]{:S(2)}, u32[]{:S(2)}) collective-permute-start(f32[960,128]{1,0:T(8,128)S(1)} %get-tuple-element.36), channel_id=1, source_target_pairs={{1,0},{2,1},{3,2},{5,4},{6,5},{7,6},{9,8},{10,9},{11,10},{13,12},{... | collective-permute-start | bytes 1474568 | tf_op jit(solution)/shard_map/ppermute | solution.py:403
  27.3 0.0 collective-permute-done.3.below
  27.3 0.0 collective-permute-done.4.above
  27.3 0.0 copy-start.3
  27.3 1.3 %section.1 = (f32[5,8,48,128]{3,2,1,0:T(8,128)S(1)}, f32[5,8,64,128]{3,2,1,0:T(8,128)S(1)}, f32[120,128]{1,0:T(8,128)S(1)}, f32[160,128]{1,0:T(8,128)S(1)}) custom-call(f32[5,8,64,128]{3,2,1,0:T(8,128)S(1)} %get-tuple-element.25.padded.start, f32[5,8,48,128]{3,2,1,0:T(8,128)S(1)} %get-tuple-element.26.rate, f32[968,128]{1,0:T(8,128)S(1)} %collective-permute-done.3.below, ...), custom_call_target="tpu_custom_call" | custom-call | tf_op jit(solution)/shard_map/section/pallas_call | solution.py:352
  28.6 1.6 %collective-permute-start.5 = (f32[160,128]{1,0:T(8,128)S(1)}, f32[160,128]{1,0:T(8,128)S(1)}, u32[]{:S(2)}, u32[]{:S(2)}) collective-permute-start(f32[160,128]{1,0:T(8,128)S(1)} %get-tuple-element.30), channel_id=1, source_target_pairs={{0,16},{4,20},{8,24},{12,28},{16,0},{20,4},{24,8},{28,12},{1,17},{... | collective-permute-start | bytes 245768 | tf_op jit(solution)/shard_map/ppermute | solution.py:373
  30.2 0.0 collective-permute-start.7
  30.2 0.5 %collective-permute-start.6 = (f32[120,128]{1,0:T(8,128)S(1)}, f32[120,128]{1,0:T(8,128)S(1)}, u32[]{:S(2)}, u32[]{:S(2)}) collective-permute-start(f32[120,128]{1,0:T(8,128)S(1)} %get-tuple-element.31), channel_id=1, source_target_pairs={{0,4},{4,8},{8,12},{12,16},{16,20},{20,24},{24,28},{28,0},{1,5},{5... | collective-permute-start | bytes 184328 | tf_op jit(solution)/shard_map/ppermute | solution.py:371
  30.7 1.8 %collective-permute-done.7.right = f32[120,128]{1,0:T(8,128)S(1)} collective-permute-done((f32[120,128]{1,0:T(8,128)S(1)}, f32[120,128]{1,0:T(8,128)S(1)}, u32[]{:S(2)}, u32[]{:S(2)}) %collective-permute-start.7) | collective-permute-done | bytes 61472 | tf_op jit(solution)/shard_map/ppermute | solution.py:372
  32.5 2.2 %collective-permute-done.6.left = f32[120,128]{1,0:T(8,128)S(1)} collective-permute-done((f32[120,128]{1,0:T(8,128)S(1)}, f32[120,128]{1,0:T(8,128)S(1)}, u32[]{:S(2)}, u32[]{:S(2)}) %collective-permute-start.6) | collective-permute-done | bytes 61472 | tf_op jit(solution)/shard_map/ppermute | solution.py:371
  34.8 0.0 collective-permute-done.5.polar
  34.8 0.0 copy-done.3
  34.8 3.4 %second.1 = (f32[5,8,64,128]{3,2,1,0:T(8,128)S(1)}, f32[5,8,48,128]{3,2,1,0:T(8,128)S(1)}, f32[960,128]{1,0:T(8,128)S(1)}, f32[960,128]{1,0:T(8,128)S(1)}) custom-call(f32[5,8,64,128]{3,2,1,0:T(8,128)S(1)} %get-tuple-element.29.given, f32[160,128]{1,0:T(8,128)S(1)} %collective-permute-done.5.polar, ...), custom_call_target="tpu_custom_call", output_to_operand_aliasing={{0}: (0, {})} | custom-call | tf_op jit(solution)/shard_map/second/pallas_call | solution.py:352
  38.2 0.0 collective-permute-done.8.below
  38.2 1.8 %collective-permute-done.9.above = f32[960,128]{1,0:T(8,128)S(1)} collective-permute-done((f32[960,128]{1,0:T(8,128)S(1)}, f32[960,128]{1,0:T(8,128)S(1)}, u32[]{:S(2)}, u32[]{:S(2)}) %collective-permute-start.9) | collective-permute-done | bytes 491552 | tf_op jit(solution)/shard_map/ppermute | solution.py:403
  40.0 1.9 %last.1 = f32[5,8,48,128]{3,2,1,0:T(8,128)} custom-call(f32[5,8,64,128]{3,2,1,0:T(8,128)S(1)} %get-tuple-element.33.padded, f32[5,8,48,128]{3,2,1,0:T(8,128)S(1)} %get-tuple-element.34.both, f32[960,128]{1,0:T(8,128)S(1)} %collective-permute-done.8.below, f32[960,128]{1,0:T(8,128)S(1)} %collective-permute-done.9.above, ...), custom_call_target="tpu_custom_call" | custom-call | tf_op jit(solution)/shard_map/last/pallas_call | solution.py:352
Async XLA Ops:
  0.0 1.2 %copy-start = (f32[5,8,48,128]{3,2,1,0:T(8,128)S(1)}, f32[5,8,48,128]{3,2,1,0:T(8,128)}, u32[]{:S(2)}) copy-start(f32[5,8,48,128]{3,2,1,0:T(8,128)} %state.1) | copy-start | bytes 2949124
  1.2 0.9 %copy-start.4 = (f32[5,8,4,128]{3,2,1,0:T(4,128)S(1)}, f32[5,8,4,128]{3,2,1,0:T(4,128)}, u32[]{:S(2)}) copy-start(f32[5,8,4,128]{3,2,1,0:T(4,128)} %outer.1) | copy-start | bytes 245764
  2.1 0.7 %copy-start.5 = (f32[8]{0:T(128)S(1)}, f32[8]{0:T(128)}, u32[]{:S(2)}) copy-start(f32[8]{0:T(128)} %kappa.9) | copy-start | bytes 100
  4.2 23.1 %collective-permute-start.3 = (f32[968,128]{1,0:T(8,128)S(1)}, f32[968,128]{1,0:T(8,128)S(1)}, u32[]{:S(2)}, u32[]{:S(2)}) collective-permute-start(f32[968,128]{1,0:T(8,128)S(1)} %get-tuple-element.27), channel_id=1, source_target_pairs={{0,1},{1,2},{2,3},{4,5},{5,6},{6,7},{8,9},{9,10},{10,11},{12,13},{... | collective-permute-start | bytes 1486856 | tf_op jit(solution)/shard_map/ppermute | solution.py:389
  9.1 18.2 %collective-permute-start.4 = (f32[968,128]{1,0:T(8,128)S(1)}, f32[968,128]{1,0:T(8,128)S(1)}, u32[]{:S(2)}, u32[]{:S(2)}) collective-permute-start(f32[968,128]{1,0:T(8,128)S(1)} %get-tuple-element.28), channel_id=1, source_target_pairs={{1,0},{2,1},{3,2},{5,4},{6,5},{7,6},{9,8},{10,9},{11,10},{13,12},{... | collective-permute-start | bytes 1486856 | tf_op jit(solution)/shard_map/ppermute | solution.py:390
  10.4 6.4 %collective-permute-start = (f32[160,128]{1,0:T(8,128)S(1)}, f32[160,128]{1,0:T(8,128)S(1)}, u32[]{:S(2)}, u32[]{:S(2)}) collective-permute-start(f32[160,128]{1,0:T(8,128)S(1)} %get-tuple-element.23), channel_id=1, source_target_pairs={{0,16},{4,20},{8,24},{12,28},{16,0},{20,4},{24,8},{28,12},{1,17},{... | collective-permute-start | bytes 245768 | tf_op jit(solution)/shard_map/ppermute | solution.py:373
  12.0 2.2 %collective-permute-start.2 = (f32[120,128]{1,0:T(8,128)S(1)}, f32[120,128]{1,0:T(8,128)S(1)}, u32[]{:S(2)}, u32[]{:S(2)}) collective-permute-start(f32[120,128]{1,0:T(8,128)S(1)} %get-tuple-element.24), channel_id=1, source_target_pairs={{4,0},{8,4},{12,8},{16,12},{20,16},{24,20},{28,24},{0,28},{5,1},{9... | collective-permute-start | bytes 184328 | tf_op jit(solution)/shard_map/ppermute | solution.py:372
  12.3 4.5 %collective-permute-start.1 = (f32[120,128]{1,0:T(8,128)S(1)}, f32[120,128]{1,0:T(8,128)S(1)}, u32[]{:S(2)}, u32[]{:S(2)}) collective-permute-start(f32[120,128]{1,0:T(8,128)S(1)} %get-tuple-element.24), channel_id=1, source_target_pairs={{0,4},{4,8},{8,12},{12,16},{16,20},{20,24},{24,28},{28,0},{1,5},{5... | collective-permute-start | bytes 184328 | tf_op jit(solution)/shard_map/ppermute | solution.py:371
  16.9 0.9 %copy-start.1 = (bf16[256,256]{1,0:T(8,128)(2,1)S(1)}, bf16[256,256]{1,0:T(8,128)(2,1)}, u32[]{:S(2)}) copy-start(bf16[256,256]{1,0:T(8,128)(2,1)} %constant.4.clone.matrix) | copy-start | bytes 393220
  17.8 0.9 %copy-start.2 = (f32[3,48,128]{2,1,0:T(8,128)S(1)}, f32[3,48,128]{2,1,0:T(8,128)}, u32[]{:S(2)}) copy-start(f32[3,48,128]{2,1,0:T(8,128)} %constant.5.clone.geo) | copy-start | bytes 221188
  21.7 16.5 %collective-permute-start.8 = (f32[960,128]{1,0:T(8,128)S(1)}, f32[960,128]{1,0:T(8,128)S(1)}, u32[]{:S(2)}, u32[]{:S(2)}) collective-permute-start(f32[960,128]{1,0:T(8,128)S(1)} %get-tuple-element.35), channel_id=1, source_target_pairs={{0,1},{1,2},{2,3},{4,5},{5,6},{6,7},{8,9},{9,10},{10,11},{12,13},{... | collective-permute-start | bytes 1474568 | tf_op jit(solution)/shard_map/ppermute | solution.py:402
  26.0 14.0 %collective-permute-start.9 = (f32[960,128]{1,0:T(8,128)S(1)}, f32[960,128]{1,0:T(8,128)S(1)}, u32[]{:S(2)}, u32[]{:S(2)}) collective-permute-start(f32[960,128]{1,0:T(8,128)S(1)} %get-tuple-element.36), channel_id=1, source_target_pairs={{1,0},{2,1},{3,2},{5,4},{6,5},{7,6},{9,8},{10,9},{11,10},{13,12},{... | collective-permute-start | bytes 1474568 | tf_op jit(solution)/shard_map/ppermute | solution.py:403
  27.3 7.5 %copy-start.3 = (f32[3,48,128]{2,1,0:T(8,128)S(1)}, f32[3,48,128]{2,1,0:T(8,128)}, u32[]{:S(2)}) copy-start(f32[3,48,128]{2,1,0:T(8,128)} %constant.5.clone.geo) | copy-start | bytes 221188
  28.6 6.1 %collective-permute-start.5 = (f32[160,128]{1,0:T(8,128)S(1)}, f32[160,128]{1,0:T(8,128)S(1)}, u32[]{:S(2)}, u32[]{:S(2)}) collective-permute-start(f32[160,128]{1,0:T(8,128)S(1)} %get-tuple-element.30), channel_id=1, source_target_pairs={{0,16},{4,20},{8,24},{12,28},{16,0},{20,4},{24,8},{28,12},{1,17},{... | collective-permute-start | bytes 245768 | tf_op jit(solution)/shard_map/ppermute | solution.py:373
  30.2 2.3 %collective-permute-start.7 = (f32[120,128]{1,0:T(8,128)S(1)}, f32[120,128]{1,0:T(8,128)S(1)}, u32[]{:S(2)}, u32[]{:S(2)}) collective-permute-start(f32[120,128]{1,0:T(8,128)S(1)} %get-tuple-element.31), channel_id=1, source_target_pairs={{4,0},{8,4},{12,8},{16,12},{20,16},{24,20},{28,24},{0,28},{5,1},{9... | collective-permute-start | bytes 184328 | tf_op jit(solution)/shard_map/ppermute | solution.py:372
  30.2 4.5 %collective-permute-start.6 = (f32[120,128]{1,0:T(8,128)S(1)}, f32[120,128]{1,0:T(8,128)S(1)}, u32[]{:S(2)}, u32[]{:S(2)}) collective-permute-start(f32[120,128]{1,0:T(8,128)S(1)} %get-tuple-element.31), channel_id=1, source_target_pairs={{0,4},{4,8},{8,12},{12,16},{16,20},{20,24},{24,28},{28,0},{1,5},{5... | collective-permute-start | bytes 184328 | tf_op jit(solution)/shard_map/ppermute | solution.py:371

commit v2 on v1

--- a/solution.py
+++ b/solution.py
@@ -27,12 +27,7 @@
 level_second = tuple(radial_ratio * radial_ratio * c for c in second_coeffs)
 
 VMEM = pl.BlockSpec(memory_space=pltpu.VMEM)
-SMEM = pl.BlockSpec(memory_space=pltpu.SMEM)
-ANY = pl.BlockSpec(memory_space=pl.ANY)
-
-
-def held(x):
-    return pltpu.with_memory_space_constraint(x, pltpu.VMEM)
+HBM = pl.BlockSpec(memory_space=pltpu.HBM)
 
 
 def in_vmem(*shape):
@@ -102,27 +97,47 @@
     return out
 
 
-def edges_kernel(levels, rows, state, outer, kappa, padded, low, high, edge, polar, sems, outer_sem):
+def edges_kernel(
+    levels, rows, state, outer, kappa, matrix_in, geo_in,
+    padded, low, high, edge, polar, kap, matrix, geo,
+    staged, outer_staged, kappa_scalars, sems,
+):
     block = REACH * rows
-    copies = []
-    for f in range(FIELDS):
-        copies.append(pltpu.make_async_copy(state.at[f], padded.at[f, :, pl.ds(TILE, rows)], sems.at[f]))
-        copies[-1].start()
-    last = pltpu.make_async_copy(outer, padded.at[:, :, pl.ds(TILE + rows, REACH)], outer_sem)
-    last.start()
-    for i in range(REACH):
-        low[pl.ds(FIELDS * block + i, 1), :] = jnp.full((1, LANES), kappa[i], jnp.float32)
-        high[pl.ds(FIELDS * block + i, 1), :] = jnp.full((1, LANES), kappa[levels - REACH + i], jnp.float32)
-    low[pl.ds(FIELDS * block + REACH, REACH), :] = jnp.ones((REACH, LANES), jnp.float32)
-    high[pl.ds(FIELDS * block + REACH, REACH), :] = jnp.ones((REACH, LANES), jnp.float32)
+    odd = lax.axis_index("rad") % 2
+    mirror = jnp.where(odd == 1, -1.0, 1.0).astype(jnp.float32)
+    reads = [(state.at[f], staged.at[f]) for f in range(FIELDS)]
+    reads += [(outer, outer_staged), (kappa, kappa_scalars), (matrix_in, matrix), (geo_in, geo)]
+    copies = [pltpu.make_async_copy(*read, sems.at[i]) for i, read in enumerate(reads)]
+    for copy in copies:
+        copy.start()
     lane = lax.broadcasted_iota(jnp.int32, (TILE, LANES), 1)
     for f in range(FIELDS):
         copies[f].wait()
-        for l in range(REACH):
-            low[pl.ds(f * block + l * rows, rows), :] = padded[f, l, pl.ds(TILE, rows), :]
-            high[pl.ds(f * block + l * rows, rows), :] = padded[f, levels - REACH + l, pl.ds(TILE, rows), :]
+        for l in range(levels):
+            whole = staged[f, jnp.where(odd == 1, levels - 1 - l, l)]
+            if f == 3:
+                whole = mirror * whole
+            padded[f, l, pl.ds(TILE, rows), :] = whole
+            if l < REACH:
+                low[pl.ds(f * block + l * rows, rows), :] = whole
+            if l >= levels - REACH:
+                high[pl.ds(f * block + (l - levels + REACH) * rows, rows), :] = whole
         pack_edges(f, levels, rows, padded, edge, polar, lane)
-    last.wait()
+    for copy in copies[FIELDS:]:
+        copy.wait()
+    for l in range(levels):
+        real = jnp.where(odd == 1, levels - 1 - l, l)
+        value = kappa_scalars[real]
+        kap[l] = jnp.full((TILE, LANES), value, jnp.float32)
+        if l < REACH:
+            low[pl.ds(FIELDS * block + l, 1), :] = jnp.full((1, LANES), value, jnp.float32)
+        if l >= levels - REACH:
+            high[pl.ds(FIELDS * block + l - levels + REACH, 1), :] = jnp.full((1, LANES), value, jnp.float32)
+        for f in range(FIELDS):
+            beyond = outer_staged[f, real]
+            padded[f, l, pl.ds(TILE + rows, REACH), :] = mirror * beyond if f == 3 else beyond
+    low[pl.ds(FIELDS * block + REACH, REACH), :] = jnp.ones((REACH, LANES), jnp.float32)
+    high[pl.ds(FIELDS * block + REACH, REACH), :] = jnp.ones((REACH, LANES), jnp.float32)
 
 
 def pack_edges(f, levels, rows, padded, edge, polar, lane):
@@ -255,6 +270,15 @@
 
 
 def halo_tile(ref, rows, r0):
+    out = [
+        [ref[pl.ds((f * REACH + REACH - 1 - b) * rows + r0, TILE), :] for b in range(REACH)]
+        for f in range(FIELDS)
+    ]
+    out[3] = [-v for v in out[3]]
+    return out
+
+
+def own_tile(ref, rows, r0):
     return [
         [ref[pl.ds((f * REACH + b) * rows + r0, TILE), :] for b in range(REACH)] for f in range(FIELDS)
     ]
@@ -305,7 +329,7 @@
             mine = [
                 [start[f, at + a, pl.ds(r0 + TILE, TILE), :] for a in range(REACH)] for f in range(FIELDS)
             ]
-            kappas = [halo_ref[pl.ds(tail + a, 1), :] for a in range(REACH)]
+            kappas = [halo_ref[pl.ds(tail + REACH - 1 - a, 1), :] for a in range(REACH)]
             there = time_step * halo_ref[pl.ds(tail + REACH, 1), :]
             extra = across_level(beyond[3], beyond[4], mine, kappas, up)
             for f in range(FIELDS):
@@ -317,11 +341,14 @@
 
 
 def last_kernel(levels, rows, padded, both, below, above, low, high, kappa, out):
+    odd = lax.axis_index("rad") % 2
+    mirror = jnp.where(odd == 1, -1.0, 1.0).astype(jnp.float32)
+
     def body(t, carry):
         r0 = pl.multiple_of(t * TILE, TILE)
         for halo_ref, more_ref, at, up in ((below, low, 0, False), (above, high, levels - REACH, True)):
             halo = halo_tile(halo_ref, rows, r0)
-            more = halo_tile(more_ref, rows, r0)
+            more = own_tile(more_ref, rows, r0)
             halo = [[halo[f][b] + more[f][b] for b in range(REACH)] for f in range(FIELDS)]
             wind = [padded[3, at + a, pl.ds(r0 + TILE, TILE), :] for a in range(REACH)]
             temper = [padded[4, at + a, pl.ds(r0 + TILE, TILE), :] for a in range(REACH)]
@@ -329,7 +356,11 @@
             for f in range(FIELDS):
                 for a in range(REACH):
                     old = both[f, at + a, pl.ds(r0, TILE), :]
-                    out[f, at + a, pl.ds(r0, TILE), :] = old + (0.5 * time_step) * extra[f][a]
+                    new = old + (0.5 * time_step) * extra[f][a]
+                    if f == 3:
+                        new = mirror * new
+                    real = jnp.where(odd == 1, levels - 1 - at - a, at + a)
+                    out[f, real, pl.ds(r0, TILE), :] = new
         return carry
 
     lax.fori_loop(0, rows // TILE, body, 0)
@@ -347,8 +378,9 @@
     pad_shape = (FIELDS, levels, rows + 2 * TILE, width)
     full_shape = (FIELDS, levels, rows, width)
 
-    def call(kernel, out_shape, in_specs, args, scratch=(), aliases=None, flops=0, name=None):
-        args = [held(a) if s is VMEM else a for s, a in zip(in_specs, args)]
+    def call(kernel, out_shape, in_specs, args, scratch=(), aliases=None, name=None):
+        spaces = {id(VMEM): pltpu.VMEM, id(HBM): pltpu.HBM}
+        args = [pltpu.with_memory_space_constraint(x, spaces[id(s)]) for s, x in zip(in_specs, args)]
         return pl.pallas_call(
             functools.partial(kernel, levels, rows),
             out_shape=out_shape,
@@ -356,7 +388,6 @@
             out_specs=jax.tree.map(lambda _: VMEM, out_shape),
             scratch_shapes=list(scratch),
             input_output_aliases=aliases or {},
-            cost_estimate=pl.CostEstimate(flops=flops, bytes_accessed=0, transcendentals=0),
             compiler_params=pltpu.CompilerParams(vmem_limit_bytes=16 * 2**20),
             name=name,
         )(*args)
@@ -364,15 +395,15 @@
     east = [(i, (i + 1) % ring) for i in range(ring)]
     west = [(b, a) for a, b in east]
     half = [(i, (i + ring // 2) % ring) for i in range(ring)]
-    up = [(i, i + 1) for i in range(depth - 1)]
-    down = [(b, a) for a, b in up]
+    swap_high = [p for i in range(0, depth - 1, 2) for p in ((i, i + 1), (i + 1, i))]
+    swap_low = [p for i in range(1, depth - 1, 2) for p in ((i, i + 1), (i + 1, i))]
 
     def around(edge, polar):
         left = lax.ppermute(edge, "lon", east)
         right = lax.ppermute(edge, "lon", west)
         return left, right, lax.ppermute(polar, "lon", half)
 
-    padded, low, high, edge, polar = call(
+    padded, low, high, edge, polar, kap, matrix, geo = call(
         edges_kernel,
         [
             in_vmem(*pad_shape),
@@ -380,27 +411,35 @@
             in_vmem(halo_rows + TILE, width),
             in_vmem(packs, width),
             in_vmem(FIELDS * levels * REACH, width),
+            in_vmem(levels, TILE, width),
+            pltpu.VMEM(matrix.shape, matrix.dtype),
+            in_vmem(*geo.shape),
         ],
-        (ANY, ANY, SMEM),
-        (state, outer_rows, kappa),
-        scratch=(pltpu.SemaphoreType.DMA((FIELDS,)), pltpu.SemaphoreType.DMA),
+        (HBM,) * 5,
+        (state, outer_rows, kappa, matrix, geo),
+        scratch=(
+            in_vmem(*full_shape),
+            in_vmem(*outer_rows.shape),
+            pltpu.SMEM(kappa.shape, jnp.float32),
+            pltpu.SemaphoreType.DMA((FIELDS + 4,)),
+        ),
         name="edges",
     )
-    below = lax.ppermute(high, "rad", up)
-    above = lax.ppermute(low, "rad", down)
+    below = lax.ppermute(low, "rad", swap_low)
+    above = lax.ppermute(high, "rad", swap_high)
     left, right, beyond = around(edge, polar)
     lon_scratch = (in_vmem(*full_shape), in_vmem(*full_shape[1:]))
-    padded, rate, low2, high2 = call(
+    padded, rate, low, high = call(
         first_kernel,
         [in_vmem(*pad_shape), in_vmem(*full_shape), in_vmem(halo_rows, width), in_vmem(halo_rows, width)],
-        (VMEM,) * 6 + (SMEM,),
-        (padded, beyond, left, right, matrix, geo, kappa),
+        (VMEM,) * 7,
+        (padded, beyond, left, right, matrix, geo, kap),
         scratch=lon_scratch,
         aliases={0: 0},
         name="first",
     )
-    below2 = lax.ppermute(high2, "rad", up)
-    above2 = lax.ppermute(low2, "rad", down)
+    below2 = lax.ppermute(low, "rad", swap_low)
+    above2 = lax.ppermute(high, "rad", swap_high)
     full, ahead, edge, polar = call(
         section_kernel,
         [
@@ -409,16 +448,16 @@
             in_vmem(packs, width),
             in_vmem(FIELDS * levels * REACH, width),
         ],
-        (VMEM,) * 4 + (SMEM,),
-        (padded, rate, below, above, kappa),
+        (VMEM,) * 5,
+        (padded, rate, below, above, kap),
         name="section",
     )
     left, right, beyond = around(edge, polar)
     ahead, both, low, high = call(
         second_kernel,
         [in_vmem(*pad_shape), in_vmem(*full_shape), in_vmem(halo_rows, width), in_vmem(halo_rows, width)],
-        (VMEM,) * 6 + (SMEM,) + (VMEM,) * 4,
-        (ahead, beyond, left, right, matrix, geo, kappa, full, padded, below, above),
+        (VMEM,) * 11,
+        (ahead, beyond, left, right, matrix, geo, kap, full, padded, below, above),
         scratch=lon_scratch,
         aliases={0: 0},
         name="second",
@@ -426,8 +465,8 @@
     return call(
         last_kernel,
         jax.ShapeDtypeStruct(full_shape, jnp.float32),
-        (VMEM,) * 6 + (SMEM,),
-        (ahead, both, below2, above2, low, high, kappa),
+        (VMEM,) * 7,
+        (ahead, both, below2, above2, low, high, kap),
         name="last",
     )
 

time: 42.2 us -> 31.7 us (0.75)
  local copies, waits for them, and re-layouts: 4.54 us -> 0 us
  starting transfers between devices: 16 us -> 13.9 us
  waiting for transfers between devices: 10.2 us -> 8.26 us
  Pallas kernels: 11 us -> 9.27 us
    unnamed x12 -> x0, local copies, waits for them, and re-layouts: 4.54 us -> none
    ppermute x4, starting transfers between devices: 11.8 us -> 9.35 us  [the longest x1 5.88 us: on_device(): above = lax.ppermute(high, 'rad', swap_high)]
    pallas_call x5, Pallas kernels: 11 us -> 9.27 us  [call(): pl.pallas_call(functools.partial(kernel, levels, rows), out_shape=out_sha...]
    ppermute x4, waiting for transfers between devices: 1.79 us -> 0.15 us  [the longest x1 0.14 us: on_device(): above2 = lax.ppermute(high, 'rad', swap_high)]
    ppermute x2, waiting for transfers between devices: 3.47 us -> 2.75 us  [around(): right = lax.ppermute(edge, 'lon', west)]
    ppermute x2, waiting for transfers between devices: 4.91 us -> 5.36 us  [around(): left = lax.ppermute(edge, 'lon', east)]
  transfers between devices with their start and end apart: 10 -> 10, of which waited for: 5 -> 5; matrix products, arithmetic and copies ran while one was open for 0% -> 0% of each run, Pallas kernels for 18% -> 19%
where the time goes in v2:
time: 31.7 us; the launch traced here: 31.5 us
  starting transfers between devices  13.9 us (44%)
  Pallas kernels  9.27 us (29%)
  waiting for transfers between devices  8.26 us (26%)
    pallas_call x5, Pallas kernels, call(): pl.pallas_call(functools.partial(kernel, levels, rows), out_shape=out_sha...  9.27 us
    ppermute x1, starting transfers between devices, on_device(): above = lax.ppermute(high, 'rad', swap_high)  5.88 us
    ppermute x2, waiting for transfers between devices, around(): left = lax.ppermute(edge, 'lon', east)  5.36 us
    ppermute x2, starting transfers between devices, around(): return (left, right, lax.ppermute(polar, 'lon', half))  3.54 us
    ppermute x2, waiting for transfers between devices, around(): right = lax.ppermute(edge, 'lon', west)  2.75 us
    ppermute x1, starting transfers between devices, on_device(): above2 = lax.ppermute(high, 'rad', swap_high)  2.09 us
    ppermute x2, starting transfers between devices, around(): left = lax.ppermute(edge, 'lon', east)  0.98 us
    ppermute x1, starting transfers between devices, on_device(): below = lax.ppermute(low, 'rad', swap_low)  0.69 us
  transfers between devices with their start and end apart: 10, of which 5 were waited for; matrix products, arithmetic and copies ran while one was open for 0% of the time, Pallas kernels for 19%

profile of v2, /device:TPU:0, one launch (start us, length us, event | category | flops | bytes accessed | tf_op | source)
XLA Modules:
  0.0 31.5 jit_solution(6692397900739555910)
XLA Ops:
  0.0 1.7 %edges.1 = (f32[5,8,64,128]{3,2,1,0:T(8,128)S(1)}, f32[968,128]{1,0:T(8,128)S(1)}, f32[968,128]{1,0:T(8,128)S(1)}, f32[120,128]{1,0:T(8,128)S(1)}, f32[160,128]{...) custom-call(f32[5,8,48,128]{3,2,1,0:T(8,128)} %state.1, ...), custom_call_target="tpu_custom_call" | custom-call | tf_op jit(solution)/shard_map/edges/pallas_call | solution.py:384
  1.7 0.7 %collective-permute-start.3 = (f32[968,128]{1,0:T(8,128)S(1)}, f32[968,128]{1,0:T(8,128)S(1)}, u32[]{:S(2)}, u32[]{:S(2)}) collective-permute-start(f32[968,128]{1,0:T(8,128)S(1)} %get-tuple-element.33), channel_id=1, source_target_pairs={{1,2},{2,1},{5,6},{6,5},{9,10},{10,9},{13,14},{14,13},{17,18},{18,... | collective-permute-start | bytes 1486856 | tf_op jit(solution)/shard_map/ppermute | solution.py:428
  2.4 5.9 %collective-permute-start.4 = (f32[968,128]{1,0:T(8,128)S(1)}, f32[968,128]{1,0:T(8,128)S(1)}, u32[]{:S(2)}, u32[]{:S(2)}) collective-permute-start(f32[968,128]{1,0:T(8,128)S(1)} %get-tuple-element.34), channel_id=1, source_target_pairs={{0,1},{1,0},{2,3},{3,2},{4,5},{5,4},{6,7},{7,6},{8,9},{9,8},{10,11... | collective-permute-start | bytes 1486856 | tf_op jit(solution)/shard_map/ppermute | solution.py:429
  8.3 1.5 %collective-permute-start = (f32[160,128]{1,0:T(8,128)S(1)}, f32[160,128]{1,0:T(8,128)S(1)}, u32[]{:S(2)}, u32[]{:S(2)}) collective-permute-start(f32[160,128]{1,0:T(8,128)S(1)} %get-tuple-element.26), channel_id=1, source_target_pairs={{0,16},{4,20},{8,24},{12,28},{16,0},{20,4},{24,8},{28,12},{1,17},{... | collective-permute-start | bytes 245768 | tf_op jit(solution)/shard_map/ppermute | solution.py:404
  9.8 0.0 collective-permute-start.2
  9.9 0.5 %collective-permute-start.1 = (f32[120,128]{1,0:T(8,128)S(1)}, f32[120,128]{1,0:T(8,128)S(1)}, u32[]{:S(2)}, u32[]{:S(2)}) collective-permute-start(f32[120,128]{1,0:T(8,128)S(1)} %get-tuple-element.27), channel_id=1, source_target_pairs={{0,4},{4,8},{8,12},{12,16},{16,20},{20,24},{24,28},{28,0},{1,5},{5... | collective-permute-start | bytes 184328 | tf_op jit(solution)/shard_map/ppermute | solution.py:402
  10.3 1.4 %collective-permute-done.2.right = f32[120,128]{1,0:T(8,128)S(1)} collective-permute-done((f32[120,128]{1,0:T(8,128)S(1)}, f32[120,128]{1,0:T(8,128)S(1)}, u32[]{:S(2)}, u32[]{:S(2)}) %collective-permute-start.2) | collective-permute-done | bytes 61472 | tf_op jit(solution)/shard_map/ppermute | solution.py:403
  11.7 2.7 %collective-permute-done.1.left = f32[120,128]{1,0:T(8,128)S(1)} collective-permute-done((f32[120,128]{1,0:T(8,128)S(1)}, f32[120,128]{1,0:T(8,128)S(1)}, u32[]{:S(2)}, u32[]{:S(2)}) %collective-permute-start.1) | collective-permute-done | bytes 61472 | tf_op jit(solution)/shard_map/ppermute | solution.py:402
  14.4 0.0 collective-permute-done.polar
  14.4 2.5 %first.1 = (f32[5,8,64,128]{3,2,1,0:T(8,128)S(1)}, f32[5,8,48,128]{3,2,1,0:T(8,128)S(1)}, f32[960,128]{1,0:T(8,128)S(1)}, f32[960,128]{1,0:T(8,128)S(1)}) custom-call(f32[5,8,64,128]{3,2,1,0:T(8,128)S(1)} %get-tuple-element.25.given, f32[160,128]{1,0:T(8,128)S(1)} %collective-permute-done.polar, ...), custom_call_target="tpu_custom_call", output_to_operand_aliasing={{0}: (0, {})} | custom-call | tf_op jit(solution)/shard_map/first/pallas_call | solution.py:384
  16.9 0.7 %collective-permute-start.8 = (f32[960,128]{1,0:T(8,128)S(1)}, f32[960,128]{1,0:T(8,128)S(1)}, u32[]{:S(2)}, u32[]{:S(2)}) collective-permute-start(f32[960,128]{1,0:T(8,128)S(1)} %get-tuple-element.41), channel_id=1, source_target_pairs={{1,2},{2,1},{5,6},{6,5},{9,10},{10,9},{13,14},{14,13},{17,18},{18,... | collective-permute-start | bytes 1474568 | tf_op jit(solution)/shard_map/ppermute | solution.py:441
  17.6 2.1 %collective-permute-start.9 = (f32[960,128]{1,0:T(8,128)S(1)}, f32[960,128]{1,0:T(8,128)S(1)}, u32[]{:S(2)}, u32[]{:S(2)}) collective-permute-start(f32[960,128]{1,0:T(8,128)S(1)} %get-tuple-element.42), channel_id=1, source_target_pairs={{0,1},{1,0},{2,3},{3,2},{4,5},{5,4},{6,7},{7,6},{8,9},{9,8},{10,11... | collective-permute-start | bytes 1474568 | tf_op jit(solution)/shard_map/ppermute | solution.py:442
  19.7 0.0 collective-permute-done.3.below
  19.7 0.0 collective-permute-done.4.above
  19.7 0.7 %section.1 = (f32[5,8,48,128]{3,2,1,0:T(8,128)S(1)}, f32[5,8,64,128]{3,2,1,0:T(8,128)S(1)}, f32[120,128]{1,0:T(8,128)S(1)}, f32[160,128]{1,0:T(8,128)S(1)}) custom-call(f32[5,8,64,128]{3,2,1,0:T(8,128)S(1)} %get-tuple-element.31.padded.start, f32[5,8,48,128]{3,2,1,0:T(8,128)S(1)} %get-tuple-element.32.rate, f32[968,128]{1,0:T(8,128)S(1)} %collective-permute-done.3.below, ...), custom_call_target="tpu_custom_call" | custom-call | tf_op jit(solution)/shard_map/section/pallas_call | solution.py:384
  20.4 2.0 %collective-permute-start.5 = (f32[160,128]{1,0:T(8,128)S(1)}, f32[160,128]{1,0:T(8,128)S(1)}, u32[]{:S(2)}, u32[]{:S(2)}) collective-permute-start(f32[160,128]{1,0:T(8,128)S(1)} %get-tuple-element.36), channel_id=1, source_target_pairs={{0,16},{4,20},{8,24},{12,28},{16,0},{20,4},{24,8},{28,12},{1,17},{... | collective-permute-start | bytes 245768 | tf_op jit(solution)/shard_map/ppermute | solution.py:404
  22.5 0.0 collective-permute-start.7
  22.5 0.5 %collective-permute-start.6 = (f32[120,128]{1,0:T(8,128)S(1)}, f32[120,128]{1,0:T(8,128)S(1)}, u32[]{:S(2)}, u32[]{:S(2)}) collective-permute-start(f32[120,128]{1,0:T(8,128)S(1)} %get-tuple-element.37), channel_id=1, source_target_pairs={{0,4},{4,8},{8,12},{12,16},{16,20},{20,24},{24,28},{28,0},{1,5},{5... | collective-permute-start | bytes 184328 | tf_op jit(solution)/shard_map/ppermute | solution.py:402
  23.0 1.4 %collective-permute-done.7.right = f32[120,128]{1,0:T(8,128)S(1)} collective-permute-done((f32[120,128]{1,0:T(8,128)S(1)}, f32[120,128]{1,0:T(8,128)S(1)}, u32[]{:S(2)}, u32[]{:S(2)}) %collective-permute-start.7) | collective-permute-done | bytes 61472 | tf_op jit(solution)/shard_map/ppermute | solution.py:403
  24.3 2.7 %collective-permute-done.6.left = f32[120,128]{1,0:T(8,128)S(1)} collective-permute-done((f32[120,128]{1,0:T(8,128)S(1)}, f32[120,128]{1,0:T(8,128)S(1)}, u32[]{:S(2)}, u32[]{:S(2)}) %collective-permute-start.6) | collective-permute-done | bytes 61472 | tf_op jit(solution)/shard_map/ppermute | solution.py:402
  27.0 0.0 collective-permute-done.5.polar
  27.0 2.9 %second.1 = (f32[5,8,64,128]{3,2,1,0:T(8,128)S(1)}, f32[5,8,48,128]{3,2,1,0:T(8,128)S(1)}, f32[960,128]{1,0:T(8,128)S(1)}, f32[960,128]{1,0:T(8,128)S(1)}) custom-call(f32[5,8,64,128]{3,2,1,0:T(8,128)S(1)} %get-tuple-element.35.given, f32[160,128]{1,0:T(8,128)S(1)} %collective-permute-done.5.polar, ...), custom_call_target="tpu_custom_call", output_to_operand_aliasing={{0}: (0, {})} | custom-call | tf_op jit(solution)/shard_map/second/pallas_call | solution.py:384
  29.9 0.0 collective-permute-done.8.below
  29.9 0.1 collective-permute-done.9.above
  30.0 1.5 %last.1 = f32[5,8,48,128]{3,2,1,0:T(8,128)} custom-call(f32[5,8,64,128]{3,2,1,0:T(8,128)S(1)} %get-tuple-element.39.padded, f32[5,8,48,128]{3,2,1,0:T(8,128)S(1)} %get-tuple-element.40.both, f32[960,128]{1,0:T(8,128)S(1)} %collective-permute-done.8.below, f32[960,128]{1,0:T(8,128)S(1)} %collective-permute-done.9.above, ...), custom_call_target="tpu_custom_call" | custom-call | tf_op jit(solution)/shard_map/last/pallas_call | solution.py:384
Async XLA Ops:
  1.7 18.0 %collective-permute-start.3 = (f32[968,128]{1,0:T(8,128)S(1)}, f32[968,128]{1,0:T(8,128)S(1)}, u32[]{:S(2)}, u32[]{:S(2)}) collective-permute-start(f32[968,128]{1,0:T(8,128)S(1)} %get-tuple-element.33), channel_id=1, source_target_pairs={{1,2},{2,1},{5,6},{6,5},{9,10},{10,9},{13,14},{14,13},{17,18},{18,... | collective-permute-start | bytes 1486856 | tf_op jit(solution)/shard_map/ppermute | solution.py:428
  2.4 17.3 %collective-permute-start.4 = (f32[968,128]{1,0:T(8,128)S(1)}, f32[968,128]{1,0:T(8,128)S(1)}, u32[]{:S(2)}, u32[]{:S(2)}) collective-permute-start(f32[968,128]{1,0:T(8,128)S(1)} %get-tuple-element.34), channel_id=1, source_target_pairs={{0,1},{1,0},{2,3},{3,2},{4,5},{5,4},{6,7},{7,6},{8,9},{9,8},{10,11... | collective-permute-start | bytes 1486856 | tf_op jit(solution)/shard_map/ppermute | solution.py:429
  8.3 6.1 %collective-permute-start = (f32[160,128]{1,0:T(8,128)S(1)}, f32[160,128]{1,0:T(8,128)S(1)}, u32[]{:S(2)}, u32[]{:S(2)}) collective-permute-start(f32[160,128]{1,0:T(8,128)S(1)} %get-tuple-element.26), channel_id=1, source_target_pairs={{0,16},{4,20},{8,24},{12,28},{16,0},{20,4},{24,8},{28,12},{1,17},{... | collective-permute-start | bytes 245768 | tf_op jit(solution)/shard_map/ppermute | solution.py:404
  9.8 1.9 %collective-permute-start.2 = (f32[120,128]{1,0:T(8,128)S(1)}, f32[120,128]{1,0:T(8,128)S(1)}, u32[]{:S(2)}, u32[]{:S(2)}) collective-permute-start(f32[120,128]{1,0:T(8,128)S(1)} %get-tuple-element.27), channel_id=1, source_target_pairs={{4,0},{8,4},{12,8},{16,12},{20,16},{24,20},{28,24},{0,28},{5,1},{9... | collective-permute-start | bytes 184328 | tf_op jit(solution)/shard_map/ppermute | solution.py:403
  9.9 4.5 %collective-permute-start.1 = (f32[120,128]{1,0:T(8,128)S(1)}, f32[120,128]{1,0:T(8,128)S(1)}, u32[]{:S(2)}, u32[]{:S(2)}) collective-permute-start(f32[120,128]{1,0:T(8,128)S(1)} %get-tuple-element.27), channel_id=1, source_target_pairs={{0,4},{4,8},{8,12},{12,16},{16,20},{20,24},{24,28},{28,0},{1,5},{5... | collective-permute-start | bytes 184328 | tf_op jit(solution)/shard_map/ppermute | solution.py:402
  16.9 13.0 %collective-permute-start.8 = (f32[960,128]{1,0:T(8,128)S(1)}, f32[960,128]{1,0:T(8,128)S(1)}, u32[]{:S(2)}, u32[]{:S(2)}) collective-permute-start(f32[960,128]{1,0:T(8,128)S(1)} %get-tuple-element.41), channel_id=1, source_target_pairs={{1,2},{2,1},{5,6},{6,5},{9,10},{10,9},{13,14},{14,13},{17,18},{18,... | collective-permute-start | bytes 1474568 | tf_op jit(solution)/shard_map/ppermute | solution.py:441
  17.6 12.4 %collective-permute-start.9 = (f32[960,128]{1,0:T(8,128)S(1)}, f32[960,128]{1,0:T(8,128)S(1)}, u32[]{:S(2)}, u32[]{:S(2)}) collective-permute-start(f32[960,128]{1,0:T(8,128)S(1)} %get-tuple-element.42), channel_id=1, source_target_pairs={{0,1},{1,0},{2,3},{3,2},{4,5},{5,4},{6,7},{7,6},{8,9},{9,8},{10,11... | collective-permute-start | bytes 1474568 | tf_op jit(solution)/shard_map/ppermute | solution.py:442
  20.4 6.6 %collective-permute-start.5 = (f32[160,128]{1,0:T(8,128)S(1)}, f32[160,128]{1,0:T(8,128)S(1)}, u32[]{:S(2)}, u32[]{:S(2)}) collective-permute-start(f32[160,128]{1,0:T(8,128)S(1)} %get-tuple-element.36), channel_id=1, source_target_pairs={{0,16},{4,20},{8,24},{12,28},{16,0},{20,4},{24,8},{28,12},{1,17},{... | collective-permute-start | bytes 245768 | tf_op jit(solution)/shard_map/ppermute | solution.py:404
  22.5 1.9 %collective-permute-start.7 = (f32[120,128]{1,0:T(8,128)S(1)}, f32[120,128]{1,0:T(8,128)S(1)}, u32[]{:S(2)}, u32[]{:S(2)}) collective-permute-start(f32[120,128]{1,0:T(8,128)S(1)} %get-tuple-element.37), channel_id=1, source_target_pairs={{4,0},{8,4},{12,8},{16,12},{20,16},{24,20},{28,24},{0,28},{5,1},{9... | collective-permute-start | bytes 184328 | tf_op jit(solution)/shard_map/ppermute | solution.py:403
  22.5 4.5 %collective-permute-start.6 = (f32[120,128]{1,0:T(8,128)S(1)}, f32[120,128]{1,0:T(8,128)S(1)}, u32[]{:S(2)}, u32[]{:S(2)}) collective-permute-start(f32[120,128]{1,0:T(8,128)S(1)} %get-tuple-element.37), channel_id=1, source_target_pairs={{0,4},{4,8},{8,12},{12,16},{16,20},{20,24},{24,28},{28,0},{1,5},{5... | collective-permute-start | bytes 184328 | tf_op jit(solution)/shard_map/ppermute | solution.py:402

commit v3 on v2

--- a/solution.py
+++ b/solution.py
@@ -34,21 +34,23 @@
     return pltpu.VMEM(shape, jnp.float32)
 
 
-def stencil_matrix(width):
-    matrix = np.zeros((2 * width, 2 * width), np.float32)
+def stencil_matrices(width):
+    own = np.zeros((width, 2 * width), np.float32)
+    first = np.zeros((width, GROUPS * width), np.float32)
+    second = np.zeros((width, GROUPS * width), np.float32)
     for out in range(width):
         for k in range(1, REACH + 1):
             for sign in (1, -1):
                 at = out + sign * k
                 if 0 <= at < width:
-                    row = at
-                elif at < 0:
-                    row = width + REACH + at
-                else:
-                    row = width + REACH + (at - width)
-                matrix[row, out] = sign * first_whole[k - 1]
-                matrix[row, width + out] = second_whole[k - 1]
-    return jnp.asarray(matrix, jnp.bfloat16)
+                    own[at, out] = sign * first_whole[k - 1]
+                    own[at, width + out] = second_whole[k - 1]
+                    continue
+                row = REACH + at if at < 0 else REACH + at - width
+                for g in range(GROUPS):
+                    first[2 * REACH * g + row, g * width + out] = sign * first_whole[k - 1]
+                    second[2 * REACH * g + row, g * width + out] = second_whole[k - 1]
+    return tuple(jnp.asarray(m, jnp.bfloat16) for m in (own, first, second))
 
 
 def geometry(rows, nlon, width):
@@ -98,8 +100,8 @@
 
 
 def edges_kernel(
-    levels, rows, state, outer, kappa, matrix_in, geo_in,
-    padded, low, high, edge, polar, kap, matrix, geo,
+    levels, rows, state, outer, kappa, matrix_in, halo1_in, halo2_in, geo_in,
+    padded, low, high, edge, polar, kap, matrix, halo1, halo2, geo,
     staged, outer_staged, kappa_scalars, sems,
 ):
     block = REACH * rows
@@ -107,6 +109,7 @@
     mirror = jnp.where(odd == 1, -1.0, 1.0).astype(jnp.float32)
     reads = [(state.at[f], staged.at[f]) for f in range(FIELDS)]
     reads += [(outer, outer_staged), (kappa, kappa_scalars), (matrix_in, matrix), (geo_in, geo)]
+    reads += [(halo1_in, halo1), (halo2_in, halo2)]
     copies = [pltpu.make_async_copy(*read, sems.at[i]) for i, read in enumerate(reads)]
     for copy in copies:
         copy.start()
@@ -118,6 +121,7 @@
             if f == 3:
                 whole = mirror * whole
             padded[f, l, pl.ds(TILE, rows), :] = whole
+            padded[f, l, pl.ds(0, TILE), :] = jnp.zeros((TILE, LANES), jnp.float32)
             if l < REACH:
                 low[pl.ds(f * block + l * rows, rows), :] = whole
             if l >= levels - REACH:
@@ -156,35 +160,75 @@
             polar[pl.ds((f * levels + l) * REACH + i, 1), :] = signs[f] * row
 
 
-def longitude_slopes(levels, rows, padded, left, right, matrix, dlon, elon):
-    lane = lax.broadcasted_iota(jnp.int32, (TILE, LANES), 1)
-    from_left = (lane % (2 * REACH)) < REACH
-    per = GROUPS // levels
-    packs = rows // TILE // per
+def pieces_of(x):
+    out = []
+    for piece in range(3):
+        out.append(x.astype(jnp.bfloat16))
+        if piece < 2:
+            x = x - out[-1].astype(jnp.float32)
+    return out
+
+
+def times_whole(pieces, m):
+    total = None
+    for piece in pieces:
+        term = jnp.dot(piece, m, preferred_element_type=jnp.float32)
+        total = term if total is None else total + term
+    return total
+
+
+def longitude_slopes(levels, rows, padded, matrix, dlon, elon):
     for f in range(FIELDS):
-        halos = [[None] * (rows // TILE) for _ in range(levels)]
-        for j in range(packs):
-            at = pl.ds((f * packs + j) * TILE, TILE)
-            both = jnp.where(from_left, left[at, :], right[at, :])
-            for u in range(per):
-                for l in range(levels):
-                    g = u * levels + l
-                    halos[l][j * per + u] = pltpu.roll(both, (LANES - 2 * REACH * g) % LANES, 1)
         x = padded[f, :, pl.ds(TILE, rows), :].reshape(levels * rows, LANES)
-        h = jnp.concatenate([halos[l][t] for l in range(levels) for t in range(rows // TILE)], axis=0)
-        x = jnp.concatenate([x, h], axis=1)
-        width = 2 * LANES if f == 4 else LANES
-        m = matrix[:, pl.ds(0, width)]
-        total = None
-        for piece in range(3):
-            part = x.astype(jnp.bfloat16)
-            if piece < 2:
-                x = x - part.astype(jnp.float32)
-            term = jnp.dot(part, m, preferred_element_type=jnp.float32)
-            total = term if total is None else total + term
+        total = times_whole(pieces_of(x), matrix[:, pl.ds(0, 2 * LANES if f == 4 else LANES)])
         dlon[f] = total[:, :LANES].reshape(levels, rows, LANES)
         if f == 4:
             elon[...] = total[:, LANES:].reshape(levels, rows, LANES)
+
+
+def add_halo(levels, rows, padded, polar, left, right, halo1, halo2, geo, kap, d1, d2, caps, store):
+    lane = lax.broadcasted_iota(jnp.int32, left.shape, 1)
+    both = jnp.where((lane % (2 * REACH)) < REACH, left[...], right[...])
+    split = pieces_of(both)
+    packs = rows // TILE // (GROUPS // levels)
+    last = slice(4 * packs * TILE, None)
+    d1[...] = times_whole(split, halo1[...])
+    d2[...] = times_whole([piece[last] for piece in pieces_of(both)], halo2[...])
+    for f in range(FIELDS):
+        for l in range(levels):
+            caps[f, l, pl.ds(TILE - REACH, REACH), :] = polar[pl.ds((f * levels + l) * REACH, REACH), :]
+            caps[f, l, pl.ds(TILE, TILE), :] = jnp.zeros((TILE, LANES), jnp.float32)
+    for t in range(rows // TILE):
+        j, u = divmod(t, GROUPS // levels)
+        here = pl.ds(t * TILE, TILE)
+        metric, metric2 = geo[0, here, :], geo[1, here, :]
+        for l in range(levels):
+            columns = pl.ds((u * levels + l) * LANES, LANES)
+            center = [padded[f, l, pl.ds((t + 1) * TILE, TILE), :] for f in range(FIELDS)]
+            wlon, wrow, temper = center[1], center[2], center[4]
+            slon = [metric * d1[pl.ds((f * packs + j) * TILE, TILE), columns] for f in range(FIELDS)]
+            laplace = metric2 * d2[pl.ds(j * TILE, TILE), columns]
+            extra = [-wlon * slope for slope in slon]
+            extra[1] = extra[1] - temper * slon[0] - slon[4]
+            spread = slon[1]
+            if t == 0:
+                srow = []
+                for f in range(FIELDS):
+                    total = None
+                    for k in range(1, REACH + 1):
+                        behind = caps[f, l, pl.ds(TILE - k, TILE), :]
+                        term = -first_coeffs[k - 1] * behind
+                        total = term if total is None else total + term
+                        if f == 4:
+                            laplace = laplace + second_coeffs[k] * behind
+                    srow.append(total)
+                extra = [e - wrow * slope for e, slope in zip(extra, srow)]
+                extra[2] = extra[2] - temper * srow[0] - srow[4]
+                spread = spread + srow[2]
+            extra[0] = extra[0] - spread
+            extra[4] = extra[4] - (gamma_less_one * temper) * spread + kap[l] * laplace
+            for f in range(FIELDS):
+                store(f, l, t * TILE, center[f], extra[f])
 
 
 def interior(levels, rows, padded, dlon, elon, geo, kappa, store):
@@ -242,23 +286,26 @@
             out[3][l] = -carried[3] - temper * slev[0] - slev[4]
             out[4][l] = -carried[4] - (gamma_less_one * temper) * spread + kappa[l] * laplace
             for f in range(FIELDS):
-                store(f, l, r0, center[f][l], out[f][l])
+                store(f, l, r0, out[f][l])
         return carry
 
     lax.fori_loop(0, rows // TILE, body, 0)
 
 
-def fill_polar(levels, padded, polar):
-    for f in range(FIELDS):
-        for l in range(levels):
-            padded[f, l, pl.ds(TILE - REACH, REACH), :] = polar[pl.ds((f * levels + l) * REACH, REACH), :]
-
-
-def first_kernel(levels, rows, given, polar, left, right, matrix, geo, kappa, padded, rate, low, high, dlon, elon):
-    fill_polar(levels, padded, polar)
-    longitude_slopes(levels, rows, padded, left, right, matrix, dlon, elon)
-
-    def store(f, l, r0, value, tendency):
+def first_kernel(levels, rows, padded, matrix, geo, kap, rate, dlon, elon):
+    longitude_slopes(levels, rows, padded, matrix, dlon, elon)
+
+    def store(f, l, r0, tendency):
+        rate[f, l, pl.ds(r0, TILE), :] = tendency
+
+    interior(levels, rows, padded, dlon, elon, geo, kap, store)
+
+
+def first_halo_kernel(
+    levels, rows, given, padded, polar, left, right, halo1, halo2, geo, kap, rate, low, high, d1, d2, caps
+):
+    def store(f, l, r0, value, extra):
+        tendency = given[f, l, pl.ds(r0, TILE), :] + extra
         rate[f, l, pl.ds(r0, TILE), :] = tendency
         ahead = value + time_step * tendency
         if l < REACH:
@@ -266,7 +313,7 @@
         if l >= levels - REACH:
             high[pl.ds((f * REACH + l - levels + REACH) * rows + r0, TILE), :] = ahead
 
-    interior(levels, rows, padded, dlon, elon, geo, kappa, store)
+    add_halo(levels, rows, padded, polar, left, right, halo1, halo2, geo, kap, d1, d2, caps, store)
 
 
 def halo_tile(ref, rows, r0):
@@ -305,21 +352,20 @@
     for f in range(FIELDS):
         pack_edges(f, levels, rows, ahead, edge, polar, lane)
         for l in range(levels):
+            ahead[f, l, pl.ds(0, TILE), :] = jnp.zeros((TILE, LANES), jnp.float32)
             ahead[f, l, pl.ds(rows + TILE, REACH), :] = padded[f, l, pl.ds(rows + TILE, REACH), :]
 
 
 def second_kernel(
-    levels, rows, given, polar, left, right, matrix, geo, kappa, full, start, below, above,
-    padded, both, low, high, dlon, elon,
+    levels, rows, padded, matrix, geo, kap, full, start, below, above, both, low, high, dlon, elon
 ):
-    fill_polar(levels, padded, polar)
-    longitude_slopes(levels, rows, padded, left, right, matrix, dlon, elon)
-
-    def store(f, l, r0, value, tendency):
+    longitude_slopes(levels, rows, padded, matrix, dlon, elon)
+
+    def store(f, l, r0, tendency):
         at = pl.ds(r0, TILE)
         both[f, l, at, :] = (0.5 * time_step) * (full[f, l, at, :] + tendency)
 
-    interior(levels, rows, padded, dlon, elon, geo, kappa, store)
+    interior(levels, rows, padded, dlon, elon, geo, kap, store)
     tail = FIELDS * REACH * rows
 
     def body(t, carry):
@@ -338,6 +384,16 @@
         return carry
 
     lax.fori_loop(0, rows // TILE, body, 0)
+
+
+def second_halo_kernel(
+    levels, rows, given, padded, polar, left, right, halo1, halo2, geo, kap, both, d1, d2, caps
+):
+    def store(f, l, r0, value, extra):
+        at = pl.ds(r0, TILE)
+        both[f, l, at, :] = given[f, l, at, :] + (0.5 * time_step) * extra
+
+    add_halo(levels, rows, padded, polar, left, right, halo1, halo2, geo, kap, d1, d2, caps, store)
 
 
 def last_kernel(levels, rows, padded, both, below, above, low, high, kappa, out):
@@ -371,14 +427,14 @@
     ring, depth = lax.axis_size("lon"), lax.axis_size("rad")
     assert width == LANES and levels >= 2 * REACH and GROUPS % levels == 0
     assert rows % (TILE * (GROUPS // levels)) == 0
-    matrix = stencil_matrix(width)
+    matrices = stencil_matrices(width)
     geo = geometry(rows, width * ring, width)
     halo_rows = FIELDS * REACH * rows
     packs = FIELDS * levels * rows // GROUPS
     pad_shape = (FIELDS, levels, rows + 2 * TILE, width)
     full_shape = (FIELDS, levels, rows, width)
 
-    def call(kernel, out_shape, in_specs, args, scratch=(), aliases=None, name=None):
+    def call(kernel, out_shape, in_specs, args, scratch=(), aliases=None, cost=1.0, name=None):
         spaces = {id(VMEM): pltpu.VMEM, id(HBM): pltpu.HBM}
         args = [pltpu.with_memory_space_constraint(x, spaces[id(s)]) for s, x in zip(in_specs, args)]
         return pl.pallas_call(
@@ -388,6 +444,7 @@
             out_specs=jax.tree.map(lambda _: VMEM, out_shape),
             scratch_shapes=list(scratch),
             input_output_aliases=aliases or {},
+            cost_estimate=pl.CostEstimate(flops=0, bytes_accessed=int(cost * 3.69e6), transcendentals=0),
             compiler_params=pltpu.CompilerParams(vmem_limit_bytes=16 * 2**20),
             name=name,
         )(*args)
@@ -403,7 +460,7 @@
         right = lax.ppermute(edge, "lon", west)
         return left, right, lax.ppermute(polar, "lon", half)
 
-    padded, low, high, edge, polar, kap, matrix, geo = call(
+    padded, low, high, edge, polar, kap, matrix, halo1, halo2, geo = call(
         edges_kernel,
         [
             in_vmem(*pad_shape),
@@ -412,16 +469,16 @@
             in_vmem(packs, width),
             in_vmem(FIELDS * levels * REACH, width),
             in_vmem(levels, TILE, width),
-            pltpu.VMEM(matrix.shape, matrix.dtype),
+            *(pltpu.VMEM(m.shape, m.dtype) for m in matrices),
             in_vmem(*geo.shape),
         ],
-        (HBM,) * 5,
-        (state, outer_rows, kappa, matrix, geo),
+        (HBM,) * 7,
+        (state, outer_rows, kappa, *matrices, geo),
         scratch=(
             in_vmem(*full_shape),
             in_vmem(*outer_rows.shape),
             pltpu.SMEM(kappa.shape, jnp.float32),
-            pltpu.SemaphoreType.DMA((FIELDS + 4,)),
+            pltpu.SemaphoreType.DMA((FIELDS + 6,)),
         ),
         name="edges",
     )
@@ -429,14 +486,29 @@
     above = lax.ppermute(high, "rad", swap_high)
     left, right, beyond = around(edge, polar)
     lon_scratch = (in_vmem(*full_shape), in_vmem(*full_shape[1:]))
-    padded, rate, low, high = call(
+    halo_scratch = (
+        in_vmem(packs, GROUPS * width),
+        in_vmem(packs // FIELDS, GROUPS * width),
+        in_vmem(FIELDS, levels, 2 * TILE, width),
+    )
+    side = in_vmem(halo_rows, width)
+    rate = call(
         first_kernel,
-        [in_vmem(*pad_shape), in_vmem(*full_shape), in_vmem(halo_rows, width), in_vmem(halo_rows, width)],
-        (VMEM,) * 7,
-        (padded, beyond, left, right, matrix, geo, kap),
+        in_vmem(*full_shape),
+        (VMEM,) * 4,
+        (padded, matrix, geo, kap),
         scratch=lon_scratch,
+        cost=2.0,
+        name="first",
+    )
+    rate, low, high = call(
+        first_halo_kernel,
+        [in_vmem(*full_shape), side, side],
+        (VMEM,) * 9,
+        (rate, padded, beyond, left, right, halo1, halo2, geo, kap),
+        scratch=halo_scratch,
         aliases={0: 0},
-        name="first",
+        name="first_halo",
     )
     below2 = lax.ppermute(low, "rad", swap_low)
     above2 = lax.ppermute(high, "rad", swap_high)
@@ -453,14 +525,23 @@
         name="section",
     )
     left, right, beyond = around(edge, polar)
-    ahead, both, low, high = call(
+    both, low, high = call(
         second_kernel,
-        [in_vmem(*pad_shape), in_vmem(*full_shape), in_vmem(halo_rows, width), in_vmem(halo_rows, width)],
-        (VMEM,) * 11,
-        (ahead, beyond, left, right, matrix, geo, kap, full, padded, below, above),
+        [in_vmem(*full_shape), side, side],
+        (VMEM,) * 8,
+        (ahead, matrix, geo, kap, full, padded, below, above),
         scratch=lon_scratch,
+        cost=2.5,
+        name="second",
+    )
+    both = call(
+        second_halo_kernel,
+        in_vmem(*full_shape),
+        (VMEM,) * 9,
+        (both, ahead, beyond, left, right, halo1, halo2, geo, kap),
+        scratch=halo_scratch,
         aliases={0: 0},
-        name="second",
+        name="second_halo",
     )
     return call(
         last_kernel,

time: 31.7 us -> 31.6 us (level)
  Pallas kernels: 9.27 us -> 10.9 us
  waiting for transfers between devices: 8.26 us -> 6.88 us
    ppermute x2, waiting for transfers between devices: 2.75 us -> 0.01 us  [around(): right = lax.ppermute(edge, 'lon', west)]
    ppermute x1, waiting for transfers between devices: 0.01 us -> 1.89 us  [on_device(): above = lax.ppermute(high, 'rad', swap_high)]
    ppermute x2, waiting for transfers between devices: 5.36 us -> 3.65 us  [around(): left = lax.ppermute(edge, 'lon', east)]
    pallas_call x5 -> x7, Pallas kernels: 9.27 us -> 10.9 us  [call(): pl.pallas_call(functools.partial(kernel, levels, rows), out_shape=out_sha...]
    ppermute x1, waiting for transfers between devices: 0.14 us -> 1.32 us  [on_device(): above2 = lax.ppermute(high, 'rad', swap_high)]
  transfers between devices with their start and end apart: 10 -> 10, of which waited for: 5 -> 4; matrix products, arithmetic and copies ran while one was open for 0% -> 0% of each run, Pallas kernels for 19% -> 24%
where the time goes in v3:
time: 31.6 us; the launch traced here: 31.4 us
  starting transfers between devices  13.6 us (43%)
  Pallas kernels  10.9 us (34%)
  waiting for transfers between devices  6.88 us (22%)
    pallas_call x7, Pallas kernels, call(): pl.pallas_call(functools.partial(kernel, levels, rows), out_shape=out_sha...  10.9 us
    ppermute x1, starting transfers between devices, on_device(): above = lax.ppermute(high, 'rad', swap_high)  5.88 us
    ppermute x2, waiting for transfers between devices, around(): left = lax.ppermute(edge, 'lon', east)  3.65 us
    ppermute x2, starting transfers between devices, around(): return (left, right, lax.ppermute(polar, 'lon', half))  3.24 us
    ppermute x1, starting transfers between devices, on_device(): above2 = lax.ppermute(high, 'rad', swap_high)  2.09 us
    ppermute x1, waiting for transfers between devices, on_device(): above = lax.ppermute(high, 'rad', swap_high)  1.89 us
    ppermute x1, waiting for transfers between devices, on_device(): above2 = lax.ppermute(high, 'rad', swap_high)  1.32 us
    ppermute x2, starting transfers between devices, around(): left = lax.ppermute(edge, 'lon', east)  0.98 us
  transfers between devices with their start and end apart: 10, of which 4 were waited for; matrix products, arithmetic and copies ran while one was open for 0% of the time, Pallas kernels for 24%

profile of v3, /device:TPU:0, one launch (start us, length us, event | category | flops | bytes accessed | tf_op | source)
XLA Modules:
  0.0 31.4 jit_solution(14524727678009541844)
XLA Ops:
  0.0 1.8 %edges.1 = (f32[5,8,64,128]{3,2,1,0:T(8,128)S(1)}, f32[968,128]{1,0:T(8,128)S(1)}, f32[968,128]{1,0:T(8,128)S(1)}, f32[120,128]{1,0:T(8,128)S(1)}, f32[160,128]{...) custom-call(f32[5,8,48,128]{3,2,1,0:T(8,128)} %state.1, ...), custom_call_target="tpu_custom_call" | custom-call | bytes 3690000 | tf_op jit(solution)/shard_map/edges/pallas_call | solution.py:440
  1.8 0.7 %collective-permute-start.3 = (f32[968,128]{1,0:T(8,128)S(1)}, f32[968,128]{1,0:T(8,128)S(1)}, u32[]{:S(2)}, u32[]{:S(2)}) collective-permute-start(f32[968,128]{1,0:T(8,128)S(1)} %get-tuple-element.34), channel_id=1, source_target_pairs={{1,2},{2,1},{5,6},{6,5},{9,10},{10,9},{13,14},{14,13},{17,18},{18,... | collective-permute-start | bytes 1486856 | tf_op jit(solution)/shard_map/ppermute | solution.py:485
  2.5 5.9 %collective-permute-start.4 = (f32[968,128]{1,0:T(8,128)S(1)}, f32[968,128]{1,0:T(8,128)S(1)}, u32[]{:S(2)}, u32[]{:S(2)}) collective-permute-start(f32[968,128]{1,0:T(8,128)S(1)} %get-tuple-element.35), channel_id=1, source_target_pairs={{0,1},{1,0},{2,3},{3,2},{4,5},{5,4},{6,7},{7,6},{8,9},{9,8},{10,11... | collective-permute-start | bytes 1486856 | tf_op jit(solution)/shard_map/ppermute | solution.py:486
  8.4 1.5 %collective-permute-start = (f32[160,128]{1,0:T(8,128)S(1)}, f32[160,128]{1,0:T(8,128)S(1)}, u32[]{:S(2)}, u32[]{:S(2)}) collective-permute-start(f32[160,128]{1,0:T(8,128)S(1)} %get-tuple-element.29), channel_id=1, source_target_pairs={{0,16},{4,20},{8,24},{12,28},{16,0},{20,4},{24,8},{28,12},{1,17},{... | collective-permute-start | bytes 245768 | tf_op jit(solution)/shard_map/ppermute | solution.py:461
  9.9 0.0 collective-permute-start.2
  9.9 0.5 %collective-permute-start.1 = (f32[120,128]{1,0:T(8,128)S(1)}, f32[120,128]{1,0:T(8,128)S(1)}, u32[]{:S(2)}, u32[]{:S(2)}) collective-permute-start(f32[120,128]{1,0:T(8,128)S(1)} %get-tuple-element.30), channel_id=1, source_target_pairs={{0,4},{4,8},{8,12},{12,16},{16,20},{20,24},{24,28},{28,0},{1,5},{5... | collective-permute-start | bytes 184328 | tf_op jit(solution)/shard_map/ppermute | solution.py:459
  10.4 2.0 %first.1.given = f32[5,8,48,128]{3,2,1,0:T(8,128)S(1)} custom-call(f32[5,8,64,128]{3,2,1,0:T(8,128)S(1)} %get-tuple-element.25.padded.start, bf16[128,256]{1,0:T(8,128)(2,1)S(1)} %get-tuple-element.26.matrix, f32[3,48,128]{2,1,0:T(8,128)S(1)} %get-tuple-element.27.geo, f32[8,8,128]{2,1,0:T(8,128)S(1)} %get-tuple-element.28.kap.kappa), custom_call_target="tpu_custom_call" | custom-call | bytes 7380000 | tf_op jit(solution)/shard_map/first/pallas_call | solution.py:440
  12.4 0.0 collective-permute-done.2.right
  12.4 2.1 %collective-permute-done.1.left = f32[120,128]{1,0:T(8,128)S(1)} collective-permute-done((f32[120,128]{1,0:T(8,128)S(1)}, f32[120,128]{1,0:T(8,128)S(1)}, u32[]{:S(2)}, u32[]{:S(2)}) %collective-permute-start.1) | collective-permute-done | bytes 61472 | tf_op jit(solution)/shard_map/ppermute | solution.py:459
  14.5 0.0 collective-permute-done.polar
  14.5 1.2 %first_halo.1 = (f32[5,8,48,128]{3,2,1,0:T(8,128)S(1)}, f32[960,128]{1,0:T(8,128)S(1)}, f32[960,128]{1,0:T(8,128)S(1)}) custom-call(f32[5,8,48,128]{3,2,1,0:T(8,128)S(1)} %first.1.given, f32[5,8,64,128]{3,2,1,0:T(8,128)S(1)} %get-tuple-element.25.padded.start, f32[160,128]{1,0:T(8,128)S(1)} %collective-permute-done.polar, ...), custom_call_target="tpu_custom_call", output_to_operand_aliasing={{0}: (0, {})} | custom-call | bytes 3690000 | tf_op jit(solution)/shard_map/first_halo/pallas_call | solution.py:440
  15.8 0.7 %collective-permute-start.8 = (f32[960,128]{1,0:T(8,128)S(1)}, f32[960,128]{1,0:T(8,128)S(1)}, u32[]{:S(2)}, u32[]{:S(2)}) collective-permute-start(f32[960,128]{1,0:T(8,128)S(1)} %get-tuple-element.41), channel_id=1, source_target_pairs={{1,2},{2,1},{5,6},{6,5},{9,10},{10,9},{13,14},{14,13},{17,18},{18,... | collective-permute-start | bytes 1474568 | tf_op jit(solution)/shard_map/ppermute | solution.py:513
  16.5 2.1 %collective-permute-start.9 = (f32[960,128]{1,0:T(8,128)S(1)}, f32[960,128]{1,0:T(8,128)S(1)}, u32[]{:S(2)}, u32[]{:S(2)}) collective-permute-start(f32[960,128]{1,0:T(8,128)S(1)} %get-tuple-element.42), channel_id=1, source_target_pairs={{0,1},{1,0},{2,3},{3,2},{4,5},{5,4},{6,7},{7,6},{8,9},{9,8},{10,11... | collective-permute-start | bytes 1474568 | tf_op jit(solution)/shard_map/ppermute | solution.py:514
  18.5 0.0 collective-permute-done.3.below
  18.5 1.9 %collective-permute-done.4.above = f32[968,128]{1,0:T(8,128)S(1)} collective-permute-done((f32[968,128]{1,0:T(8,128)S(1)}, f32[968,128]{1,0:T(8,128)S(1)}, u32[]{:S(2)}, u32[]{:S(2)}) %collective-permute-start.4) | collective-permute-done | bytes 495648 | tf_op jit(solution)/shard_map/ppermute | solution.py:486
  20.4 0.7 %section.1 = (f32[5,8,48,128]{3,2,1,0:T(8,128)S(1)}, f32[5,8,64,128]{3,2,1,0:T(8,128)S(1)}, f32[120,128]{1,0:T(8,128)S(1)}, f32[160,128]{1,0:T(8,128)S(1)}) custom-call(f32[5,8,64,128]{3,2,1,0:T(8,128)S(1)} %get-tuple-element.25.padded.start, f32[5,8,48,128]{3,2,1,0:T(8,128)S(1)} %get-tuple-element.33.rate, f32[968,128]{1,0:T(8,128)S(1)} %collective-permute-done.3.below, ...), custom_call_target="tpu_custom_call" | custom-call | bytes 3690000 | tf_op jit(solution)/shard_map/section/pallas_call | solution.py:440
  21.2 1.7 %collective-permute-start.5 = (f32[160,128]{1,0:T(8,128)S(1)}, f32[160,128]{1,0:T(8,128)S(1)}, u32[]{:S(2)}, u32[]{:S(2)}) collective-permute-start(f32[160,128]{1,0:T(8,128)S(1)} %get-tuple-element.39), channel_id=1, source_target_pairs={{0,16},{4,20},{8,24},{12,28},{16,0},{20,4},{24,8},{28,12},{1,17},{... | collective-permute-start | bytes 245768 | tf_op jit(solution)/shard_map/ppermute | solution.py:461
  22.9 0.0 collective-permute-start.7
  22.9 0.5 %collective-permute-start.6 = (f32[120,128]{1,0:T(8,128)S(1)}, f32[120,128]{1,0:T(8,128)S(1)}, u32[]{:S(2)}, u32[]{:S(2)}) collective-permute-start(f32[120,128]{1,0:T(8,128)S(1)} %get-tuple-element.40), channel_id=1, source_target_pairs={{0,4},{4,8},{8,12},{12,16},{16,20},{20,24},{24,28},{28,0},{1,5},{5... | collective-permute-start | bytes 184328 | tf_op jit(solution)/shard_map/ppermute | solution.py:459
  23.4 2.4 %second.1 = (f32[5,8,48,128]{3,2,1,0:T(8,128)S(1)}, f32[960,128]{1,0:T(8,128)S(1)}, f32[960,128]{1,0:T(8,128)S(1)}) custom-call(f32[5,8,64,128]{3,2,1,0:T(8,128)S(1)} %get-tuple-element.36.padded, bf16[128,256]{1,0:T(8,128)(2,1)S(1)} %get-tuple-element.26.matrix, f32[3,48,128]{2,1,0:T(8,128)S(1)} %get-tuple-element.27.geo, ...), custom_call_target="tpu_custom_call" | custom-call | bytes 9225000 | tf_op jit(solution)/shard_map/second/pallas_call | solution.py:440
  25.9 0.0 collective-permute-done.7.right
  25.9 1.6 %collective-permute-done.6.left = f32[120,128]{1,0:T(8,128)S(1)} collective-permute-done((f32[120,128]{1,0:T(8,128)S(1)}, f32[120,128]{1,0:T(8,128)S(1)}, u32[]{:S(2)}, u32[]{:S(2)}) %collective-permute-start.6) | collective-permute-done | bytes 61472 | tf_op jit(solution)/shard_map/ppermute | solution.py:459
  27.5 0.0 collective-permute-done.5.polar
  27.5 1.2 %second_halo.1.both = f32[5,8,48,128]{3,2,1,0:T(8,128)S(1)} custom-call(f32[5,8,48,128]{3,2,1,0:T(8,128)S(1)} %get-tuple-element.38.given, f32[5,8,64,128]{3,2,1,0:T(8,128)S(1)} %get-tuple-element.36.padded, f32[160,128]{1,0:T(8,128)S(1)} %collective-permute-done.5.polar, ...), custom_call_target="tpu_custom_call", output_to_operand_aliasing={{}: (0, {})} | custom-call | bytes 3690000 | tf_op jit(solution)/shard_map/second_halo/pallas_call | solution.py:440
  28.6 0.0 collective-permute-done.8.below
  28.6 1.3 %collective-permute-done.9.above = f32[960,128]{1,0:T(8,128)S(1)} collective-permute-done((f32[960,128]{1,0:T(8,128)S(1)}, f32[960,128]{1,0:T(8,128)S(1)}, u32[]{:S(2)}, u32[]{:S(2)}) %collective-permute-start.9) | collective-permute-done | bytes 491552 | tf_op jit(solution)/shard_map/ppermute | solution.py:514
  30.0 1.5 %last.1 = f32[5,8,48,128]{3,2,1,0:T(8,128)} custom-call(f32[5,8,64,128]{3,2,1,0:T(8,128)S(1)} %get-tuple-element.36.padded, f32[5,8,48,128]{3,2,1,0:T(8,128)S(1)} %second_halo.1.both, f32[960,128]{1,0:T(8,128)S(1)} %collective-permute-done.8.below, f32[960,128]{1,0:T(8,128)S(1)} %collective-permute-done.9.above, f32[960,128]{1,0:T(8,128)S(1)} %get-tuple-element.43.low, ...), custom_call_target="tpu_custom_call" | custom-call | bytes 3690000 | tf_op jit(solution)/shard_map/last/pallas_call | solution.py:440
Async XLA Ops:
  1.8 16.7 %collective-permute-start.3 = (f32[968,128]{1,0:T(8,128)S(1)}, f32[968,128]{1,0:T(8,128)S(1)}, u32[]{:S(2)}, u32[]{:S(2)}) collective-permute-start(f32[968,128]{1,0:T(8,128)S(1)} %get-tuple-element.34), channel_id=1, source_target_pairs={{1,2},{2,1},{5,6},{6,5},{9,10},{10,9},{13,14},{14,13},{17,18},{18,... | collective-permute-start | bytes 1486856 | tf_op jit(solution)/shard_map/ppermute | solution.py:485
  2.5 17.9 %collective-permute-start.4 = (f32[968,128]{1,0:T(8,128)S(1)}, f32[968,128]{1,0:T(8,128)S(1)}, u32[]{:S(2)}, u32[]{:S(2)}) collective-permute-start(f32[968,128]{1,0:T(8,128)S(1)} %get-tuple-element.35), channel_id=1, source_target_pairs={{0,1},{1,0},{2,3},{3,2},{4,5},{5,4},{6,7},{7,6},{8,9},{9,8},{10,11... | collective-permute-start | bytes 1486856 | tf_op jit(solution)/shard_map/ppermute | solution.py:486
  8.4 6.1 %collective-permute-start = (f32[160,128]{1,0:T(8,128)S(1)}, f32[160,128]{1,0:T(8,128)S(1)}, u32[]{:S(2)}, u32[]{:S(2)}) collective-permute-start(f32[160,128]{1,0:T(8,128)S(1)} %get-tuple-element.29), channel_id=1, source_target_pairs={{0,16},{4,20},{8,24},{12,28},{16,0},{20,4},{24,8},{28,12},{1,17},{... | collective-permute-start | bytes 245768 | tf_op jit(solution)/shard_map/ppermute | solution.py:461
  9.9 2.5 %collective-permute-start.2 = (f32[120,128]{1,0:T(8,128)S(1)}, f32[120,128]{1,0:T(8,128)S(1)}, u32[]{:S(2)}, u32[]{:S(2)}) collective-permute-start(f32[120,128]{1,0:T(8,128)S(1)} %get-tuple-element.30), channel_id=1, source_target_pairs={{4,0},{8,4},{12,8},{16,12},{20,16},{24,20},{28,24},{0,28},{5,1},{9... | collective-permute-start | bytes 184328 | tf_op jit(solution)/shard_map/ppermute | solution.py:460
  9.9 4.5 %collective-permute-start.1 = (f32[120,128]{1,0:T(8,128)S(1)}, f32[120,128]{1,0:T(8,128)S(1)}, u32[]{:S(2)}, u32[]{:S(2)}) collective-permute-start(f32[120,128]{1,0:T(8,128)S(1)} %get-tuple-element.30), channel_id=1, source_target_pairs={{0,4},{4,8},{8,12},{12,16},{16,20},{20,24},{24,28},{28,0},{1,5},{5... | collective-permute-start | bytes 184328 | tf_op jit(solution)/shard_map/ppermute | solution.py:459
  15.8 12.9 %collective-permute-start.8 = (f32[960,128]{1,0:T(8,128)S(1)}, f32[960,128]{1,0:T(8,128)S(1)}, u32[]{:S(2)}, u32[]{:S(2)}) collective-permute-start(f32[960,128]{1,0:T(8,128)S(1)} %get-tuple-element.41), channel_id=1, source_target_pairs={{1,2},{2,1},{5,6},{6,5},{9,10},{10,9},{13,14},{14,13},{17,18},{18,... | collective-permute-start | bytes 1474568 | tf_op jit(solution)/shard_map/ppermute | solution.py:513
  16.5 13.5 %collective-permute-start.9 = (f32[960,128]{1,0:T(8,128)S(1)}, f32[960,128]{1,0:T(8,128)S(1)}, u32[]{:S(2)}, u32[]{:S(2)}) collective-permute-start(f32[960,128]{1,0:T(8,128)S(1)} %get-tuple-element.42), channel_id=1, source_target_pairs={{0,1},{1,0},{2,3},{3,2},{4,5},{5,4},{6,7},{7,6},{8,9},{9,8},{10,11... | collective-permute-start | bytes 1474568 | tf_op jit(solution)/shard_map/ppermute | solution.py:514
  21.2 6.3 %collective-permute-start.5 = (f32[160,128]{1,0:T(8,128)S(1)}, f32[160,128]{1,0:T(8,128)S(1)}, u32[]{:S(2)}, u32[]{:S(2)}) collective-permute-start(f32[160,128]{1,0:T(8,128)S(1)} %get-tuple-element.39), channel_id=1, source_target_pairs={{0,16},{4,20},{8,24},{12,28},{16,0},{20,4},{24,8},{28,12},{1,17},{... | collective-permute-start | bytes 245768 | tf_op jit(solution)/shard_map/ppermute | solution.py:461
  22.9 2.9 %collective-permute-start.7 = (f32[120,128]{1,0:T(8,128)S(1)}, f32[120,128]{1,0:T(8,128)S(1)}, u32[]{:S(2)}, u32[]{:S(2)}) collective-permute-start(f32[120,128]{1,0:T(8,128)S(1)} %get-tuple-element.40), channel_id=1, source_target_pairs={{4,0},{8,4},{12,8},{16,12},{20,16},{24,20},{28,24},{0,28},{5,1},{9... | collective-permute-start | bytes 184328 | tf_op jit(solution)/shard_map/ppermute | solution.py:460
  22.9 4.5 %collective-permute-start.6 = (f32[120,128]{1,0:T(8,128)S(1)}, f32[120,128]{1,0:T(8,128)S(1)}, u32[]{:S(2)}, u32[]{:S(2)}) collective-permute-start(f32[120,128]{1,0:T(8,128)S(1)} %get-tuple-element.40), channel_id=1, source_target_pairs={{0,4},{4,8},{8,12},{12,16},{16,20},{20,24},{24,28},{28,0},{1,5},{5... | collective-permute-start | bytes 184328 | tf_op jit(solution)/shard_map/ppermute | solution.py:459

commit v4 on v3

--- a/solution.py
+++ b/solution.py
@@ -99,49 +99,55 @@
     return out
 
 
+def mirrored():
+    odd = (lax.axis_index("rad") + lax.axis_index("lon")) % 2
+    return odd, jnp.where(odd == 1, -1.0, 1.0).astype(jnp.float32)
+
+
 def edges_kernel(
-    levels, rows, state, outer, kappa, matrix_in, halo1_in, halo2_in, geo_in,
-    padded, low, high, edge, polar, kap, matrix, halo1, halo2, geo,
+    levels, rows, state, outer, kappa, matrix_in, geo_in,
+    padded, low, high, edge, polar, kap, matrix, geo,
     staged, outer_staged, kappa_scalars, sems,
 ):
-    block = REACH * rows
-    odd = lax.axis_index("rad") % 2
-    mirror = jnp.where(odd == 1, -1.0, 1.0).astype(jnp.float32)
-    reads = [(state.at[f], staged.at[f]) for f in range(FIELDS)]
-    reads += [(outer, outer_staged), (kappa, kappa_scalars), (matrix_in, matrix), (geo_in, geo)]
-    reads += [(halo1_in, halo1), (halo2_in, halo2)]
+    block, field = REACH * rows, levels * rows
+    odd, mirror = mirrored()
+    starts = [jnp.where(odd == side, 0, levels - REACH) for side in (0, 1)]
+    reads = [(kappa, kappa_scalars)]
+    for start, side in zip(starts[::-1], (high, low)):
+        for f in range(FIELDS):
+            at = pl.multiple_of(f * field + start * rows, TILE)
+            reads.append((state.at[pl.ds(at, block)], side.at[pl.ds(f * block, block)]))
+    for f in range(FIELDS):
+        at = pl.ds(f * field, field)
+        reads.append((state.at[at], staged.at[at]))
+    reads += [(outer, outer_staged), (matrix_in, matrix), (geo_in, geo)]
     copies = [pltpu.make_async_copy(*read, sems.at[i]) for i, read in enumerate(reads)]
     for copy in copies:
         copy.start()
+    copies[0].wait()
+    for l in range(levels):
+        kap[l] = jnp.full((TILE, LANES), kappa_scalars[jnp.where(odd == 1, levels - 1 - l, l)], jnp.float32)
+    for start, side in zip(starts, (low, high)):
+        for i in range(REACH):
+            value = kappa_scalars[start + i]
+            side[pl.ds(FIELDS * block + i, 1), :] = jnp.full((1, LANES), value, jnp.float32)
+        side[pl.ds(FIELDS * block + REACH, REACH), :] = jnp.ones((REACH, LANES), jnp.float32)
     lane = lax.broadcasted_iota(jnp.int32, (TILE, LANES), 1)
     for f in range(FIELDS):
-        copies[f].wait()
+        copies[1 + 2 * FIELDS + f].wait()
         for l in range(levels):
-            whole = staged[f, jnp.where(odd == 1, levels - 1 - l, l)]
-            if f == 3:
-                whole = mirror * whole
-            padded[f, l, pl.ds(TILE, rows), :] = whole
+            at = f * field + jnp.where(odd == 1, levels - 1 - l, l) * rows
+            whole = staged[pl.ds(pl.multiple_of(at, TILE), rows), :]
+            padded[f, l, pl.ds(TILE, rows), :] = mirror * whole if f == 3 else whole
             padded[f, l, pl.ds(0, TILE), :] = jnp.zeros((TILE, LANES), jnp.float32)
-            if l < REACH:
-                low[pl.ds(f * block + l * rows, rows), :] = whole
-            if l >= levels - REACH:
-                high[pl.ds(f * block + (l - levels + REACH) * rows, rows), :] = whole
         pack_edges(f, levels, rows, padded, edge, polar, lane)
-    for copy in copies[FIELDS:]:
-        copy.wait()
+    for i, copy in enumerate(copies):
+        if 1 <= i <= 2 * FIELDS or i > 3 * FIELDS:
+            copy.wait()
     for l in range(levels):
-        real = jnp.where(odd == 1, levels - 1 - l, l)
-        value = kappa_scalars[real]
-        kap[l] = jnp.full((TILE, LANES), value, jnp.float32)
-        if l < REACH:
-            low[pl.ds(FIELDS * block + l, 1), :] = jnp.full((1, LANES), value, jnp.float32)
-        if l >= levels - REACH:
-            high[pl.ds(FIELDS * block + l - levels + REACH, 1), :] = jnp.full((1, LANES), value, jnp.float32)
         for f in range(FIELDS):
-            beyond = outer_staged[f, real]
+            beyond = outer_staged[f, jnp.where(odd == 1, levels - 1 - l, l)]
             padded[f, l, pl.ds(TILE + rows, REACH), :] = mirror * beyond if f == 3 else beyond
-    low[pl.ds(FIELDS * block + REACH, REACH), :] = jnp.ones((REACH, LANES), jnp.float32)
-    high[pl.ds(FIELDS * block + REACH, REACH), :] = jnp.ones((REACH, LANES), jnp.float32)
 
 
 def pack_edges(f, levels, rows, padded, edge, polar, lane):
@@ -203,10 +209,11 @@
         here = pl.ds(t * TILE, TILE)
         metric, metric2 = geo[0, here, :], geo[1, here, :]
         for l in range(levels):
-            columns = pl.ds((u * levels + l) * LANES, LANES)
+            columns = pl.ds((u * levels + levels - 1 - l) * LANES, LANES)
             center = [padded[f, l, pl.ds((t + 1) * TILE, TILE), :] for f in range(FIELDS)]
             wlon, wrow, temper = center[1], center[2], center[4]
             slon = [metric * d1[pl.ds((f * packs + j) * TILE, TILE), columns] for f in range(FIELDS)]
+            slon[3] = -slon[3]
             laplace = metric2 * d2[pl.ds(j * TILE, TILE), columns]
             extra = [-wlon * slope for slope in slon]
             extra[1] = extra[1] - temper * slon[0] - slon[4]
@@ -292,13 +299,21 @@
     lax.fori_loop(0, rows // TILE, body, 0)
 
 
-def first_kernel(levels, rows, padded, matrix, geo, kap, rate, dlon, elon):
+def first_kernel(
+    levels, rows, padded, matrix, geo, kap, halo1_in, halo2_in, rate, halo1, halo2, dlon, elon, sems
+):
+    reads = ((halo1_in, halo1), (halo2_in, halo2))
+    copies = [pltpu.make_async_copy(*read, sems.at[i]) for i, read in enumerate(reads)]
+    for copy in copies:
+        copy.start()
     longitude_slopes(levels, rows, padded, matrix, dlon, elon)
 
     def store(f, l, r0, tendency):
         rate[f, l, pl.ds(r0, TILE), :] = tendency
 
     interior(levels, rows, padded, dlon, elon, geo, kap, store)
+    for copy in copies:
+        copy.wait()
 
 
 def first_halo_kernel(
@@ -316,6 +331,15 @@
     add_halo(levels, rows, padded, polar, left, right, halo1, halo2, geo, kap, d1, d2, caps, store)
 
 
+def raw_tile(ref, rows, r0, odd, mirror):
+    out = []
+    for f in range(FIELDS):
+        ats = [(f * REACH + jnp.where(odd == 1, REACH - 1 - b, b)) * rows + r0 for b in range(REACH)]
+        out.append([ref[pl.ds(pl.multiple_of(at, TILE), TILE), :] for at in ats])
+    out[3] = [mirror * v for v in out[3]]
+    return out
+
+
 def halo_tile(ref, rows, r0):
     out = [
         [ref[pl.ds((f * REACH + REACH - 1 - b) * rows + r0, TILE), :] for b in range(REACH)]
@@ -332,10 +356,12 @@
 
 
 def section_kernel(levels, rows, padded, rate, below, above, kappa, full, ahead, edge, polar):
+    odd, mirror = mirrored()
+
     def body(t, carry):
         r0 = pl.multiple_of(t * TILE, TILE)
         for halo_ref, at, up in ((below, 0, False), (above, levels - REACH, True)):
-            halo = halo_tile(halo_ref, rows, r0)
+            halo = raw_tile(halo_ref, rows, r0, odd, mirror)
             center = [
                 [padded[f, at + a, pl.ds(r0 + TILE, TILE), :] for a in range(REACH)] for f in range(FIELDS)
             ]
@@ -367,15 +393,18 @@
 
     interior(levels, rows, padded, dlon, elon, geo, kap, store)
     tail = FIELDS * REACH * rows
+    odd, mirror = mirrored()
 
     def body(t, carry):
         r0 = pl.multiple_of(t * TILE, TILE)
         for halo_ref, out, at, up in ((below, low, 0, True), (above, high, levels - REACH, False)):
-            beyond = halo_tile(halo_ref, rows, r0)
+            beyond = raw_tile(halo_ref, rows, r0, odd, mirror)
             mine = [
                 [start[f, at + a, pl.ds(r0 + TILE, TILE), :] for a in range(REACH)] for f in range(FIELDS)
             ]
-            kappas = [halo_ref[pl.ds(tail + REACH - 1 - a, 1), :] for a in range(REACH)]
+            kappas = [
+                halo_ref[pl.ds(tail + jnp.where(odd == 1, REACH - 1 - a, a), 1), :] for a in range(REACH)
+            ]
             there = time_step * halo_ref[pl.ds(tail + REACH, 1), :]
             extra = across_level(beyond[3], beyond[4], mine, kappas, up)
             for f in range(FIELDS):
@@ -397,8 +426,7 @@
 
 
 def last_kernel(levels, rows, padded, both, below, above, low, high, kappa, out):
-    odd = lax.axis_index("rad") % 2
-    mirror = jnp.where(odd == 1, -1.0, 1.0).astype(jnp.float32)
+    odd, mirror = mirrored()
 
     def body(t, carry):
         r0 = pl.multiple_of(t * TILE, TILE)
@@ -425,6 +453,7 @@
 def on_device(state, outer_rows, kappa):
     levels, rows, width = state.shape[1:]
     ring, depth = lax.axis_size("lon"), lax.axis_size("rad")
+    assert ring % 4 == 0
     assert width == LANES and levels >= 2 * REACH and GROUPS % levels == 0
     assert rows % (TILE * (GROUPS // levels)) == 0
     matrices = stencil_matrices(width)
@@ -452,15 +481,22 @@
     east = [(i, (i + 1) % ring) for i in range(ring)]
     west = [(b, a) for a, b in east]
     half = [(i, (i + ring // 2) % ring) for i in range(ring)]
-    swap_high = [p for i in range(0, depth - 1, 2) for p in ((i, i + 1), (i + 1, i))]
-    swap_low = [p for i in range(1, depth - 1, 2) for p in ((i, i + 1), (i + 1, i))]
+    def swaps(first):
+        pairs = [
+            (lon * depth + i, lon * depth + i + 1)
+            for lon in range(ring)
+            for i in range((lon + first) % 2, depth - 1, 2)
+        ]
+        return pairs + [(b, a) for a, b in pairs]
+
+    swap_high, swap_low = swaps(0), swaps(1)
 
     def around(edge, polar):
         left = lax.ppermute(edge, "lon", east)
         right = lax.ppermute(edge, "lon", west)
         return left, right, lax.ppermute(polar, "lon", half)
 
-    padded, low, high, edge, polar, kap, matrix, halo1, halo2, geo = call(
+    padded, low, high, edge, polar, kap, matrix, geo = call(
         edges_kernel,
         [
             in_vmem(*pad_shape),
@@ -469,21 +505,21 @@
             in_vmem(packs, width),
             in_vmem(FIELDS * levels * REACH, width),
             in_vmem(levels, TILE, width),
-            *(pltpu.VMEM(m.shape, m.dtype) for m in matrices),
+            pltpu.VMEM(matrices[0].shape, matrices[0].dtype),
             in_vmem(*geo.shape),
         ],
-        (HBM,) * 7,
-        (state, outer_rows, kappa, *matrices, geo),
+        (HBM,) * 5,
+        (state.reshape(-1, width), outer_rows, kappa, matrices[0], geo),
         scratch=(
-            in_vmem(*full_shape),
+            in_vmem(FIELDS * levels * rows, width),
             in_vmem(*outer_rows.shape),
             pltpu.SMEM(kappa.shape, jnp.float32),
-            pltpu.SemaphoreType.DMA((FIELDS + 6,)),
+            pltpu.SemaphoreType.DMA((3 * FIELDS + 4,)),
         ),
         name="edges",
     )
-    below = lax.ppermute(low, "rad", swap_low)
-    above = lax.ppermute(high, "rad", swap_high)
+    below = lax.ppermute(low, ("lon", "rad"), swap_low)
+    above = lax.ppermute(high, ("lon", "rad"), swap_high)
     left, right, beyond = around(edge, polar)
     lon_scratch = (in_vmem(*full_shape), in_vmem(*full_shape[1:]))
     halo_scratch = (
@@ -492,12 +528,12 @@
         in_vmem(FIELDS, levels, 2 * TILE, width),
     )
     side = in_vmem(halo_rows, width)
-    rate = call(
+    rate, halo1, halo2 = call(
         first_kernel,
-        in_vmem(*full_shape),
-        (VMEM,) * 4,
-        (padded, matrix, geo, kap),
-        scratch=lon_scratch,
+        [in_vmem(*full_shape), *(pltpu.VMEM(m.shape, m.dtype) for m in matrices[1:])],
+        (VMEM,) * 4 + (HBM,) * 2,
+        (padded, matrix, geo, kap, *matrices[1:]),
+        scratch=(*lon_scratch, pltpu.SemaphoreType.DMA((2,))),
         cost=2.0,
         name="first",
     )
@@ -510,8 +546,8 @@
         aliases={0: 0},
         name="first_halo",
     )
-    below2 = lax.ppermute(low, "rad", swap_low)
-    above2 = lax.ppermute(high, "rad", swap_high)
+    below2 = lax.ppermute(low, ("lon", "rad"), swap_low)
+    above2 = lax.ppermute(high, ("lon", "rad"), swap_high)
     full, ahead, edge, polar = call(
         section_kernel,
         [

time: 31.6 us -> 34.7 us (1.098)
  starting transfers between devices: 13.6 us -> 18.3 us
  waiting for transfers between devices: 6.88 us -> 4.62 us
  Pallas kernels: 10.9 us -> 11.4 us
    ppermute x4, starting transfers between devices: 9.35 us -> 14.1 us  [the longest x1 7.72 us: on_device(): above = lax.ppermute(high, ('lon', 'rad'), swap_high)]
    ppermute x4, waiting for transfers between devices: 3.21 us -> 1.02 us  [the longest x1 1.01 us: on_device(): above2 = lax.ppermute(high, ('lon', 'rad'), swap_high)]
    pallas_call x7, Pallas kernels: 10.9 us -> 11.4 us  [call(): pl.pallas_call(functools.partial(kernel, levels, rows), out_shape=out_sha...]
  transfers between devices with their start and end apart: 10 -> 10, of which waited for: 4 -> 3; matrix products, arithmetic and copies ran while one was open for 0% -> 0% of each run, Pallas kernels for 24% -> 22%
where the time goes in v4:
time: 34.7 us; the launch traced here: 34.5 us
  starting transfers between devices  18.3 us (53%)
  Pallas kernels  11.4 us (33%)
  waiting for transfers between devices  4.62 us (13%)
    pallas_call x7, Pallas kernels, call(): pl.pallas_call(functools.partial(kernel, levels, rows), out_shape=out_sha...  11.4 us
    ppermute x1, starting transfers between devices, on_device(): above = lax.ppermute(high, ('lon', 'rad'), swap_high)  7.72 us
    ppermute x1, starting transfers between devices, on_device(): above2 = lax.ppermute(high, ('lon', 'rad'), swap_high)  5.02 us
    ppermute x2, waiting for transfers between devices, around(): left = lax.ppermute(edge, 'lon', east)  3.59 us
    ppermute x2, starting transfers between devices, around(): return (left, right, lax.ppermute(polar, 'lon', half))  3.17 us
    ppermute x2, starting transfers between devices, around(): left = lax.ppermute(edge, 'lon', east)  1.01 us
    ppermute x1, waiting for transfers between devices, on_device(): above2 = lax.ppermute(high, ('lon', 'rad'), swap_high)  1.01 us
  transfers between devices with their start and end apart: 10, of which 3 were waited for; matrix products, arithmetic and copies ran while one was open for 0% of the time, Pallas kernels for 22%

profile of v4, /device:TPU:0, one launch (start us, length us, event | category | flops | bytes accessed | tf_op | source)
XLA Modules:
  0.0 34.5 jit_solution(6724603022829201354)
XLA Ops:
  0.0 2.3 %edges.1 = (f32[5,8,64,128]{3,2,1,0:T(8,128)S(1)}, f32[968,128]{1,0:T(8,128)S(1)}, f32[968,128]{1,0:T(8,128)S(1)}, f32[120,128]{1,0:T(8,128)S(1)}, f32[160,128]{...) custom-call(f32[1920,128]{1,0:T(8,128)} %bitcast.1, ...), custom_call_target="tpu_custom_call" | custom-call | bytes 3690000 | tf_op jit(solution)/shard_map/edges/pallas_call | solution.py:469
  2.3 0.7 %collective-permute-start.3 = (f32[968,128]{1,0:T(8,128)S(1)}, f32[968,128]{1,0:T(8,128)S(1)}, u32[]{:S(2)}, u32[]{:S(2)}) collective-permute-start(f32[968,128]{1,0:T(8,128)S(1)} %get-tuple-element.36), channel_id=1, source_target_pairs={{1,2},{4,5},{6,7},{9,10},{12,13},{14,15},{17,18},{20,21},{22,23},{... | collective-permute-start | bytes 1486856 | tf_op jit(solution)/shard_map/ppermute | solution.py:521
  3.0 7.7 %collective-permute-start.4 = (f32[968,128]{1,0:T(8,128)S(1)}, f32[968,128]{1,0:T(8,128)S(1)}, u32[]{:S(2)}, u32[]{:S(2)}) collective-permute-start(f32[968,128]{1,0:T(8,128)S(1)} %get-tuple-element.37), channel_id=1, source_target_pairs={{0,1},{2,3},{5,6},{8,9},{10,11},{13,14},{16,17},{18,19},{21,22},{2... | collective-permute-start | bytes 1486856 | tf_op jit(solution)/shard_map/ppermute | solution.py:522
  10.8 1.6 %collective-permute-start = (f32[160,128]{1,0:T(8,128)S(1)}, f32[160,128]{1,0:T(8,128)S(1)}, u32[]{:S(2)}, u32[]{:S(2)}) collective-permute-start(f32[160,128]{1,0:T(8,128)S(1)} %get-tuple-element.31), channel_id=1, source_target_pairs={{0,16},{4,20},{8,24},{12,28},{16,0},{20,4},{24,8},{28,12},{1,17},{... | collective-permute-start | bytes 245768 | tf_op jit(solution)/shard_map/ppermute | solution.py:497
  12.4 0.0 collective-permute-start.2
  12.4 0.5 %collective-permute-start.1 = (f32[120,128]{1,0:T(8,128)S(1)}, f32[120,128]{1,0:T(8,128)S(1)}, u32[]{:S(2)}, u32[]{:S(2)}) collective-permute-start(f32[120,128]{1,0:T(8,128)S(1)} %get-tuple-element.32), channel_id=1, source_target_pairs={{0,4},{4,8},{8,12},{12,16},{16,20},{20,24},{24,28},{28,0},{1,5},{5... | collective-permute-start | bytes 184328 | tf_op jit(solution)/shard_map/ppermute | solution.py:495
  12.9 2.0 %first.1 = (f32[5,8,48,128]{3,2,1,0:T(8,128)S(1)}, bf16[128,2048]{1,0:T(8,128)(2,1)S(1)}, bf16[128,2048]{1,0:T(8,128)(2,1)S(1)}) custom-call(f32[5,8,64,128]{3,2,1,0:T(8,128)S(1)} %get-tuple-element.26.padded.start, bf16[128,256]{1,0:T(8,128)(2,1)S(1)} %get-tuple-element.27.matrix, f32[3,48,128]{2,1,0:T(8,128)S(1)} %get-tuple-element.28.geo, ...), custom_call_target="tpu_custom_call" | custom-call | bytes 7380000 | tf_op jit(solution)/shard_map/first/pallas_call | solution.py:469
  14.9 0.0 collective-permute-done.2.right
  14.9 2.0 %collective-permute-done.1.left = f32[120,128]{1,0:T(8,128)S(1)} collective-permute-done((f32[120,128]{1,0:T(8,128)S(1)}, f32[120,128]{1,0:T(8,128)S(1)}, u32[]{:S(2)}, u32[]{:S(2)}) %collective-permute-start.1) | collective-permute-done | bytes 61472 | tf_op jit(solution)/shard_map/ppermute | solution.py:495
  16.9 0.0 collective-permute-done.polar
  16.9 1.2 %first_halo.1 = (f32[5,8,48,128]{3,2,1,0:T(8,128)S(1)}, f32[960,128]{1,0:T(8,128)S(1)}, f32[960,128]{1,0:T(8,128)S(1)}) custom-call(f32[5,8,48,128]{3,2,1,0:T(8,128)S(1)} %get-tuple-element.30.given, f32[5,8,64,128]{3,2,1,0:T(8,128)S(1)} %get-tuple-element.26.padded.start, ...), custom_call_target="tpu_custom_call", output_to_operand_aliasing={{0}: (0, {})} | custom-call | bytes 3690000 | tf_op jit(solution)/shard_map/first_halo/pallas_call | solution.py:469
  18.1 0.7 %collective-permute-start.8 = (f32[960,128]{1,0:T(8,128)S(1)}, f32[960,128]{1,0:T(8,128)S(1)}, u32[]{:S(2)}, u32[]{:S(2)}) collective-permute-start(f32[960,128]{1,0:T(8,128)S(1)} %get-tuple-element.43), channel_id=1, source_target_pairs={{1,2},{4,5},{6,7},{9,10},{12,13},{14,15},{17,18},{20,21},{22,23},{... | collective-permute-start | bytes 1474568 | tf_op jit(solution)/shard_map/ppermute | solution.py:549
  18.8 5.0 %collective-permute-start.9 = (f32[960,128]{1,0:T(8,128)S(1)}, f32[960,128]{1,0:T(8,128)S(1)}, u32[]{:S(2)}, u32[]{:S(2)}) collective-permute-start(f32[960,128]{1,0:T(8,128)S(1)} %get-tuple-element.44), channel_id=1, source_target_pairs={{0,1},{2,3},{5,6},{8,9},{10,11},{13,14},{16,17},{18,19},{21,22},{2... | collective-permute-start | bytes 1474568 | tf_op jit(solution)/shard_map/ppermute | solution.py:550
  23.9 0.0 collective-permute-done.3.below
  23.9 0.0 collective-permute-done.4.above
  23.9 0.8 %section.1 = (f32[5,8,48,128]{3,2,1,0:T(8,128)S(1)}, f32[5,8,64,128]{3,2,1,0:T(8,128)S(1)}, f32[120,128]{1,0:T(8,128)S(1)}, f32[160,128]{1,0:T(8,128)S(1)}) custom-call(f32[5,8,64,128]{3,2,1,0:T(8,128)S(1)} %get-tuple-element.26.padded.start, f32[5,8,48,128]{3,2,1,0:T(8,128)S(1)} %get-tuple-element.35.rate, f32[968,128]{1,0:T(8,128)S(1)} %collective-permute-done.3.below, ...), custom_call_target="tpu_custom_call" | custom-call | bytes 3690000 | tf_op jit(solution)/shard_map/section/pallas_call | solution.py:469
  24.7 1.6 %collective-permute-start.5 = (f32[160,128]{1,0:T(8,128)S(1)}, f32[160,128]{1,0:T(8,128)S(1)}, u32[]{:S(2)}, u32[]{:S(2)}) collective-permute-start(f32[160,128]{1,0:T(8,128)S(1)} %get-tuple-element.41), channel_id=1, source_target_pairs={{0,16},{4,20},{8,24},{12,28},{16,0},{20,4},{24,8},{28,12},{1,17},{... | collective-permute-start | bytes 245768 | tf_op jit(solution)/shard_map/ppermute | solution.py:497
  26.3 0.0 collective-permute-start.7
  26.3 0.5 %collective-permute-start.6 = (f32[120,128]{1,0:T(8,128)S(1)}, f32[120,128]{1,0:T(8,128)S(1)}, u32[]{:S(2)}, u32[]{:S(2)}) collective-permute-start(f32[120,128]{1,0:T(8,128)S(1)} %get-tuple-element.42), channel_id=1, source_target_pairs={{0,4},{4,8},{8,12},{12,16},{16,20},{20,24},{24,28},{28,0},{1,5},{5... | collective-permute-start | bytes 184328 | tf_op jit(solution)/shard_map/ppermute | solution.py:495
  26.8 2.4 %second.1 = (f32[5,8,48,128]{3,2,1,0:T(8,128)S(1)}, f32[960,128]{1,0:T(8,128)S(1)}, f32[960,128]{1,0:T(8,128)S(1)}) custom-call(f32[5,8,64,128]{3,2,1,0:T(8,128)S(1)} %get-tuple-element.38.padded, bf16[128,256]{1,0:T(8,128)(2,1)S(1)} %get-tuple-element.27.matrix, f32[3,48,128]{2,1,0:T(8,128)S(1)} %get-tuple-element.28.geo, ...), custom_call_target="tpu_custom_call" | custom-call | bytes 9225000 | tf_op jit(solution)/shard_map/second/pallas_call | solution.py:469
  29.2 0.0 collective-permute-done.7.right
  29.2 1.6 %collective-permute-done.6.left = f32[120,128]{1,0:T(8,128)S(1)} collective-permute-done((f32[120,128]{1,0:T(8,128)S(1)}, f32[120,128]{1,0:T(8,128)S(1)}, u32[]{:S(2)}, u32[]{:S(2)}) %collective-permute-start.6) | collective-permute-done | bytes 61472 | tf_op jit(solution)/shard_map/ppermute | solution.py:495
  30.8 0.0 collective-permute-done.5.polar
  30.8 1.1 %second_halo.1.both = f32[5,8,48,128]{3,2,1,0:T(8,128)S(1)} custom-call(f32[5,8,48,128]{3,2,1,0:T(8,128)S(1)} %get-tuple-element.40.given, f32[5,8,64,128]{3,2,1,0:T(8,128)S(1)} %get-tuple-element.38.padded, f32[160,128]{1,0:T(8,128)S(1)} %collective-permute-done.5.polar, ...), custom_call_target="tpu_custom_call", output_to_operand_aliasing={{}: (0, {})} | custom-call | bytes 3690000 | tf_op jit(solution)/shard_map/second_halo/pallas_call | solution.py:469
  32.0 0.0 collective-permute-done.8.below
  32.0 1.0 %collective-permute-done.9.above = f32[960,128]{1,0:T(8,128)S(1)} collective-permute-done((f32[960,128]{1,0:T(8,128)S(1)}, f32[960,128]{1,0:T(8,128)S(1)}, u32[]{:S(2)}, u32[]{:S(2)}) %collective-permute-start.9) | collective-permute-done | bytes 491552 | tf_op jit(solution)/shard_map/ppermute | solution.py:550
  33.0 1.5 %last.1 = f32[5,8,48,128]{3,2,1,0:T(8,128)} custom-call(f32[5,8,64,128]{3,2,1,0:T(8,128)S(1)} %get-tuple-element.38.padded, f32[5,8,48,128]{3,2,1,0:T(8,128)S(1)} %second_halo.1.both, f32[960,128]{1,0:T(8,128)S(1)} %collective-permute-done.8.below, f32[960,128]{1,0:T(8,128)S(1)} %collective-permute-done.9.above, f32[960,128]{1,0:T(8,128)S(1)} %get-tuple-element.45.low, ...), custom_call_target="tpu_custom_call" | custom-call | bytes 3690000 | tf_op jit(solution)/shard_map/last/pallas_call | solution.py:469
Async XLA Ops:
  2.3 21.5 %collective-permute-start.3 = (f32[968,128]{1,0:T(8,128)S(1)}, f32[968,128]{1,0:T(8,128)S(1)}, u32[]{:S(2)}, u32[]{:S(2)}) collective-permute-start(f32[968,128]{1,0:T(8,128)S(1)} %get-tuple-element.36), channel_id=1, source_target_pairs={{1,2},{4,5},{6,7},{9,10},{12,13},{14,15},{17,18},{20,21},{22,23},{... | collective-permute-start | bytes 1486856 | tf_op jit(solution)/shard_map/ppermute | solution.py:521
  3.0 20.9 %collective-permute-start.4 = (f32[968,128]{1,0:T(8,128)S(1)}, f32[968,128]{1,0:T(8,128)S(1)}, u32[]{:S(2)}, u32[]{:S(2)}) collective-permute-start(f32[968,128]{1,0:T(8,128)S(1)} %get-tuple-element.37), channel_id=1, source_target_pairs={{0,1},{2,3},{5,6},{8,9},{10,11},{13,14},{16,17},{18,19},{21,22},{2... | collective-permute-start | bytes 1486856 | tf_op jit(solution)/shard_map/ppermute | solution.py:522
  10.8 6.1 %collective-permute-start = (f32[160,128]{1,0:T(8,128)S(1)}, f32[160,128]{1,0:T(8,128)S(1)}, u32[]{:S(2)}, u32[]{:S(2)}) collective-permute-start(f32[160,128]{1,0:T(8,128)S(1)} %get-tuple-element.31), channel_id=1, source_target_pairs={{0,16},{4,20},{8,24},{12,28},{16,0},{20,4},{24,8},{28,12},{1,17},{... | collective-permute-start | bytes 245768 | tf_op jit(solution)/shard_map/ppermute | solution.py:497
  12.4 2.5 %collective-permute-start.2 = (f32[120,128]{1,0:T(8,128)S(1)}, f32[120,128]{1,0:T(8,128)S(1)}, u32[]{:S(2)}, u32[]{:S(2)}) collective-permute-start(f32[120,128]{1,0:T(8,128)S(1)} %get-tuple-element.32), channel_id=1, source_target_pairs={{4,0},{8,4},{12,8},{16,12},{20,16},{24,20},{28,24},{0,28},{5,1},{9... | collective-permute-start | bytes 184328 | tf_op jit(solution)/shard_map/ppermute | solution.py:496
  12.4 4.5 %collective-permute-start.1 = (f32[120,128]{1,0:T(8,128)S(1)}, f32[120,128]{1,0:T(8,128)S(1)}, u32[]{:S(2)}, u32[]{:S(2)}) collective-permute-start(f32[120,128]{1,0:T(8,128)S(1)} %get-tuple-element.32), channel_id=1, source_target_pairs={{0,4},{4,8},{8,12},{12,16},{16,20},{20,24},{24,28},{28,0},{1,5},{5... | collective-permute-start | bytes 184328 | tf_op jit(solution)/shard_map/ppermute | solution.py:495
  18.1 13.8 %collective-permute-start.8 = (f32[960,128]{1,0:T(8,128)S(1)}, f32[960,128]{1,0:T(8,128)S(1)}, u32[]{:S(2)}, u32[]{:S(2)}) collective-permute-start(f32[960,128]{1,0:T(8,128)S(1)} %get-tuple-element.43), channel_id=1, source_target_pairs={{1,2},{4,5},{6,7},{9,10},{12,13},{14,15},{17,18},{20,21},{22,23},{... | collective-permute-start | bytes 1474568 | tf_op jit(solution)/shard_map/ppermute | solution.py:549
  18.8 14.2 %collective-permute-start.9 = (f32[960,128]{1,0:T(8,128)S(1)}, f32[960,128]{1,0:T(8,128)S(1)}, u32[]{:S(2)}, u32[]{:S(2)}) collective-permute-start(f32[960,128]{1,0:T(8,128)S(1)} %get-tuple-element.44), channel_id=1, source_target_pairs={{0,1},{2,3},{5,6},{8,9},{10,11},{13,14},{16,17},{18,19},{21,22},{2... | collective-permute-start | bytes 1474568 | tf_op jit(solution)/shard_map/ppermute | solution.py:550
  24.7 6.1 %collective-permute-start.5 = (f32[160,128]{1,0:T(8,128)S(1)}, f32[160,128]{1,0:T(8,128)S(1)}, u32[]{:S(2)}, u32[]{:S(2)}) collective-permute-start(f32[160,128]{1,0:T(8,128)S(1)} %get-tuple-element.41), channel_id=1, source_target_pairs={{0,16},{4,20},{8,24},{12,28},{16,0},{20,4},{24,8},{28,12},{1,17},{... | collective-permute-start | bytes 245768 | tf_op jit(solution)/shard_map/ppermute | solution.py:497
  26.3 3.0 %collective-permute-start.7 = (f32[120,128]{1,0:T(8,128)S(1)}, f32[120,128]{1,0:T(8,128)S(1)}, u32[]{:S(2)}, u32[]{:S(2)}) collective-permute-start(f32[120,128]{1,0:T(8,128)S(1)} %get-tuple-element.42), channel_id=1, source_target_pairs={{4,0},{8,4},{12,8},{16,12},{20,16},{24,20},{28,24},{0,28},{5,1},{9... | collective-permute-start | bytes 184328 | tf_op jit(solution)/shard_map/ppermute | solution.py:496
  26.3 4.5 %collective-permute-start.6 = (f32[120,128]{1,0:T(8,128)S(1)}, f32[120,128]{1,0:T(8,128)S(1)}, u32[]{:S(2)}, u32[]{:S(2)}) collective-permute-start(f32[120,128]{1,0:T(8,128)S(1)} %get-tuple-element.42), channel_id=1, source_target_pairs={{0,4},{4,8},{8,12},{12,16},{16,20},{20,24},{24,28},{28,0},{1,5},{5... | collective-permute-start | bytes 184328 | tf_op jit(solution)/shard_map/ppermute | solution.py:495

commit v5 on v3

--- a/solution.py
+++ b/solution.py
@@ -100,8 +100,8 @@
 
 
 def edges_kernel(
-    levels, rows, state, outer, kappa, matrix_in, halo1_in, halo2_in, geo_in,
-    padded, low, high, edge, polar, kap, matrix, halo1, halo2, geo,
+    levels, rows, state, outer, kappa, matrix_in, geo_in,
+    padded, low, high, edge, polar, kap, matrix, geo,
     staged, outer_staged, kappa_scalars, sems,
 ):
     block = REACH * rows
@@ -109,7 +109,6 @@
     mirror = jnp.where(odd == 1, -1.0, 1.0).astype(jnp.float32)
     reads = [(state.at[f], staged.at[f]) for f in range(FIELDS)]
     reads += [(outer, outer_staged), (kappa, kappa_scalars), (matrix_in, matrix), (geo_in, geo)]
-    reads += [(halo1_in, halo1), (halo2_in, halo2)]
     copies = [pltpu.make_async_copy(*read, sems.at[i]) for i, read in enumerate(reads)]
     for copy in copies:
         copy.start()
@@ -292,13 +291,21 @@
     lax.fori_loop(0, rows // TILE, body, 0)
 
 
-def first_kernel(levels, rows, padded, matrix, geo, kap, rate, dlon, elon):
+def first_kernel(
+    levels, rows, padded, matrix, geo, kap, halo1_in, halo2_in, rate, halo1, halo2, dlon, elon, sems
+):
+    reads = ((halo1_in, halo1), (halo2_in, halo2))
+    copies = [pltpu.make_async_copy(*read, sems.at[i]) for i, read in enumerate(reads)]
+    for copy in copies:
+        copy.start()
     longitude_slopes(levels, rows, padded, matrix, dlon, elon)
 
     def store(f, l, r0, tendency):
         rate[f, l, pl.ds(r0, TILE), :] = tendency
 
     interior(levels, rows, padded, dlon, elon, geo, kap, store)
+    for copy in copies:
+        copy.wait()
 
 
 def first_halo_kernel(
@@ -396,30 +403,30 @@
     add_halo(levels, rows, padded, polar, left, right, halo1, halo2, geo, kap, d1, d2, caps, store)
 
 
-def last_kernel(levels, rows, padded, both, below, above, low, high, kappa, out):
+def last_kernel(at, up, levels, rows, *refs):
+    padded, both, sent, more, kap = refs[:5]
+    out, staged, sems = refs[-3:]
     odd = lax.axis_index("rad") % 2
     mirror = jnp.where(odd == 1, -1.0, 1.0).astype(jnp.float32)
-
-    def body(t, carry):
-        r0 = pl.multiple_of(t * TILE, TILE)
-        for halo_ref, more_ref, at, up in ((below, low, 0, False), (above, high, levels - REACH, True)):
-            halo = halo_tile(halo_ref, rows, r0)
-            more = own_tile(more_ref, rows, r0)
-            halo = [[halo[f][b] + more[f][b] for b in range(REACH)] for f in range(FIELDS)]
-            wind = [padded[3, at + a, pl.ds(r0 + TILE, TILE), :] for a in range(REACH)]
-            temper = [padded[4, at + a, pl.ds(r0 + TILE, TILE), :] for a in range(REACH)]
-            extra = across_level(wind, temper, halo, [kappa[at + a] for a in range(REACH)], up)
-            for f in range(FIELDS):
-                for a in range(REACH):
-                    old = both[f, at + a, pl.ds(r0, TILE), :]
-                    new = old + (0.5 * time_step) * extra[f][a]
-                    if f == 3:
-                        new = mirror * new
-                    real = jnp.where(odd == 1, levels - 1 - at - a, at + a)
-                    out[f, real, pl.ds(r0, TILE), :] = new
-        return carry
-
-    lax.fori_loop(0, rows // TILE, body, 0)
+    real = jnp.where(odd == 1, levels - at - REACH, at)
+    copies = []
+    for t in range(rows // TILE):
+        here = pl.ds(t * TILE, TILE)
+        halo = halo_tile(sent, rows, t * TILE)
+        there = own_tile(more, rows, t * TILE)
+        halo = [[halo[f][b] + there[f][b] for b in range(REACH)] for f in range(FIELDS)]
+        wind = [padded[3, at + a, pl.ds((t + 1) * TILE, TILE), :] for a in range(REACH)]
+        temper = [padded[4, at + a, pl.ds((t + 1) * TILE, TILE), :] for a in range(REACH)]
+        extra = across_level(wind, temper, halo, [kap[at + a] for a in range(REACH)], up)
+        for f in range(FIELDS):
+            for a in range(REACH):
+                new = both[f, at + a, here, :] + (0.5 * time_step) * extra[f][a]
+                staged[f, jnp.where(odd == 1, REACH - 1 - a, a), here, :] = mirror * new if f == 3 else new
+        target = out.at[:, pl.ds(real, REACH), here]
+        copies.append(pltpu.make_async_copy(staged.at[:, :, here], target, sems.at[t]))
+        copies[-1].start()
+    for copy in copies:
+        copy.wait()
 
 
 def on_device(state, outer_rows, kappa):
@@ -441,7 +448,7 @@
             functools.partial(kernel, levels, rows),
             out_shape=out_shape,
             in_specs=list(in_specs),
-            out_specs=jax.tree.map(lambda _: VMEM, out_shape),
+            out_specs=jax.tree.map(lambda o: HBM if o.memory_space is pltpu.HBM else VMEM, out_shape),
             scratch_shapes=list(scratch),
             input_output_aliases=aliases or {},
             cost_estimate=pl.CostEstimate(flops=0, bytes_accessed=int(cost * 3.69e6), transcendentals=0),
@@ -460,7 +467,7 @@
         right = lax.ppermute(edge, "lon", west)
         return left, right, lax.ppermute(polar, "lon", half)
 
-    padded, low, high, edge, polar, kap, matrix, halo1, halo2, geo = call(
+    padded, low, high, edge, polar, kap, matrix, geo = call(
         edges_kernel,
         [
             in_vmem(*pad_shape),
@@ -469,16 +476,16 @@
             in_vmem(packs, width),
             in_vmem(FIELDS * levels * REACH, width),
             in_vmem(levels, TILE, width),
-            *(pltpu.VMEM(m.shape, m.dtype) for m in matrices),
+            pltpu.VMEM(matrices[0].shape, matrices[0].dtype),
             in_vmem(*geo.shape),
         ],
-        (HBM,) * 7,
-        (state, outer_rows, kappa, *matrices, geo),
+        (HBM,) * 5,
+        (state, outer_rows, kappa, matrices[0], geo),
         scratch=(
             in_vmem(*full_shape),
             in_vmem(*outer_rows.shape),
             pltpu.SMEM(kappa.shape, jnp.float32),
-            pltpu.SemaphoreType.DMA((FIELDS + 6,)),
+            pltpu.SemaphoreType.DMA((FIELDS + 4,)),
         ),
         name="edges",
     )
@@ -492,12 +499,12 @@
         in_vmem(FIELDS, levels, 2 * TILE, width),
     )
     side = in_vmem(halo_rows, width)
-    rate = call(
+    rate, halo1, halo2 = call(
         first_kernel,
-        in_vmem(*full_shape),
-        (VMEM,) * 4,
-        (padded, matrix, geo, kap),
-        scratch=lon_scratch,
+        [in_vmem(*full_shape), *(pltpu.VMEM(m.shape, m.dtype) for m in matrices[1:])],
+        (VMEM,) * 4 + (HBM,) * 2,
+        (padded, matrix, geo, kap, *matrices[1:]),
+        scratch=(*lon_scratch, pltpu.SemaphoreType.DMA((2,))),
         cost=2.0,
         name="first",
     )
@@ -543,12 +550,28 @@
         aliases={0: 0},
         name="second_halo",
     )
+    last_scratch = (
+        in_vmem(FIELDS, REACH, rows, width),
+        pltpu.SemaphoreType.DMA((rows // TILE,)),
+    )
+    result = pltpu.HBM(full_shape, jnp.float32)
+    out = call(
+        functools.partial(last_kernel, 0, False),
+        result,
+        (VMEM,) * 5,
+        (ahead, both, below2, low, kap),
+        scratch=last_scratch,
+        cost=0.5,
+        name="last_low",
+    )
     return call(
-        last_kernel,
-        jax.ShapeDtypeStruct(full_shape, jnp.float32),
-        (VMEM,) * 7,
-        (ahead, both, below2, above2, low, high, kap),
-        name="last",
+        functools.partial(last_kernel, levels - REACH, True),
+        result,
+        (VMEM,) * 5 + (HBM,),
+        (ahead, both, above2, high, kap, out),
+        scratch=last_scratch,
+        aliases={5: 0},
+        name="last_high",
     )
 
 

time: 31.6 us -> 31 us (0.981)
  waiting for transfers between devices: 6.88 us -> 5.9 us
    ppermute x1, waiting for transfers between devices: 1.32 us -> 0.39 us  [on_device(): above2 = lax.ppermute(high, 'rad', swap_high)]
    pallas_call x7 -> x8, Pallas kernels: 10.9 us -> 11.2 us  [call(): pl.pallas_call(functools.partial(kernel, levels, rows), out_shape=out_sha...]
  transfers between devices with their start and end apart: 10 -> 10, of which waited for: 4 -> 4; matrix products, arithmetic and copies ran while one was open for 0% -> 0% of each run, Pallas kernels for 24% -> 28%
where the time goes in v5:
time: 31 us; the launch traced here: 30.8 us
  starting transfers between devices  13.6 us (44%)
  Pallas kernels  11.2 us (36%)
  waiting for transfers between devices  5.9 us (19%)
    pallas_call x8, Pallas kernels, call(): pl.pallas_call(functools.partial(kernel, levels, rows), out_shape=out_sha...  11.2 us
    ppermute x1, starting transfers between devices, on_device(): above = lax.ppermute(high, 'rad', swap_high)  5.88 us
    ppermute x2, waiting for transfers between devices, around(): left = lax.ppermute(edge, 'lon', east)  3.63 us
    ppermute x2, starting transfers between devices, around(): return (left, right, lax.ppermute(polar, 'lon', half))  3.24 us
    ppermute x1, starting transfers between devices, on_device(): above2 = lax.ppermute(high, 'rad', swap_high)  2.1 us
    ppermute x1, waiting for transfers between devices, on_device(): above = lax.ppermute(high, 'rad', swap_high)  1.87 us
    ppermute x2, starting transfers between devices, around(): left = lax.ppermute(edge, 'lon', east)  0.98 us
    ppermute x1, starting transfers between devices, on_device(): below = lax.ppermute(low, 'rad', swap_low)  0.69 us
  transfers between devices with their start and end apart: 10, of which 4 were waited for; matrix products, arithmetic and copies ran while one was open for 0% of the time, Pallas kernels for 28%

profile of v5, /device:TPU:0, one launch (start us, length us, event | category | flops | bytes accessed | tf_op | source)
XLA Modules:
  0.0 30.8 jit_solution(8214924816762973375)
XLA Ops:
  0.0 1.7 %edges.1 = (f32[5,8,64,128]{3,2,1,0:T(8,128)S(1)}, f32[968,128]{1,0:T(8,128)S(1)}, f32[968,128]{1,0:T(8,128)S(1)}, f32[120,128]{1,0:T(8,128)S(1)}, f32[160,128]{...) custom-call(f32[5,8,48,128]{3,2,1,0:T(8,128)} %state.1, ...), custom_call_target="tpu_custom_call" | custom-call | bytes 3690000 | tf_op jit(solution)/shard_map/edges/pallas_call | solution.py:447
  1.7 0.7 %collective-permute-start.3 = (f32[968,128]{1,0:T(8,128)S(1)}, f32[968,128]{1,0:T(8,128)S(1)}, u32[]{:S(2)}, u32[]{:S(2)}) collective-permute-start(f32[968,128]{1,0:T(8,128)S(1)} %get-tuple-element.36), channel_id=1, source_target_pairs={{1,2},{2,1},{5,6},{6,5},{9,10},{10,9},{13,14},{14,13},{17,18},{18,... | collective-permute-start | bytes 1486856 | tf_op jit(solution)/shard_map/ppermute | solution.py:492
  2.4 5.9 %collective-permute-start.4 = (f32[968,128]{1,0:T(8,128)S(1)}, f32[968,128]{1,0:T(8,128)S(1)}, u32[]{:S(2)}, u32[]{:S(2)}) collective-permute-start(f32[968,128]{1,0:T(8,128)S(1)} %get-tuple-element.37), channel_id=1, source_target_pairs={{0,1},{1,0},{2,3},{3,2},{4,5},{5,4},{6,7},{7,6},{8,9},{9,8},{10,11... | collective-permute-start | bytes 1486856 | tf_op jit(solution)/shard_map/ppermute | solution.py:493
  8.3 1.5 %collective-permute-start = (f32[160,128]{1,0:T(8,128)S(1)}, f32[160,128]{1,0:T(8,128)S(1)}, u32[]{:S(2)}, u32[]{:S(2)}) collective-permute-start(f32[160,128]{1,0:T(8,128)S(1)} %get-tuple-element.31), channel_id=1, source_target_pairs={{0,16},{4,20},{8,24},{12,28},{16,0},{20,4},{24,8},{28,12},{1,17},{... | collective-permute-start | bytes 245768 | tf_op jit(solution)/shard_map/ppermute | solution.py:468
  9.8 0.0 collective-permute-start.2
  9.9 0.5 %collective-permute-start.1 = (f32[120,128]{1,0:T(8,128)S(1)}, f32[120,128]{1,0:T(8,128)S(1)}, u32[]{:S(2)}, u32[]{:S(2)}) collective-permute-start(f32[120,128]{1,0:T(8,128)S(1)} %get-tuple-element.32), channel_id=1, source_target_pairs={{0,4},{4,8},{8,12},{12,16},{16,20},{20,24},{24,28},{28,0},{1,5},{5... | collective-permute-start | bytes 184328 | tf_op jit(solution)/shard_map/ppermute | solution.py:466
  10.3 2.0 %first.1 = (f32[5,8,48,128]{3,2,1,0:T(8,128)S(1)}, bf16[128,2048]{1,0:T(8,128)(2,1)S(1)}, bf16[128,2048]{1,0:T(8,128)(2,1)S(1)}) custom-call(f32[5,8,64,128]{3,2,1,0:T(8,128)S(1)} %get-tuple-element.26.padded.start, bf16[128,256]{1,0:T(8,128)(2,1)S(1)} %get-tuple-element.27.matrix, f32[3,48,128]{2,1,0:T(8,128)S(1)} %get-tuple-element.28.geo, ...), custom_call_target="tpu_custom_call" | custom-call | bytes 7380000 | tf_op jit(solution)/shard_map/first/pallas_call | solution.py:447
  12.4 0.0 collective-permute-done.2.right
  12.4 2.0 %collective-permute-done.1.left = f32[120,128]{1,0:T(8,128)S(1)} collective-permute-done((f32[120,128]{1,0:T(8,128)S(1)}, f32[120,128]{1,0:T(8,128)S(1)}, u32[]{:S(2)}, u32[]{:S(2)}) %collective-permute-start.1) | collective-permute-done | bytes 61472 | tf_op jit(solution)/shard_map/ppermute | solution.py:466
  14.4 0.0 collective-permute-done.polar
  14.4 1.3 %first_halo.1 = (f32[5,8,48,128]{3,2,1,0:T(8,128)S(1)}, f32[960,128]{1,0:T(8,128)S(1)}, f32[960,128]{1,0:T(8,128)S(1)}) custom-call(f32[5,8,48,128]{3,2,1,0:T(8,128)S(1)} %get-tuple-element.30.given, f32[5,8,64,128]{3,2,1,0:T(8,128)S(1)} %get-tuple-element.26.padded.start, ...), custom_call_target="tpu_custom_call", output_to_operand_aliasing={{0}: (0, {})} | custom-call | bytes 3690000 | tf_op jit(solution)/shard_map/first_halo/pallas_call | solution.py:447
  15.7 0.7 %collective-permute-start.9 = (f32[960,128]{1,0:T(8,128)S(1)}, f32[960,128]{1,0:T(8,128)S(1)}, u32[]{:S(2)}, u32[]{:S(2)}) collective-permute-start(f32[960,128]{1,0:T(8,128)S(1)} %get-tuple-element.45), channel_id=1, source_target_pairs={{1,2},{2,1},{5,6},{6,5},{9,10},{10,9},{13,14},{14,13},{17,18},{18,... | collective-permute-start | bytes 1474568 | tf_op jit(solution)/shard_map/ppermute | solution.py:520
  16.4 2.1 %collective-permute-start.8 = (f32[960,128]{1,0:T(8,128)S(1)}, f32[960,128]{1,0:T(8,128)S(1)}, u32[]{:S(2)}, u32[]{:S(2)}) collective-permute-start(f32[960,128]{1,0:T(8,128)S(1)} %get-tuple-element.43), channel_id=1, source_target_pairs={{0,1},{1,0},{2,3},{3,2},{4,5},{5,4},{6,7},{7,6},{8,9},{9,8},{10,11... | collective-permute-start | bytes 1474568 | tf_op jit(solution)/shard_map/ppermute | solution.py:521
  18.5 0.0 collective-permute-done.3.below
  18.5 1.9 %collective-permute-done.4.above = f32[968,128]{1,0:T(8,128)S(1)} collective-permute-done((f32[968,128]{1,0:T(8,128)S(1)}, f32[968,128]{1,0:T(8,128)S(1)}, u32[]{:S(2)}, u32[]{:S(2)}) %collective-permute-start.4) | collective-permute-done | bytes 495648 | tf_op jit(solution)/shard_map/ppermute | solution.py:493
  20.4 0.7 %section.1 = (f32[5,8,48,128]{3,2,1,0:T(8,128)S(1)}, f32[5,8,64,128]{3,2,1,0:T(8,128)S(1)}, f32[120,128]{1,0:T(8,128)S(1)}, f32[160,128]{1,0:T(8,128)S(1)}) custom-call(f32[5,8,64,128]{3,2,1,0:T(8,128)S(1)} %get-tuple-element.26.padded.start, f32[5,8,48,128]{3,2,1,0:T(8,128)S(1)} %get-tuple-element.35.rate, f32[968,128]{1,0:T(8,128)S(1)} %collective-permute-done.3.below, ...), custom_call_target="tpu_custom_call" | custom-call | bytes 3690000 | tf_op jit(solution)/shard_map/section/pallas_call | solution.py:447
  21.1 1.7 %collective-permute-start.5 = (f32[160,128]{1,0:T(8,128)S(1)}, f32[160,128]{1,0:T(8,128)S(1)}, u32[]{:S(2)}, u32[]{:S(2)}) collective-permute-start(f32[160,128]{1,0:T(8,128)S(1)} %get-tuple-element.41), channel_id=1, source_target_pairs={{0,16},{4,20},{8,24},{12,28},{16,0},{20,4},{24,8},{28,12},{1,17},{... | collective-permute-start | bytes 245768 | tf_op jit(solution)/shard_map/ppermute | solution.py:468
  22.8 0.0 collective-permute-start.7
  22.8 0.5 %collective-permute-start.6 = (f32[120,128]{1,0:T(8,128)S(1)}, f32[120,128]{1,0:T(8,128)S(1)}, u32[]{:S(2)}, u32[]{:S(2)}) collective-permute-start(f32[120,128]{1,0:T(8,128)S(1)} %get-tuple-element.42), channel_id=1, source_target_pairs={{0,4},{4,8},{8,12},{12,16},{16,20},{20,24},{24,28},{28,0},{1,5},{5... | collective-permute-start | bytes 184328 | tf_op jit(solution)/shard_map/ppermute | solution.py:466
  23.3 2.4 %second.1 = (f32[5,8,48,128]{3,2,1,0:T(8,128)S(1)}, f32[960,128]{1,0:T(8,128)S(1)}, f32[960,128]{1,0:T(8,128)S(1)}) custom-call(f32[5,8,64,128]{3,2,1,0:T(8,128)S(1)} %get-tuple-element.38.padded.refs_0_, bf16[128,256]{1,0:T(8,128)(2,1)S(1)} %get-tuple-element.27.matrix, f32[3,48,128]{2,1,0:T(8,128)S(1)} %get-tuple-element.28.geo, ...), custom_call_target="tpu_custom_call" | custom-call | bytes 9225000 | tf_op jit(solution)/shard_map/second/pallas_call | solution.py:447
  25.8 0.0 collective-permute-done.7.right
  25.8 1.6 %collective-permute-done.6.left = f32[120,128]{1,0:T(8,128)S(1)} collective-permute-done((f32[120,128]{1,0:T(8,128)S(1)}, f32[120,128]{1,0:T(8,128)S(1)}, u32[]{:S(2)}, u32[]{:S(2)}) %collective-permute-start.6) | collective-permute-done | bytes 61472 | tf_op jit(solution)/shard_map/ppermute | solution.py:466
  27.4 0.0 collective-permute-done.5.polar
  27.4 1.2 %second_halo.1.refs_1_ = f32[5,8,48,128]{3,2,1,0:T(8,128)S(1)} custom-call(f32[5,8,48,128]{3,2,1,0:T(8,128)S(1)} %get-tuple-element.40.given, f32[5,8,64,128]{3,2,1,0:T(8,128)S(1)} %get-tuple-element.38.padded.refs_0_, f32[160,128]{1,0:T(8,128)S(1)} %collective-permute-done.5.polar, ...), custom_call_target="tpu_custom_call", output_to_operand_aliasing={{}: (0, {})} | custom-call | bytes 3690000 | tf_op jit(solution)/shard_map/second_halo/pallas_call | solution.py:447
  28.6 0.0 collective-permute-done.9.refs_2_
  28.6 0.9 %last_low.1.refs_5_ = f32[5,8,48,128]{3,2,1,0:T(8,128)} custom-call(f32[5,8,64,128]{3,2,1,0:T(8,128)S(1)} %get-tuple-element.38.padded.refs_0_, f32[5,8,48,128]{3,2,1,0:T(8,128)S(1)} %second_halo.1.refs_1_, f32[960,128]{1,0:T(8,128)S(1)} %collective-permute-done.9.refs_2_, f32[960,128]{1,0:T(8,128)S(1)} %get-tuple-element.46.refs_3_, ...), custom_call_target="tpu_custom_call" | custom-call | bytes 1845000 | tf_op jit(solution)/shard_map/last_low/pallas_call | solution.py:447
  29.5 0.4 %collective-permute-done.8.refs_2_ = f32[960,128]{1,0:T(8,128)S(1)} collective-permute-done((f32[960,128]{1,0:T(8,128)S(1)}, f32[960,128]{1,0:T(8,128)S(1)}, u32[]{:S(2)}, u32[]{:S(2)}) %collective-permute-start.8) | collective-permute-done | bytes 491552 | tf_op jit(solution)/shard_map/ppermute | solution.py:521
  29.9 0.9 %last_high.1 = f32[5,8,48,128]{3,2,1,0:T(8,128)} custom-call(f32[5,8,64,128]{3,2,1,0:T(8,128)S(1)} %get-tuple-element.38.padded.refs_0_, f32[5,8,48,128]{3,2,1,0:T(8,128)S(1)} %second_halo.1.refs_1_, f32[960,128]{1,0:T(8,128)S(1)} %collective-permute-done.8.refs_2_, f32[960,128]{1,0:T(8,128)S(1)} %get-tuple-element.44.refs_3_, ...), custom_call_target="tpu_custom_call", output_to_operand_aliasing={{}: (5, {})} | custom-call | bytes 3690000 | tf_op jit(solution)/shard_map/last_high/pallas_call | solution.py:447
Async XLA Ops:
  1.7 16.7 %collective-permute-start.3 = (f32[968,128]{1,0:T(8,128)S(1)}, f32[968,128]{1,0:T(8,128)S(1)}, u32[]{:S(2)}, u32[]{:S(2)}) collective-permute-start(f32[968,128]{1,0:T(8,128)S(1)} %get-tuple-element.36), channel_id=1, source_target_pairs={{1,2},{2,1},{5,6},{6,5},{9,10},{10,9},{13,14},{14,13},{17,18},{18,... | collective-permute-start | bytes 1486856 | tf_op jit(solution)/shard_map/ppermute | solution.py:492
  2.4 17.9 %collective-permute-start.4 = (f32[968,128]{1,0:T(8,128)S(1)}, f32[968,128]{1,0:T(8,128)S(1)}, u32[]{:S(2)}, u32[]{:S(2)}) collective-permute-start(f32[968,128]{1,0:T(8,128)S(1)} %get-tuple-element.37), channel_id=1, source_target_pairs={{0,1},{1,0},{2,3},{3,2},{4,5},{5,4},{6,7},{7,6},{8,9},{9,8},{10,11... | collective-permute-start | bytes 1486856 | tf_op jit(solution)/shard_map/ppermute | solution.py:493
  8.3 6.1 %collective-permute-start = (f32[160,128]{1,0:T(8,128)S(1)}, f32[160,128]{1,0:T(8,128)S(1)}, u32[]{:S(2)}, u32[]{:S(2)}) collective-permute-start(f32[160,128]{1,0:T(8,128)S(1)} %get-tuple-element.31), channel_id=1, source_target_pairs={{0,16},{4,20},{8,24},{12,28},{16,0},{20,4},{24,8},{28,12},{1,17},{... | collective-permute-start | bytes 245768 | tf_op jit(solution)/shard_map/ppermute | solution.py:468
  9.8 2.5 %collective-permute-start.2 = (f32[120,128]{1,0:T(8,128)S(1)}, f32[120,128]{1,0:T(8,128)S(1)}, u32[]{:S(2)}, u32[]{:S(2)}) collective-permute-start(f32[120,128]{1,0:T(8,128)S(1)} %get-tuple-element.32), channel_id=1, source_target_pairs={{4,0},{8,4},{12,8},{16,12},{20,16},{24,20},{28,24},{0,28},{5,1},{9... | collective-permute-start | bytes 184328 | tf_op jit(solution)/shard_map/ppermute | solution.py:467
  9.9 4.5 %collective-permute-start.1 = (f32[120,128]{1,0:T(8,128)S(1)}, f32[120,128]{1,0:T(8,128)S(1)}, u32[]{:S(2)}, u32[]{:S(2)}) collective-permute-start(f32[120,128]{1,0:T(8,128)S(1)} %get-tuple-element.32), channel_id=1, source_target_pairs={{0,4},{4,8},{8,12},{12,16},{16,20},{20,24},{24,28},{28,0},{1,5},{5... | collective-permute-start | bytes 184328 | tf_op jit(solution)/shard_map/ppermute | solution.py:466
  15.7 12.9 %collective-permute-start.9 = (f32[960,128]{1,0:T(8,128)S(1)}, f32[960,128]{1,0:T(8,128)S(1)}, u32[]{:S(2)}, u32[]{:S(2)}) collective-permute-start(f32[960,128]{1,0:T(8,128)S(1)} %get-tuple-element.45), channel_id=1, source_target_pairs={{1,2},{2,1},{5,6},{6,5},{9,10},{10,9},{13,14},{14,13},{17,18},{18,... | collective-permute-start | bytes 1474568 | tf_op jit(solution)/shard_map/ppermute | solution.py:520
  16.4 13.5 %collective-permute-start.8 = (f32[960,128]{1,0:T(8,128)S(1)}, f32[960,128]{1,0:T(8,128)S(1)}, u32[]{:S(2)}, u32[]{:S(2)}) collective-permute-start(f32[960,128]{1,0:T(8,128)S(1)} %get-tuple-element.43), channel_id=1, source_target_pairs={{0,1},{1,0},{2,3},{3,2},{4,5},{5,4},{6,7},{7,6},{8,9},{9,8},{10,11... | collective-permute-start | bytes 1474568 | tf_op jit(solution)/shard_map/ppermute | solution.py:521
  21.1 6.3 %collective-permute-start.5 = (f32[160,128]{1,0:T(8,128)S(1)}, f32[160,128]{1,0:T(8,128)S(1)}, u32[]{:S(2)}, u32[]{:S(2)}) collective-permute-start(f32[160,128]{1,0:T(8,128)S(1)} %get-tuple-element.41), channel_id=1, source_target_pairs={{0,16},{4,20},{8,24},{12,28},{16,0},{20,4},{24,8},{28,12},{1,17},{... | collective-permute-start | bytes 245768 | tf_op jit(solution)/shard_map/ppermute | solution.py:468
  22.8 2.9 %collective-permute-start.7 = (f32[120,128]{1,0:T(8,128)S(1)}, f32[120,128]{1,0:T(8,128)S(1)}, u32[]{:S(2)}, u32[]{:S(2)}) collective-permute-start(f32[120,128]{1,0:T(8,128)S(1)} %get-tuple-element.42), channel_id=1, source_target_pairs={{4,0},{8,4},{12,8},{16,12},{20,16},{24,20},{28,24},{0,28},{5,1},{9... | collective-permute-start | bytes 184328 | tf_op jit(solution)/shard_map/ppermute | solution.py:467
  22.8 4.5 %collective-permute-start.6 = (f32[120,128]{1,0:T(8,128)S(1)}, f32[120,128]{1,0:T(8,128)S(1)}, u32[]{:S(2)}, u32[]{:S(2)}) collective-permute-start(f32[120,128]{1,0:T(8,128)S(1)} %get-tuple-element.42), channel_id=1, source_target_pairs={{0,4},{4,8},{8,12},{12,16},{16,20},{20,24},{24,28},{28,0},{1,5},{5... | collective-permute-start | bytes 184328 | tf_op jit(solution)/shard_map/ppermute | solution.py:466

commit v6 on v5

--- a/solution.py
+++ b/solution.py
@@ -34,23 +34,15 @@
     return pltpu.VMEM(shape, jnp.float32)
 
 
-def stencil_matrices(width):
-    own = np.zeros((width, 2 * width), np.float32)
-    first = np.zeros((width, GROUPS * width), np.float32)
-    second = np.zeros((width, GROUPS * width), np.float32)
+def stencil_matrix(width):
+    matrix = np.zeros((width, 2 * width), np.float32)
     for out in range(width):
         for k in range(1, REACH + 1):
             for sign in (1, -1):
-                at = out + sign * k
-                if 0 <= at < width:
-                    own[at, out] = sign * first_whole[k - 1]
-                    own[at, width + out] = second_whole[k - 1]
-                    continue
-                row = REACH + at if at < 0 else REACH + at - width
-                for g in range(GROUPS):
-                    first[2 * REACH * g + row, g * width + out] = sign * first_whole[k - 1]
-                    second[2 * REACH * g + row, g * width + out] = second_whole[k - 1]
-    return tuple(jnp.asarray(m, jnp.bfloat16) for m in (own, first, second))
+                if 0 <= out + sign * k < width:
+                    matrix[out + sign * k, out] = sign * first_whole[k - 1]
+                    matrix[out + sign * k, width + out] = second_whole[k - 1]
+    return jnp.asarray(matrix, jnp.bfloat16)
 
 
 def geometry(rows, nlon, width):
@@ -100,63 +92,92 @@
 
 
 def edges_kernel(
-    levels, rows, state, outer, kappa, matrix_in, geo_in,
-    padded, low, high, edge, polar, kap, matrix, geo,
-    staged, outer_staged, kappa_scalars, sems,
+    levels, rows, state, outer_rows, kappa, matrix_in, geo_in,
+    staged, beyond, low, high, inner, outer, polar, kap, matrix, geo,
+    kappa_scalars, sems,
 ):
     block = REACH * rows
-    odd = lax.axis_index("rad") % 2
-    mirror = jnp.where(odd == 1, -1.0, 1.0).astype(jnp.float32)
+    odd, mirror = mirrored()
     reads = [(state.at[f], staged.at[f]) for f in range(FIELDS)]
-    reads += [(outer, outer_staged), (kappa, kappa_scalars), (matrix_in, matrix), (geo_in, geo)]
+    reads += [(kappa, kappa_scalars), (outer_rows, beyond), (matrix_in, matrix), (geo_in, geo)]
     copies = [pltpu.make_async_copy(*read, sems.at[i]) for i, read in enumerate(reads)]
     for copy in copies:
         copy.start()
-    lane = lax.broadcasted_iota(jnp.int32, (TILE, LANES), 1)
+    packs = []
     for f in range(FIELDS):
         copies[f].wait()
+        real = [jnp.where(odd == 1, levels - 1 - l, l) for l in range(levels)]
+        tiles = []
         for l in range(levels):
-            whole = staged[f, jnp.where(odd == 1, levels - 1 - l, l)]
+            whole = staged[f, real[l]]
             if f == 3:
                 whole = mirror * whole
-            padded[f, l, pl.ds(TILE, rows), :] = whole
-            padded[f, l, pl.ds(0, TILE), :] = jnp.zeros((TILE, LANES), jnp.float32)
             if l < REACH:
                 low[pl.ds(f * block + l * rows, rows), :] = whole
             if l >= levels - REACH:
                 high[pl.ds(f * block + (l - levels + REACH) * rows, rows), :] = whole
-        pack_edges(f, levels, rows, padded, edge, polar, lane)
-    for copy in copies[FIELDS:]:
-        copy.wait()
+            tiles.append([whole[t * TILE : (t + 1) * TILE] for t in range(rows // TILE)])
+            polar[pl.ds((f * levels + l) * REACH, REACH), :] = whole[:REACH]
+        packs += packed(levels, rows, tiles)
+    store_packs(packs, inner, outer)
+    copies[FIELDS].wait()
     for l in range(levels):
-        real = jnp.where(odd == 1, levels - 1 - l, l)
-        value = kappa_scalars[real]
+        value = kappa_scalars[jnp.where(odd == 1, levels - 1 - l, l)]
         kap[l] = jnp.full((TILE, LANES), value, jnp.float32)
         if l < REACH:
             low[pl.ds(FIELDS * block + l, 1), :] = jnp.full((1, LANES), value, jnp.float32)
         if l >= levels - REACH:
             high[pl.ds(FIELDS * block + l - levels + REACH, 1), :] = jnp.full((1, LANES), value, jnp.float32)
-        for f in range(FIELDS):
-            beyond = outer_staged[f, real]
-            padded[f, l, pl.ds(TILE + rows, REACH), :] = mirror * beyond if f == 3 else beyond
     low[pl.ds(FIELDS * block + REACH, REACH), :] = jnp.ones((REACH, LANES), jnp.float32)
     high[pl.ds(FIELDS * block + REACH, REACH), :] = jnp.ones((REACH, LANES), jnp.float32)
-
-
-def pack_edges(f, levels, rows, padded, edge, polar, lane):
+    for copy in copies[FIELDS + 1 :]:
+        copy.wait()
+
+
+def mirrored():
+    odd = lax.axis_index("rad") % 2
+    return odd, jnp.where(odd == 1, -1.0, 1.0).astype(jnp.float32)
+
+
+def lanes():
+    return lax.broadcasted_iota(jnp.int32, (TILE, LANES), 1)
+
+
+def packed(levels, rows, tiles):
     per = GROUPS // levels
+    out = []
     for j in range(rows // TILE // per):
-        tiles = [
-            padded[f, l, pl.ds(TILE + (j * per + u) * TILE, TILE), :]
-            for u in range(per)
-            for l in range(levels)
-        ]
-        at = (f * (rows // TILE // per) + j) * TILE
-        edge[pl.ds(at, TILE), :] = packed(tiles, lane)
-    for l in range(levels):
-        for i in range(REACH):
-            row = padded[f, l, pl.ds(TILE + REACH - 1 - i, 1), :]
-            polar[pl.ds((f * levels + l) * REACH + i, 1), :] = signs[f] * row
+        total = None
+        for g in range(GROUPS):
+            moved = pltpu.roll(tiles[g % levels][j * per + g // levels], (REACH + 2 * REACH * g) % LANES, 1)
+            total = moved if total is None else jnp.where(lanes() >= 2 * REACH * g, moved, total)
+        out.append(total)
+    return out
+
+
+def store_packs(packs, inner, outer):
+    first_half = lanes() % (2 * REACH) < REACH
+    odd = lax.axis_index("lon") % 2 == 1
+    for i in range(0, len(packs), 2):
+        a, b = packs[i], packs[min(i + 1, len(packs) - 1)]
+        at = pl.ds(i // 2 * TILE, TILE)
+        east = jnp.where(first_half, a, pltpu.roll(b, REACH, 1))
+        west = jnp.where(first_half, pltpu.roll(a, LANES - REACH, 1), b)
+        inner[at, :] = jnp.where(odd, west, east)
+        outer[at, :] = jnp.where(odd, east, west)
+
+
+def load_packs(count, inner, outer):
+    first_half = lanes() % (2 * REACH) < REACH
+    odd = lax.axis_index("lon") % 2 == 1
+    out = []
+    for i in range(0, count, 2):
+        at = pl.ds(i // 2 * TILE, TILE)
+        before = jnp.where(odd, inner[at, :], outer[at, :])
+        after = jnp.where(odd, outer[at, :], inner[at, :])
+        out.append(jnp.where(first_half, before, pltpu.roll(after, REACH, 1)))
+        out.append(jnp.where(first_half, pltpu.roll(before, LANES - REACH, 1), after))
+    return out[:count]
 
 
 def pieces_of(x):
@@ -185,28 +206,49 @@
             elon[...] = total[:, LANES:].reshape(levels, rows, LANES)
 
 
-def add_halo(levels, rows, padded, polar, left, right, halo1, halo2, geo, kap, d1, d2, caps, store):
-    lane = lax.broadcasted_iota(jnp.int32, left.shape, 1)
-    both = jnp.where((lane % (2 * REACH)) < REACH, left[...], right[...])
-    split = pieces_of(both)
-    packs = rows // TILE // (GROUPS // levels)
-    last = slice(4 * packs * TILE, None)
-    d1[...] = times_whole(split, halo1[...])
-    d2[...] = times_whole([piece[last] for piece in pieces_of(both)], halo2[...])
-    for f in range(FIELDS):
+def groups_slope(pack, coeffs, sign):
+    place = lanes() % (2 * REACH)
+    total = None
+    for k in range(1, REACH + 1):
+        ahead = pltpu.roll(pack, LANES - k, 1)
+        behind = pltpu.roll(pack, k, 1)
+        from_after = (place < REACH) & (place >= REACH - k)
+        from_before = (place >= REACH) & (place < REACH + k)
+        term = jnp.where(from_after, coeffs[k - 1] * ahead, 0.0)
+        term = jnp.where(from_before, (sign * coeffs[k - 1]) * behind, term)
+        total = term if total is None else total + term
+    return total
+
+
+def add_halo(levels, rows, padded, polar, inner, outer, geo, kap, store):
+    per = GROUPS // levels
+    count = rows // TILE // per
+    packs = load_packs(FIELDS * count, inner, outer)
+    slopes = [groups_slope(pack, first_whole, -1.0) for pack in packs]
+    bends = [groups_slope(pack, second_whole, 1.0) for pack in packs[4 * count :]]
+    lane = lanes()
+    at_side = (lane < REACH) | (lane >= LANES - REACH)
+    row = lax.broadcasted_iota(jnp.int32, (TILE, LANES), 0)
+
+    def by_row(coeffs, m):
+        total = jnp.zeros((TILE, LANES), jnp.float32)
+        for k in range(m + 1, REACH + 1):
+            total = jnp.where(row == k - m - 1, coeffs[k - 1], total)
+        return total
+
+    first_rows = [by_row([-c for c in first_coeffs], m) for m in range(REACH)]
+    second_rows = [by_row(second_coeffs[1:], m) for m in range(REACH)]
+    for t in range(rows // TILE):
+        j, u = divmod(t, per)
+        here = pl.ds(t * TILE, TILE)
+        metric = jnp.where(at_side, geo[0, here, :], 0.0)
+        metric2 = jnp.where(at_side, geo[1, here, :], 0.0)
         for l in range(levels):
-            caps[f, l, pl.ds(TILE - REACH, REACH), :] = polar[pl.ds((f * levels + l) * REACH, REACH), :]
-            caps[f, l, pl.ds(TILE, TILE), :] = jnp.zeros((TILE, LANES), jnp.float32)
-    for t in range(rows // TILE):
-        j, u = divmod(t, GROUPS // levels)
-        here = pl.ds(t * TILE, TILE)
-        metric, metric2 = geo[0, here, :], geo[1, here, :]
-        for l in range(levels):
-            columns = pl.ds((u * levels + l) * LANES, LANES)
+            shift = (LANES - REACH - 2 * REACH * (u * levels + l)) % LANES
             center = [padded[f, l, pl.ds((t + 1) * TILE, TILE), :] for f in range(FIELDS)]
             wlon, wrow, temper = center[1], center[2], center[4]
-            slon = [metric * d1[pl.ds((f * packs + j) * TILE, TILE), columns] for f in range(FIELDS)]
-            laplace = metric2 * d2[pl.ds(j * TILE, TILE), columns]
+            slon = [metric * pltpu.roll(slopes[f * count + j], shift, 1) for f in range(FIELDS)]
+            laplace = metric2 * pltpu.roll(bends[j], shift, 1)
             extra = [-wlon * slope for slope in slon]
             extra[1] = extra[1] - temper * slon[0] - slon[4]
             spread = slon[1]
@@ -214,12 +256,12 @@
                 srow = []
                 for f in range(FIELDS):
                     total = None
-                    for k in range(1, REACH + 1):
-                        behind = caps[f, l, pl.ds(TILE - k, TILE), :]
-                        term = -first_coeffs[k - 1] * behind
+                    for m in range(REACH):
+                        across = signs[f] * polar[pl.ds((f * levels + l) * REACH + m, 1), :]
+                        term = first_rows[m] * across
                         total = term if total is None else total + term
                         if f == 4:
-                            laplace = laplace + second_coeffs[k] * behind
+                            laplace = laplace + second_rows[m] * across
                     srow.append(total)
                 extra = [e - wrow * slope for e, slope in zip(extra, srow)]
                 extra[2] = extra[2] - temper * srow[0] - srow[4]
@@ -291,25 +333,27 @@
     lax.fori_loop(0, rows // TILE, body, 0)
 
 
-def first_kernel(
-    levels, rows, padded, matrix, geo, kap, halo1_in, halo2_in, rate, halo1, halo2, dlon, elon, sems
-):
-    reads = ((halo1_in, halo1), (halo2_in, halo2))
-    copies = [pltpu.make_async_copy(*read, sems.at[i]) for i, read in enumerate(reads)]
-    for copy in copies:
-        copy.start()
+def first_kernel(levels, rows, staged, beyond, matrix, geo, kap, padded, rate, dlon, elon):
+    odd, mirror = mirrored()
+    for f in range(FIELDS):
+        for l in range(levels):
+            real = jnp.where(odd == 1, levels - 1 - l, l)
+            whole, after = staged[f, real], beyond[f, real]
+            if f == 3:
+                whole, after = mirror * whole, mirror * after
+            padded[f, l, pl.ds(0, TILE), :] = jnp.zeros((TILE, LANES), jnp.float32)
+            padded[f, l, pl.ds(TILE, rows), :] = whole
+            padded[f, l, pl.ds(TILE + rows, REACH), :] = after
     longitude_slopes(levels, rows, padded, matrix, dlon, elon)
 
     def store(f, l, r0, tendency):
         rate[f, l, pl.ds(r0, TILE), :] = tendency
 
     interior(levels, rows, padded, dlon, elon, geo, kap, store)
-    for copy in copies:
-        copy.wait()
 
 
 def first_halo_kernel(
-    levels, rows, given, padded, polar, left, right, halo1, halo2, geo, kap, rate, low, high, d1, d2, caps
+    levels, rows, given, padded, polar, inner, outer, geo, kap, rate, low, high
 ):
     def store(f, l, r0, value, extra):
         tendency = given[f, l, pl.ds(r0, TILE), :] + extra
@@ -320,7 +364,7 @@
         if l >= levels - REACH:
             high[pl.ds((f * REACH + l - levels + REACH) * rows + r0, TILE), :] = ahead
 
-    add_halo(levels, rows, padded, polar, left, right, halo1, halo2, geo, kap, d1, d2, caps, store)
+    add_halo(levels, rows, padded, polar, inner, outer, geo, kap, store)
 
 
 def halo_tile(ref, rows, r0):
@@ -338,7 +382,7 @@
     ]
 
 
-def section_kernel(levels, rows, padded, rate, below, above, kappa, full, ahead, edge, polar):
+def section_kernel(levels, rows, padded, rate, below, above, kappa, full, ahead, inner, outer, polar):
     def body(t, carry):
         r0 = pl.multiple_of(t * TILE, TILE)
         for halo_ref, at, up in ((below, 0, False), (above, levels - REACH, True)):
@@ -355,12 +399,15 @@
         return carry
 
     lax.fori_loop(0, rows // TILE, body, 0)
-    lane = lax.broadcasted_iota(jnp.int32, (TILE, LANES), 1)
+    packs = []
     for f in range(FIELDS):
-        pack_edges(f, levels, rows, ahead, edge, polar, lane)
+        tiles = [[ahead[f, l, pl.ds((t + 1) * TILE, TILE), :] for t in range(rows // TILE)] for l in range(levels)]
+        packs += packed(levels, rows, tiles)
         for l in range(levels):
+            polar[pl.ds((f * levels + l) * REACH, REACH), :] = ahead[f, l, pl.ds(TILE, REACH), :]
             ahead[f, l, pl.ds(0, TILE), :] = jnp.zeros((TILE, LANES), jnp.float32)
             ahead[f, l, pl.ds(rows + TILE, REACH), :] = padded[f, l, pl.ds(rows + TILE, REACH), :]
+    store_packs(packs, inner, outer)
 
 
 def second_kernel(
@@ -394,20 +441,19 @@
 
 
 def second_halo_kernel(
-    levels, rows, given, padded, polar, left, right, halo1, halo2, geo, kap, both, d1, d2, caps
+    levels, rows, given, padded, polar, inner, outer, geo, kap, both
 ):
     def store(f, l, r0, value, extra):
         at = pl.ds(r0, TILE)
         both[f, l, at, :] = given[f, l, at, :] + (0.5 * time_step) * extra
 
-    add_halo(levels, rows, padded, polar, left, right, halo1, halo2, geo, kap, d1, d2, caps, store)
+    add_halo(levels, rows, padded, polar, inner, outer, geo, kap, store)
 
 
 def last_kernel(at, up, levels, rows, *refs):
     padded, both, sent, more, kap = refs[:5]
     out, staged, sems = refs[-3:]
-    odd = lax.axis_index("rad") % 2
-    mirror = jnp.where(odd == 1, -1.0, 1.0).astype(jnp.float32)
+    odd, mirror = mirrored()
     real = jnp.where(odd == 1, levels - at - REACH, at)
     copies = []
     for t in range(rows // TILE):
@@ -432,12 +478,12 @@
 def on_device(state, outer_rows, kappa):
     levels, rows, width = state.shape[1:]
     ring, depth = lax.axis_size("lon"), lax.axis_size("rad")
-    assert width == LANES and levels >= 2 * REACH and GROUPS % levels == 0
+    assert ring % 4 == 0 and width == LANES and levels >= 2 * REACH and GROUPS % levels == 0
     assert rows % (TILE * (GROUPS // levels)) == 0
-    matrices = stencil_matrices(width)
+    matrix = stencil_matrix(width)
     geo = geometry(rows, width * ring, width)
     halo_rows = FIELDS * REACH * rows
-    packs = FIELDS * levels * rows // GROUPS
+    packs = -(-(FIELDS * levels * rows // TILE // GROUPS) // 2) * TILE
     pad_shape = (FIELDS, levels, rows + 2 * TILE, width)
     full_shape = (FIELDS, levels, rows, width)
 
@@ -456,82 +502,73 @@
             name=name,
         )(*args)
 
-    east = [(i, (i + 1) % ring) for i in range(ring)]
-    west = [(b, a) for a, b in east]
+    pairs = [(i, i + 1) for i in range(0, ring, 2)]
+    swap_inner = pairs + [(b, a) for a, b in pairs]
+    pairs = [(i, (i + 1) % ring) for i in range(1, ring, 2)]
+    swap_outer = pairs + [(b, a) for a, b in pairs]
     half = [(i, (i + ring // 2) % ring) for i in range(ring)]
     swap_high = [p for i in range(0, depth - 1, 2) for p in ((i, i + 1), (i + 1, i))]
     swap_low = [p for i in range(1, depth - 1, 2) for p in ((i, i + 1), (i + 1, i))]
 
-    def around(edge, polar):
-        left = lax.ppermute(edge, "lon", east)
-        right = lax.ppermute(edge, "lon", west)
-        return left, right, lax.ppermute(polar, "lon", half)
-
-    padded, low, high, edge, polar, kap, matrix, geo = call(
+    def around(inner, outer, polar):
+        inner = lax.ppermute(inner, "lon", swap_inner)
+        outer = lax.ppermute(outer, "lon", swap_outer)
+        return inner, outer, lax.ppermute(polar, "lon", half)
+
+    edge_shapes = [in_vmem(packs, width), in_vmem(packs, width), in_vmem(FIELDS * levels * REACH, width)]
+    staged, after, low, high, *edges, kap, matrix, geo = call(
         edges_kernel,
         [
-            in_vmem(*pad_shape),
+            in_vmem(*full_shape),
+            in_vmem(*outer_rows.shape),
             in_vmem(halo_rows + TILE, width),
             in_vmem(halo_rows + TILE, width),
-            in_vmem(packs, width),
-            in_vmem(FIELDS * levels * REACH, width),
+            *edge_shapes,
             in_vmem(levels, TILE, width),
-            pltpu.VMEM(matrices[0].shape, matrices[0].dtype),
+            pltpu.VMEM(matrix.shape, matrix.dtype),
             in_vmem(*geo.shape),
         ],
         (HBM,) * 5,
-        (state, outer_rows, kappa, matrices[0], geo),
-        scratch=(
-            in_vmem(*full_shape),
-            in_vmem(*outer_rows.shape),
-            pltpu.SMEM(kappa.shape, jnp.float32),
-            pltpu.SemaphoreType.DMA((FIELDS + 4,)),
-        ),
+        (state, outer_rows, kappa, matrix, geo),
+        scratch=(pltpu.SMEM(kappa.shape, jnp.float32), pltpu.SemaphoreType.DMA((FIELDS + 4,))),
         name="edges",
     )
     below = lax.ppermute(low, "rad", swap_low)
     above = lax.ppermute(high, "rad", swap_high)
-    left, right, beyond = around(edge, polar)
+    inner, outer, beyond = around(*edges)
     lon_scratch = (in_vmem(*full_shape), in_vmem(*full_shape[1:]))
-    halo_scratch = (
-        in_vmem(packs, GROUPS * width),
-        in_vmem(packs // FIELDS, GROUPS * width),
-        in_vmem(FIELDS, levels, 2 * TILE, width),
-    )
     side = in_vmem(halo_rows, width)
-    rate, halo1, halo2 = call(
+    padded, rate = call(
         first_kernel,
-        [in_vmem(*full_shape), *(pltpu.VMEM(m.shape, m.dtype) for m in matrices[1:])],
-        (VMEM,) * 4 + (HBM,) * 2,
-        (padded, matrix, geo, kap, *matrices[1:]),
-        scratch=(*lon_scratch, pltpu.SemaphoreType.DMA((2,))),
+        [in_vmem(*pad_shape), in_vmem(*full_shape)],
+        (VMEM,) * 5,
+        (staged, after, matrix, geo, kap),
+        scratch=lon_scratch,
         cost=2.0,
         name="first",
     )
     rate, low, high = call(
         first_halo_kernel,
         [in_vmem(*full_shape), side, side],
-        (VMEM,) * 9,
-        (rate, padded, beyond, left, right, halo1, halo2, geo, kap),
-        scratch=halo_scratch,
+        (VMEM,) * 7,
+        (rate, padded, beyond, inner, outer, geo, kap),
         aliases={0: 0},
         name="first_halo",
     )
     below2 = lax.ppermute(low, "rad", swap_low)
     above2 = lax.ppermute(high, "rad", swap_high)
-    full, ahead, edge, polar = call(
+    full, ahead, *edges = call(
         section_kernel,
         [
             in_vmem(*full_shape),
             in_vmem(*pad_shape),
-            in_vmem(packs, width),
-            in_vmem(FIELDS * levels * REACH, width),
+            *edge_shapes,
         ],
         (VMEM,) * 5,
         (padded, rate, below, above, kap),
         name="section",
     )
-    left, right, beyond = around(edge, polar)
+    inner, outer, beyond = around(*edges)
     both, low, high = call(
         second_kernel,
         [in_vmem(*full_shape), side, side],
@@ -544,9 +581,8 @@
     both = call(
         second_halo_kernel,
         in_vmem(*full_shape),
-        (VMEM,) * 9,
-        (both, ahead, beyond, left, right, halo1, halo2, geo, kap),
-        scratch=halo_scratch,
+        (VMEM,) * 7,
+        (both, ahead, beyond, inner, outer, geo, kap),
         aliases={0: 0},
         name="second_halo",
     )

time: 31 us -> 31 us (level)
  starting transfers between devices: 13.6 us -> 15 us
  waiting for transfers between devices: 5.9 us -> 4.94 us
  Pallas kernels: 11.2 us -> 10.7 us
    ppermute x6, waiting for transfers between devices: 3.64 us -> 1.45 us  [the longest x2 1.44 us: around(): outer = lax.ppermute(outer, 'lon', swap_outer)]
    ppermute x6, starting transfers between devices: 4.26 us -> 5.97 us  [the longest x2 3.31 us: around(): return (inner, outer, lax.ppermute(polar, 'lon', half))]
    ppermute x1, waiting for transfers between devices: 1.87 us -> 2.56 us  [on_device(): above = lax.ppermute(high, 'rad', swap_high)]
    ppermute x1, waiting for transfers between devices: 0.39 us -> 0.93 us  [on_device(): above2 = lax.ppermute(high, 'rad', swap_high)]
    pallas_call x8, Pallas kernels: 11.2 us -> 10.7 us  [call(): pl.pallas_call(functools.partial(kernel, levels, rows), out_shape=out_sha...]
  transfers between devices with their start and end apart: 10 -> 10, of which waited for: 4 -> 4; matrix products, arithmetic and copies ran while one was open for 0% -> 0% of each run, Pallas kernels for 28% -> 26%
where the time goes in v6:
time: 31 us; the launch traced here: 30.8 us
  starting transfers between devices  15 us (48%)
  Pallas kernels  10.7 us (35%)
  waiting for transfers between devices  4.94 us (16%)
    pallas_call x8, Pallas kernels, call(): pl.pallas_call(functools.partial(kernel, levels, rows), out_shape=out_sha...  10.7 us
    ppermute x1, starting transfers between devices, on_device(): above = lax.ppermute(high, 'rad', swap_high)  5.88 us
    ppermute x2, starting transfers between devices, around(): return (inner, outer, lax.ppermute(polar, 'lon', half))  3.31 us
    ppermute x2, starting transfers between devices, around(): outer = lax.ppermute(outer, 'lon', swap_outer)  2.66 us
    ppermute x1, waiting for transfers between devices, on_device(): above = lax.ppermute(high, 'rad', swap_high)  2.56 us
    ppermute x1, starting transfers between devices, on_device(): above2 = lax.ppermute(high, 'rad', swap_high)  1.81 us
    ppermute x2, waiting for transfers between devices, around(): outer = lax.ppermute(outer, 'lon', swap_outer)  1.44 us
    ppermute x1, waiting for transfers between devices, on_device(): above2 = lax.ppermute(high, 'rad', swap_high)  0.93 us
  transfers between devices with their start and end apart: 10, of which 4 were waited for; matrix products, arithmetic and copies ran while one was open for 0% of the time, Pallas kernels for 26%

profile of v6, /device:TPU:0, one launch (start us, length us, event | category | flops | bytes accessed | tf_op | source)
XLA Modules:
  0.0 30.8 jit_solution(4814381016698641033)
XLA Ops:
  0.0 1.7 %edges.1 = (f32[5,8,48,128]{3,2,1,0:T(8,128)S(1)}, f32[5,8,4,128]{3,2,1,0:T(4,128)S(1)}, f32[968,128]{1,0:T(8,128)S(1)}, f32[968,128]{1,0:T(8,128)S(1)}, f32[64,...) custom-call(f32[5,8,48,128]{3,2,1,0:T(8,128)} %state.1, ...), custom_call_target="tpu_custom_call" | custom-call | bytes 3690000 | tf_op jit(solution)/shard_map/edges/pallas_call | solution.py:493
  1.7 0.7 %collective-permute-start.3 = (f32[968,128]{1,0:T(8,128)S(1)}, f32[968,128]{1,0:T(8,128)S(1)}, u32[]{:S(2)}, u32[]{:S(2)}) collective-permute-start(f32[968,128]{1,0:T(8,128)S(1)} %get-tuple-element.39), channel_id=1, source_target_pairs={{1,2},{2,1},{5,6},{6,5},{9,10},{10,9},{13,14},{14,13},{17,18},{18,... | collective-permute-start | bytes 1486856 | tf_op jit(solution)/shard_map/ppermute | solution.py:536
  2.4 5.9 %collective-permute-start.4 = (f32[968,128]{1,0:T(8,128)S(1)}, f32[968,128]{1,0:T(8,128)S(1)}, u32[]{:S(2)}, u32[]{:S(2)}) collective-permute-start(f32[968,128]{1,0:T(8,128)S(1)} %get-tuple-element.40), channel_id=1, source_target_pairs={{0,1},{1,0},{2,3},{3,2},{4,5},{5,4},{6,7},{7,6},{8,9},{9,8},{10,11... | collective-permute-start | bytes 1486856 | tf_op jit(solution)/shard_map/ppermute | solution.py:537
  8.3 1.5 %collective-permute-start = (f32[160,128]{1,0:T(8,128)S(1)}, f32[160,128]{1,0:T(8,128)S(1)}, u32[]{:S(2)}, u32[]{:S(2)}) collective-permute-start(f32[160,128]{1,0:T(8,128)S(1)} %get-tuple-element.35), channel_id=1, source_target_pairs={{0,16},{4,20},{8,24},{12,28},{16,0},{20,4},{24,8},{28,12},{1,17},{... | collective-permute-start | bytes 245768 | tf_op jit(solution)/shard_map/ppermute | solution.py:516
  9.8 0.0 collective-permute-start.1
  9.8 1.5 %collective-permute-start.2 = (f32[64,128]{1,0:T(8,128)S(1)}, f32[64,128]{1,0:T(8,128)S(1)}, u32[]{:S(2)}, u32[]{:S(2)}) collective-permute-start(f32[64,128]{1,0:T(8,128)S(1)} %get-tuple-element.37), channel_id=1, source_target_pairs={{4,8},{12,16},{20,24},{28,0},{8,4},{16,12},{24,20},{0,28},{5,9},{1... | collective-permute-start | bytes 98312 | tf_op jit(solution)/shard_map/ppermute | solution.py:515
  11.4 2.0 %first.1 = (f32[5,8,64,128]{3,2,1,0:T(8,128)S(1)}, f32[5,8,48,128]{3,2,1,0:T(8,128)S(1)}) custom-call(f32[5,8,48,128]{3,2,1,0:T(8,128)S(1)} %get-tuple-element.28.staged, f32[5,8,4,128]{3,2,1,0:T(4,128)S(1)} %get-tuple-element.29.beyond, bf16[128,256]{1,0:T(8,128)(2,1)S(1)} %get-tuple-element.30.matrix, f32[3,48,128]{2,1,0:T(8,128)S(1)} %get-tuple-element.31.geo, ...), custom_call_target="tpu_custom_call" | custom-call | bytes 7380000 | tf_op jit(solution)/shard_map/first/pallas_call | solution.py:493
  13.4 0.0 collective-permute-done.1.inner
  13.4 0.7 %collective-permute-done.2.outer = f32[64,128]{1,0:T(8,128)S(1)} collective-permute-done((f32[64,128]{1,0:T(8,128)S(1)}, f32[64,128]{1,0:T(8,128)S(1)}, u32[]{:S(2)}, u32[]{:S(2)}) %collective-permute-start.2) | collective-permute-done | bytes 32800 | tf_op jit(solution)/shard_map/ppermute | solution.py:515
  14.2 0.0 collective-permute-done.polar
  14.2 1.0 %first_halo.1 = (f32[5,8,48,128]{3,2,1,0:T(8,128)S(1)}, f32[960,128]{1,0:T(8,128)S(1)}, f32[960,128]{1,0:T(8,128)S(1)}) custom-call(f32[5,8,48,128]{3,2,1,0:T(8,128)S(1)} %get-tuple-element.34.given, f32[5,8,64,128]{3,2,1,0:T(8,128)S(1)} %get-tuple-element.33.padded.start, ...), custom_call_target="tpu_custom_call", output_to_operand_aliasing={{0}: (0, {})} | custom-call | bytes 3690000 | tf_op jit(solution)/shard_map/first_halo/pallas_call | solution.py:493
  15.2 0.7 %collective-permute-start.9 = (f32[960,128]{1,0:T(8,128)S(1)}, f32[960,128]{1,0:T(8,128)S(1)}, u32[]{:S(2)}, u32[]{:S(2)}) collective-permute-start(f32[960,128]{1,0:T(8,128)S(1)} %get-tuple-element.49), channel_id=1, source_target_pairs={{1,2},{2,1},{5,6},{6,5},{9,10},{10,9},{13,14},{14,13},{17,18},{18,... | collective-permute-start | bytes 1474568 | tf_op jit(solution)/shard_map/ppermute | solution.py:558
  15.9 1.8 %collective-permute-start.8 = (f32[960,128]{1,0:T(8,128)S(1)}, f32[960,128]{1,0:T(8,128)S(1)}, u32[]{:S(2)}, u32[]{:S(2)}) collective-permute-start(f32[960,128]{1,0:T(8,128)S(1)} %get-tuple-element.47), channel_id=1, source_target_pairs={{0,1},{1,0},{2,3},{3,2},{4,5},{5,4},{6,7},{7,6},{8,9},{9,8},{10,11... | collective-permute-start | bytes 1474568 | tf_op jit(solution)/shard_map/ppermute | solution.py:559
  17.7 0.0 collective-permute-done.3.below
  17.7 2.6 %collective-permute-done.4.above = f32[968,128]{1,0:T(8,128)S(1)} collective-permute-done((f32[968,128]{1,0:T(8,128)S(1)}, f32[968,128]{1,0:T(8,128)S(1)}, u32[]{:S(2)}, u32[]{:S(2)}) %collective-permute-start.4) | collective-permute-done | bytes 495648 | tf_op jit(solution)/shard_map/ppermute | solution.py:537
  20.3 0.8 %section.1 = (f32[5,8,48,128]{3,2,1,0:T(8,128)S(1)}, f32[5,8,64,128]{3,2,1,0:T(8,128)S(1)}, f32[64,128]{1,0:T(8,128)S(1)}, f32[64,128]{1,0:T(8,128)S(1)}, f32[160,128]{1,0:T(8,128)S(1)}) custom-call(f32[5,8,64,128]{3,2,1,0:T(8,128)S(1)} %get-tuple-element.33.padded.start, f32[5,8,48,128]{3,2,1,0:T(8,128)S(1)} %get-tuple-element.38.rate, ...), custom_call_target="tpu_custom_call" | custom-call | bytes 3690000 | tf_op jit(solution)/shard_map/section/pallas_call | solution.py:493
  21.1 1.8 %collective-permute-start.5 = (f32[160,128]{1,0:T(8,128)S(1)}, f32[160,128]{1,0:T(8,128)S(1)}, u32[]{:S(2)}, u32[]{:S(2)}) collective-permute-start(f32[160,128]{1,0:T(8,128)S(1)} %get-tuple-element.44), channel_id=1, source_target_pairs={{0,16},{4,20},{8,24},{12,28},{16,0},{20,4},{24,8},{28,12},{1,17},{... | collective-permute-start | bytes 245768 | tf_op jit(solution)/shard_map/ppermute | solution.py:516
  22.8 0.0 collective-permute-start.6
  22.8 1.1 %collective-permute-start.7 = (f32[64,128]{1,0:T(8,128)S(1)}, f32[64,128]{1,0:T(8,128)S(1)}, u32[]{:S(2)}, u32[]{:S(2)}) collective-permute-start(f32[64,128]{1,0:T(8,128)S(1)} %get-tuple-element.46), channel_id=1, source_target_pairs={{4,8},{12,16},{20,24},{28,0},{8,4},{16,12},{24,20},{0,28},{5,9},{1... | collective-permute-start | bytes 98312 | tf_op jit(solution)/shard_map/ppermute | solution.py:515
  24.0 2.4 %second.1 = (f32[5,8,48,128]{3,2,1,0:T(8,128)S(1)}, f32[960,128]{1,0:T(8,128)S(1)}, f32[960,128]{1,0:T(8,128)S(1)}) custom-call(f32[5,8,64,128]{3,2,1,0:T(8,128)S(1)} %get-tuple-element.41.padded.refs_0_, bf16[128,256]{1,0:T(8,128)(2,1)S(1)} %get-tuple-element.30.matrix, f32[3,48,128]{2,1,0:T(8,128)S(1)} %get-tuple-element.31.geo, ...), custom_call_target="tpu_custom_call" | custom-call | bytes 9225000 | tf_op jit(solution)/shard_map/second/pallas_call | solution.py:493
  26.4 0.0 collective-permute-done.6.inner
  26.4 0.7 %collective-permute-done.7.outer = f32[64,128]{1,0:T(8,128)S(1)} collective-permute-done((f32[64,128]{1,0:T(8,128)S(1)}, f32[64,128]{1,0:T(8,128)S(1)}, u32[]{:S(2)}, u32[]{:S(2)}) %collective-permute-start.7) | collective-permute-done | bytes 32800 | tf_op jit(solution)/shard_map/ppermute | solution.py:515
  27.1 0.0 collective-permute-done.5.polar
  27.1 0.9 %second_halo.1.refs_1_ = f32[5,8,48,128]{3,2,1,0:T(8,128)S(1)} custom-call(f32[5,8,48,128]{3,2,1,0:T(8,128)S(1)} %get-tuple-element.43.given, f32[5,8,64,128]{3,2,1,0:T(8,128)S(1)} %get-tuple-element.41.padded.refs_0_, f32[160,128]{1,0:T(8,128)S(1)} %collective-permute-done.5.polar, ...), custom_call_target="tpu_custom_call", output_to_operand_aliasing={{}: (0, {})} | custom-call | bytes 3690000 | tf_op jit(solution)/shard_map/second_halo/pallas_call | solution.py:493
  28.0 0.0 collective-permute-done.9.refs_2_
  28.0 0.9 %last_low.1.refs_5_ = f32[5,8,48,128]{3,2,1,0:T(8,128)} custom-call(f32[5,8,64,128]{3,2,1,0:T(8,128)S(1)} %get-tuple-element.41.padded.refs_0_, f32[5,8,48,128]{3,2,1,0:T(8,128)S(1)} %second_halo.1.refs_1_, f32[960,128]{1,0:T(8,128)S(1)} %collective-permute-done.9.refs_2_, f32[960,128]{1,0:T(8,128)S(1)} %get-tuple-element.50.refs_3_, ...), custom_call_target="tpu_custom_call" | custom-call | bytes 1845000 | tf_op jit(solution)/shard_map/last_low/pallas_call | solution.py:493
  29.0 0.9 %collective-permute-done.8.refs_2_ = f32[960,128]{1,0:T(8,128)S(1)} collective-permute-done((f32[960,128]{1,0:T(8,128)S(1)}, f32[960,128]{1,0:T(8,128)S(1)}, u32[]{:S(2)}, u32[]{:S(2)}) %collective-permute-start.8) | collective-permute-done | bytes 491552 | tf_op jit(solution)/shard_map/ppermute | solution.py:559
  29.9 0.9 %last_high.1 = f32[5,8,48,128]{3,2,1,0:T(8,128)} custom-call(f32[5,8,64,128]{3,2,1,0:T(8,128)S(1)} %get-tuple-element.41.padded.refs_0_, f32[5,8,48,128]{3,2,1,0:T(8,128)S(1)} %second_halo.1.refs_1_, f32[960,128]{1,0:T(8,128)S(1)} %collective-permute-done.8.refs_2_, f32[960,128]{1,0:T(8,128)S(1)} %get-tuple-element.48.refs_3_, ...), custom_call_target="tpu_custom_call", output_to_operand_aliasing={{}: (5, {})} | custom-call | bytes 3690000 | tf_op jit(solution)/shard_map/last_high/pallas_call | solution.py:493
Async XLA Ops:
  1.7 16.0 %collective-permute-start.3 = (f32[968,128]{1,0:T(8,128)S(1)}, f32[968,128]{1,0:T(8,128)S(1)}, u32[]{:S(2)}, u32[]{:S(2)}) collective-permute-start(f32[968,128]{1,0:T(8,128)S(1)} %get-tuple-element.39), channel_id=1, source_target_pairs={{1,2},{2,1},{5,6},{6,5},{9,10},{10,9},{13,14},{14,13},{17,18},{18,... | collective-permute-start | bytes 1486856 | tf_op jit(solution)/shard_map/ppermute | solution.py:536
  2.4 17.8 %collective-permute-start.4 = (f32[968,128]{1,0:T(8,128)S(1)}, f32[968,128]{1,0:T(8,128)S(1)}, u32[]{:S(2)}, u32[]{:S(2)}) collective-permute-start(f32[968,128]{1,0:T(8,128)S(1)} %get-tuple-element.40), channel_id=1, source_target_pairs={{0,1},{1,0},{2,3},{3,2},{4,5},{5,4},{6,7},{7,6},{8,9},{9,8},{10,11... | collective-permute-start | bytes 1486856 | tf_op jit(solution)/shard_map/ppermute | solution.py:537
  8.3 5.8 %collective-permute-start = (f32[160,128]{1,0:T(8,128)S(1)}, f32[160,128]{1,0:T(8,128)S(1)}, u32[]{:S(2)}, u32[]{:S(2)}) collective-permute-start(f32[160,128]{1,0:T(8,128)S(1)} %get-tuple-element.35), channel_id=1, source_target_pairs={{0,16},{4,20},{8,24},{12,28},{16,0},{20,4},{24,8},{28,12},{1,17},{... | collective-permute-start | bytes 245768 | tf_op jit(solution)/shard_map/ppermute | solution.py:516
  9.8 3.6 %collective-permute-start.1 = (f32[64,128]{1,0:T(8,128)S(1)}, f32[64,128]{1,0:T(8,128)S(1)}, u32[]{:S(2)}, u32[]{:S(2)}) collective-permute-start(f32[64,128]{1,0:T(8,128)S(1)} %get-tuple-element.36), channel_id=1, source_target_pairs={{0,4},{8,12},{16,20},{24,28},{4,0},{12,8},{20,16},{28,24},{1,5},{9... | collective-permute-start | bytes 98312 | tf_op jit(solution)/shard_map/ppermute | solution.py:514
  9.8 4.3 %collective-permute-start.2 = (f32[64,128]{1,0:T(8,128)S(1)}, f32[64,128]{1,0:T(8,128)S(1)}, u32[]{:S(2)}, u32[]{:S(2)}) collective-permute-start(f32[64,128]{1,0:T(8,128)S(1)} %get-tuple-element.37), channel_id=1, source_target_pairs={{4,8},{12,16},{20,24},{28,0},{8,4},{16,12},{24,20},{0,28},{5,9},{1... | collective-permute-start | bytes 98312 | tf_op jit(solution)/shard_map/ppermute | solution.py:515
  15.2 12.8 %collective-permute-start.9 = (f32[960,128]{1,0:T(8,128)S(1)}, f32[960,128]{1,0:T(8,128)S(1)}, u32[]{:S(2)}, u32[]{:S(2)}) collective-permute-start(f32[960,128]{1,0:T(8,128)S(1)} %get-tuple-element.49), channel_id=1, source_target_pairs={{1,2},{2,1},{5,6},{6,5},{9,10},{10,9},{13,14},{14,13},{17,18},{18,... | collective-permute-start | bytes 1474568 | tf_op jit(solution)/shard_map/ppermute | solution.py:558
  15.9 14.0 %collective-permute-start.8 = (f32[960,128]{1,0:T(8,128)S(1)}, f32[960,128]{1,0:T(8,128)S(1)}, u32[]{:S(2)}, u32[]{:S(2)}) collective-permute-start(f32[960,128]{1,0:T(8,128)S(1)} %get-tuple-element.47), channel_id=1, source_target_pairs={{0,1},{1,0},{2,3},{3,2},{4,5},{5,4},{6,7},{7,6},{8,9},{9,8},{10,11... | collective-permute-start | bytes 1474568 | tf_op jit(solution)/shard_map/ppermute | solution.py:559
  21.1 6.0 %collective-permute-start.5 = (f32[160,128]{1,0:T(8,128)S(1)}, f32[160,128]{1,0:T(8,128)S(1)}, u32[]{:S(2)}, u32[]{:S(2)}) collective-permute-start(f32[160,128]{1,0:T(8,128)S(1)} %get-tuple-element.44), channel_id=1, source_target_pairs={{0,16},{4,20},{8,24},{12,28},{16,0},{20,4},{24,8},{28,12},{1,17},{... | collective-permute-start | bytes 245768 | tf_op jit(solution)/shard_map/ppermute | solution.py:516
  22.8 3.5 %collective-permute-start.6 = (f32[64,128]{1,0:T(8,128)S(1)}, f32[64,128]{1,0:T(8,128)S(1)}, u32[]{:S(2)}, u32[]{:S(2)}) collective-permute-start(f32[64,128]{1,0:T(8,128)S(1)} %get-tuple-element.45), channel_id=1, source_target_pairs={{0,4},{8,12},{16,20},{24,28},{4,0},{12,8},{20,16},{28,24},{1,5},{9... | collective-permute-start | bytes 98312 | tf_op jit(solution)/shard_map/ppermute | solution.py:514
  22.8 4.2 %collective-permute-start.7 = (f32[64,128]{1,0:T(8,128)S(1)}, f32[64,128]{1,0:T(8,128)S(1)}, u32[]{:S(2)}, u32[]{:S(2)}) collective-permute-start(f32[64,128]{1,0:T(8,128)S(1)} %get-tuple-element.46), channel_id=1, source_target_pairs={{4,8},{12,16},{20,24},{28,0},{8,4},{16,12},{24,20},{0,28},{5,9},{1... | collective-permute-start | bytes 98312 | tf_op jit(solution)/shard_map/ppermute | solution.py:515

commit v7 on v6

--- a/solution.py
+++ b/solution.py
@@ -91,52 +91,64 @@
     return out
 
 
-def edges_kernel(
+def levels_kernel(
     levels, rows, state, outer_rows, kappa, matrix_in, geo_in,
-    staged, beyond, low, high, inner, outer, polar, kap, matrix, geo,
-    kappa_scalars, sems,
+    high, low, beyond, kap, matrix, geo, kappa_scalars, sems,
 ):
     block = REACH * rows
-    odd, mirror = mirrored()
-    reads = [(state.at[f], staged.at[f]) for f in range(FIELDS)]
+    odd, _ = mirrored()
+    starts = (jnp.where(odd == 1, 0, REACH), jnp.where(odd == 1, REACH, 0))
+    reads = [
+        (state.at[pl.ds(pl.multiple_of((f * levels + start) * rows, TILE), block)], side.at[pl.ds(f * block, block)])
+        for start, side in zip(starts, (high, low))
+        for f in range(FIELDS)
+    ]
     reads += [(kappa, kappa_scalars), (outer_rows, beyond), (matrix_in, matrix), (geo_in, geo)]
     copies = [pltpu.make_async_copy(*read, sems.at[i]) for i, read in enumerate(reads)]
     for copy in copies:
         copy.start()
-    packs = []
-    for f in range(FIELDS):
-        copies[f].wait()
-        real = [jnp.where(odd == 1, levels - 1 - l, l) for l in range(levels)]
-        tiles = []
-        for l in range(levels):
-            whole = staged[f, real[l]]
-            if f == 3:
-                whole = mirror * whole
-            if l < REACH:
-                low[pl.ds(f * block + l * rows, rows), :] = whole
-            if l >= levels - REACH:
-                high[pl.ds(f * block + (l - levels + REACH) * rows, rows), :] = whole
-            tiles.append([whole[t * TILE : (t + 1) * TILE] for t in range(rows // TILE)])
-            polar[pl.ds((f * levels + l) * REACH, REACH), :] = whole[:REACH]
-        packs += packed(levels, rows, tiles)
-    store_packs(packs, inner, outer)
-    copies[FIELDS].wait()
+    copies[2 * FIELDS].wait()
+    for start, side in zip(starts, (high, low)):
+        for i in range(REACH):
+            value = jnp.full((1, LANES), kappa_scalars[start + i], jnp.float32)
+            side[pl.ds(FIELDS * block + i, 1), :] = value
     for l in range(levels):
         value = kappa_scalars[jnp.where(odd == 1, levels - 1 - l, l)]
         kap[l] = jnp.full((TILE, LANES), value, jnp.float32)
-        if l < REACH:
-            low[pl.ds(FIELDS * block + l, 1), :] = jnp.full((1, LANES), value, jnp.float32)
-        if l >= levels - REACH:
-            high[pl.ds(FIELDS * block + l - levels + REACH, 1), :] = jnp.full((1, LANES), value, jnp.float32)
-    low[pl.ds(FIELDS * block + REACH, REACH), :] = jnp.ones((REACH, LANES), jnp.float32)
-    high[pl.ds(FIELDS * block + REACH, REACH), :] = jnp.ones((REACH, LANES), jnp.float32)
-    for copy in copies[FIELDS + 1 :]:
-        copy.wait()
+    for i, copy in enumerate(copies):
+        if i != 2 * FIELDS:
+            copy.wait()
+
+
+def own_level(high, low, rows, f, l, odd):
+    i = l % REACH
+    at = (f * REACH + jnp.where(odd == 1, REACH - 1 - i, i)) * rows
+    return (low if l < REACH else high), pl.multiple_of(at, TILE)
+
+
+def edges_kernel(levels, rows, given, high, low, inner, outer, polar):
+    odd, mirror = mirrored()
+    packs = []
+    for f in range(FIELDS):
+        tiles = []
+        for l in range(levels):
+            side, at = own_level(high, low, rows, f, l, odd)
+            tiles.append([side[pl.ds(at + t * TILE, TILE), :] for t in range(rows // TILE)])
+            cap = side[pl.ds(at, REACH), :]
+            polar[pl.ds((f * levels + l) * REACH, REACH), :] = mirror * cap if f == 3 else cap
+        packs += [mirror * pack if f == 3 else pack for pack in packed(levels, rows, tiles)]
+    store_packs(packs, inner, outer)
 
 
 def mirrored():
     odd = lax.axis_index("rad") % 2
     return odd, jnp.where(odd == 1, -1.0, 1.0).astype(jnp.float32)
+
+
+def bordered(at):
+    here, depth = lax.axis_index("rad"), lax.axis_size("rad")
+    inside = jnp.where((here > 0) & (here < depth - 1), 1.0, 0.0)
+    return inside.astype(jnp.float32) if at == 0 else jnp.float32(1.0)
 
 
 def lanes():
@@ -220,7 +232,7 @@
     return total
 
 
-def add_halo(levels, rows, padded, polar, inner, outer, geo, kap, store):
+def add_halo(levels, rows, own, padded, polar, inner, outer, geo, kap, store):
     per = GROUPS // levels
     count = rows // TILE // per
     packs = load_packs(FIELDS * count, inner, outer)
@@ -243,7 +255,7 @@
         here = pl.ds(t * TILE, TILE)
         metric = jnp.where(at_side, geo[0, here, :], 0.0)
         metric2 = jnp.where(at_side, geo[1, here, :], 0.0)
-        for l in range(levels):
+        for l in own:
             shift = (LANES - REACH - 2 * REACH * (u * levels + l)) % LANES
             center = [padded[f, l, pl.ds((t + 1) * TILE, TILE), :] for f in range(FIELDS)]
             wlon, wrow, temper = center[1], center[2], center[4]
@@ -333,12 +345,13 @@
     lax.fori_loop(0, rows // TILE, body, 0)
 
 
-def first_kernel(levels, rows, staged, beyond, matrix, geo, kap, padded, rate, dlon, elon):
+def first_kernel(levels, rows, high, low, beyond, matrix, geo, kap, padded, rate, dlon, elon):
     odd, mirror = mirrored()
     for f in range(FIELDS):
         for l in range(levels):
-            real = jnp.where(odd == 1, levels - 1 - l, l)
-            whole, after = staged[f, real], beyond[f, real]
+            side, at = own_level(high, low, rows, f, l, odd)
+            whole = side[pl.ds(at, rows), :]
+            after = beyond[f, jnp.where(odd == 1, levels - 1 - l, l)]
             if f == 3:
                 whole, after = mirror * whole, mirror * after
             padded[f, l, pl.ds(0, TILE), :] = jnp.zeros((TILE, LANES), jnp.float32)
@@ -352,19 +365,23 @@
     interior(levels, rows, padded, dlon, elon, geo, kap, store)
 
 
-def first_halo_kernel(
-    levels, rows, given, padded, polar, inner, outer, geo, kap, rate, low, high
-):
+def first_halo_kernel(at, levels, rows, given, padded, polar, inner, outer, geo, kap, rate, side):
     def store(f, l, r0, value, extra):
         tendency = given[f, l, pl.ds(r0, TILE), :] + extra
         rate[f, l, pl.ds(r0, TILE), :] = tendency
-        ahead = value + time_step * tendency
-        if l < REACH:
-            low[pl.ds((f * REACH + l) * rows + r0, TILE), :] = ahead
-        if l >= levels - REACH:
-            high[pl.ds((f * REACH + l - levels + REACH) * rows + r0, TILE), :] = ahead
-
-    add_halo(levels, rows, padded, polar, inner, outer, geo, kap, store)
+        side[pl.ds((f * REACH + l - at) * rows + r0, TILE), :] = value + time_step * tendency
+
+    own = range(at, at + REACH)
+    add_halo(levels, rows, own, padded, polar, inner, outer, geo, kap, store)
+
+
+def raw_tile(ref, rows, r0, odd, mirror):
+    out = []
+    for f in range(FIELDS):
+        ats = [(f * REACH + jnp.where(odd == 1, REACH - 1 - b, b)) * rows + r0 for b in range(REACH)]
+        out.append([ref[pl.ds(pl.multiple_of(at, TILE), TILE), :] for at in ats])
+    out[3] = [mirror * v for v in out[3]]
+    return out
 
 
 def halo_tile(ref, rows, r0):
@@ -382,31 +399,45 @@
     ]
 
 
-def section_kernel(levels, rows, padded, rate, below, above, kappa, full, ahead, inner, outer, polar):
+def section_side(at, up, levels, rows, padded, rate, sent, kappa, full, ahead):
+    odd, mirror = mirrored()
+    there = bordered(at)
+
     def body(t, carry):
         r0 = pl.multiple_of(t * TILE, TILE)
-        for halo_ref, at, up in ((below, 0, False), (above, levels - REACH, True)):
-            halo = halo_tile(halo_ref, rows, r0)
-            center = [
-                [padded[f, at + a, pl.ds(r0 + TILE, TILE), :] for a in range(REACH)] for f in range(FIELDS)
-            ]
-            extra = across_level(center[3], center[4], halo, [kappa[at + a] for a in range(REACH)], up)
-            for f in range(FIELDS):
-                for a in range(REACH):
-                    total = rate[f, at + a, pl.ds(r0, TILE), :] + extra[f][a]
-                    full[f, at + a, pl.ds(r0, TILE), :] = total
-                    ahead[f, at + a, pl.ds(r0 + TILE, TILE), :] = center[f][a] + time_step * total
+        here, inside = pl.ds(r0, TILE), pl.ds(r0 + TILE, TILE)
+        halo = raw_tile(sent, rows, r0, odd, mirror)
+        center = [[padded[f, at + a, inside, :] for a in range(REACH)] for f in range(FIELDS)]
+        extra = across_level(center[3], center[4], halo, [kappa[at + a] for a in range(REACH)], up)
+        for f in range(FIELDS):
+            for a in range(REACH):
+                more = extra[f][a] if at else there * extra[f][a]
+                total = rate[f, at + a, here, :] + more
+                full[f, at + a, here, :] = total
+                ahead[f, at + a, inside, :] = center[f][a] + time_step * total
         return carry
 
     lax.fori_loop(0, rows // TILE, body, 0)
+    for f in range(FIELDS):
+        for l in range(at, at + REACH):
+            ahead[f, l, pl.ds(0, TILE), :] = jnp.zeros((TILE, LANES), jnp.float32)
+            ahead[f, l, pl.ds(rows + TILE, REACH), :] = padded[f, l, pl.ds(rows + TILE, REACH), :]
+
+
+def section_high_kernel(levels, rows, padded, rate, above, kappa, full, ahead):
+    section_side(levels - REACH, True, levels, rows, padded, rate, above, kappa, full, ahead)
+
+
+def section_low_kernel(
+    levels, rows, padded, rate, below, kappa, given1, given2, full, ahead, inner, outer, polar
+):
+    section_side(0, False, levels, rows, padded, rate, below, kappa, full, ahead)
     packs = []
     for f in range(FIELDS):
         tiles = [[ahead[f, l, pl.ds((t + 1) * TILE, TILE), :] for t in range(rows // TILE)] for l in range(levels)]
         packs += packed(levels, rows, tiles)
         for l in range(levels):
             polar[pl.ds((f * levels + l) * REACH, REACH), :] = ahead[f, l, pl.ds(TILE, REACH), :]
-            ahead[f, l, pl.ds(0, TILE), :] = jnp.zeros((TILE, LANES), jnp.float32)
-            ahead[f, l, pl.ds(rows + TILE, REACH), :] = padded[f, l, pl.ds(rows + TILE, REACH), :]
     store_packs(packs, inner, outer)
 
 
@@ -421,16 +452,19 @@
 
     interior(levels, rows, padded, dlon, elon, geo, kap, store)
     tail = FIELDS * REACH * rows
+    odd, mirror = mirrored()
 
     def body(t, carry):
         r0 = pl.multiple_of(t * TILE, TILE)
         for halo_ref, out, at, up in ((below, low, 0, True), (above, high, levels - REACH, False)):
-            beyond = halo_tile(halo_ref, rows, r0)
+            beyond = raw_tile(halo_ref, rows, r0, odd, mirror)
             mine = [
                 [start[f, at + a, pl.ds(r0 + TILE, TILE), :] for a in range(REACH)] for f in range(FIELDS)
             ]
-            kappas = [halo_ref[pl.ds(tail + REACH - 1 - a, 1), :] for a in range(REACH)]
-            there = time_step * halo_ref[pl.ds(tail + REACH, 1), :]
+            kappas = [
+                halo_ref[pl.ds(tail + jnp.where(odd == 1, REACH - 1 - a, a), 1), :] for a in range(REACH)
+            ]
+            there = time_step * bordered(at)
             extra = across_level(beyond[3], beyond[4], mine, kappas, up)
             for f in range(FIELDS):
                 for a in range(REACH):
@@ -447,13 +481,14 @@
         at = pl.ds(r0, TILE)
         both[f, l, at, :] = given[f, l, at, :] + (0.5 * time_step) * extra
 
-    add_halo(levels, rows, padded, polar, inner, outer, geo, kap, store)
+    add_halo(levels, rows, range(levels), padded, polar, inner, outer, geo, kap, store)
 
 
 def last_kernel(at, up, levels, rows, *refs):
     padded, both, sent, more, kap = refs[:5]
     out, staged, sems = refs[-3:]
     odd, mirror = mirrored()
+    scale = (0.5 * time_step) * bordered(at)
     real = jnp.where(odd == 1, levels - at - REACH, at)
     copies = []
     for t in range(rows // TILE):
@@ -466,7 +501,7 @@
         extra = across_level(wind, temper, halo, [kap[at + a] for a in range(REACH)], up)
         for f in range(FIELDS):
             for a in range(REACH):
-                new = both[f, at + a, here, :] + (0.5 * time_step) * extra[f][a]
+                new = both[f, at + a, here, :] + scale * extra[f][a]
                 staged[f, jnp.where(odd == 1, REACH - 1 - a, a), here, :] = mirror * new if f == 3 else new
         target = out.at[:, pl.ds(real, REACH), here]
         copies.append(pltpu.make_async_copy(staged.at[:, :, here], target, sems.at[t]))
@@ -478,7 +513,7 @@
 def on_device(state, outer_rows, kappa):
     levels, rows, width = state.shape[1:]
     ring, depth = lax.axis_size("lon"), lax.axis_size("rad")
-    assert ring % 4 == 0 and width == LANES and levels >= 2 * REACH and GROUPS % levels == 0
+    assert ring % 4 == 0 and depth % 2 == 0 and width == LANES and levels == 2 * REACH and GROUPS % levels == 0
     assert rows % (TILE * (GROUPS // levels)) == 0
     matrix = stencil_matrix(width)
     geo = geometry(rows, width * ring, width)
@@ -507,8 +542,11 @@
     pairs = [(i, (i + 1) % ring) for i in range(1, ring, 2)]
     swap_outer = pairs + [(b, a) for a, b in pairs]
     half = [(i, (i + ring // 2) % ring) for i in range(ring)]
-    swap_high = [p for i in range(0, depth - 1, 2) for p in ((i, i + 1), (i + 1, i))]
-    swap_low = [p for i in range(1, depth - 1, 2) for p in ((i, i + 1), (i + 1, i))]
+    pairs = [(i, i + 1) for i in range(0, depth, 2)]
+    swap_high = pairs + [(b, a) for a, b in pairs]
+    pairs = [(lon * depth + i, lon * depth + i + 1) for lon in range(ring) for i in range(1, depth - 1, 2)]
+    pairs += [(lon * depth + i, (lon + 1) * depth + i) for lon in range(0, ring, 2) for i in (0, depth - 1)]
+    swap_low = pairs + [(b, a) for a, b in pairs]
 
     def around(inner, outer, polar):
         inner = lax.ppermute(inner, "lon", swap_inner)
@@ -516,57 +554,76 @@
         return inner, outer, lax.ppermute(polar, "lon", half)
 
     edge_shapes = [in_vmem(packs, width), in_vmem(packs, width), in_vmem(FIELDS * levels * REACH, width)]
-    staged, after, low, high, *edges, kap, matrix, geo = call(
-        edges_kernel,
+    payload = in_vmem(halo_rows + TILE, width)
+    high, low, after, kap, matrix, geo = call(
+        levels_kernel,
         [
-            in_vmem(*full_shape),
+            payload,
+            payload,
             in_vmem(*outer_rows.shape),
-            in_vmem(halo_rows + TILE, width),
-            in_vmem(halo_rows + TILE, width),
-            *edge_shapes,
             in_vmem(levels, TILE, width),
             pltpu.VMEM(matrix.shape, matrix.dtype),
             in_vmem(*geo.shape),
         ],
         (HBM,) * 5,
-        (state, outer_rows, kappa, matrix, geo),
-        scratch=(pltpu.SMEM(kappa.shape, jnp.float32), pltpu.SemaphoreType.DMA((FIELDS + 4,))),
+        (state.reshape(-1, width), outer_rows, kappa, matrix, geo),
+        scratch=(pltpu.SMEM(kappa.shape, jnp.float32), pltpu.SemaphoreType.DMA((2 * FIELDS + 4,))),
+        name="levels",
+    )
+    above = lax.ppermute(high, "rad", swap_high)
+    low, *edges = call(
+        edges_kernel,
+        [payload, *edge_shapes],
+        (VMEM,) * 2,
+        (low, high),
+        aliases={0: 0},
         name="edges",
     )
-    below = lax.ppermute(low, "rad", swap_low)
-    above = lax.ppermute(high, "rad", swap_high)
+    below = lax.ppermute(low, ("lon", "rad"), swap_low)
     inner, outer, beyond = around(*edges)
     lon_scratch = (in_vmem(*full_shape), in_vmem(*full_shape[1:]))
     side = in_vmem(halo_rows, width)
     padded, rate = call(
         first_kernel,
         [in_vmem(*pad_shape), in_vmem(*full_shape)],
-        (VMEM,) * 5,
-        (staged, after, matrix, geo, kap),
+        (VMEM,) * 6,
+        (high, low, after, matrix, geo, kap),
         scratch=lon_scratch,
         cost=2.0,
         name="first",
     )
-    rate, low, high = call(
-        first_halo_kernel,
-        [in_vmem(*full_shape), side, side],
-        (VMEM,) * 7,
-        (rate, padded, beyond, inner, outer, geo, kap),
-        aliases={0: 0},
-        name="first_halo",
-    )
-    below2 = lax.ppermute(low, "rad", swap_low)
+
+    def first_halo(rate, at):
+        return call(
+            functools.partial(first_halo_kernel, at),
+            [in_vmem(*full_shape), side],
+            (VMEM,) * 7,
+            (rate, padded, beyond, inner, outer, geo, kap),
+            aliases={0: 0},
+            cost=0.6,
+            name="first_halo",
+        )
+
+    rate, high = first_halo(rate, levels - REACH)
     above2 = lax.ppermute(high, "rad", swap_high)
+    rate, low = first_halo(rate, 0)
+    below2 = lax.ppermute(low, ("lon", "rad"), swap_low)
+    full, ahead = call(
+        section_high_kernel,
+        [in_vmem(*full_shape), in_vmem(*pad_shape)],
+        (VMEM,) * 4,
+        (padded, rate, above, kap),
+        cost=0.4,
+        name="section_high",
+    )
     full, ahead, *edges = call(
-        section_kernel,
-        [
-            in_vmem(*full_shape),
-            in_vmem(*pad_shape),
-            *edge_shapes,
-        ],
-        (VMEM,) * 5,
-        (padded, rate, below, above, kap),
-        name="section",
+        section_low_kernel,
+        [in_vmem(*full_shape), in_vmem(*pad_shape), *edge_shapes],
+        (VMEM,) * 6,
+        (padded, rate, below, kap, full, ahead),
+        aliases={4: 0, 5: 1},
+        cost=0.5,
+        name="section_low",
     )
     inner, outer, beyond = around(*edges)
     both, low, high = call(
@@ -592,22 +649,22 @@
     )
     result = pltpu.HBM(full_shape, jnp.float32)
     out = call(
+        functools.partial(last_kernel, levels - REACH, True),
+        result,
+        (VMEM,) * 5,
+        (ahead, both, above2, high, kap),
+        scratch=last_scratch,
+        cost=0.5,
+        name="last_high",
+    )
+    return call(
         functools.partial(last_kernel, 0, False),
         result,
-        (VMEM,) * 5,
-        (ahead, both, below2, low, kap),
-        scratch=last_scratch,
-        cost=0.5,
-        name="last_low",
-    )
-    return call(
-        functools.partial(last_kernel, levels - REACH, True),
-        result,
         (VMEM,) * 5 + (HBM,),
-        (ahead, both, above2, high, kap, out),
+        (ahead, both, below2, low, kap, out),
         scratch=last_scratch,
         aliases={5: 0},
-        name="last_high",
+        name="last_low",
     )
 
 

time: 31 us -> 28.4 us (0.916)
  starting transfers between devices: 15 us -> 12.8 us
  waiting for transfers between devices: 4.94 us -> 3.98 us
  Pallas kernels: 10.7 us -> 11.4 us
    ppermute x1, starting transfers between devices: 5.88 us -> 3.09 us  [on_device(): above = lax.ppermute(high, 'rad', swap_high)]
    ppermute x1, waiting for transfers between devices: 2.56 us -> 0.77 us  [on_device(): above = lax.ppermute(high, 'rad', swap_high)]
    ppermute x2, starting transfers between devices: 1.38 us -> 0.11 us  [the longest x1 0.07 us: on_device(): below2 = lax.ppermute(low, ('lon', 'rad'), swap_low)]
    ppermute x1, starting transfers between devices: 1.81 us -> 3.06 us  [on_device(): above2 = lax.ppermute(high, 'rad', swap_high)]
    ppermute x2, starting transfers between devices: 3.31 us -> 4.05 us  [around(): return (inner, outer, lax.ppermute(polar, 'lon', half))]
    pallas_call x8 -> x11, Pallas kernels: 10.7 us -> 11.4 us  [call(): pl.pallas_call(functools.partial(kernel, levels, rows), out_shape=out_sha...]
    ppermute x1, waiting for transfers between devices: 0.93 us -> 1.56 us  [on_device(): above2 = lax.ppermute(high, 'rad', swap_high)]
    ppermute x2, starting transfers between devices: 2.66 us -> 2.32 us  [around(): outer = lax.ppermute(outer, 'lon', swap_outer)]
  transfers between devices with their start and end apart: 10 -> 10, of which waited for: 4 -> 4; matrix products, arithmetic and copies ran while one was open for 0% -> 0% of each run, Pallas kernels for 26% -> 32%
where the time goes in v7:
time: 28.4 us; the launch traced here: 28.3 us
  starting transfers between devices  12.8 us (45%)
  Pallas kernels  11.4 us (40%)
  waiting for transfers between devices  3.98 us (14%)
    pallas_call x11, Pallas kernels, call(): pl.pallas_call(functools.partial(kernel, levels, rows), out_shape=out_sha...  11.4 us
    ppermute x2, starting transfers between devices, around(): return (inner, outer, lax.ppermute(polar, 'lon', half))  4.05 us
    ppermute x1, starting transfers between devices, on_device(): above = lax.ppermute(high, 'rad', swap_high)  3.09 us
    ppermute x1, starting transfers between devices, on_device(): above2 = lax.ppermute(high, 'rad', swap_high)  3.06 us
    ppermute x2, starting transfers between devices, around(): outer = lax.ppermute(outer, 'lon', swap_outer)  2.32 us
    ppermute x2, waiting for transfers between devices, around(): outer = lax.ppermute(outer, 'lon', swap_outer)  1.63 us
    ppermute x1, waiting for transfers between devices, on_device(): above2 = lax.ppermute(high, 'rad', swap_high)  1.56 us
    ppermute x1, waiting for transfers between devices, on_device(): above = lax.ppermute(high, 'rad', swap_high)  0.77 us
  transfers between devices with their start and end apart: 10, of which 4 were waited for; matrix products, arithmetic and copies ran while one was open for 0% of the time, Pallas kernels for 32%

profile of v7, /device:TPU:0, one launch (start us, length us, event | category | flops | bytes accessed | tf_op | source)
XLA Modules:
  0.0 28.3 jit_solution(14050800526312378230)
XLA Ops:
  0.0 1.5 %levels.1 = (f32[968,128]{1,0:T(8,128)S(1)}, f32[968,128]{1,0:T(8,128)S(1)}, f32[5,8,4,128]{3,2,1,0:T(4,128)S(1)}, f32[8,8,128]{2,1,0:T(8,128)S(1)}, bf16[128,25...) custom-call(f32[1920,128]{1,0:T(8,128)} %bitcast.1, f32[5,8,4,128]{3,2,1,0:T(4,128)} %outer_rows.1, f32[8]{0:T(128)} %kappa.1, ...), custom_call_target="tpu_custom_call" | custom-call | bytes 3690000 | tf_op jit(solution)/shard_map/levels/pallas_call | solution.py:528
  1.5 3.1 %collective-permute-start.4 = (f32[968,128]{1,0:T(8,128)S(1)}, f32[968,128]{1,0:T(8,128)S(1)}, u32[]{:S(2)}, u32[]{:S(2)}) collective-permute-start(f32[968,128]{1,0:T(8,128)S(1)} %get-tuple-element.31.high), channel_id=1, source_target_pairs={{0,1},{2,3},{1,0},{3,2},{4,5},{6,7},{5,4},{7,6},{8,9},{10,11},{9,8... | collective-permute-start | bytes 1486856 | tf_op jit(solution)/shard_map/ppermute | solution.py:573
  4.6 0.4 %edges.1 = (f32[968,128]{1,0:T(8,128)S(1)}, f32[64,128]{1,0:T(8,128)S(1)}, f32[64,128]{1,0:T(8,128)S(1)}, f32[160,128]{1,0:T(8,128)S(1)}) custom-call(f32[968,128]{1,0:T(8,128)S(1)} %get-tuple-element.32.given, f32[968,128]{1,0:T(8,128)S(1)} %get-tuple-element.31.high), custom_call_target="tpu_custom_call", output_to_operand_aliasing={{0}: (0, {})} | custom-call | bytes 3690000 | tf_op jit(solution)/shard_map/edges/pallas_call | solution.py:528
  5.0 0.0 collective-permute-start.3
  5.0 1.6 %collective-permute-start = (f32[160,128]{1,0:T(8,128)S(1)}, f32[160,128]{1,0:T(8,128)S(1)}, u32[]{:S(2)}, u32[]{:S(2)}) collective-permute-start(f32[160,128]{1,0:T(8,128)S(1)} %get-tuple-element.40), channel_id=1, source_target_pairs={{0,16},{4,20},{8,24},{12,28},{16,0},{20,4},{24,8},{28,12},{1,17},{... | collective-permute-start | bytes 245768 | tf_op jit(solution)/shard_map/ppermute | solution.py:554
  6.6 0.2 collective-permute-start.1
  6.7 1.4 %collective-permute-start.2 = (f32[64,128]{1,0:T(8,128)S(1)}, f32[64,128]{1,0:T(8,128)S(1)}, u32[]{:S(2)}, u32[]{:S(2)}) collective-permute-start(f32[64,128]{1,0:T(8,128)S(1)} %get-tuple-element.42), channel_id=1, source_target_pairs={{4,8},{12,16},{20,24},{28,0},{8,4},{16,12},{24,20},{0,28},{5,9},{1... | collective-permute-start | bytes 98312 | tf_op jit(solution)/shard_map/ppermute | solution.py:553
  8.1 2.0 %first.1 = (f32[5,8,64,128]{3,2,1,0:T(8,128)S(1)}, f32[5,8,48,128]{3,2,1,0:T(8,128)S(1)}) custom-call(f32[968,128]{1,0:T(8,128)S(1)} %get-tuple-element.31.high, f32[968,128]{1,0:T(8,128)S(1)} %get-tuple-element.33.low, f32[5,8,4,128]{3,2,1,0:T(4,128)S(1)} %get-tuple-element.34.beyond, bf16[128,256]{1,0:T(8,128)(2,1)S(1)} %get-tuple-element.35.matrix, ...), custom_call_target="tpu_custom_call" | custom-call | bytes 7380000 | tf_op jit(solution)/shard_map/first/pallas_call | solution.py:528
  10.2 0.0 collective-permute-done.1.inner
  10.2 0.8 %collective-permute-done.2.outer = f32[64,128]{1,0:T(8,128)S(1)} collective-permute-done((f32[64,128]{1,0:T(8,128)S(1)}, f32[64,128]{1,0:T(8,128)S(1)}, u32[]{:S(2)}, u32[]{:S(2)}) %collective-permute-start.2) | collective-permute-done | bytes 32800 | tf_op jit(solution)/shard_map/ppermute | solution.py:553
  11.0 0.0 collective-permute-done.polar
  11.0 0.7 %first_halo.2 = (f32[5,8,48,128]{3,2,1,0:T(8,128)S(1)}, f32[960,128]{1,0:T(8,128)S(1)}) custom-call(f32[5,8,48,128]{3,2,1,0:T(8,128)S(1)} %get-tuple-element.39.given, f32[5,8,64,128]{3,2,1,0:T(8,128)S(1)} %get-tuple-element.38.padded.start, f32[160,128]{1,0:T(8,128)S(1)} %collective-permute-done.polar, ...), custom_call_target="tpu_custom_call", output_to_operand_aliasing={{0}: (0, {})} | custom-call | bytes 2214000 | tf_op jit(solution)/shard_map/first_halo/pallas_call | solution.py:528
  11.7 3.1 %collective-permute-start.9 = (f32[960,128]{1,0:T(8,128)S(1)}, f32[960,128]{1,0:T(8,128)S(1)}, u32[]{:S(2)}, u32[]{:S(2)}) collective-permute-start(f32[960,128]{1,0:T(8,128)S(1)} %get-tuple-element.55), channel_id=1, source_target_pairs={{0,1},{2,3},{1,0},{3,2},{4,5},{6,7},{5,4},{7,6},{8,9},{10,11},{9,8... | collective-permute-start | bytes 1474568 | tf_op jit(solution)/shard_map/ppermute | solution.py:608
  14.7 0.7 %first_halo.3 = (f32[5,8,48,128]{3,2,1,0:T(8,128)S(1)}, f32[960,128]{1,0:T(8,128)S(1)}) custom-call(f32[5,8,48,128]{3,2,1,0:T(8,128)S(1)} %get-tuple-element.43.given, f32[5,8,64,128]{3,2,1,0:T(8,128)S(1)} %get-tuple-element.38.padded.start, f32[160,128]{1,0:T(8,128)S(1)} %collective-permute-done.polar, ...), custom_call_target="tpu_custom_call", output_to_operand_aliasing={{0}: (0, {})} | custom-call | bytes 2214000 | tf_op jit(solution)/shard_map/first_halo/pallas_call | solution.py:528
  15.4 0.1 collective-permute-start.8
  15.5 0.8 %collective-permute-done.4.above = f32[968,128]{1,0:T(8,128)S(1)} collective-permute-done((f32[968,128]{1,0:T(8,128)S(1)}, f32[968,128]{1,0:T(8,128)S(1)}, u32[]{:S(2)}, u32[]{:S(2)}) %collective-permute-start.4) | collective-permute-done | bytes 495648 | tf_op jit(solution)/shard_map/ppermute | solution.py:573
  16.3 0.3 section_high.1
  16.5 0.0 collective-permute-done.3.below
  16.5 0.7 %section_low.1 = (f32[5,8,48,128]{3,2,1,0:T(8,128)S(1)}, f32[5,8,64,128]{3,2,1,0:T(8,128)S(1)}, f32[64,128]{1,0:T(8,128)S(1)}, f32[64,128]{1,0:T(8,128)S(1)}, f32[160,128]{1,0:T(8,128)S(1)}) custom-call(f32[5,8,64,128]{3,2,1,0:T(8,128)S(1)} %get-tuple-element.38.padded.start, ...), custom_call_target="tpu_custom_call", output_to_operand_aliasing={{0}: (4, {}), {1}: (5, {})} | custom-call | bytes 1845000 | tf_op jit(solution)/shard_map/section_low/pallas_call | solution.py:528
  17.2 2.5 %collective-permute-start.5 = (f32[160,128]{1,0:T(8,128)S(1)}, f32[160,128]{1,0:T(8,128)S(1)}, u32[]{:S(2)}, u32[]{:S(2)}) collective-permute-start(f32[160,128]{1,0:T(8,128)S(1)} %get-tuple-element.50), channel_id=1, source_target_pairs={{0,16},{4,20},{8,24},{12,28},{16,0},{20,4},{24,8},{28,12},{1,17},{... | collective-permute-start | bytes 245768 | tf_op jit(solution)/shard_map/ppermute | solution.py:554
  19.7 0.0 collective-permute-start.6
  19.7 0.9 %collective-permute-start.7 = (f32[64,128]{1,0:T(8,128)S(1)}, f32[64,128]{1,0:T(8,128)S(1)}, u32[]{:S(2)}, u32[]{:S(2)}) collective-permute-start(f32[64,128]{1,0:T(8,128)S(1)} %get-tuple-element.52), channel_id=1, source_target_pairs={{4,8},{12,16},{20,24},{28,0},{8,4},{16,12},{24,20},{0,28},{5,9},{1... | collective-permute-start | bytes 98312 | tf_op jit(solution)/shard_map/ppermute | solution.py:553
  20.6 2.5 %second.1 = (f32[5,8,48,128]{3,2,1,0:T(8,128)S(1)}, f32[960,128]{1,0:T(8,128)S(1)}, f32[960,128]{1,0:T(8,128)S(1)}) custom-call(f32[5,8,64,128]{3,2,1,0:T(8,128)S(1)} %get-tuple-element.47.padded.refs_0_, bf16[128,256]{1,0:T(8,128)(2,1)S(1)} %get-tuple-element.35.matrix, f32[3,48,128]{2,1,0:T(8,128)S(1)} %get-tuple-element.36.geo, ...), custom_call_target="tpu_custom_call" | custom-call | bytes 9225000 | tf_op jit(solution)/shard_map/second/pallas_call | solution.py:528
  23.1 0.0 collective-permute-done.6.inner
  23.1 0.8 %collective-permute-done.7.outer = f32[64,128]{1,0:T(8,128)S(1)} collective-permute-done((f32[64,128]{1,0:T(8,128)S(1)}, f32[64,128]{1,0:T(8,128)S(1)}, u32[]{:S(2)}, u32[]{:S(2)}) %collective-permute-start.7) | collective-permute-done | bytes 32800 | tf_op jit(solution)/shard_map/ppermute | solution.py:553
  23.9 0.0 collective-permute-done.5.polar
  23.9 0.9 %second_halo.1.refs_1_ = f32[5,8,48,128]{3,2,1,0:T(8,128)S(1)} custom-call(f32[5,8,48,128]{3,2,1,0:T(8,128)S(1)} %get-tuple-element.49.given, f32[5,8,64,128]{3,2,1,0:T(8,128)S(1)} %get-tuple-element.47.padded.refs_0_, f32[160,128]{1,0:T(8,128)S(1)} %collective-permute-done.5.polar, ...), custom_call_target="tpu_custom_call", output_to_operand_aliasing={{}: (0, {})} | custom-call | bytes 3690000 | tf_op jit(solution)/shard_map/second_halo/pallas_call | solution.py:528
  24.8 1.6 %collective-permute-done.9.refs_2_ = f32[960,128]{1,0:T(8,128)S(1)} collective-permute-done((f32[960,128]{1,0:T(8,128)S(1)}, f32[960,128]{1,0:T(8,128)S(1)}, u32[]{:S(2)}, u32[]{:S(2)}) %collective-permute-start.9) | collective-permute-done | bytes 491552 | tf_op jit(solution)/shard_map/ppermute | solution.py:608
  26.4 0.9 %last_high.1.refs_5_ = f32[5,8,48,128]{3,2,1,0:T(8,128)} custom-call(f32[5,8,64,128]{3,2,1,0:T(8,128)S(1)} %get-tuple-element.47.padded.refs_0_, f32[5,8,48,128]{3,2,1,0:T(8,128)S(1)} %second_halo.1.refs_1_, f32[960,128]{1,0:T(8,128)S(1)} %collective-permute-done.9.refs_2_, f32[960,128]{1,0:T(8,128)S(1)} %get-tuple-element.56.refs_3_, ...), custom_call_target="tpu_custom_call" | custom-call | bytes 1845000 | tf_op jit(solution)/shard_map/last_high/pallas_call | solution.py:528
  27.4 0.0 collective-permute-done.8.refs_2_
  27.4 0.9 %last_low.1 = f32[5,8,48,128]{3,2,1,0:T(8,128)} custom-call(f32[5,8,64,128]{3,2,1,0:T(8,128)S(1)} %get-tuple-element.47.padded.refs_0_, f32[5,8,48,128]{3,2,1,0:T(8,128)S(1)} %second_halo.1.refs_1_, f32[960,128]{1,0:T(8,128)S(1)} %collective-permute-done.8.refs_2_, f32[960,128]{1,0:T(8,128)S(1)} %get-tuple-element.54.refs_3_, ...), custom_call_target="tpu_custom_call", output_to_operand_aliasing={{}: (5, {})} | custom-call | bytes 3690000 | tf_op jit(solution)/shard_map/last_low/pallas_call | solution.py:528
Async XLA Ops:
  1.5 14.8 %collective-permute-start.4 = (f32[968,128]{1,0:T(8,128)S(1)}, f32[968,128]{1,0:T(8,128)S(1)}, u32[]{:S(2)}, u32[]{:S(2)}) collective-permute-start(f32[968,128]{1,0:T(8,128)S(1)} %get-tuple-element.31.high), channel_id=1, source_target_pairs={{0,1},{2,3},{1,0},{3,2},{4,5},{6,7},{5,4},{7,6},{8,9},{10,11},{9,8... | collective-permute-start | bytes 1486856 | tf_op jit(solution)/shard_map/ppermute | solution.py:573
  5.0 11.6 %collective-permute-start.3 = (f32[968,128]{1,0:T(8,128)S(1)}, f32[968,128]{1,0:T(8,128)S(1)}, u32[]{:S(2)}, u32[]{:S(2)}) collective-permute-start(f32[968,128]{1,0:T(8,128)S(1)} %get-tuple-element.33.low), channel_id=1, source_target_pairs={{1,2},{5,6},{9,10},{13,14},{17,18},{21,22},{25,26},{29,30},{0,4},{... | collective-permute-start | bytes 1486856 | tf_op jit(solution)/shard_map/ppermute | solution.py:582
  5.0 6.0 %collective-permute-start = (f32[160,128]{1,0:T(8,128)S(1)}, f32[160,128]{1,0:T(8,128)S(1)}, u32[]{:S(2)}, u32[]{:S(2)}) collective-permute-start(f32[160,128]{1,0:T(8,128)S(1)} %get-tuple-element.40), channel_id=1, source_target_pairs={{0,16},{4,20},{8,24},{12,28},{16,0},{20,4},{24,8},{28,12},{1,17},{... | collective-permute-start | bytes 245768 | tf_op jit(solution)/shard_map/ppermute | solution.py:554
  6.6 3.6 %collective-permute-start.1 = (f32[64,128]{1,0:T(8,128)S(1)}, f32[64,128]{1,0:T(8,128)S(1)}, u32[]{:S(2)}, u32[]{:S(2)}) collective-permute-start(f32[64,128]{1,0:T(8,128)S(1)} %get-tuple-element.41), channel_id=1, source_target_pairs={{0,4},{8,12},{16,20},{24,28},{4,0},{12,8},{20,16},{28,24},{1,5},{9... | collective-permute-start | bytes 98312 | tf_op jit(solution)/shard_map/ppermute | solution.py:552
  6.7 4.2 %collective-permute-start.2 = (f32[64,128]{1,0:T(8,128)S(1)}, f32[64,128]{1,0:T(8,128)S(1)}, u32[]{:S(2)}, u32[]{:S(2)}) collective-permute-start(f32[64,128]{1,0:T(8,128)S(1)} %get-tuple-element.42), channel_id=1, source_target_pairs={{4,8},{12,16},{20,24},{28,0},{8,4},{16,12},{24,20},{0,28},{5,9},{1... | collective-permute-start | bytes 98312 | tf_op jit(solution)/shard_map/ppermute | solution.py:553
  11.7 14.7 %collective-permute-start.9 = (f32[960,128]{1,0:T(8,128)S(1)}, f32[960,128]{1,0:T(8,128)S(1)}, u32[]{:S(2)}, u32[]{:S(2)}) collective-permute-start(f32[960,128]{1,0:T(8,128)S(1)} %get-tuple-element.55), channel_id=1, source_target_pairs={{0,1},{2,3},{1,0},{3,2},{4,5},{6,7},{5,4},{7,6},{8,9},{10,11},{9,8... | collective-permute-start | bytes 1474568 | tf_op jit(solution)/shard_map/ppermute | solution.py:608
  15.4 12.0 %collective-permute-start.8 = (f32[960,128]{1,0:T(8,128)S(1)}, f32[960,128]{1,0:T(8,128)S(1)}, u32[]{:S(2)}, u32[]{:S(2)}) collective-permute-start(f32[960,128]{1,0:T(8,128)S(1)} %get-tuple-element.53), channel_id=1, source_target_pairs={{1,2},{5,6},{9,10},{13,14},{17,18},{21,22},{25,26},{29,30},{0,4},{... | collective-permute-start | bytes 1474568 | tf_op jit(solution)/shard_map/ppermute | solution.py:610
  17.2 6.7 %collective-permute-start.5 = (f32[160,128]{1,0:T(8,128)S(1)}, f32[160,128]{1,0:T(8,128)S(1)}, u32[]{:S(2)}, u32[]{:S(2)}) collective-permute-start(f32[160,128]{1,0:T(8,128)S(1)} %get-tuple-element.50), channel_id=1, source_target_pairs={{0,16},{4,20},{8,24},{12,28},{16,0},{20,4},{24,8},{28,12},{1,17},{... | collective-permute-start | bytes 245768 | tf_op jit(solution)/shard_map/ppermute | solution.py:554
  19.7 3.4 %collective-permute-start.6 = (f32[64,128]{1,0:T(8,128)S(1)}, f32[64,128]{1,0:T(8,128)S(1)}, u32[]{:S(2)}, u32[]{:S(2)}) collective-permute-start(f32[64,128]{1,0:T(8,128)S(1)} %get-tuple-element.51), channel_id=1, source_target_pairs={{0,4},{8,12},{16,20},{24,28},{4,0},{12,8},{20,16},{28,24},{1,5},{9... | collective-permute-start | bytes 98312 | tf_op jit(solution)/shard_map/ppermute | solution.py:552
  19.7 4.2 %collective-permute-start.7 = (f32[64,128]{1,0:T(8,128)S(1)}, f32[64,128]{1,0:T(8,128)S(1)}, u32[]{:S(2)}, u32[]{:S(2)}) collective-permute-start(f32[64,128]{1,0:T(8,128)S(1)} %get-tuple-element.52), channel_id=1, source_target_pairs={{4,8},{12,16},{20,24},{28,0},{8,4},{16,12},{24,20},{0,28},{5,9},{1... | collective-permute-start | bytes 98312 | tf_op jit(solution)/shard_map/ppermute | solution.py:553

commit v8 on v7

--- a/solution.py
+++ b/solution.py
@@ -42,7 +42,7 @@
                 if 0 <= out + sign * k < width:
                     matrix[out + sign * k, out] = sign * first_whole[k - 1]
                     matrix[out + sign * k, width + out] = second_whole[k - 1]
-    return jnp.asarray(matrix, jnp.bfloat16)
+    return jnp.asarray(matrix)
 
 
 def geometry(rows, nlon, width):
@@ -91,33 +91,40 @@
     return out
 
 
-def levels_kernel(
-    levels, rows, state, outer_rows, kappa, matrix_in, geo_in,
-    high, low, beyond, kap, matrix, geo, kappa_scalars, sems,
+def high_kernel(
+    levels, rows, state, kappa, high, kap, raw_kap, kappa_scalars, sems
 ):
     block = REACH * rows
     odd, _ = mirrored()
-    starts = (jnp.where(odd == 1, 0, REACH), jnp.where(odd == 1, REACH, 0))
+    start = jnp.where(odd == 1, 0, REACH)
     reads = [
-        (state.at[pl.ds(pl.multiple_of((f * levels + start) * rows, TILE), block)], side.at[pl.ds(f * block, block)])
-        for start, side in zip(starts, (high, low))
+        (state.at[pl.ds(pl.multiple_of((f * levels + start) * rows, TILE), block)], high.at[pl.ds(f * block, block)])
         for f in range(FIELDS)
     ]
-    reads += [(kappa, kappa_scalars), (outer_rows, beyond), (matrix_in, matrix), (geo_in, geo)]
+    reads.append((kappa, kappa_scalars))
     copies = [pltpu.make_async_copy(*read, sems.at[i]) for i, read in enumerate(reads)]
     for copy in copies:
         copy.start()
-    copies[2 * FIELDS].wait()
-    for start, side in zip(starts, (high, low)):
-        for i in range(REACH):
-            value = jnp.full((1, LANES), kappa_scalars[start + i], jnp.float32)
-            side[pl.ds(FIELDS * block + i, 1), :] = value
+    copies[FIELDS].wait()
+    for i in range(REACH):
+        row = pl.ds(FIELDS * block + i, 1)
+        high[row, :] = jnp.full((1, LANES), kappa_scalars[start + i], jnp.float32)
+        raw_kap[pl.ds(i, 1), :] = jnp.full((1, LANES), kappa_scalars[REACH - start + i], jnp.float32)
     for l in range(levels):
         value = kappa_scalars[jnp.where(odd == 1, levels - 1 - l, l)]
         kap[l] = jnp.full((TILE, LANES), value, jnp.float32)
-    for i, copy in enumerate(copies):
-        if i != 2 * FIELDS:
-            copy.wait()
+    for copy in copies[:FIELDS]:
+        copy.wait()
+
+
+def low_kernel(levels, rows, state, raw_kap, low):
+    block = REACH * rows
+    odd, _ = mirrored()
+    start = jnp.where(odd == 1, REACH, 0)
+    for f in range(FIELDS):
+        at = pl.multiple_of((f * levels + start) * rows, TILE)
+        low[pl.ds(f * block, block), :] = state[pl.ds(at, block), :]
+    low[pl.ds(FIELDS * block, REACH), :] = raw_kap[pl.ds(0, REACH), :]
 
 
 def own_level(high, low, rows, f, l, odd):
@@ -126,7 +133,7 @@
     return (low if l < REACH else high), pl.multiple_of(at, TILE)
 
 
-def edges_kernel(levels, rows, given, high, low, inner, outer, polar):
+def edges_kernel(levels, rows, high, low, inner, outer, polar):
     odd, mirror = mirrored()
     packs = []
     for f in range(FIELDS):
@@ -212,7 +219,8 @@
 def longitude_slopes(levels, rows, padded, matrix, dlon, elon):
     for f in range(FIELDS):
         x = padded[f, :, pl.ds(TILE, rows), :].reshape(levels * rows, LANES)
-        total = times_whole(pieces_of(x), matrix[:, pl.ds(0, 2 * LANES if f == 4 else LANES)])
+        whole = matrix[:, pl.ds(0, 2 * LANES if f == 4 else LANES)].astype(jnp.bfloat16)
+        total = times_whole(pieces_of(x), whole)
         dlon[f] = total[:, :LANES].reshape(levels, rows, LANES)
         if f == 4:
             elon[...] = total[:, LANES:].reshape(levels, rows, LANES)
@@ -484,30 +492,71 @@
     add_halo(levels, rows, range(levels), padded, polar, inner, outer, geo, kap, store)
 
 
-def last_kernel(at, up, levels, rows, *refs):
-    padded, both, sent, more, kap = refs[:5]
-    out, staged, sems = refs[-3:]
+def write_side(at, more, levels, rows, padded, both, kap, out, staged, sems):
     odd, mirror = mirrored()
-    scale = (0.5 * time_step) * bordered(at)
-    real = jnp.where(odd == 1, levels - at - REACH, at)
-    copies = []
     for t in range(rows // TILE):
-        here = pl.ds(t * TILE, TILE)
-        halo = halo_tile(sent, rows, t * TILE)
-        there = own_tile(more, rows, t * TILE)
-        halo = [[halo[f][b] + there[f][b] for b in range(REACH)] for f in range(FIELDS)]
-        wind = [padded[3, at + a, pl.ds((t + 1) * TILE, TILE), :] for a in range(REACH)]
-        temper = [padded[4, at + a, pl.ds((t + 1) * TILE, TILE), :] for a in range(REACH)]
-        extra = across_level(wind, temper, halo, [kap[at + a] for a in range(REACH)], up)
+        here, inside = pl.ds(t * TILE, TILE), pl.ds((t + 1) * TILE, TILE)
+        extra = None
+        if more is not None:
+            wind = [padded[3, at + a, inside, :] for a in range(REACH)]
+            temper = [padded[4, at + a, inside, :] for a in range(REACH)]
+            extra = more(t * TILE, wind, temper, [kap[at + a] for a in range(REACH)])
         for f in range(FIELDS):
             for a in range(REACH):
-                new = both[f, at + a, here, :] + scale * extra[f][a]
+                new = both[f, at + a, here, :]
+                if extra is not None:
+                    new = new + (0.5 * time_step) * extra[f][a]
                 staged[f, jnp.where(odd == 1, REACH - 1 - a, a), here, :] = mirror * new if f == 3 else new
-        target = out.at[:, pl.ds(real, REACH), here]
-        copies.append(pltpu.make_async_copy(staged.at[:, :, here], target, sems.at[t]))
-        copies[-1].start()
-    for copy in copies:
-        copy.wait()
+        side_copy(at, t, levels, odd, out, staged, sems).start()
+
+
+def side_copy(at, t, levels, odd, out, staged, sems):
+    real, here = jnp.where(odd == 1, levels - at - REACH, at), pl.ds(t * TILE, TILE)
+    return pltpu.make_async_copy(staged.at[:, :, here], out.at[:, pl.ds(real, REACH), here], sems.at[t])
+
+
+def wait_side(at, levels, rows, out, staged, sems):
+    odd, _ = mirrored()
+    for t in range(rows // TILE):
+        side_copy(at, t, levels, odd, out, staged, sems).wait()
+
+
+def second_share(sent, more, up, rows):
+    def share(r0, wind, temper, kappa):
+        halo, there = halo_tile(sent, rows, r0), own_tile(more, rows, r0)
+        halo = [[halo[f][b] + there[f][b] for b in range(REACH)] for f in range(FIELDS)]
+        return across_level(wind, temper, halo, kappa, up)
+
+    return share
+
+
+def at_end():
+    here, depth = lax.axis_index("rad"), lax.axis_size("rad")
+    return (here == 0) | (here == depth - 1)
+
+
+def last_high_kernel(
+    levels, rows, padded, both, sent, more, kap, out, staged, sems, low_staged, low_sems
+):
+    @pl.when(at_end())
+    def _():
+        write_side(0, None, levels, rows, padded, both, kap, out, low_staged, low_sems)
+
+    share = second_share(sent, more, True, rows)
+    write_side(levels - REACH, share, levels, rows, padded, both, kap, out, staged, sems)
+    wait_side(levels - REACH, levels, rows, out, staged, sems)
+
+    @pl.when(at_end())
+    def _():
+        wait_side(0, levels, rows, out, low_staged, low_sems)
+
+
+def last_low_kernel(levels, rows, padded, both, sent, more, kap, given, out, staged, sems):
+    @pl.when(jnp.logical_not(at_end()))
+    def _():
+        share = second_share(sent, more, False, rows)
+        write_side(0, share, levels, rows, padded, both, kap, out, staged, sems)
+        wait_side(0, levels, rows, out, staged, sems)
 
 
 def on_device(state, outer_rows, kappa):
@@ -555,31 +604,19 @@
 
     edge_shapes = [in_vmem(packs, width), in_vmem(packs, width), in_vmem(FIELDS * levels * REACH, width)]
     payload = in_vmem(halo_rows + TILE, width)
-    high, low, after, kap, matrix, geo = call(
-        levels_kernel,
-        [
-            payload,
-            payload,
-            in_vmem(*outer_rows.shape),
-            in_vmem(levels, TILE, width),
-            pltpu.VMEM(matrix.shape, matrix.dtype),
-            in_vmem(*geo.shape),
-        ],
-        (HBM,) * 5,
-        (state.reshape(-1, width), outer_rows, kappa, matrix, geo),
-        scratch=(pltpu.SMEM(kappa.shape, jnp.float32), pltpu.SemaphoreType.DMA((2 * FIELDS + 4,))),
-        name="levels",
+    flat = state.reshape(-1, width)
+    high, kap, raw_kap = call(
+        high_kernel,
+        [payload, in_vmem(levels, TILE, width), in_vmem(TILE, width)],
+        (HBM,) * 2,
+        (flat, kappa),
+        scratch=(pltpu.SMEM(kappa.shape, jnp.float32), pltpu.SemaphoreType.DMA((FIELDS + 1,))),
+        name="high",
     )
     above = lax.ppermute(high, "rad", swap_high)
-    low, *edges = call(
-        edges_kernel,
-        [payload, *edge_shapes],
-        (VMEM,) * 2,
-        (low, high),
-        aliases={0: 0},
-        name="edges",
-    )
+    low = call(low_kernel, payload, (VMEM,) * 2, (flat, raw_kap), cost=0.2, name="low")
     below = lax.ppermute(low, ("lon", "rad"), swap_low)
+    edges = call(edges_kernel, edge_shapes, (VMEM,) * 2, (high, low), cost=0.4, name="edges")
     inner, outer, beyond = around(*edges)
     lon_scratch = (in_vmem(*full_shape), in_vmem(*full_shape[1:]))
     side = in_vmem(halo_rows, width)
@@ -587,7 +624,7 @@
         first_kernel,
         [in_vmem(*pad_shape), in_vmem(*full_shape)],
         (VMEM,) * 6,
-        (high, low, after, matrix, geo, kap),
+        (high, low, outer_rows, matrix, geo, kap),
         scratch=lon_scratch,
         cost=2.0,
         name="first",
@@ -649,16 +686,16 @@
     )
     result = pltpu.HBM(full_shape, jnp.float32)
     out = call(
-        functools.partial(last_kernel, levels - REACH, True),
+        last_high_kernel,
         result,
         (VMEM,) * 5,
         (ahead, both, above2, high, kap),
-        scratch=last_scratch,
+        scratch=last_scratch * 2,
         cost=0.5,
         name="last_high",
     )
     return call(
-        functools.partial(last_kernel, 0, False),
+        last_low_kernel,
         result,
         (VMEM,) * 5 + (HBM,),
         (ahead, both, below2, low, kap, out),

time: 28.4 us -> 27.5 us (0.968)
  Pallas kernels: 11.4 us -> 10.5 us
    pallas_call x11 -> x12, Pallas kernels: 11.4 us -> 10.5 us  [call(): pl.pallas_call(functools.partial(kernel, levels, rows), out_shape=out_sha...]
  transfers between devices with their start and end apart: 10 -> 10, of which waited for: 4 -> 4; matrix products, arithmetic and copies ran while one was open for 0% -> 0% of each run, Pallas kernels for 32% -> 34%
where the time goes in v8:
time: 27.5 us; the launch traced here: 27.4 us
  starting transfers between devices  12.8 us (47%)
  Pallas kernels  10.5 us (38%)
  waiting for transfers between devices  3.92 us (14%)
    pallas_call x12, Pallas kernels, call(): pl.pallas_call(functools.partial(kernel, levels, rows), out_shape=out_sha...  10.5 us
    ppermute x2, starting transfers between devices, around(): return (inner, outer, lax.ppermute(polar, 'lon', half))  4.11 us
    ppermute x1, starting transfers between devices, on_device(): above = lax.ppermute(high, 'rad', swap_high)  3.09 us
    ppermute x1, starting transfers between devices, on_device(): above2 = lax.ppermute(high, 'rad', swap_high)  3.07 us
    ppermute x2, starting transfers between devices, around(): outer = lax.ppermute(outer, 'lon', swap_outer)  2.18 us
    ppermute x2, waiting for transfers between devices, around(): outer = lax.ppermute(outer, 'lon', swap_outer)  1.76 us
    ppermute x1, waiting for transfers between devices, on_device(): above2 = lax.ppermute(high, 'rad', swap_high)  1.57 us
    ppermute x1, waiting for transfers between devices, on_device(): above = lax.ppermute(high, 'rad', swap_high)  0.57 us
  transfers between devices with their start and end apart: 10, of which 4 were waited for; matrix products, arithmetic and copies ran while one was open for 0% of the time, Pallas kernels for 34%

profile of v8, /device:TPU:0, one launch (start us, length us, event | category | flops | bytes accessed | tf_op | source)
XLA Modules:
  0.0 27.4 jit_solution(5720052953961646504)
XLA Ops:
  0.0 0.0 copy-start
  0.0 1.2 %high.1 = (f32[968,128]{1,0:T(8,128)S(1)}, f32[8,8,128]{2,1,0:T(8,128)S(1)}, f32[8,128]{1,0:T(8,128)S(1)}) custom-call(f32[1920,128]{1,0:T(8,128)} %bitcast.1, f32[8]{0:T(128)} %kappa.1), custom_call_target="tpu_custom_call" | custom-call | bytes 3690000 | tf_op jit(solution)/shard_map/high/pallas_call | solution.py:577
  1.2 0.0 copy-start.1
  1.2 0.0 copy-start.2
  1.3 0.0 copy-start.3
  1.3 3.1 %collective-permute-start.4 = (f32[968,128]{1,0:T(8,128)S(1)}, f32[968,128]{1,0:T(8,128)S(1)}, u32[]{:S(2)}, u32[]{:S(2)}) collective-permute-start(f32[968,128]{1,0:T(8,128)S(1)} %get-tuple-element.27.high), channel_id=1, source_target_pairs={{0,1},{2,3},{1,0},{3,2},{4,5},{6,7},{5,4},{7,6},{8,9},{10,11},{9,8... | collective-permute-start | bytes 1486856 | tf_op jit(solution)/shard_map/ppermute | solution.py:616
  4.4 0.0 copy-done
  4.4 0.1 collective-permute-start.3
  4.5 0.4 %edges.1 = (f32[64,128]{1,0:T(8,128)S(1)}, f32[64,128]{1,0:T(8,128)S(1)}, f32[160,128]{1,0:T(8,128)S(1)}) custom-call(f32[968,128]{1,0:T(8,128)S(1)} %get-tuple-element.27.high, f32[968,128]{1,0:T(8,128)S(1)} %low.1), custom_call_target="tpu_custom_call" | custom-call | bytes 1476000 | tf_op jit(solution)/shard_map/edges/pallas_call | solution.py:577
  4.9 1.6 %collective-permute-start = (f32[160,128]{1,0:T(8,128)S(1)}, f32[160,128]{1,0:T(8,128)S(1)}, u32[]{:S(2)}, u32[]{:S(2)}) collective-permute-start(f32[160,128]{1,0:T(8,128)S(1)} %get-tuple-element.32), channel_id=1, source_target_pairs={{0,16},{4,20},{8,24},{12,28},{16,0},{20,4},{24,8},{28,12},{1,17},{... | collective-permute-start | bytes 245768 | tf_op jit(solution)/shard_map/ppermute | solution.py:603
  6.4 0.2 collective-permute-start.1
  6.6 1.3 %collective-permute-start.2 = (f32[64,128]{1,0:T(8,128)S(1)}, f32[64,128]{1,0:T(8,128)S(1)}, u32[]{:S(2)}, u32[]{:S(2)}) collective-permute-start(f32[64,128]{1,0:T(8,128)S(1)} %get-tuple-element.34), channel_id=1, source_target_pairs={{4,8},{12,16},{20,24},{28,0},{8,4},{16,12},{24,20},{0,28},{5,9},{1... | collective-permute-start | bytes 98312 | tf_op jit(solution)/shard_map/ppermute | solution.py:602
  8.0 0.0 copy-done.1
  8.0 0.0 copy-done.2
  8.0 0.0 copy-done.3
  8.0 2.0 %first.1 = (f32[5,8,64,128]{3,2,1,0:T(8,128)S(1)}, f32[5,8,48,128]{3,2,1,0:T(8,128)S(1)}) custom-call(f32[968,128]{1,0:T(8,128)S(1)} %get-tuple-element.27.high, f32[968,128]{1,0:T(8,128)S(1)} %low.1, f32[5,8,4,128]{3,2,1,0:T(4,128)S(1)} %copy-done.3, f32[128,256]{1,0:T(8,128)S(1)} %copy-done.2, f32[3,48,128]{2,1,0:T(8,128)S(1)} %copy-done.1, ...), custom_call_target="tpu_custom_call" | custom-call | bytes 7380000 | tf_op jit(solution)/shard_map/first/pallas_call | solution.py:577
  10.0 0.0 collective-permute-done.1.inner
  10.0 0.8 %collective-permute-done.2.outer = f32[64,128]{1,0:T(8,128)S(1)} collective-permute-done((f32[64,128]{1,0:T(8,128)S(1)}, f32[64,128]{1,0:T(8,128)S(1)}, u32[]{:S(2)}, u32[]{:S(2)}) %collective-permute-start.2) | collective-permute-done | bytes 32800 | tf_op jit(solution)/shard_map/ppermute | solution.py:602
  10.9 0.0 collective-permute-done.polar
  10.9 0.7 %first_halo.2 = (f32[5,8,48,128]{3,2,1,0:T(8,128)S(1)}, f32[960,128]{1,0:T(8,128)S(1)}) custom-call(f32[5,8,48,128]{3,2,1,0:T(8,128)S(1)} %get-tuple-element.31.given, f32[5,8,64,128]{3,2,1,0:T(8,128)S(1)} %get-tuple-element.30.padded.start, f32[160,128]{1,0:T(8,128)S(1)} %collective-permute-done.polar, ...), custom_call_target="tpu_custom_call", output_to_operand_aliasing={{0}: (0, {})} | custom-call | bytes 2214000 | tf_op jit(solution)/shard_map/first_halo/pallas_call | solution.py:577
  11.6 3.1 %collective-permute-start.9 = (f32[960,128]{1,0:T(8,128)S(1)}, f32[960,128]{1,0:T(8,128)S(1)}, u32[]{:S(2)}, u32[]{:S(2)}) collective-permute-start(f32[960,128]{1,0:T(8,128)S(1)} %get-tuple-element.47), channel_id=1, source_target_pairs={{0,1},{2,3},{1,0},{3,2},{4,5},{6,7},{5,4},{7,6},{8,9},{10,11},{9,8... | collective-permute-start | bytes 1474568 | tf_op jit(solution)/shard_map/ppermute | solution.py:645
  14.6 0.7 %first_halo.3 = (f32[5,8,48,128]{3,2,1,0:T(8,128)S(1)}, f32[960,128]{1,0:T(8,128)S(1)}) custom-call(f32[5,8,48,128]{3,2,1,0:T(8,128)S(1)} %get-tuple-element.35.given, f32[5,8,64,128]{3,2,1,0:T(8,128)S(1)} %get-tuple-element.30.padded.start, f32[160,128]{1,0:T(8,128)S(1)} %collective-permute-done.polar, ...), custom_call_target="tpu_custom_call", output_to_operand_aliasing={{0}: (0, {})} | custom-call | bytes 2214000 | tf_op jit(solution)/shard_map/first_halo/pallas_call | solution.py:577
  15.3 0.1 collective-permute-start.8
  15.4 0.6 %collective-permute-done.4.above = f32[968,128]{1,0:T(8,128)S(1)} collective-permute-done((f32[968,128]{1,0:T(8,128)S(1)}, f32[968,128]{1,0:T(8,128)S(1)}, u32[]{:S(2)}, u32[]{:S(2)}) %collective-permute-start.4) | collective-permute-done | bytes 495648 | tf_op jit(solution)/shard_map/ppermute | solution.py:616
  16.0 0.3 section_high.1
  16.2 0.0 collective-permute-done.3.below
  16.2 0.7 %section_low.1 = (f32[5,8,48,128]{3,2,1,0:T(8,128)S(1)}, f32[5,8,64,128]{3,2,1,0:T(8,128)S(1)}, f32[64,128]{1,0:T(8,128)S(1)}, f32[64,128]{1,0:T(8,128)S(1)}, f32[160,128]{1,0:T(8,128)S(1)}) custom-call(f32[5,8,64,128]{3,2,1,0:T(8,128)S(1)} %get-tuple-element.30.padded.start, ...), custom_call_target="tpu_custom_call", output_to_operand_aliasing={{0}: (4, {}), {1}: (5, {})} | custom-call | bytes 1845000 | tf_op jit(solution)/shard_map/section_low/pallas_call | solution.py:577
  16.9 2.6 %collective-permute-start.5 = (f32[160,128]{1,0:T(8,128)S(1)}, f32[160,128]{1,0:T(8,128)S(1)}, u32[]{:S(2)}, u32[]{:S(2)}) collective-permute-start(f32[160,128]{1,0:T(8,128)S(1)} %get-tuple-element.42), channel_id=1, source_target_pairs={{0,16},{4,20},{8,24},{12,28},{16,0},{20,4},{24,8},{28,12},{1,17},{... | collective-permute-start | bytes 245768 | tf_op jit(solution)/shard_map/ppermute | solution.py:603
  19.5 0.0 collective-permute-start.6
  19.5 0.8 %collective-permute-start.7 = (f32[64,128]{1,0:T(8,128)S(1)}, f32[64,128]{1,0:T(8,128)S(1)}, u32[]{:S(2)}, u32[]{:S(2)}) collective-permute-start(f32[64,128]{1,0:T(8,128)S(1)} %get-tuple-element.44), channel_id=1, source_target_pairs={{4,8},{12,16},{20,24},{28,0},{8,4},{16,12},{24,20},{0,28},{5,9},{1... | collective-permute-start | bytes 98312 | tf_op jit(solution)/shard_map/ppermute | solution.py:602
  20.3 2.5 %second.1 = (f32[5,8,48,128]{3,2,1,0:T(8,128)S(1)}, f32[960,128]{1,0:T(8,128)S(1)}, f32[960,128]{1,0:T(8,128)S(1)}) custom-call(f32[5,8,64,128]{3,2,1,0:T(8,128)S(1)} %get-tuple-element.39.padded, f32[128,256]{1,0:T(8,128)S(1)} %copy-done.2, f32[3,48,128]{2,1,0:T(8,128)S(1)} %copy-done.1, f32[8,8,128]{2,1,0:T(8,128)S(1)} %get-tuple-element.29.kap.kappa, ...), custom_call_target="tpu_custom_call" | custom-call | bytes 9225000 | tf_op jit(solution)/shard_map/second/pallas_call | solution.py:577
  22.8 0.0 collective-permute-done.6.inner
  22.8 0.9 %collective-permute-done.7.outer = f32[64,128]{1,0:T(8,128)S(1)} collective-permute-done((f32[64,128]{1,0:T(8,128)S(1)}, f32[64,128]{1,0:T(8,128)S(1)}, u32[]{:S(2)}, u32[]{:S(2)}) %collective-permute-start.7) | collective-permute-done | bytes 32800 | tf_op jit(solution)/shard_map/ppermute | solution.py:602
  23.7 0.0 collective-permute-done.5.polar
  23.7 0.9 %second_halo.1.both = f32[5,8,48,128]{3,2,1,0:T(8,128)S(1)} custom-call(f32[5,8,48,128]{3,2,1,0:T(8,128)S(1)} %get-tuple-element.41.given, f32[5,8,64,128]{3,2,1,0:T(8,128)S(1)} %get-tuple-element.39.padded, f32[160,128]{1,0:T(8,128)S(1)} %collective-permute-done.5.polar, ...), custom_call_target="tpu_custom_call", output_to_operand_aliasing={{}: (0, {})} | custom-call | bytes 3690000 | tf_op jit(solution)/shard_map/second_halo/pallas_call | solution.py:577
  24.6 1.6 %collective-permute-done.9.sent = f32[960,128]{1,0:T(8,128)S(1)} collective-permute-done((f32[960,128]{1,0:T(8,128)S(1)}, f32[960,128]{1,0:T(8,128)S(1)}, u32[]{:S(2)}, u32[]{:S(2)}) %collective-permute-start.9) | collective-permute-done | bytes 491552 | tf_op jit(solution)/shard_map/ppermute | solution.py:645
  26.2 1.1 %last_high.1.given = f32[5,8,48,128]{3,2,1,0:T(8,128)} custom-call(f32[5,8,64,128]{3,2,1,0:T(8,128)S(1)} %get-tuple-element.39.padded, f32[5,8,48,128]{3,2,1,0:T(8,128)S(1)} %second_halo.1.both, f32[960,128]{1,0:T(8,128)S(1)} %collective-permute-done.9.sent, f32[960,128]{1,0:T(8,128)S(1)} %get-tuple-element.48.more, f32[8,8,128]{2,1,0:T(8,128)S(1)} %get-tuple-element.29.kap.kappa), custom_call_target="tpu_custom_call" | custom-call | bytes 1845000 | tf_op jit(solution)/shard_map/last_high/pallas_call | solution.py:577
  27.3 0.0 collective-permute-done.8.sent
  27.3 0.1 last_low.1
  (1 shorter events, 0.0 us)
Async XLA Ops:
  0.0 4.4 %copy-start = (f32[5,8,48,128]{3,2,1,0:T(8,128)S(1)}, f32[5,8,48,128]{3,2,1,0:T(8,128)}, u32[]{:S(2)}) copy-start(f32[5,8,48,128]{3,2,1,0:T(8,128)} %param.5) | copy-start | bytes 2949124
  1.2 6.8 %copy-start.1 = (f32[3,48,128]{2,1,0:T(8,128)S(1)}, f32[3,48,128]{2,1,0:T(8,128)}, u32[]{:S(2)}) copy-start(f32[3,48,128]{2,1,0:T(8,128)} %constant.5.clone.geo) | copy-start | bytes 221188
  1.2 6.8 %copy-start.2 = (f32[128,256]{1,0:T(8,128)S(1)}, f32[128,256]{1,0:T(8,128)}, u32[]{:S(2)}) copy-start(f32[128,256]{1,0:T(8,128)} %constant.4.clone.matrix) | copy-start | bytes 393220
  1.3 6.7 %copy-start.3 = (f32[5,8,4,128]{3,2,1,0:T(4,128)S(1)}, f32[5,8,4,128]{3,2,1,0:T(4,128)}, u32[]{:S(2)}) copy-start(f32[5,8,4,128]{3,2,1,0:T(4,128)} %beyond.1) | copy-start | bytes 245764
  1.3 14.7 %collective-permute-start.4 = (f32[968,128]{1,0:T(8,128)S(1)}, f32[968,128]{1,0:T(8,128)S(1)}, u32[]{:S(2)}, u32[]{:S(2)}) collective-permute-start(f32[968,128]{1,0:T(8,128)S(1)} %get-tuple-element.27.high), channel_id=1, source_target_pairs={{0,1},{2,3},{1,0},{3,2},{4,5},{6,7},{5,4},{7,6},{8,9},{10,11},{9,8... | collective-permute-start | bytes 1486856 | tf_op jit(solution)/shard_map/ppermute | solution.py:616
  4.4 11.8 %collective-permute-start.3 = (f32[968,128]{1,0:T(8,128)S(1)}, f32[968,128]{1,0:T(8,128)S(1)}, u32[]{:S(2)}, u32[]{:S(2)}) collective-permute-start(f32[968,128]{1,0:T(8,128)S(1)} %low.1), channel_id=1, source_target_pairs={{1,2},{5,6},{9,10},{13,14},{17,18},{21,22},{25,26},{29,30},{0,4},{... | collective-permute-start | bytes 1486856 | tf_op jit(solution)/shard_map/ppermute | solution.py:618
  4.9 6.0 %collective-permute-start = (f32[160,128]{1,0:T(8,128)S(1)}, f32[160,128]{1,0:T(8,128)S(1)}, u32[]{:S(2)}, u32[]{:S(2)}) collective-permute-start(f32[160,128]{1,0:T(8,128)S(1)} %get-tuple-element.32), channel_id=1, source_target_pairs={{0,16},{4,20},{8,24},{12,28},{16,0},{20,4},{24,8},{28,12},{1,17},{... | collective-permute-start | bytes 245768 | tf_op jit(solution)/shard_map/ppermute | solution.py:603
  6.4 3.6 %collective-permute-start.1 = (f32[64,128]{1,0:T(8,128)S(1)}, f32[64,128]{1,0:T(8,128)S(1)}, u32[]{:S(2)}, u32[]{:S(2)}) collective-permute-start(f32[64,128]{1,0:T(8,128)S(1)} %get-tuple-element.33), channel_id=1, source_target_pairs={{0,4},{8,12},{16,20},{24,28},{4,0},{12,8},{20,16},{28,24},{1,5},{9... | collective-permute-start | bytes 98312 | tf_op jit(solution)/shard_map/ppermute | solution.py:601
  6.6 4.2 %collective-permute-start.2 = (f32[64,128]{1,0:T(8,128)S(1)}, f32[64,128]{1,0:T(8,128)S(1)}, u32[]{:S(2)}, u32[]{:S(2)}) collective-permute-start(f32[64,128]{1,0:T(8,128)S(1)} %get-tuple-element.34), channel_id=1, source_target_pairs={{4,8},{12,16},{20,24},{28,0},{8,4},{16,12},{24,20},{0,28},{5,9},{1... | collective-permute-start | bytes 98312 | tf_op jit(solution)/shard_map/ppermute | solution.py:602
  11.6 14.6 %collective-permute-start.9 = (f32[960,128]{1,0:T(8,128)S(1)}, f32[960,128]{1,0:T(8,128)S(1)}, u32[]{:S(2)}, u32[]{:S(2)}) collective-permute-start(f32[960,128]{1,0:T(8,128)S(1)} %get-tuple-element.47), channel_id=1, source_target_pairs={{0,1},{2,3},{1,0},{3,2},{4,5},{6,7},{5,4},{7,6},{8,9},{10,11},{9,8... | collective-permute-start | bytes 1474568 | tf_op jit(solution)/shard_map/ppermute | solution.py:645
  15.3 12.0 %collective-permute-start.8 = (f32[960,128]{1,0:T(8,128)S(1)}, f32[960,128]{1,0:T(8,128)S(1)}, u32[]{:S(2)}, u32[]{:S(2)}) collective-permute-start(f32[960,128]{1,0:T(8,128)S(1)} %get-tuple-element.45), channel_id=1, source_target_pairs={{1,2},{5,6},{9,10},{13,14},{17,18},{21,22},{25,26},{29,30},{0,4},{... | collective-permute-start | bytes 1474568 | tf_op jit(solution)/shard_map/ppermute | solution.py:647
  16.9 6.8 %collective-permute-start.5 = (f32[160,128]{1,0:T(8,128)S(1)}, f32[160,128]{1,0:T(8,128)S(1)}, u32[]{:S(2)}, u32[]{:S(2)}) collective-permute-start(f32[160,128]{1,0:T(8,128)S(1)} %get-tuple-element.42), channel_id=1, source_target_pairs={{0,16},{4,20},{8,24},{12,28},{16,0},{20,4},{24,8},{28,12},{1,17},{... | collective-permute-start | bytes 245768 | tf_op jit(solution)/shard_map/ppermute | solution.py:603
  19.5 3.3 %collective-permute-start.6 = (f32[64,128]{1,0:T(8,128)S(1)}, f32[64,128]{1,0:T(8,128)S(1)}, u32[]{:S(2)}, u32[]{:S(2)}) collective-permute-start(f32[64,128]{1,0:T(8,128)S(1)} %get-tuple-element.43), channel_id=1, source_target_pairs={{0,4},{8,12},{16,20},{24,28},{4,0},{12,8},{20,16},{28,24},{1,5},{9... | collective-permute-start | bytes 98312 | tf_op jit(solution)/shard_map/ppermute | solution.py:601
  19.5 4.2 %collective-permute-start.7 = (f32[64,128]{1,0:T(8,128)S(1)}, f32[64,128]{1,0:T(8,128)S(1)}, u32[]{:S(2)}, u32[]{:S(2)}) collective-permute-start(f32[64,128]{1,0:T(8,128)S(1)} %get-tuple-element.44), channel_id=1, source_target_pairs={{4,8},{12,16},{20,24},{28,0},{8,4},{16,12},{24,20},{0,28},{5,9},{1... | collective-permute-start | bytes 98312 | tf_op jit(solution)/shard_map/ppermute | solution.py:602

commit v9 on v8

--- a/solution.py
+++ b/solution.py
@@ -97,15 +97,15 @@
     block = REACH * rows
     odd, _ = mirrored()
     start = jnp.where(odd == 1, 0, REACH)
-    reads = [
-        (state.at[pl.ds(pl.multiple_of((f * levels + start) * rows, TILE), block)], high.at[pl.ds(f * block, block)])
-        for f in range(FIELDS)
-    ]
-    reads.append((kappa, kappa_scalars))
+    half, reads = block // 2, [(kappa, kappa_scalars)]
+    for f in range(FIELDS):
+        for part in range(2):
+            at = pl.multiple_of((f * levels + start) * rows + part * half, TILE)
+            reads.append((state.at[pl.ds(at, half)], high.at[pl.ds(f * block + part * half, half)]))
     copies = [pltpu.make_async_copy(*read, sems.at[i]) for i, read in enumerate(reads)]
     for copy in copies:
         copy.start()
-    copies[FIELDS].wait()
+    copies[0].wait()
     for i in range(REACH):
         row = pl.ds(FIELDS * block + i, 1)
         high[row, :] = jnp.full((1, LANES), kappa_scalars[start + i], jnp.float32)
@@ -113,7 +113,7 @@
     for l in range(levels):
         value = kappa_scalars[jnp.where(odd == 1, levels - 1 - l, l)]
         kap[l] = jnp.full((TILE, LANES), value, jnp.float32)
-    for copy in copies[:FIELDS]:
+    for copy in copies[1:]:
         copy.wait()
 
 
@@ -535,20 +535,17 @@
     return (here == 0) | (here == depth - 1)
 
 
-def last_high_kernel(
-    levels, rows, padded, both, sent, more, kap, out, staged, sems, low_staged, low_sems
-):
+def end_low_kernel(levels, rows, padded, both, kap, out, staged, sems):
     @pl.when(at_end())
     def _():
-        write_side(0, None, levels, rows, padded, both, kap, out, low_staged, low_sems)
-
+        write_side(0, None, levels, rows, padded, both, kap, out, staged, sems)
+        wait_side(0, levels, rows, out, staged, sems)
+
+
+def last_high_kernel(levels, rows, padded, both, sent, more, kap, given, out, staged, sems):
     share = second_share(sent, more, True, rows)
     write_side(levels - REACH, share, levels, rows, padded, both, kap, out, staged, sems)
     wait_side(levels - REACH, levels, rows, out, staged, sems)
-
-    @pl.when(at_end())
-    def _():
-        wait_side(0, levels, rows, out, low_staged, low_sems)
 
 
 def last_low_kernel(levels, rows, padded, both, sent, more, kap, given, out, staged, sems):
@@ -610,7 +607,7 @@
         [payload, in_vmem(levels, TILE, width), in_vmem(TILE, width)],
         (HBM,) * 2,
         (flat, kappa),
-        scratch=(pltpu.SMEM(kappa.shape, jnp.float32), pltpu.SemaphoreType.DMA((FIELDS + 1,))),
+        scratch=(pltpu.SMEM(kappa.shape, jnp.float32), pltpu.SemaphoreType.DMA((2 * FIELDS + 1,))),
         name="high",
     )
     above = lax.ppermute(high, "rad", swap_high)
@@ -686,11 +683,21 @@
     )
     result = pltpu.HBM(full_shape, jnp.float32)
     out = call(
+        end_low_kernel,
+        result,
+        (VMEM,) * 3,
+        (ahead, both, kap),
+        scratch=last_scratch,
+        cost=0.5,
+        name="end_low",
+    )
+    out = call(
         last_high_kernel,
         result,
-        (VMEM,) * 5,
-        (ahead, both, above2, high, kap),
-        scratch=last_scratch * 2,
+        (VMEM,) * 5 + (HBM,),
+        (ahead, both, above2, high, kap, out),
+        scratch=last_scratch,
+        aliases={5: 0},
         cost=0.5,
         name="last_high",
     )

time: 27.5 us -> 27.4 us (level)
  waiting for transfers between devices: 3.92 us -> 3.06 us
  Pallas kernels: 10.5 us -> 11.2 us
    ppermute x1, waiting for transfers between devices: 1.57 us -> 0.72 us  [on_device(): above2 = lax.ppermute(high, 'rad', swap_high)]
    pallas_call x12 -> x13, Pallas kernels: 10.5 us -> 11.2 us  [call(): pl.pallas_call(functools.partial(kernel, levels, rows), out_shape=out_sha...]
  transfers between devices with their start and end apart: 10 -> 10, of which waited for: 4 -> 4; matrix products, arithmetic and copies ran while one was open for 0% -> 0% of each run, Pallas kernels for 34% -> 36%
where the time goes in v9:
time: 27.4 us; the launch traced here: 27.2 us
  starting transfers between devices  12.8 us (47%)
  Pallas kernels  11.2 us (41%)
  waiting for transfers between devices  3.06 us (11%)
    pallas_call x13, Pallas kernels, call(): pl.pallas_call(functools.partial(kernel, levels, rows), out_shape=out_sha...  11.2 us
    ppermute x2, starting transfers between devices, around(): return (inner, outer, lax.ppermute(polar, 'lon', half))  4.11 us
    ppermute x1, starting transfers between devices, on_device(): above = lax.ppermute(high, 'rad', swap_high)  3.09 us
    ppermute x1, starting transfers between devices, on_device(): above2 = lax.ppermute(high, 'rad', swap_high)  3.07 us
    ppermute x2, starting transfers between devices, around(): outer = lax.ppermute(outer, 'lon', swap_outer)  2.18 us
    ppermute x2, waiting for transfers between devices, around(): outer = lax.ppermute(outer, 'lon', swap_outer)  1.76 us
    ppermute x1, waiting for transfers between devices, on_device(): above2 = lax.ppermute(high, 'rad', swap_high)  0.72 us
    ppermute x1, waiting for transfers between devices, on_device(): above = lax.ppermute(high, 'rad', swap_high)  0.57 us
  transfers between devices with their start and end apart: 10, of which 4 were waited for; matrix products, arithmetic and copies ran while one was open for 0% of the time, Pallas kernels for 36%

profile of v9, /device:TPU:0, one launch (start us, length us, event | category | flops | bytes accessed | tf_op | source)
XLA Modules:
  0.0 27.2 jit_solution(7107823768767864384)
XLA Ops:
  0.0 0.0 copy-start
  0.0 1.2 %high.1 = (f32[968,128]{1,0:T(8,128)S(1)}, f32[8,8,128]{2,1,0:T(8,128)S(1)}, f32[8,128]{1,0:T(8,128)S(1)}) custom-call(f32[1920,128]{1,0:T(8,128)} %bitcast.1, f32[8]{0:T(128)} %kappa.1), custom_call_target="tpu_custom_call" | custom-call | bytes 3690000 | tf_op jit(solution)/shard_map/high/pallas_call | solution.py:574
  1.2 0.0 copy-start.1
  1.2 0.0 copy-start.2
  1.2 0.0 copy-start.3
  1.2 3.1 %collective-permute-start.4 = (f32[968,128]{1,0:T(8,128)S(1)}, f32[968,128]{1,0:T(8,128)S(1)}, u32[]{:S(2)}, u32[]{:S(2)}) collective-permute-start(f32[968,128]{1,0:T(8,128)S(1)} %get-tuple-element.27.high), channel_id=1, source_target_pairs={{0,1},{2,3},{1,0},{3,2},{4,5},{6,7},{5,4},{7,6},{8,9},{10,11},{9,8... | collective-permute-start | bytes 1486856 | tf_op jit(solution)/shard_map/ppermute | solution.py:613
  4.3 0.0 copy-done
  4.4 0.1 collective-permute-start.3
  4.4 0.4 %edges.1 = (f32[64,128]{1,0:T(8,128)S(1)}, f32[64,128]{1,0:T(8,128)S(1)}, f32[160,128]{1,0:T(8,128)S(1)}) custom-call(f32[968,128]{1,0:T(8,128)S(1)} %get-tuple-element.27.high, f32[968,128]{1,0:T(8,128)S(1)} %low.1), custom_call_target="tpu_custom_call" | custom-call | bytes 1476000 | tf_op jit(solution)/shard_map/edges/pallas_call | solution.py:574
  4.9 1.6 %collective-permute-start = (f32[160,128]{1,0:T(8,128)S(1)}, f32[160,128]{1,0:T(8,128)S(1)}, u32[]{:S(2)}, u32[]{:S(2)}) collective-permute-start(f32[160,128]{1,0:T(8,128)S(1)} %get-tuple-element.32), channel_id=1, source_target_pairs={{0,16},{4,20},{8,24},{12,28},{16,0},{20,4},{24,8},{28,12},{1,17},{... | collective-permute-start | bytes 245768 | tf_op jit(solution)/shard_map/ppermute | solution.py:600
  6.4 0.2 collective-permute-start.1
  6.6 1.3 %collective-permute-start.2 = (f32[64,128]{1,0:T(8,128)S(1)}, f32[64,128]{1,0:T(8,128)S(1)}, u32[]{:S(2)}, u32[]{:S(2)}) collective-permute-start(f32[64,128]{1,0:T(8,128)S(1)} %get-tuple-element.34), channel_id=1, source_target_pairs={{4,8},{12,16},{20,24},{28,0},{8,4},{16,12},{24,20},{0,28},{5,9},{1... | collective-permute-start | bytes 98312 | tf_op jit(solution)/shard_map/ppermute | solution.py:599
  8.0 0.0 copy-done.1
  8.0 0.0 copy-done.2
  8.0 0.0 copy-done.3
  8.0 2.0 %first.1 = (f32[5,8,64,128]{3,2,1,0:T(8,128)S(1)}, f32[5,8,48,128]{3,2,1,0:T(8,128)S(1)}) custom-call(f32[968,128]{1,0:T(8,128)S(1)} %get-tuple-element.27.high, f32[968,128]{1,0:T(8,128)S(1)} %low.1, f32[5,8,4,128]{3,2,1,0:T(4,128)S(1)} %copy-done.3, f32[128,256]{1,0:T(8,128)S(1)} %copy-done.2, f32[3,48,128]{2,1,0:T(8,128)S(1)} %copy-done.1, ...), custom_call_target="tpu_custom_call" | custom-call | bytes 7380000 | tf_op jit(solution)/shard_map/first/pallas_call | solution.py:574
  10.0 0.0 collective-permute-done.1.inner
  10.0 0.8 %collective-permute-done.2.outer = f32[64,128]{1,0:T(8,128)S(1)} collective-permute-done((f32[64,128]{1,0:T(8,128)S(1)}, f32[64,128]{1,0:T(8,128)S(1)}, u32[]{:S(2)}, u32[]{:S(2)}) %collective-permute-start.2) | collective-permute-done | bytes 32800 | tf_op jit(solution)/shard_map/ppermute | solution.py:599
  10.8 0.0 collective-permute-done.polar
  10.9 0.7 %first_halo.2 = (f32[5,8,48,128]{3,2,1,0:T(8,128)S(1)}, f32[960,128]{1,0:T(8,128)S(1)}) custom-call(f32[5,8,48,128]{3,2,1,0:T(8,128)S(1)} %get-tuple-element.31.given, f32[5,8,64,128]{3,2,1,0:T(8,128)S(1)} %get-tuple-element.30.padded.start, f32[160,128]{1,0:T(8,128)S(1)} %collective-permute-done.polar, ...), custom_call_target="tpu_custom_call", output_to_operand_aliasing={{0}: (0, {})} | custom-call | bytes 2214000 | tf_op jit(solution)/shard_map/first_halo/pallas_call | solution.py:574
  11.5 3.1 %collective-permute-start.9 = (f32[960,128]{1,0:T(8,128)S(1)}, f32[960,128]{1,0:T(8,128)S(1)}, u32[]{:S(2)}, u32[]{:S(2)}) collective-permute-start(f32[960,128]{1,0:T(8,128)S(1)} %get-tuple-element.47), channel_id=1, source_target_pairs={{0,1},{2,3},{1,0},{3,2},{4,5},{6,7},{5,4},{7,6},{8,9},{10,11},{9,8... | collective-permute-start | bytes 1474568 | tf_op jit(solution)/shard_map/ppermute | solution.py:642
  14.6 0.7 %first_halo.3 = (f32[5,8,48,128]{3,2,1,0:T(8,128)S(1)}, f32[960,128]{1,0:T(8,128)S(1)}) custom-call(f32[5,8,48,128]{3,2,1,0:T(8,128)S(1)} %get-tuple-element.35.given, f32[5,8,64,128]{3,2,1,0:T(8,128)S(1)} %get-tuple-element.30.padded.start, f32[160,128]{1,0:T(8,128)S(1)} %collective-permute-done.polar, ...), custom_call_target="tpu_custom_call", output_to_operand_aliasing={{0}: (0, {})} | custom-call | bytes 2214000 | tf_op jit(solution)/shard_map/first_halo/pallas_call | solution.py:574
  15.3 0.1 collective-permute-start.8
  15.4 0.6 %collective-permute-done.4.above = f32[968,128]{1,0:T(8,128)S(1)} collective-permute-done((f32[968,128]{1,0:T(8,128)S(1)}, f32[968,128]{1,0:T(8,128)S(1)}, u32[]{:S(2)}, u32[]{:S(2)}) %collective-permute-start.4) | collective-permute-done | bytes 495648 | tf_op jit(solution)/shard_map/ppermute | solution.py:613
  15.9 0.3 section_high.1
  16.2 0.0 collective-permute-done.3.below
  16.2 0.7 %section_low.1 = (f32[5,8,48,128]{3,2,1,0:T(8,128)S(1)}, f32[5,8,64,128]{3,2,1,0:T(8,128)S(1)}, f32[64,128]{1,0:T(8,128)S(1)}, f32[64,128]{1,0:T(8,128)S(1)}, f32[160,128]{1,0:T(8,128)S(1)}) custom-call(f32[5,8,64,128]{3,2,1,0:T(8,128)S(1)} %get-tuple-element.30.padded.start, ...), custom_call_target="tpu_custom_call", output_to_operand_aliasing={{0}: (4, {}), {1}: (5, {})} | custom-call | bytes 1845000 | tf_op jit(solution)/shard_map/section_low/pallas_call | solution.py:574
  16.9 2.6 %collective-permute-start.5 = (f32[160,128]{1,0:T(8,128)S(1)}, f32[160,128]{1,0:T(8,128)S(1)}, u32[]{:S(2)}, u32[]{:S(2)}) collective-permute-start(f32[160,128]{1,0:T(8,128)S(1)} %get-tuple-element.42), channel_id=1, source_target_pairs={{0,16},{4,20},{8,24},{12,28},{16,0},{20,4},{24,8},{28,12},{1,17},{... | collective-permute-start | bytes 245768 | tf_op jit(solution)/shard_map/ppermute | solution.py:600
  19.4 0.0 collective-permute-start.6
  19.4 0.8 %collective-permute-start.7 = (f32[64,128]{1,0:T(8,128)S(1)}, f32[64,128]{1,0:T(8,128)S(1)}, u32[]{:S(2)}, u32[]{:S(2)}) collective-permute-start(f32[64,128]{1,0:T(8,128)S(1)} %get-tuple-element.44), channel_id=1, source_target_pairs={{4,8},{12,16},{20,24},{28,0},{8,4},{16,12},{24,20},{0,28},{5,9},{1... | collective-permute-start | bytes 98312 | tf_op jit(solution)/shard_map/ppermute | solution.py:599
  20.3 2.5 %second.1 = (f32[5,8,48,128]{3,2,1,0:T(8,128)S(1)}, f32[960,128]{1,0:T(8,128)S(1)}, f32[960,128]{1,0:T(8,128)S(1)}) custom-call(f32[5,8,64,128]{3,2,1,0:T(8,128)S(1)} %get-tuple-element.39.padded, f32[128,256]{1,0:T(8,128)S(1)} %copy-done.2, f32[3,48,128]{2,1,0:T(8,128)S(1)} %copy-done.1, f32[8,8,128]{2,1,0:T(8,128)S(1)} %get-tuple-element.29.kap.kappa, ...), custom_call_target="tpu_custom_call" | custom-call | bytes 9225000 | tf_op jit(solution)/shard_map/second/pallas_call | solution.py:574
  22.7 0.0 collective-permute-done.6.inner
  22.8 0.9 %collective-permute-done.7.outer = f32[64,128]{1,0:T(8,128)S(1)} collective-permute-done((f32[64,128]{1,0:T(8,128)S(1)}, f32[64,128]{1,0:T(8,128)S(1)}, u32[]{:S(2)}, u32[]{:S(2)}) %collective-permute-start.7) | collective-permute-done | bytes 32800 | tf_op jit(solution)/shard_map/ppermute | solution.py:599
  23.7 0.0 collective-permute-done.5.polar
  23.7 0.9 %second_halo.1.both = f32[5,8,48,128]{3,2,1,0:T(8,128)S(1)} custom-call(f32[5,8,48,128]{3,2,1,0:T(8,128)S(1)} %get-tuple-element.41.given, f32[5,8,64,128]{3,2,1,0:T(8,128)S(1)} %get-tuple-element.39.padded, f32[160,128]{1,0:T(8,128)S(1)} %collective-permute-done.5.polar, ...), custom_call_target="tpu_custom_call", output_to_operand_aliasing={{}: (0, {})} | custom-call | bytes 3690000 | tf_op jit(solution)/shard_map/second_halo/pallas_call | solution.py:574
  24.6 0.8 %end_low.1.given = f32[5,8,48,128]{3,2,1,0:T(8,128)} custom-call(f32[5,8,64,128]{3,2,1,0:T(8,128)S(1)} %get-tuple-element.39.padded, f32[5,8,48,128]{3,2,1,0:T(8,128)S(1)} %second_halo.1.both, f32[8,8,128]{2,1,0:T(8,128)S(1)} %get-tuple-element.29.kap.kappa), custom_call_target="tpu_custom_call" | custom-call | bytes 1845000 | tf_op jit(solution)/shard_map/end_low/pallas_call | solution.py:574
  25.5 0.7 %collective-permute-done.9.sent = f32[960,128]{1,0:T(8,128)S(1)} collective-permute-done((f32[960,128]{1,0:T(8,128)S(1)}, f32[960,128]{1,0:T(8,128)S(1)}, u32[]{:S(2)}, u32[]{:S(2)}) %collective-permute-start.9) | collective-permute-done | bytes 491552 | tf_op jit(solution)/shard_map/ppermute | solution.py:642
  26.2 0.9 %last_high.1.given = f32[5,8,48,128]{3,2,1,0:T(8,128)} custom-call(f32[5,8,64,128]{3,2,1,0:T(8,128)S(1)} %get-tuple-element.39.padded, f32[5,8,48,128]{3,2,1,0:T(8,128)S(1)} %second_halo.1.both, f32[960,128]{1,0:T(8,128)S(1)} %collective-permute-done.9.sent, f32[960,128]{1,0:T(8,128)S(1)} %get-tuple-element.48.more, ...), custom_call_target="tpu_custom_call", output_to_operand_aliasing={{}: (5, {})} | custom-call | bytes 1845000 | tf_op jit(solution)/shard_map/last_high/pallas_call | solution.py:574
  27.1 0.0 collective-permute-done.8.sent
  27.1 0.1 last_low.1
  (1 shorter events, 0.0 us)
Async XLA Ops:
  0.0 4.3 %copy-start = (f32[5,8,48,128]{3,2,1,0:T(8,128)S(1)}, f32[5,8,48,128]{3,2,1,0:T(8,128)}, u32[]{:S(2)}) copy-start(f32[5,8,48,128]{3,2,1,0:T(8,128)} %param.5) | copy-start | bytes 2949124
  1.2 6.8 %copy-start.1 = (f32[3,48,128]{2,1,0:T(8,128)S(1)}, f32[3,48,128]{2,1,0:T(8,128)}, u32[]{:S(2)}) copy-start(f32[3,48,128]{2,1,0:T(8,128)} %constant.5.clone.geo) | copy-start | bytes 221188
  1.2 6.8 %copy-start.2 = (f32[128,256]{1,0:T(8,128)S(1)}, f32[128,256]{1,0:T(8,128)}, u32[]{:S(2)}) copy-start(f32[128,256]{1,0:T(8,128)} %constant.4.clone.matrix) | copy-start | bytes 393220
  1.2 6.7 %copy-start.3 = (f32[5,8,4,128]{3,2,1,0:T(4,128)S(1)}, f32[5,8,4,128]{3,2,1,0:T(4,128)}, u32[]{:S(2)}) copy-start(f32[5,8,4,128]{3,2,1,0:T(4,128)} %beyond.1) | copy-start | bytes 245764
  1.2 14.7 %collective-permute-start.4 = (f32[968,128]{1,0:T(8,128)S(1)}, f32[968,128]{1,0:T(8,128)S(1)}, u32[]{:S(2)}, u32[]{:S(2)}) collective-permute-start(f32[968,128]{1,0:T(8,128)S(1)} %get-tuple-element.27.high), channel_id=1, source_target_pairs={{0,1},{2,3},{1,0},{3,2},{4,5},{6,7},{5,4},{7,6},{8,9},{10,11},{9,8... | collective-permute-start | bytes 1486856 | tf_op jit(solution)/shard_map/ppermute | solution.py:613
  4.4 11.8 %collective-permute-start.3 = (f32[968,128]{1,0:T(8,128)S(1)}, f32[968,128]{1,0:T(8,128)S(1)}, u32[]{:S(2)}, u32[]{:S(2)}) collective-permute-start(f32[968,128]{1,0:T(8,128)S(1)} %low.1), channel_id=1, source_target_pairs={{1,2},{5,6},{9,10},{13,14},{17,18},{21,22},{25,26},{29,30},{0,4},{... | collective-permute-start | bytes 1486856 | tf_op jit(solution)/shard_map/ppermute | solution.py:615
  4.9 6.0 %collective-permute-start = (f32[160,128]{1,0:T(8,128)S(1)}, f32[160,128]{1,0:T(8,128)S(1)}, u32[]{:S(2)}, u32[]{:S(2)}) collective-permute-start(f32[160,128]{1,0:T(8,128)S(1)} %get-tuple-element.32), channel_id=1, source_target_pairs={{0,16},{4,20},{8,24},{12,28},{16,0},{20,4},{24,8},{28,12},{1,17},{... | collective-permute-start | bytes 245768 | tf_op jit(solution)/shard_map/ppermute | solution.py:600
  6.4 3.6 %collective-permute-start.1 = (f32[64,128]{1,0:T(8,128)S(1)}, f32[64,128]{1,0:T(8,128)S(1)}, u32[]{:S(2)}, u32[]{:S(2)}) collective-permute-start(f32[64,128]{1,0:T(8,128)S(1)} %get-tuple-element.33), channel_id=1, source_target_pairs={{0,4},{8,12},{16,20},{24,28},{4,0},{12,8},{20,16},{28,24},{1,5},{9... | collective-permute-start | bytes 98312 | tf_op jit(solution)/shard_map/ppermute | solution.py:598
  6.6 4.2 %collective-permute-start.2 = (f32[64,128]{1,0:T(8,128)S(1)}, f32[64,128]{1,0:T(8,128)S(1)}, u32[]{:S(2)}, u32[]{:S(2)}) collective-permute-start(f32[64,128]{1,0:T(8,128)S(1)} %get-tuple-element.34), channel_id=1, source_target_pairs={{4,8},{12,16},{20,24},{28,0},{8,4},{16,12},{24,20},{0,28},{5,9},{1... | collective-permute-start | bytes 98312 | tf_op jit(solution)/shard_map/ppermute | solution.py:599
  11.5 14.6 %collective-permute-start.9 = (f32[960,128]{1,0:T(8,128)S(1)}, f32[960,128]{1,0:T(8,128)S(1)}, u32[]{:S(2)}, u32[]{:S(2)}) collective-permute-start(f32[960,128]{1,0:T(8,128)S(1)} %get-tuple-element.47), channel_id=1, source_target_pairs={{0,1},{2,3},{1,0},{3,2},{4,5},{6,7},{5,4},{7,6},{8,9},{10,11},{9,8... | collective-permute-start | bytes 1474568 | tf_op jit(solution)/shard_map/ppermute | solution.py:642
  15.3 11.8 %collective-permute-start.8 = (f32[960,128]{1,0:T(8,128)S(1)}, f32[960,128]{1,0:T(8,128)S(1)}, u32[]{:S(2)}, u32[]{:S(2)}) collective-permute-start(f32[960,128]{1,0:T(8,128)S(1)} %get-tuple-element.45), channel_id=1, source_target_pairs={{1,2},{5,6},{9,10},{13,14},{17,18},{21,22},{25,26},{29,30},{0,4},{... | collective-permute-start | bytes 1474568 | tf_op jit(solution)/shard_map/ppermute | solution.py:644
  16.9 6.8 %collective-permute-start.5 = (f32[160,128]{1,0:T(8,128)S(1)}, f32[160,128]{1,0:T(8,128)S(1)}, u32[]{:S(2)}, u32[]{:S(2)}) collective-permute-start(f32[160,128]{1,0:T(8,128)S(1)} %get-tuple-element.42), channel_id=1, source_target_pairs={{0,16},{4,20},{8,24},{12,28},{16,0},{20,4},{24,8},{28,12},{1,17},{... | collective-permute-start | bytes 245768 | tf_op jit(solution)/shard_map/ppermute | solution.py:600
  19.4 3.3 %collective-permute-start.6 = (f32[64,128]{1,0:T(8,128)S(1)}, f32[64,128]{1,0:T(8,128)S(1)}, u32[]{:S(2)}, u32[]{:S(2)}) collective-permute-start(f32[64,128]{1,0:T(8,128)S(1)} %get-tuple-element.43), channel_id=1, source_target_pairs={{0,4},{8,12},{16,20},{24,28},{4,0},{12,8},{20,16},{28,24},{1,5},{9... | collective-permute-start | bytes 98312 | tf_op jit(solution)/shard_map/ppermute | solution.py:598
  19.4 4.2 %collective-permute-start.7 = (f32[64,128]{1,0:T(8,128)S(1)}, f32[64,128]{1,0:T(8,128)S(1)}, u32[]{:S(2)}, u32[]{:S(2)}) collective-permute-start(f32[64,128]{1,0:T(8,128)S(1)} %get-tuple-element.44), channel_id=1, source_target_pairs={{4,8},{12,16},{20,24},{28,0},{8,4},{16,12},{24,20},{0,28},{5,9},{1... | collective-permute-start | bytes 98312 | tf_op jit(solution)/shard_map/ppermute | solution.py:599

commit v10 on v9

--- a/solution.py
+++ b/solution.py
@@ -148,14 +148,20 @@
 
 
 def mirrored():
-    odd = lax.axis_index("rad") % 2
+    odd = lax.axis_index("lon") % 2
     return odd, jnp.where(odd == 1, -1.0, 1.0).astype(jnp.float32)
 
 
 def bordered(at):
-    here, depth = lax.axis_index("rad"), lax.axis_size("rad")
-    inside = jnp.where((here > 0) & (here < depth - 1), 1.0, 0.0)
-    return inside.astype(jnp.float32) if at == 0 else jnp.float32(1.0)
+    last = lax.axis_size("rad") - 1
+    here = lax.axis_index("rad")
+    odd, _ = mirrored()
+    from_first = jnp.where(odd == 1, last - here, here)
+    return from_first > 0 if at == 0 else from_first < last
+
+
+def share_of(at, factor):
+    return jnp.where(bordered(at), factor, 0.0).astype(jnp.float32)
 
 
 def lanes():
@@ -264,10 +270,11 @@
         metric = jnp.where(at_side, geo[0, here, :], 0.0)
         metric2 = jnp.where(at_side, geo[1, here, :], 0.0)
         for l in own:
-            shift = (LANES - REACH - 2 * REACH * (u * levels + l)) % LANES
+            shift = (LANES - REACH - 2 * REACH * (u * levels + levels - 1 - l)) % LANES
             center = [padded[f, l, pl.ds((t + 1) * TILE, TILE), :] for f in range(FIELDS)]
             wlon, wrow, temper = center[1], center[2], center[4]
             slon = [metric * pltpu.roll(slopes[f * count + j], shift, 1) for f in range(FIELDS)]
+            slon[3] = -slon[3]
             laplace = metric2 * pltpu.roll(bends[j], shift, 1)
             extra = [-wlon * slope for slope in slon]
             extra[1] = extra[1] - temper * slon[0] - slon[4]
@@ -392,15 +399,6 @@
     return out
 
 
-def halo_tile(ref, rows, r0):
-    out = [
-        [ref[pl.ds((f * REACH + REACH - 1 - b) * rows + r0, TILE), :] for b in range(REACH)]
-        for f in range(FIELDS)
-    ]
-    out[3] = [-v for v in out[3]]
-    return out
-
-
 def own_tile(ref, rows, r0):
     return [
         [ref[pl.ds((f * REACH + b) * rows + r0, TILE), :] for b in range(REACH)] for f in range(FIELDS)
@@ -409,7 +407,7 @@
 
 def section_side(at, up, levels, rows, padded, rate, sent, kappa, full, ahead):
     odd, mirror = mirrored()
-    there = bordered(at)
+    there = share_of(at, 1.0)
 
     def body(t, carry):
         r0 = pl.multiple_of(t * TILE, TILE)
@@ -419,8 +417,7 @@
         extra = across_level(center[3], center[4], halo, [kappa[at + a] for a in range(REACH)], up)
         for f in range(FIELDS):
             for a in range(REACH):
-                more = extra[f][a] if at else there * extra[f][a]
-                total = rate[f, at + a, here, :] + more
+                total = rate[f, at + a, here, :] + there * extra[f][a]
                 full[f, at + a, here, :] = total
                 ahead[f, at + a, inside, :] = center[f][a] + time_step * total
         return carry
@@ -432,14 +429,14 @@
             ahead[f, l, pl.ds(rows + TILE, REACH), :] = padded[f, l, pl.ds(rows + TILE, REACH), :]
 
 
-def section_high_kernel(levels, rows, padded, rate, above, kappa, full, ahead):
+def section_low_kernel(levels, rows, padded, rate, below, kappa, full, ahead):
+    section_side(0, False, levels, rows, padded, rate, below, kappa, full, ahead)
+
+
+def section_high_kernel(
+    levels, rows, padded, rate, above, kappa, given1, given2, full, ahead, inner, outer, polar
+):
     section_side(levels - REACH, True, levels, rows, padded, rate, above, kappa, full, ahead)
-
-
-def section_low_kernel(
-    levels, rows, padded, rate, below, kappa, given1, given2, full, ahead, inner, outer, polar
-):
-    section_side(0, False, levels, rows, padded, rate, below, kappa, full, ahead)
     packs = []
     for f in range(FIELDS):
         tiles = [[ahead[f, l, pl.ds((t + 1) * TILE, TILE), :] for t in range(rows // TILE)] for l in range(levels)]
@@ -472,7 +469,7 @@
             kappas = [
                 halo_ref[pl.ds(tail + jnp.where(odd == 1, REACH - 1 - a, a), 1), :] for a in range(REACH)
             ]
-            there = time_step * bordered(at)
+            there = share_of(at, time_step)
             extra = across_level(beyond[3], beyond[4], mine, kappas, up)
             for f in range(FIELDS):
                 for a in range(REACH):
@@ -492,74 +489,33 @@
     add_halo(levels, rows, range(levels), padded, polar, inner, outer, geo, kap, store)
 
 
-def write_side(at, more, levels, rows, padded, both, kap, out, staged, sems):
+def last_kernel(levels, rows, padded, both, below, above, more_low, more_high, kap, out, staged, sems):
     odd, mirror = mirrored()
+    copies = []
     for t in range(rows // TILE):
         here, inside = pl.ds(t * TILE, TILE), pl.ds((t + 1) * TILE, TILE)
-        extra = None
-        if more is not None:
+        for sent, more, at, up in ((below, more_low, 0, False), (above, more_high, levels - REACH, True)):
+            halo, there = own_tile(sent, rows, t * TILE), own_tile(more, rows, t * TILE)
+            halo = [[halo[f][b] + there[f][b] for b in range(REACH)] for f in range(FIELDS)]
             wind = [padded[3, at + a, inside, :] for a in range(REACH)]
             temper = [padded[4, at + a, inside, :] for a in range(REACH)]
-            extra = more(t * TILE, wind, temper, [kap[at + a] for a in range(REACH)])
-        for f in range(FIELDS):
-            for a in range(REACH):
-                new = both[f, at + a, here, :]
-                if extra is not None:
-                    new = new + (0.5 * time_step) * extra[f][a]
-                staged[f, jnp.where(odd == 1, REACH - 1 - a, a), here, :] = mirror * new if f == 3 else new
-        side_copy(at, t, levels, odd, out, staged, sems).start()
-
-
-def side_copy(at, t, levels, odd, out, staged, sems):
-    real, here = jnp.where(odd == 1, levels - at - REACH, at), pl.ds(t * TILE, TILE)
-    return pltpu.make_async_copy(staged.at[:, :, here], out.at[:, pl.ds(real, REACH), here], sems.at[t])
-
-
-def wait_side(at, levels, rows, out, staged, sems):
-    odd, _ = mirrored()
-    for t in range(rows // TILE):
-        side_copy(at, t, levels, odd, out, staged, sems).wait()
-
-
-def second_share(sent, more, up, rows):
-    def share(r0, wind, temper, kappa):
-        halo, there = halo_tile(sent, rows, r0), own_tile(more, rows, r0)
-        halo = [[halo[f][b] + there[f][b] for b in range(REACH)] for f in range(FIELDS)]
-        return across_level(wind, temper, halo, kappa, up)
-
-    return share
-
-
-def at_end():
-    here, depth = lax.axis_index("rad"), lax.axis_size("rad")
-    return (here == 0) | (here == depth - 1)
-
-
-def end_low_kernel(levels, rows, padded, both, kap, out, staged, sems):
-    @pl.when(at_end())
-    def _():
-        write_side(0, None, levels, rows, padded, both, kap, out, staged, sems)
-        wait_side(0, levels, rows, out, staged, sems)
-
-
-def last_high_kernel(levels, rows, padded, both, sent, more, kap, given, out, staged, sems):
-    share = second_share(sent, more, True, rows)
-    write_side(levels - REACH, share, levels, rows, padded, both, kap, out, staged, sems)
-    wait_side(levels - REACH, levels, rows, out, staged, sems)
-
-
-def last_low_kernel(levels, rows, padded, both, sent, more, kap, given, out, staged, sems):
-    @pl.when(jnp.logical_not(at_end()))
-    def _():
-        share = second_share(sent, more, False, rows)
-        write_side(0, share, levels, rows, padded, both, kap, out, staged, sems)
-        wait_side(0, levels, rows, out, staged, sems)
+            extra = across_level(wind, temper, halo, [kap[at + a] for a in range(REACH)], up)
+            scale = share_of(at, 0.5 * time_step)
+            for f in range(FIELDS):
+                for a in range(REACH):
+                    new = both[f, at + a, here, :] + scale * extra[f][a]
+                    real = jnp.where(odd == 1, levels - 1 - at - a, at + a)
+                    staged[f, real, here, :] = mirror * new if f == 3 else new
+        copies.append(pltpu.make_async_copy(staged.at[:, :, here], out.at[:, :, here], sems.at[t]))
+        copies[-1].start()
+    for copy in copies:
+        copy.wait()
 
 
 def on_device(state, outer_rows, kappa):
     levels, rows, width = state.shape[1:]
     ring, depth = lax.axis_size("lon"), lax.axis_size("rad")
-    assert ring % 4 == 0 and depth % 2 == 0 and width == LANES and levels == 2 * REACH and GROUPS % levels == 0
+    assert ring % 4 == 0 and width == LANES and levels == 2 * REACH and GROUPS % levels == 0
     assert rows % (TILE * (GROUPS // levels)) == 0
     matrix = stencil_matrix(width)
     geo = geometry(rows, width * ring, width)
@@ -588,11 +544,13 @@
     pairs = [(i, (i + 1) % ring) for i in range(1, ring, 2)]
     swap_outer = pairs + [(b, a) for a, b in pairs]
     half = [(i, (i + ring // 2) % ring) for i in range(ring)]
-    pairs = [(i, i + 1) for i in range(0, depth, 2)]
-    swap_high = pairs + [(b, a) for a, b in pairs]
-    pairs = [(lon * depth + i, lon * depth + i + 1) for lon in range(ring) for i in range(1, depth - 1, 2)]
-    pairs += [(lon * depth + i, (lon + 1) * depth + i) for lon in range(0, ring, 2) for i in (0, depth - 1)]
-    swap_low = pairs + [(b, a) for a, b in pairs]
+    onward = []
+    for lon in range(0, ring, 2):
+        even, odd = lon * depth, (lon + 1) * depth
+        onward += [(even + i, even + i + 1) for i in range(depth - 1)] + [(even + depth - 1, odd + depth - 1)]
+        onward += [(odd + i + 1, odd + i) for i in range(depth - 1)] + [(odd, even)]
+    back = [(b, a) for a, b in onward]
+    axes = ("lon", "rad")
 
     def around(inner, outer, polar):
         inner = lax.ppermute(inner, "lon", swap_inner)
@@ -610,9 +568,9 @@
         scratch=(pltpu.SMEM(kappa.shape, jnp.float32), pltpu.SemaphoreType.DMA((2 * FIELDS + 1,))),
         name="high",
     )
-    above = lax.ppermute(high, "rad", swap_high)
+    below = lax.ppermute(high, axes, onward)
     low = call(low_kernel, payload, (VMEM,) * 2, (flat, raw_kap), cost=0.2, name="low")
-    below = lax.ppermute(low, ("lon", "rad"), swap_low)
+    above = lax.ppermute(low, axes, back)
     edges = call(edges_kernel, edge_shapes, (VMEM,) * 2, (high, low), cost=0.4, name="edges")
     inner, outer, beyond = around(*edges)
     lon_scratch = (in_vmem(*full_shape), in_vmem(*full_shape[1:]))
@@ -639,25 +597,26 @@
         )
 
     rate, high = first_halo(rate, levels - REACH)
-    above2 = lax.ppermute(high, "rad", swap_high)
+    below2 = lax.ppermute(high, axes, onward)
     rate, low = first_halo(rate, 0)
-    below2 = lax.ppermute(low, ("lon", "rad"), swap_low)
+    above2 = lax.ppermute(low, axes, back)
+    section_shapes = [in_vmem(*full_shape), in_vmem(*pad_shape)]
     full, ahead = call(
+        section_low_kernel,
+        section_shapes,
+        (VMEM,) * 4,
+        (padded, rate, below, kap),
+        cost=0.4,
+        name="section_low",
+    )
+    full, ahead, *edges = call(
         section_high_kernel,
-        [in_vmem(*full_shape), in_vmem(*pad_shape)],
-        (VMEM,) * 4,
-        (padded, rate, above, kap),
-        cost=0.4,
-        name="section_high",
-    )
-    full, ahead, *edges = call(
-        section_low_kernel,
-        [in_vmem(*full_shape), in_vmem(*pad_shape), *edge_shapes],
+        [*section_shapes, *edge_shapes],
         (VMEM,) * 6,
-        (padded, rate, below, kap, full, ahead),
+        (padded, rate, above, kap, full, ahead),
         aliases={4: 0, 5: 1},
         cost=0.5,
-        name="section_low",
+        name="section_high",
     )
     inner, outer, beyond = around(*edges)
     both, low, high = call(
@@ -677,38 +636,13 @@
         aliases={0: 0},
         name="second_halo",
     )
-    last_scratch = (
-        in_vmem(FIELDS, REACH, rows, width),
-        pltpu.SemaphoreType.DMA((rows // TILE,)),
-    )
-    result = pltpu.HBM(full_shape, jnp.float32)
-    out = call(
-        end_low_kernel,
-        result,
-        (VMEM,) * 3,
-        (ahead, both, kap),
-        scratch=last_scratch,
-        cost=0.5,
-        name="end_low",
-    )
-    out = call(
-        last_high_kernel,
-        result,
-        (VMEM,) * 5 + (HBM,),
-        (ahead, both, above2, high, kap, out),
-        scratch=last_scratch,
-        aliases={5: 0},
-        cost=0.5,
-        name="last_high",
-    )
     return call(
-        last_low_kernel,
-        result,
-        (VMEM,) * 5 + (HBM,),
-        (ahead, both, below2, low, kap, out),
-        scratch=last_scratch,
-        aliases={5: 0},
-        name="last_low",
+        last_kernel,
+        pltpu.HBM(full_shape, jnp.float32),
+        (VMEM,) * 7,
+        (ahead, both, below2, above2, low, high, kap),
+        scratch=(in_vmem(*full_shape), pltpu.SemaphoreType.DMA((rows // TILE,))),
+        name="last",
     )
 
 

time: 27.4 us -> 27 us (0.985)
  waiting for transfers between devices: 3.06 us -> 5.19 us
  starting transfers between devices: 12.8 us -> 10.9 us
  Pallas kernels: 11.2 us -> 10.7 us
    ppermute x4, waiting for transfers between devices: 1.29 us -> 3.71 us  [the longest x1 1.9 us: on_device(): above2 = lax.ppermute(low, axes, back)]
    ppermute x4, starting transfers between devices: 6.3 us -> 5.1 us  [the longest x1 3.04 us: on_device(): below = lax.ppermute(high, axes, onward)]
    ppermute x2, starting transfers between devices: 4.11 us -> 3.09 us  [around(): return (inner, outer, lax.ppermute(polar, 'lon', half))]
    pallas_call x13 -> x11, Pallas kernels: 11.2 us -> 10.7 us  [call(): pl.pallas_call(functools.partial(kernel, levels, rows), out_shape=out_sha...]
    ppermute x2, starting transfers between devices: 2.18 us -> 2.66 us  [around(): outer = lax.ppermute(outer, 'lon', swap_outer)]
    ppermute x2, waiting for transfers between devices: 1.76 us -> 1.47 us  [around(): outer = lax.ppermute(outer, 'lon', swap_outer)]
  transfers between devices with their start and end apart: 10 -> 10, of which waited for: 4 -> 4; matrix products, arithmetic and copies ran while one was open for 0% -> 0% of each run, Pallas kernels for 36% -> 31%
where the time goes in v10:
time: 27 us; the launch traced here: 26.9 us
  starting transfers between devices  10.9 us (40%)
  Pallas kernels  10.7 us (40%)
  waiting for transfers between devices  5.19 us (19%)
    pallas_call x11, Pallas kernels, call(): pl.pallas_call(functools.partial(kernel, levels, rows), out_shape=out_sha...  10.7 us
    ppermute x2, starting transfers between devices, around(): return (inner, outer, lax.ppermute(polar, 'lon', half))  3.09 us
    ppermute x1, starting transfers between devices, on_device(): below = lax.ppermute(high, axes, onward)  3.04 us
    ppermute x2, starting transfers between devices, around(): outer = lax.ppermute(outer, 'lon', swap_outer)  2.66 us
    ppermute x1, starting transfers between devices, on_device(): below2 = lax.ppermute(high, axes, onward)  2.01 us
    ppermute x1, waiting for transfers between devices, on_device(): above2 = lax.ppermute(low, axes, back)  1.9 us
    ppermute x1, waiting for transfers between devices, on_device(): below = lax.ppermute(high, axes, onward)  1.8 us
    ppermute x2, waiting for transfers between devices, around(): outer = lax.ppermute(outer, 'lon', swap_outer)  1.47 us
  transfers between devices with their start and end apart: 10, of which 4 were waited for; matrix products, arithmetic and copies ran while one was open for 0% of the time, Pallas kernels for 31%

profile of v10, /device:TPU:0, one launch (start us, length us, event | category | flops | bytes accessed | tf_op | source)
XLA Modules:
  0.0 26.9 jit_solution(14015310040130492374)
XLA Ops:
  0.0 0.0 copy-start
  0.0 1.2 %high.1 = (f32[968,128]{1,0:T(8,128)S(1)}, f32[8,8,128]{2,1,0:T(8,128)S(1)}, f32[8,128]{1,0:T(8,128)S(1)}) custom-call(f32[1920,128]{1,0:T(8,128)} %bitcast.1, f32[8]{0:T(128)} %kappa.1), custom_call_target="tpu_custom_call" | custom-call | bytes 3690000 | tf_op jit(solution)/shard_map/high/pallas_call | solution.py:530
  1.2 0.0 copy-start.1
  1.2 0.0 copy-start.2
  1.2 0.0 copy-start.3
  1.2 3.0 %collective-permute-start.4 = (f32[968,128]{1,0:T(8,128)S(1)}, f32[968,128]{1,0:T(8,128)S(1)}, u32[]{:S(2)}, u32[]{:S(2)}) collective-permute-start(f32[968,128]{1,0:T(8,128)S(1)} %get-tuple-element.27.high), channel_id=1, source_target_pairs={{0,1},{1,2},{2,3},{3,7},{5,4},{6,5},{7,6},{4,0},{8,9},{9,10},{10,1... | collective-permute-start | bytes 1486856 | tf_op jit(solution)/shard_map/ppermute | solution.py:571
  4.3 0.0 copy-done
  4.3 0.0 collective-permute-start.3
  4.3 0.4 %edges.1 = (f32[64,128]{1,0:T(8,128)S(1)}, f32[64,128]{1,0:T(8,128)S(1)}, f32[160,128]{1,0:T(8,128)S(1)}) custom-call(f32[968,128]{1,0:T(8,128)S(1)} %get-tuple-element.27.high, f32[968,128]{1,0:T(8,128)S(1)} %low.1), custom_call_target="tpu_custom_call" | custom-call | bytes 1476000 | tf_op jit(solution)/shard_map/edges/pallas_call | solution.py:530
  4.8 1.6 %collective-permute-start = (f32[160,128]{1,0:T(8,128)S(1)}, f32[160,128]{1,0:T(8,128)S(1)}, u32[]{:S(2)}, u32[]{:S(2)}) collective-permute-start(f32[160,128]{1,0:T(8,128)S(1)} %get-tuple-element.32), channel_id=1, source_target_pairs={{0,16},{4,20},{8,24},{12,28},{16,0},{20,4},{24,8},{28,12},{1,17},{... | collective-permute-start | bytes 245768 | tf_op jit(solution)/shard_map/ppermute | solution.py:558
  6.3 0.0 collective-permute-start.1
  6.3 1.5 %collective-permute-start.2 = (f32[64,128]{1,0:T(8,128)S(1)}, f32[64,128]{1,0:T(8,128)S(1)}, u32[]{:S(2)}, u32[]{:S(2)}) collective-permute-start(f32[64,128]{1,0:T(8,128)S(1)} %get-tuple-element.34), channel_id=1, source_target_pairs={{4,8},{12,16},{20,24},{28,0},{8,4},{16,12},{24,20},{0,28},{5,9},{1... | collective-permute-start | bytes 98312 | tf_op jit(solution)/shard_map/ppermute | solution.py:557
  7.9 0.0 copy-done.1
  7.9 0.0 copy-done.2
  7.9 0.0 copy-done.3
  7.9 2.0 %first.1 = (f32[5,8,64,128]{3,2,1,0:T(8,128)S(1)}, f32[5,8,48,128]{3,2,1,0:T(8,128)S(1)}) custom-call(f32[968,128]{1,0:T(8,128)S(1)} %get-tuple-element.27.high, f32[968,128]{1,0:T(8,128)S(1)} %low.1, f32[5,8,4,128]{3,2,1,0:T(4,128)S(1)} %copy-done.3, f32[128,256]{1,0:T(8,128)S(1)} %copy-done.2, f32[3,48,128]{2,1,0:T(8,128)S(1)} %copy-done.1, ...), custom_call_target="tpu_custom_call" | custom-call | bytes 7380000 | tf_op jit(solution)/shard_map/first/pallas_call | solution.py:530
  9.9 0.0 collective-permute-done.1.inner
  9.9 0.7 %collective-permute-done.2.outer = f32[64,128]{1,0:T(8,128)S(1)} collective-permute-done((f32[64,128]{1,0:T(8,128)S(1)}, f32[64,128]{1,0:T(8,128)S(1)}, u32[]{:S(2)}, u32[]{:S(2)}) %collective-permute-start.2) | collective-permute-done | bytes 32800 | tf_op jit(solution)/shard_map/ppermute | solution.py:557
  10.6 0.0 collective-permute-done.polar
  10.6 0.7 %first_halo.2 = (f32[5,8,48,128]{3,2,1,0:T(8,128)S(1)}, f32[960,128]{1,0:T(8,128)S(1)}) custom-call(f32[5,8,48,128]{3,2,1,0:T(8,128)S(1)} %get-tuple-element.31.given, f32[5,8,64,128]{3,2,1,0:T(8,128)S(1)} %get-tuple-element.30.padded.start, f32[160,128]{1,0:T(8,128)S(1)} %collective-permute-done.polar, ...), custom_call_target="tpu_custom_call", output_to_operand_aliasing={{0}: (0, {})} | custom-call | bytes 2214000 | tf_op jit(solution)/shard_map/first_halo/pallas_call | solution.py:530
  11.4 0.7 %first_halo.3 = (f32[5,8,48,128]{3,2,1,0:T(8,128)S(1)}, f32[960,128]{1,0:T(8,128)S(1)}) custom-call(f32[5,8,48,128]{3,2,1,0:T(8,128)S(1)} %get-tuple-element.35.given, f32[5,8,64,128]{3,2,1,0:T(8,128)S(1)} %get-tuple-element.30.padded.start, f32[160,128]{1,0:T(8,128)S(1)} %collective-permute-done.polar, ...), custom_call_target="tpu_custom_call", output_to_operand_aliasing={{0}: (0, {})} | custom-call | bytes 2214000 | tf_op jit(solution)/shard_map/first_halo/pallas_call | solution.py:530
  12.1 0.0 collective-permute-start.9
  12.1 2.0 %collective-permute-start.8 = (f32[960,128]{1,0:T(8,128)S(1)}, f32[960,128]{1,0:T(8,128)S(1)}, u32[]{:S(2)}, u32[]{:S(2)}) collective-permute-start(f32[960,128]{1,0:T(8,128)S(1)} %get-tuple-element.45), channel_id=1, source_target_pairs={{0,1},{1,2},{2,3},{3,7},{5,4},{6,5},{7,6},{4,0},{8,9},{9,10},{10,1... | collective-permute-start | bytes 1474568 | tf_op jit(solution)/shard_map/ppermute | solution.py:600
  14.2 1.8 %collective-permute-done.4.below = f32[968,128]{1,0:T(8,128)S(1)} collective-permute-done((f32[968,128]{1,0:T(8,128)S(1)}, f32[968,128]{1,0:T(8,128)S(1)}, u32[]{:S(2)}, u32[]{:S(2)}) %collective-permute-start.4) | collective-permute-done | bytes 495648 | tf_op jit(solution)/shard_map/ppermute | solution.py:571
  16.0 0.3 %section_low.1 = (f32[5,8,48,128]{3,2,1,0:T(8,128)S(1)}, f32[5,8,64,128]{3,2,1,0:T(8,128)S(1)}) custom-call(f32[5,8,64,128]{3,2,1,0:T(8,128)S(1)} %get-tuple-element.30.padded.start, f32[5,8,48,128]{3,2,1,0:T(8,128)S(1)} %get-tuple-element.36.rate, f32[968,128]{1,0:T(8,128)S(1)} %collective-permute-done.4.below, f32[8,8,128]{2,1,0:T(8,128)S(1)} %get-tuple-element.29.kap.kappa), custom_call_target="tpu_custom_call" | custom-call | bytes 1476000 | tf_op jit(solution)/shard_map/section_low/pallas_call | solution.py:530
  16.2 0.0 collective-permute-done.3.above
  16.3 0.7 %section_high.1 = (f32[5,8,48,128]{3,2,1,0:T(8,128)S(1)}, f32[5,8,64,128]{3,2,1,0:T(8,128)S(1)}, f32[64,128]{1,0:T(8,128)S(1)}, f32[64,128]{1,0:T(8,128)S(1)}, f32[160,128]{1,0:T(8,128)S(1)}) custom-call(f32[5,8,64,128]{3,2,1,0:T(8,128)S(1)} %get-tuple-element.30.padded.start, ...), custom_call_target="tpu_custom_call", output_to_operand_aliasing={{0}: (4, {}), {1}: (5, {})} | custom-call | bytes 1845000 | tf_op jit(solution)/shard_map/section_high/pallas_call | solution.py:530
  16.9 1.5 %collective-permute-start.5 = (f32[160,128]{1,0:T(8,128)S(1)}, f32[160,128]{1,0:T(8,128)S(1)}, u32[]{:S(2)}, u32[]{:S(2)}) collective-permute-start(f32[160,128]{1,0:T(8,128)S(1)} %get-tuple-element.42), channel_id=1, source_target_pairs={{0,16},{4,20},{8,24},{12,28},{16,0},{20,4},{24,8},{28,12},{1,17},{... | collective-permute-start | bytes 245768 | tf_op jit(solution)/shard_map/ppermute | solution.py:558
  18.5 0.0 collective-permute-start.6
  18.5 1.1 %collective-permute-start.7 = (f32[64,128]{1,0:T(8,128)S(1)}, f32[64,128]{1,0:T(8,128)S(1)}, u32[]{:S(2)}, u32[]{:S(2)}) collective-permute-start(f32[64,128]{1,0:T(8,128)S(1)} %get-tuple-element.44), channel_id=1, source_target_pairs={{4,8},{12,16},{20,24},{28,0},{8,4},{16,12},{24,20},{0,28},{5,9},{1... | collective-permute-start | bytes 98312 | tf_op jit(solution)/shard_map/ppermute | solution.py:557
  19.6 2.5 %second.1 = (f32[5,8,48,128]{3,2,1,0:T(8,128)S(1)}, f32[960,128]{1,0:T(8,128)S(1)}, f32[960,128]{1,0:T(8,128)S(1)}) custom-call(f32[5,8,64,128]{3,2,1,0:T(8,128)S(1)} %get-tuple-element.39.padded, f32[128,256]{1,0:T(8,128)S(1)} %copy-done.2, f32[3,48,128]{2,1,0:T(8,128)S(1)} %copy-done.1, f32[8,8,128]{2,1,0:T(8,128)S(1)} %get-tuple-element.29.kap.kappa, ...), custom_call_target="tpu_custom_call" | custom-call | bytes 9225000 | tf_op jit(solution)/shard_map/second/pallas_call | solution.py:530
  22.1 0.0 collective-permute-done.6.inner
  22.1 0.7 %collective-permute-done.7.outer = f32[64,128]{1,0:T(8,128)S(1)} collective-permute-done((f32[64,128]{1,0:T(8,128)S(1)}, f32[64,128]{1,0:T(8,128)S(1)}, u32[]{:S(2)}, u32[]{:S(2)}) %collective-permute-start.7) | collective-permute-done | bytes 32800 | tf_op jit(solution)/shard_map/ppermute | solution.py:557
  22.8 0.0 collective-permute-done.5.polar
  22.8 1.0 %second_halo.1.both = f32[5,8,48,128]{3,2,1,0:T(8,128)S(1)} custom-call(f32[5,8,48,128]{3,2,1,0:T(8,128)S(1)} %get-tuple-element.41.given, f32[5,8,64,128]{3,2,1,0:T(8,128)S(1)} %get-tuple-element.39.padded, f32[160,128]{1,0:T(8,128)S(1)} %collective-permute-done.5.polar, ...), custom_call_target="tpu_custom_call", output_to_operand_aliasing={{}: (0, {})} | custom-call | bytes 3690000 | tf_op jit(solution)/shard_map/second_halo/pallas_call | solution.py:530
  23.8 1.9 %collective-permute-done.9.above = f32[960,128]{1,0:T(8,128)S(1)} collective-permute-done((f32[960,128]{1,0:T(8,128)S(1)}, f32[960,128]{1,0:T(8,128)S(1)}, u32[]{:S(2)}, u32[]{:S(2)}) %collective-permute-start.9) | collective-permute-done | bytes 491552 | tf_op jit(solution)/shard_map/ppermute | solution.py:602
  25.7 0.0 collective-permute-done.8.below
  25.7 1.1 %last.1 = f32[5,8,48,128]{3,2,1,0:T(8,128)} custom-call(f32[5,8,64,128]{3,2,1,0:T(8,128)S(1)} %get-tuple-element.39.padded, f32[5,8,48,128]{3,2,1,0:T(8,128)S(1)} %second_halo.1.both, f32[960,128]{1,0:T(8,128)S(1)} %collective-permute-done.8.below, f32[960,128]{1,0:T(8,128)S(1)} %collective-permute-done.9.above, f32[960,128]{1,0:T(8,128)S(1)} %get-tuple-element.47.more_low, ...), custom_call_target="tpu_custom_call" | custom-call | bytes 3690000 | tf_op jit(solution)/shard_map/last/pallas_call | solution.py:530
  (1 shorter events, 0.0 us)
Async XLA Ops:
  0.0 4.3 %copy-start = (f32[5,8,48,128]{3,2,1,0:T(8,128)S(1)}, f32[5,8,48,128]{3,2,1,0:T(8,128)}, u32[]{:S(2)}) copy-start(f32[5,8,48,128]{3,2,1,0:T(8,128)} %param.5) | copy-start | bytes 2949124
  1.2 6.7 %copy-start.1 = (f32[3,48,128]{2,1,0:T(8,128)S(1)}, f32[3,48,128]{2,1,0:T(8,128)}, u32[]{:S(2)}) copy-start(f32[3,48,128]{2,1,0:T(8,128)} %constant.5.clone.geo) | copy-start | bytes 221188
  1.2 6.7 %copy-start.2 = (f32[128,256]{1,0:T(8,128)S(1)}, f32[128,256]{1,0:T(8,128)}, u32[]{:S(2)}) copy-start(f32[128,256]{1,0:T(8,128)} %constant.4.clone.matrix) | copy-start | bytes 393220
  1.2 6.6 %copy-start.3 = (f32[5,8,4,128]{3,2,1,0:T(4,128)S(1)}, f32[5,8,4,128]{3,2,1,0:T(4,128)}, u32[]{:S(2)}) copy-start(f32[5,8,4,128]{3,2,1,0:T(4,128)} %beyond.1) | copy-start | bytes 245764
  1.2 14.7 %collective-permute-start.4 = (f32[968,128]{1,0:T(8,128)S(1)}, f32[968,128]{1,0:T(8,128)S(1)}, u32[]{:S(2)}, u32[]{:S(2)}) collective-permute-start(f32[968,128]{1,0:T(8,128)S(1)} %get-tuple-element.27.high), channel_id=1, source_target_pairs={{0,1},{1,2},{2,3},{3,7},{5,4},{6,5},{7,6},{4,0},{8,9},{9,10},{10,1... | collective-permute-start | bytes 1486856 | tf_op jit(solution)/shard_map/ppermute | solution.py:571
  4.3 11.9 %collective-permute-start.3 = (f32[968,128]{1,0:T(8,128)S(1)}, f32[968,128]{1,0:T(8,128)S(1)}, u32[]{:S(2)}, u32[]{:S(2)}) collective-permute-start(f32[968,128]{1,0:T(8,128)S(1)} %low.1), channel_id=1, source_target_pairs={{1,0},{2,1},{3,2},{7,3},{4,5},{5,6},{6,7},{0,4},{9,8},{10,9},{11,1... | collective-permute-start | bytes 1486856 | tf_op jit(solution)/shard_map/ppermute | solution.py:573
  4.8 5.9 %collective-permute-start = (f32[160,128]{1,0:T(8,128)S(1)}, f32[160,128]{1,0:T(8,128)S(1)}, u32[]{:S(2)}, u32[]{:S(2)}) collective-permute-start(f32[160,128]{1,0:T(8,128)S(1)} %get-tuple-element.32), channel_id=1, source_target_pairs={{0,16},{4,20},{8,24},{12,28},{16,0},{20,4},{24,8},{28,12},{1,17},{... | collective-permute-start | bytes 245768 | tf_op jit(solution)/shard_map/ppermute | solution.py:558
  6.3 3.6 %collective-permute-start.1 = (f32[64,128]{1,0:T(8,128)S(1)}, f32[64,128]{1,0:T(8,128)S(1)}, u32[]{:S(2)}, u32[]{:S(2)}) collective-permute-start(f32[64,128]{1,0:T(8,128)S(1)} %get-tuple-element.33), channel_id=1, source_target_pairs={{0,4},{8,12},{16,20},{24,28},{4,0},{12,8},{20,16},{28,24},{1,5},{9... | collective-permute-start | bytes 98312 | tf_op jit(solution)/shard_map/ppermute | solution.py:556
  6.3 4.3 %collective-permute-start.2 = (f32[64,128]{1,0:T(8,128)S(1)}, f32[64,128]{1,0:T(8,128)S(1)}, u32[]{:S(2)}, u32[]{:S(2)}) collective-permute-start(f32[64,128]{1,0:T(8,128)S(1)} %get-tuple-element.34), channel_id=1, source_target_pairs={{4,8},{12,16},{20,24},{28,0},{8,4},{16,12},{24,20},{0,28},{5,9},{1... | collective-permute-start | bytes 98312 | tf_op jit(solution)/shard_map/ppermute | solution.py:557
  12.1 13.6 %collective-permute-start.9 = (f32[960,128]{1,0:T(8,128)S(1)}, f32[960,128]{1,0:T(8,128)S(1)}, u32[]{:S(2)}, u32[]{:S(2)}) collective-permute-start(f32[960,128]{1,0:T(8,128)S(1)} %get-tuple-element.46), channel_id=1, source_target_pairs={{1,0},{2,1},{3,2},{7,3},{4,5},{5,6},{6,7},{0,4},{9,8},{10,9},{11,1... | collective-permute-start | bytes 1474568 | tf_op jit(solution)/shard_map/ppermute | solution.py:602
  12.1 13.6 %collective-permute-start.8 = (f32[960,128]{1,0:T(8,128)S(1)}, f32[960,128]{1,0:T(8,128)S(1)}, u32[]{:S(2)}, u32[]{:S(2)}) collective-permute-start(f32[960,128]{1,0:T(8,128)S(1)} %get-tuple-element.45), channel_id=1, source_target_pairs={{0,1},{1,2},{2,3},{3,7},{5,4},{6,5},{7,6},{4,0},{8,9},{9,10},{10,1... | collective-permute-start | bytes 1474568 | tf_op jit(solution)/shard_map/ppermute | solution.py:600
  16.9 5.9 %collective-permute-start.5 = (f32[160,128]{1,0:T(8,128)S(1)}, f32[160,128]{1,0:T(8,128)S(1)}, u32[]{:S(2)}, u32[]{:S(2)}) collective-permute-start(f32[160,128]{1,0:T(8,128)S(1)} %get-tuple-element.42), channel_id=1, source_target_pairs={{0,16},{4,20},{8,24},{12,28},{16,0},{20,4},{24,8},{28,12},{1,17},{... | collective-permute-start | bytes 245768 | tf_op jit(solution)/shard_map/ppermute | solution.py:558
  18.5 3.6 %collective-permute-start.6 = (f32[64,128]{1,0:T(8,128)S(1)}, f32[64,128]{1,0:T(8,128)S(1)}, u32[]{:S(2)}, u32[]{:S(2)}) collective-permute-start(f32[64,128]{1,0:T(8,128)S(1)} %get-tuple-element.43), channel_id=1, source_target_pairs={{0,4},{8,12},{16,20},{24,28},{4,0},{12,8},{20,16},{28,24},{1,5},{9... | collective-permute-start | bytes 98312 | tf_op jit(solution)/shard_map/ppermute | solution.py:556
  18.5 4.3 %collective-permute-start.7 = (f32[64,128]{1,0:T(8,128)S(1)}, f32[64,128]{1,0:T(8,128)S(1)}, u32[]{:S(2)}, u32[]{:S(2)}) collective-permute-start(f32[64,128]{1,0:T(8,128)S(1)} %get-tuple-element.44), channel_id=1, source_target_pairs={{4,8},{12,16},{20,24},{28,0},{8,4},{16,12},{24,20},{0,28},{5,9},{1... | collective-permute-start | bytes 98312 | tf_op jit(solution)/shard_map/ppermute | solution.py:557

commit v11 on v10

--- a/solution.py
+++ b/solution.py
@@ -489,27 +489,74 @@
     add_halo(levels, rows, range(levels), padded, polar, inner, outer, geo, kap, store)
 
 
-def last_kernel(levels, rows, padded, both, below, above, more_low, more_high, kap, out, staged, sems):
+def side_copy(at, t, levels, odd, out, staged, sems):
+    real, here = jnp.where(odd == 1, levels - at - REACH, at), pl.ds(t * TILE, TILE)
+    there = (slice(None), pl.ds(real, REACH), here)
+    return pltpu.make_async_copy(staged.at[there], out.at[there], sems.at[at // REACH, t])
+
+
+def write_tile(at, t, share, levels, padded, both, kap, staged):
     odd, mirror = mirrored()
-    copies = []
-    for t in range(rows // TILE):
-        here, inside = pl.ds(t * TILE, TILE), pl.ds((t + 1) * TILE, TILE)
-        for sent, more, at, up in ((below, more_low, 0, False), (above, more_high, levels - REACH, True)):
-            halo, there = own_tile(sent, rows, t * TILE), own_tile(more, rows, t * TILE)
+    here, inside = pl.ds(t * TILE, TILE), pl.ds((t + 1) * TILE, TILE)
+    extra = None
+    if share is not None:
+        wind = [padded[3, at + a, inside, :] for a in range(REACH)]
+        temper = [padded[4, at + a, inside, :] for a in range(REACH)]
+        extra = share(t * TILE, wind, temper, [kap[at + a] for a in range(REACH)])
+    for f in range(FIELDS):
+        for a in range(REACH):
+            new = both[f, at + a, here, :]
+            if extra is not None:
+                new = new + (0.5 * time_step) * extra[f][a]
+            real = jnp.where(odd == 1, levels - 1 - at - a, at + a)
+            staged[f, real, here, :] = mirror * new if f == 3 else new
+
+
+def end_kernel(levels, rows, padded, both, kap, out, staged, sems):
+    odd, _ = mirrored()
+    for at in (0, levels - REACH):
+
+        @pl.when(jnp.logical_not(bordered(at)))
+        def _():
+            copies = [side_copy(at, t, levels, odd, out, staged, sems) for t in range(rows // TILE)]
+            for t, copy in enumerate(copies):
+                write_tile(at, t, None, levels, padded, both, kap, staged)
+                copy.start()
+            for copy in copies:
+                copy.wait()
+
+
+def last_kernel(
+    levels, rows, padded, both, below, above, more_low, more_high, kap, given, out, staged, sems
+):
+    odd, _ = mirrored()
+
+    def share_by(sent, more, up):
+        def share(r0, wind, temper, kappa):
+            halo, there = own_tile(sent, rows, r0), own_tile(more, rows, r0)
             halo = [[halo[f][b] + there[f][b] for b in range(REACH)] for f in range(FIELDS)]
-            wind = [padded[3, at + a, inside, :] for a in range(REACH)]
-            temper = [padded[4, at + a, inside, :] for a in range(REACH)]
-            extra = across_level(wind, temper, halo, [kap[at + a] for a in range(REACH)], up)
-            scale = share_of(at, 0.5 * time_step)
-            for f in range(FIELDS):
-                for a in range(REACH):
-                    new = both[f, at + a, here, :] + scale * extra[f][a]
-                    real = jnp.where(odd == 1, levels - 1 - at - a, at + a)
-                    staged[f, real, here, :] = mirror * new if f == 3 else new
-        copies.append(pltpu.make_async_copy(staged.at[:, :, here], out.at[:, :, here], sems.at[t]))
-        copies[-1].start()
-    for copy in copies:
-        copy.wait()
+            return across_level(wind, temper, halo, kappa, up)
+
+        return share
+
+    sides = (
+        (0, share_by(below, more_low, False)),
+        (levels - REACH, share_by(above, more_high, True)),
+    )
+    for at, share in sides:
+
+        @pl.when(bordered(at))
+        def _():
+            for t in range(rows // TILE):
+                write_tile(at, t, share, levels, padded, both, kap, staged)
+                side_copy(at, t, levels, odd, out, staged, sems).start()
+
+    for at, _ in sides:
+
+        @pl.when(bordered(at))
+        def _():
+            for t in range(rows // TILE):
+                side_copy(at, t, levels, odd, out, staged, sems).wait()
 
 
 def on_device(state, outer_rows, kappa):
@@ -636,12 +683,23 @@
         aliases={0: 0},
         name="second_halo",
     )
+    last_scratch = (in_vmem(*full_shape), pltpu.SemaphoreType.DMA((2, rows // TILE)))
+    out = call(
+        end_kernel,
+        pltpu.HBM(full_shape, jnp.float32),
+        (VMEM,) * 3,
+        (ahead, both, kap),
+        scratch=last_scratch,
+        cost=0.5,
+        name="end",
+    )
     return call(
         last_kernel,
         pltpu.HBM(full_shape, jnp.float32),
-        (VMEM,) * 7,
-        (ahead, both, below2, above2, low, high, kap),
-        scratch=(in_vmem(*full_shape), pltpu.SemaphoreType.DMA((rows // TILE,))),
+        (VMEM,) * 7 + (HBM,),
+        (ahead, both, below2, above2, low, high, kap, out),
+        scratch=last_scratch,
+        aliases={7: 0},
         name="last",
     )
 

time: 27 us -> 26.9 us (level)
  waiting for transfers between devices: 5.19 us -> 4.28 us
  Pallas kernels: 10.7 us -> 11.4 us
    ppermute x1, waiting for transfers between devices: 1.9 us -> 0.99 us  [on_device(): above2 = lax.ppermute(low, axes, back)]
    pallas_call x11 -> x12, Pallas kernels: 10.7 us -> 11.4 us  [call(): pl.pallas_call(functools.partial(kernel, levels, rows), out_shape=out_sha...]
  transfers between devices with their start and end apart: 10 -> 10, of which waited for: 4 -> 4; matrix products, arithmetic and copies ran while one was open for 0% -> 0% of each run, Pallas kernels for 31% -> 35%
where the time goes in v11:
time: 26.9 us; the launch traced here: 26.7 us
  Pallas kernels  11.4 us (42%)
  starting transfers between devices  10.9 us (41%)
  waiting for transfers between devices  4.28 us (16%)
    pallas_call x12, Pallas kernels, call(): pl.pallas_call(functools.partial(kernel, levels, rows), out_shape=out_sha...  11.4 us
    ppermute x2, starting transfers between devices, around(): return (inner, outer, lax.ppermute(polar, 'lon', half))  3.09 us
    ppermute x1, starting transfers between devices, on_device(): below = lax.ppermute(high, axes, onward)  3.04 us
    ppermute x2, starting transfers between devices, around(): outer = lax.ppermute(outer, 'lon', swap_outer)  2.66 us
    ppermute x1, starting transfers between devices, on_device(): below2 = lax.ppermute(high, axes, onward)  2.01 us
    ppermute x1, waiting for transfers between devices, on_device(): below = lax.ppermute(high, axes, onward)  1.8 us
    ppermute x2, waiting for transfers between devices, around(): outer = lax.ppermute(outer, 'lon', swap_outer)  1.47 us
    ppermute x1, waiting for transfers between devices, on_device(): above2 = lax.ppermute(low, axes, back)  0.99 us
  transfers between devices with their start and end apart: 10, of which 4 were waited for; matrix products, arithmetic and copies ran while one was open for 0% of the time, Pallas kernels for 35%

profile of v11, /device:TPU:0, one launch (start us, length us, event | category | flops | bytes accessed | tf_op | source)
XLA Modules:
  0.0 26.7 jit_solution(10153318492334703933)
XLA Ops:
  0.0 0.0 copy-start
  0.0 1.2 %high.1 = (f32[968,128]{1,0:T(8,128)S(1)}, f32[8,8,128]{2,1,0:T(8,128)S(1)}, f32[8,128]{1,0:T(8,128)S(1)}) custom-call(f32[1920,128]{1,0:T(8,128)} %bitcast.1, f32[8]{0:T(128)} %kappa.1), custom_call_target="tpu_custom_call" | custom-call | bytes 3690000 | tf_op jit(solution)/shard_map/high/pallas_call | solution.py:577
  1.2 0.0 copy-start.1
  1.2 0.0 copy-start.2
  1.2 0.0 copy-start.3
  1.2 3.0 %collective-permute-start.4 = (f32[968,128]{1,0:T(8,128)S(1)}, f32[968,128]{1,0:T(8,128)S(1)}, u32[]{:S(2)}, u32[]{:S(2)}) collective-permute-start(f32[968,128]{1,0:T(8,128)S(1)} %get-tuple-element.27.high), channel_id=1, source_target_pairs={{0,1},{1,2},{2,3},{3,7},{5,4},{6,5},{7,6},{4,0},{8,9},{9,10},{10,1... | collective-permute-start | bytes 1486856 | tf_op jit(solution)/shard_map/ppermute | solution.py:618
  4.3 0.0 copy-done
  4.3 0.0 collective-permute-start.3
  4.3 0.4 %edges.1 = (f32[64,128]{1,0:T(8,128)S(1)}, f32[64,128]{1,0:T(8,128)S(1)}, f32[160,128]{1,0:T(8,128)S(1)}) custom-call(f32[968,128]{1,0:T(8,128)S(1)} %get-tuple-element.27.high, f32[968,128]{1,0:T(8,128)S(1)} %low.1), custom_call_target="tpu_custom_call" | custom-call | bytes 1476000 | tf_op jit(solution)/shard_map/edges/pallas_call | solution.py:577
  4.8 1.6 %collective-permute-start = (f32[160,128]{1,0:T(8,128)S(1)}, f32[160,128]{1,0:T(8,128)S(1)}, u32[]{:S(2)}, u32[]{:S(2)}) collective-permute-start(f32[160,128]{1,0:T(8,128)S(1)} %get-tuple-element.32), channel_id=1, source_target_pairs={{0,16},{4,20},{8,24},{12,28},{16,0},{20,4},{24,8},{28,12},{1,17},{... | collective-permute-start | bytes 245768 | tf_op jit(solution)/shard_map/ppermute | solution.py:605
  6.3 0.0 collective-permute-start.1
  6.3 1.5 %collective-permute-start.2 = (f32[64,128]{1,0:T(8,128)S(1)}, f32[64,128]{1,0:T(8,128)S(1)}, u32[]{:S(2)}, u32[]{:S(2)}) collective-permute-start(f32[64,128]{1,0:T(8,128)S(1)} %get-tuple-element.34), channel_id=1, source_target_pairs={{4,8},{12,16},{20,24},{28,0},{8,4},{16,12},{24,20},{0,28},{5,9},{1... | collective-permute-start | bytes 98312 | tf_op jit(solution)/shard_map/ppermute | solution.py:604
  7.9 0.0 copy-done.1
  7.9 0.0 copy-done.2
  7.9 0.0 copy-done.3
  7.9 2.0 %first.1 = (f32[5,8,64,128]{3,2,1,0:T(8,128)S(1)}, f32[5,8,48,128]{3,2,1,0:T(8,128)S(1)}) custom-call(f32[968,128]{1,0:T(8,128)S(1)} %get-tuple-element.27.high, f32[968,128]{1,0:T(8,128)S(1)} %low.1, f32[5,8,4,128]{3,2,1,0:T(4,128)S(1)} %copy-done.3, f32[128,256]{1,0:T(8,128)S(1)} %copy-done.2, f32[3,48,128]{2,1,0:T(8,128)S(1)} %copy-done.1, ...), custom_call_target="tpu_custom_call" | custom-call | bytes 7380000 | tf_op jit(solution)/shard_map/first/pallas_call | solution.py:577
  9.9 0.0 collective-permute-done.1.inner
  9.9 0.7 %collective-permute-done.2.outer = f32[64,128]{1,0:T(8,128)S(1)} collective-permute-done((f32[64,128]{1,0:T(8,128)S(1)}, f32[64,128]{1,0:T(8,128)S(1)}, u32[]{:S(2)}, u32[]{:S(2)}) %collective-permute-start.2) | collective-permute-done | bytes 32800 | tf_op jit(solution)/shard_map/ppermute | solution.py:604
  10.6 0.0 collective-permute-done.polar
  10.6 0.7 %first_halo.2 = (f32[5,8,48,128]{3,2,1,0:T(8,128)S(1)}, f32[960,128]{1,0:T(8,128)S(1)}) custom-call(f32[5,8,48,128]{3,2,1,0:T(8,128)S(1)} %get-tuple-element.31.given, f32[5,8,64,128]{3,2,1,0:T(8,128)S(1)} %get-tuple-element.30.padded.start, f32[160,128]{1,0:T(8,128)S(1)} %collective-permute-done.polar, ...), custom_call_target="tpu_custom_call", output_to_operand_aliasing={{0}: (0, {})} | custom-call | bytes 2214000 | tf_op jit(solution)/shard_map/first_halo/pallas_call | solution.py:577
  11.4 0.7 %first_halo.3 = (f32[5,8,48,128]{3,2,1,0:T(8,128)S(1)}, f32[960,128]{1,0:T(8,128)S(1)}) custom-call(f32[5,8,48,128]{3,2,1,0:T(8,128)S(1)} %get-tuple-element.35.given, f32[5,8,64,128]{3,2,1,0:T(8,128)S(1)} %get-tuple-element.30.padded.start, f32[160,128]{1,0:T(8,128)S(1)} %collective-permute-done.polar, ...), custom_call_target="tpu_custom_call", output_to_operand_aliasing={{0}: (0, {})} | custom-call | bytes 2214000 | tf_op jit(solution)/shard_map/first_halo/pallas_call | solution.py:577
  12.1 0.0 collective-permute-start.9
  12.1 2.0 %collective-permute-start.8 = (f32[960,128]{1,0:T(8,128)S(1)}, f32[960,128]{1,0:T(8,128)S(1)}, u32[]{:S(2)}, u32[]{:S(2)}) collective-permute-start(f32[960,128]{1,0:T(8,128)S(1)} %get-tuple-element.45), channel_id=1, source_target_pairs={{0,1},{1,2},{2,3},{3,7},{5,4},{6,5},{7,6},{4,0},{8,9},{9,10},{10,1... | collective-permute-start | bytes 1474568 | tf_op jit(solution)/shard_map/ppermute | solution.py:647
  14.2 1.8 %collective-permute-done.4.below = f32[968,128]{1,0:T(8,128)S(1)} collective-permute-done((f32[968,128]{1,0:T(8,128)S(1)}, f32[968,128]{1,0:T(8,128)S(1)}, u32[]{:S(2)}, u32[]{:S(2)}) %collective-permute-start.4) | collective-permute-done | bytes 495648 | tf_op jit(solution)/shard_map/ppermute | solution.py:618
  16.0 0.3 %section_low.1 = (f32[5,8,48,128]{3,2,1,0:T(8,128)S(1)}, f32[5,8,64,128]{3,2,1,0:T(8,128)S(1)}) custom-call(f32[5,8,64,128]{3,2,1,0:T(8,128)S(1)} %get-tuple-element.30.padded.start, f32[5,8,48,128]{3,2,1,0:T(8,128)S(1)} %get-tuple-element.36.rate, f32[968,128]{1,0:T(8,128)S(1)} %collective-permute-done.4.below, f32[8,8,128]{2,1,0:T(8,128)S(1)} %get-tuple-element.29.kap.kappa), custom_call_target="tpu_custom_call" | custom-call | bytes 1476000 | tf_op jit(solution)/shard_map/section_low/pallas_call | solution.py:577
  16.2 0.0 collective-permute-done.3.above
  16.3 0.7 %section_high.1 = (f32[5,8,48,128]{3,2,1,0:T(8,128)S(1)}, f32[5,8,64,128]{3,2,1,0:T(8,128)S(1)}, f32[64,128]{1,0:T(8,128)S(1)}, f32[64,128]{1,0:T(8,128)S(1)}, f32[160,128]{1,0:T(8,128)S(1)}) custom-call(f32[5,8,64,128]{3,2,1,0:T(8,128)S(1)} %get-tuple-element.30.padded.start, ...), custom_call_target="tpu_custom_call", output_to_operand_aliasing={{0}: (4, {}), {1}: (5, {})} | custom-call | bytes 1845000 | tf_op jit(solution)/shard_map/section_high/pallas_call | solution.py:577
  16.9 1.5 %collective-permute-start.5 = (f32[160,128]{1,0:T(8,128)S(1)}, f32[160,128]{1,0:T(8,128)S(1)}, u32[]{:S(2)}, u32[]{:S(2)}) collective-permute-start(f32[160,128]{1,0:T(8,128)S(1)} %get-tuple-element.42), channel_id=1, source_target_pairs={{0,16},{4,20},{8,24},{12,28},{16,0},{20,4},{24,8},{28,12},{1,17},{... | collective-permute-start | bytes 245768 | tf_op jit(solution)/shard_map/ppermute | solution.py:605
  18.5 0.0 collective-permute-start.6
  18.5 1.1 %collective-permute-start.7 = (f32[64,128]{1,0:T(8,128)S(1)}, f32[64,128]{1,0:T(8,128)S(1)}, u32[]{:S(2)}, u32[]{:S(2)}) collective-permute-start(f32[64,128]{1,0:T(8,128)S(1)} %get-tuple-element.44), channel_id=1, source_target_pairs={{4,8},{12,16},{20,24},{28,0},{8,4},{16,12},{24,20},{0,28},{5,9},{1... | collective-permute-start | bytes 98312 | tf_op jit(solution)/shard_map/ppermute | solution.py:604
  19.6 2.5 %second.1 = (f32[5,8,48,128]{3,2,1,0:T(8,128)S(1)}, f32[960,128]{1,0:T(8,128)S(1)}, f32[960,128]{1,0:T(8,128)S(1)}) custom-call(f32[5,8,64,128]{3,2,1,0:T(8,128)S(1)} %get-tuple-element.39.padded, f32[128,256]{1,0:T(8,128)S(1)} %copy-done.2, f32[3,48,128]{2,1,0:T(8,128)S(1)} %copy-done.1, f32[8,8,128]{2,1,0:T(8,128)S(1)} %get-tuple-element.29.kap.kappa, ...), custom_call_target="tpu_custom_call" | custom-call | bytes 9225000 | tf_op jit(solution)/shard_map/second/pallas_call | solution.py:577
  22.1 0.0 collective-permute-done.6.inner
  22.1 0.7 %collective-permute-done.7.outer = f32[64,128]{1,0:T(8,128)S(1)} collective-permute-done((f32[64,128]{1,0:T(8,128)S(1)}, f32[64,128]{1,0:T(8,128)S(1)}, u32[]{:S(2)}, u32[]{:S(2)}) %collective-permute-start.7) | collective-permute-done | bytes 32800 | tf_op jit(solution)/shard_map/ppermute | solution.py:604
  22.8 0.0 collective-permute-done.5.polar
  22.8 1.0 %second_halo.1.both = f32[5,8,48,128]{3,2,1,0:T(8,128)S(1)} custom-call(f32[5,8,48,128]{3,2,1,0:T(8,128)S(1)} %get-tuple-element.41.given, f32[5,8,64,128]{3,2,1,0:T(8,128)S(1)} %get-tuple-element.39.padded, f32[160,128]{1,0:T(8,128)S(1)} %collective-permute-done.5.polar, ...), custom_call_target="tpu_custom_call", output_to_operand_aliasing={{}: (0, {})} | custom-call | bytes 3690000 | tf_op jit(solution)/shard_map/second_halo/pallas_call | solution.py:577
  23.8 0.9 %end.1.given = f32[5,8,48,128]{3,2,1,0:T(8,128)} custom-call(f32[5,8,64,128]{3,2,1,0:T(8,128)S(1)} %get-tuple-element.39.padded, f32[5,8,48,128]{3,2,1,0:T(8,128)S(1)} %second_halo.1.both, f32[8,8,128]{2,1,0:T(8,128)S(1)} %get-tuple-element.29.kap.kappa), custom_call_target="tpu_custom_call" | custom-call | bytes 1845000 | tf_op jit(solution)/shard_map/end/pallas_call | solution.py:577
  24.7 1.0 %collective-permute-done.9.above = f32[960,128]{1,0:T(8,128)S(1)} collective-permute-done((f32[960,128]{1,0:T(8,128)S(1)}, f32[960,128]{1,0:T(8,128)S(1)}, u32[]{:S(2)}, u32[]{:S(2)}) %collective-permute-start.9) | collective-permute-done | bytes 491552 | tf_op jit(solution)/shard_map/ppermute | solution.py:649
  25.7 0.0 collective-permute-done.8.below
  25.7 1.0 %last.1 = f32[5,8,48,128]{3,2,1,0:T(8,128)} custom-call(f32[5,8,64,128]{3,2,1,0:T(8,128)S(1)} %get-tuple-element.39.padded, f32[5,8,48,128]{3,2,1,0:T(8,128)S(1)} %second_halo.1.both, f32[960,128]{1,0:T(8,128)S(1)} %collective-permute-done.8.below, f32[960,128]{1,0:T(8,128)S(1)} %collective-permute-done.9.above, ...), custom_call_target="tpu_custom_call", output_to_operand_aliasing={{}: (7, {})} | custom-call | bytes 3690000 | tf_op jit(solution)/shard_map/last/pallas_call | solution.py:577
  (1 shorter events, 0.0 us)
Async XLA Ops:
  0.0 4.3 %copy-start = (f32[5,8,48,128]{3,2,1,0:T(8,128)S(1)}, f32[5,8,48,128]{3,2,1,0:T(8,128)}, u32[]{:S(2)}) copy-start(f32[5,8,48,128]{3,2,1,0:T(8,128)} %param.5) | copy-start | bytes 2949124
  1.2 6.7 %copy-start.1 = (f32[3,48,128]{2,1,0:T(8,128)S(1)}, f32[3,48,128]{2,1,0:T(8,128)}, u32[]{:S(2)}) copy-start(f32[3,48,128]{2,1,0:T(8,128)} %constant.5.clone.geo) | copy-start | bytes 221188
  1.2 6.7 %copy-start.2 = (f32[128,256]{1,0:T(8,128)S(1)}, f32[128,256]{1,0:T(8,128)}, u32[]{:S(2)}) copy-start(f32[128,256]{1,0:T(8,128)} %constant.4.clone.matrix) | copy-start | bytes 393220
  1.2 6.6 %copy-start.3 = (f32[5,8,4,128]{3,2,1,0:T(4,128)S(1)}, f32[5,8,4,128]{3,2,1,0:T(4,128)}, u32[]{:S(2)}) copy-start(f32[5,8,4,128]{3,2,1,0:T(4,128)} %beyond.1) | copy-start | bytes 245764
  1.2 14.7 %collective-permute-start.4 = (f32[968,128]{1,0:T(8,128)S(1)}, f32[968,128]{1,0:T(8,128)S(1)}, u32[]{:S(2)}, u32[]{:S(2)}) collective-permute-start(f32[968,128]{1,0:T(8,128)S(1)} %get-tuple-element.27.high), channel_id=1, source_target_pairs={{0,1},{1,2},{2,3},{3,7},{5,4},{6,5},{7,6},{4,0},{8,9},{9,10},{10,1... | collective-permute-start | bytes 1486856 | tf_op jit(solution)/shard_map/ppermute | solution.py:618
  4.3 11.9 %collective-permute-start.3 = (f32[968,128]{1,0:T(8,128)S(1)}, f32[968,128]{1,0:T(8,128)S(1)}, u32[]{:S(2)}, u32[]{:S(2)}) collective-permute-start(f32[968,128]{1,0:T(8,128)S(1)} %low.1), channel_id=1, source_target_pairs={{1,0},{2,1},{3,2},{7,3},{4,5},{5,6},{6,7},{0,4},{9,8},{10,9},{11,1... | collective-permute-start | bytes 1486856 | tf_op jit(solution)/shard_map/ppermute | solution.py:620
  4.8 5.9 %collective-permute-start = (f32[160,128]{1,0:T(8,128)S(1)}, f32[160,128]{1,0:T(8,128)S(1)}, u32[]{:S(2)}, u32[]{:S(2)}) collective-permute-start(f32[160,128]{1,0:T(8,128)S(1)} %get-tuple-element.32), channel_id=1, source_target_pairs={{0,16},{4,20},{8,24},{12,28},{16,0},{20,4},{24,8},{28,12},{1,17},{... | collective-permute-start | bytes 245768 | tf_op jit(solution)/shard_map/ppermute | solution.py:605
  6.3 3.6 %collective-permute-start.1 = (f32[64,128]{1,0:T(8,128)S(1)}, f32[64,128]{1,0:T(8,128)S(1)}, u32[]{:S(2)}, u32[]{:S(2)}) collective-permute-start(f32[64,128]{1,0:T(8,128)S(1)} %get-tuple-element.33), channel_id=1, source_target_pairs={{0,4},{8,12},{16,20},{24,28},{4,0},{12,8},{20,16},{28,24},{1,5},{9... | collective-permute-start | bytes 98312 | tf_op jit(solution)/shard_map/ppermute | solution.py:603
  6.3 4.3 %collective-permute-start.2 = (f32[64,128]{1,0:T(8,128)S(1)}, f32[64,128]{1,0:T(8,128)S(1)}, u32[]{:S(2)}, u32[]{:S(2)}) collective-permute-start(f32[64,128]{1,0:T(8,128)S(1)} %get-tuple-element.34), channel_id=1, source_target_pairs={{4,8},{12,16},{20,24},{28,0},{8,4},{16,12},{24,20},{0,28},{5,9},{1... | collective-permute-start | bytes 98312 | tf_op jit(solution)/shard_map/ppermute | solution.py:604
  12.1 13.6 %collective-permute-start.9 = (f32[960,128]{1,0:T(8,128)S(1)}, f32[960,128]{1,0:T(8,128)S(1)}, u32[]{:S(2)}, u32[]{:S(2)}) collective-permute-start(f32[960,128]{1,0:T(8,128)S(1)} %get-tuple-element.46), channel_id=1, source_target_pairs={{1,0},{2,1},{3,2},{7,3},{4,5},{5,6},{6,7},{0,4},{9,8},{10,9},{11,1... | collective-permute-start | bytes 1474568 | tf_op jit(solution)/shard_map/ppermute | solution.py:649
  12.1 13.6 %collective-permute-start.8 = (f32[960,128]{1,0:T(8,128)S(1)}, f32[960,128]{1,0:T(8,128)S(1)}, u32[]{:S(2)}, u32[]{:S(2)}) collective-permute-start(f32[960,128]{1,0:T(8,128)S(1)} %get-tuple-element.45), channel_id=1, source_target_pairs={{0,1},{1,2},{2,3},{3,7},{5,4},{6,5},{7,6},{4,0},{8,9},{9,10},{10,1... | collective-permute-start | bytes 1474568 | tf_op jit(solution)/shard_map/ppermute | solution.py:647
  16.9 5.9 %collective-permute-start.5 = (f32[160,128]{1,0:T(8,128)S(1)}, f32[160,128]{1,0:T(8,128)S(1)}, u32[]{:S(2)}, u32[]{:S(2)}) collective-permute-start(f32[160,128]{1,0:T(8,128)S(1)} %get-tuple-element.42), channel_id=1, source_target_pairs={{0,16},{4,20},{8,24},{12,28},{16,0},{20,4},{24,8},{28,12},{1,17},{... | collective-permute-start | bytes 245768 | tf_op jit(solution)/shard_map/ppermute | solution.py:605
  18.5 3.6 %collective-permute-start.6 = (f32[64,128]{1,0:T(8,128)S(1)}, f32[64,128]{1,0:T(8,128)S(1)}, u32[]{:S(2)}, u32[]{:S(2)}) collective-permute-start(f32[64,128]{1,0:T(8,128)S(1)} %get-tuple-element.43), channel_id=1, source_target_pairs={{0,4},{8,12},{16,20},{24,28},{4,0},{12,8},{20,16},{28,24},{1,5},{9... | collective-permute-start | bytes 98312 | tf_op jit(solution)/shard_map/ppermute | solution.py:603
  18.5 4.3 %collective-permute-start.7 = (f32[64,128]{1,0:T(8,128)S(1)}, f32[64,128]{1,0:T(8,128)S(1)}, u32[]{:S(2)}, u32[]{:S(2)}) collective-permute-start(f32[64,128]{1,0:T(8,128)S(1)} %get-tuple-element.44), channel_id=1, source_target_pairs={{4,8},{12,16},{20,24},{28,0},{8,4},{16,12},{24,20},{0,28},{5,9},{1... | collective-permute-start | bytes 98312 | tf_op jit(solution)/shard_map/ppermute | solution.py:604

commit v12 on v11

--- a/solution.py
+++ b/solution.py
@@ -246,7 +246,7 @@
     return total
 
 
-def add_halo(levels, rows, own, padded, polar, inner, outer, geo, kap, store):
+def add_halo(levels, rows, padded, polar, inner, outer, geo, kap, store):
     per = GROUPS // levels
     count = rows // TILE // per
     packs = load_packs(FIELDS * count, inner, outer)
@@ -269,7 +269,7 @@
         here = pl.ds(t * TILE, TILE)
         metric = jnp.where(at_side, geo[0, here, :], 0.0)
         metric2 = jnp.where(at_side, geo[1, here, :], 0.0)
-        for l in own:
+        for l in range(levels):
             shift = (LANES - REACH - 2 * REACH * (u * levels + levels - 1 - l)) % LANES
             center = [padded[f, l, pl.ds((t + 1) * TILE, TILE), :] for f in range(FIELDS)]
             wlon, wrow, temper = center[1], center[2], center[4]
@@ -380,14 +380,14 @@
     interior(levels, rows, padded, dlon, elon, geo, kap, store)
 
 
-def first_halo_kernel(at, levels, rows, given, padded, polar, inner, outer, geo, kap, rate, side):
+def first_halo_kernel(levels, rows, given, padded, polar, inner, outer, geo, kap, rate, low, high):
     def store(f, l, r0, value, extra):
         tendency = given[f, l, pl.ds(r0, TILE), :] + extra
         rate[f, l, pl.ds(r0, TILE), :] = tendency
-        side[pl.ds((f * REACH + l - at) * rows + r0, TILE), :] = value + time_step * tendency
-
-    own = range(at, at + REACH)
-    add_halo(levels, rows, own, padded, polar, inner, outer, geo, kap, store)
+        side = low if l < REACH else high
+        side[pl.ds((f * REACH + l % REACH) * rows + r0, TILE), :] = value + time_step * tendency
+
+    add_halo(levels, rows, padded, polar, inner, outer, geo, kap, store)
 
 
 def raw_tile(ref, rows, r0, odd, mirror):
@@ -405,7 +405,7 @@
     ]
 
 
-def section_side(at, up, levels, rows, padded, rate, sent, kappa, full, ahead):
+def section_side(at, up, rows, padded, rate, sent, kappa, store):
     odd, mirror = mirrored()
     there = share_of(at, 1.0)
 
@@ -418,31 +418,41 @@
         for f in range(FIELDS):
             for a in range(REACH):
                 total = rate[f, at + a, here, :] + there * extra[f][a]
-                full[f, at + a, here, :] = total
-                ahead[f, at + a, inside, :] = center[f][a] + time_step * total
+                store(f, a, r0, total, center[f][a] + time_step * total)
         return carry
 
     lax.fori_loop(0, rows // TILE, body, 0)
+
+
+def section_low_kernel(levels, rows, padded, rate, below, kappa, full_low, ahead_low):
+    def store(f, a, r0, total, ahead):
+        full_low[f, a, pl.ds(r0, TILE), :] = total
+        ahead_low[f, a, pl.ds(r0, TILE), :] = ahead
+
+    section_side(0, False, rows, padded, rate, below, kappa, store)
+
+
+def section_high_kernel(
+    levels, rows, padded, rate, above, kappa, full_low, ahead_low, full, ahead, inner, outer, polar
+):
+    at = levels - REACH
+
+    def store(f, a, r0, total, value):
+        full[f, at + a, pl.ds(r0, TILE), :] = total
+        ahead[f, at + a, pl.ds(r0 + TILE, TILE), :] = value
+
+    section_side(at, True, rows, padded, rate, above, kappa, store)
+    packs = []
     for f in range(FIELDS):
-        for l in range(at, at + REACH):
+        for l in range(levels):
+            if l < REACH:
+                full[f, l] = full_low[f, l]
+                ahead[f, l, pl.ds(TILE, rows), :] = ahead_low[f, l]
             ahead[f, l, pl.ds(0, TILE), :] = jnp.zeros((TILE, LANES), jnp.float32)
             ahead[f, l, pl.ds(rows + TILE, REACH), :] = padded[f, l, pl.ds(rows + TILE, REACH), :]
-
-
-def section_low_kernel(levels, rows, padded, rate, below, kappa, full, ahead):
-    section_side(0, False, levels, rows, padded, rate, below, kappa, full, ahead)
-
-
-def section_high_kernel(
-    levels, rows, padded, rate, above, kappa, given1, given2, full, ahead, inner, outer, polar
-):
-    section_side(levels - REACH, True, levels, rows, padded, rate, above, kappa, full, ahead)
-    packs = []
-    for f in range(FIELDS):
+            polar[pl.ds((f * levels + l) * REACH, REACH), :] = ahead[f, l, pl.ds(TILE, REACH), :]
         tiles = [[ahead[f, l, pl.ds((t + 1) * TILE, TILE), :] for t in range(rows // TILE)] for l in range(levels)]
         packs += packed(levels, rows, tiles)
-        for l in range(levels):
-            polar[pl.ds((f * levels + l) * REACH, REACH), :] = ahead[f, l, pl.ds(TILE, REACH), :]
     store_packs(packs, inner, outer)
 
 
@@ -486,7 +496,7 @@
         at = pl.ds(r0, TILE)
         both[f, l, at, :] = given[f, l, at, :] + (0.5 * time_step) * extra
 
-    add_halo(levels, rows, range(levels), padded, polar, inner, outer, geo, kap, store)
+    add_halo(levels, rows, padded, polar, inner, outer, geo, kap, store)
 
 
 def side_copy(at, t, levels, odd, out, staged, sems):
@@ -527,7 +537,7 @@
 
 
 def last_kernel(
-    levels, rows, padded, both, below, above, more_low, more_high, kap, given, out, staged, sems
+    levels, rows, padded, both, above, below, more_low, more_high, kap, given, out, staged, sems
 ):
     odd, _ = mirrored()
 
@@ -632,25 +642,21 @@
         name="first",
     )
 
-    def first_halo(rate, at):
-        return call(
-            functools.partial(first_halo_kernel, at),
-            [in_vmem(*full_shape), side],
-            (VMEM,) * 7,
-            (rate, padded, beyond, inner, outer, geo, kap),
-            aliases={0: 0},
-            cost=0.6,
-            name="first_halo",
-        )
-
-    rate, high = first_halo(rate, levels - REACH)
+    rate, low, high = call(
+        first_halo_kernel,
+        [in_vmem(*full_shape), side, side],
+        (VMEM,) * 7,
+        (rate, padded, beyond, inner, outer, geo, kap),
+        aliases={0: 0},
+        cost=1.2,
+        name="first_halo",
+    )
     below2 = lax.ppermute(high, axes, onward)
-    rate, low = first_halo(rate, 0)
     above2 = lax.ppermute(low, axes, back)
-    section_shapes = [in_vmem(*full_shape), in_vmem(*pad_shape)]
-    full, ahead = call(
+    four = in_vmem(FIELDS, REACH, rows, width)
+    full_low, ahead_low = call(
         section_low_kernel,
-        section_shapes,
+        [four, four],
         (VMEM,) * 4,
         (padded, rate, below, kap),
         cost=0.4,
@@ -658,10 +664,9 @@
     )
     full, ahead, *edges = call(
         section_high_kernel,
-        [*section_shapes, *edge_shapes],
+        [in_vmem(*full_shape), in_vmem(*pad_shape), *edge_shapes],
         (VMEM,) * 6,
-        (padded, rate, above, kap, full, ahead),
-        aliases={4: 0, 5: 1},
+        (padded, rate, above, kap, full_low, ahead_low),
         cost=0.5,
         name="section_high",
     )
@@ -680,7 +685,6 @@
         in_vmem(*full_shape),
         (VMEM,) * 7,
         (both, ahead, beyond, inner, outer, geo, kap),
-        aliases={0: 0},
         name="second_halo",
     )
     last_scratch = (in_vmem(*full_shape), pltpu.SemaphoreType.DMA((2, rows // TILE)))
@@ -697,7 +701,7 @@
         last_kernel,
         pltpu.HBM(full_shape, jnp.float32),
         (VMEM,) * 7 + (HBM,),
-        (ahead, both, below2, above2, low, high, kap, out),
+        (ahead, both, above2, below2, low, high, kap, out),
         scratch=last_scratch,
         aliases={7: 0},
         name="last",

time: 26.9 us -> 26.8 us (level)
  Pallas kernels: 11.4 us -> 10.8 us
  waiting for transfers between devices: 4.28 us -> 4.65 us
    pallas_call x12 -> x11, Pallas kernels: 11.4 us -> 10.8 us  [call(): pl.pallas_call(functools.partial(kernel, levels, rows), out_shape=out_sha...]
    ppermute x1, waiting for transfers between devices: 1.8 us -> 2.14 us  [on_device(): below = lax.ppermute(high, axes, onward)]
  transfers between devices with their start and end apart: 10 -> 10, of which waited for: 4 -> 4; matrix products, arithmetic and copies ran while one was open for 0% -> 0% of each run, Pallas kernels for 35% -> 32%
where the time goes in v12:
time: 26.8 us; the launch traced here: 26.7 us
  starting transfers between devices  11.1 us (41%)
  Pallas kernels  10.8 us (40%)
  waiting for transfers between devices  4.65 us (17%)
    pallas_call x11, Pallas kernels, call(): pl.pallas_call(functools.partial(kernel, levels, rows), out_shape=out_sha...  10.8 us
    ppermute x2, starting transfers between devices, around(): return (inner, outer, lax.ppermute(polar, 'lon', half))  3.32 us
    ppermute x1, starting transfers between devices, on_device(): below = lax.ppermute(high, axes, onward)  3.04 us
    ppermute x2, starting transfers between devices, around(): outer = lax.ppermute(outer, 'lon', swap_outer)  2.71 us
    ppermute x1, waiting for transfers between devices, on_device(): below = lax.ppermute(high, axes, onward)  2.14 us
    ppermute x1, starting transfers between devices, on_device(): below2 = lax.ppermute(high, axes, onward)  2.01 us
    ppermute x2, waiting for transfers between devices, around(): outer = lax.ppermute(outer, 'lon', swap_outer)  1.32 us
    ppermute x1, waiting for transfers between devices, on_device(): above2 = lax.ppermute(low, axes, back)  1.17 us
  transfers between devices with their start and end apart: 10, of which 4 were waited for; matrix products, arithmetic and copies ran while one was open for 0% of the time, Pallas kernels for 32%

profile of v12, /device:TPU:0, one launch (start us, length us, event | category | flops | bytes accessed | tf_op | source)
XLA Modules:
  0.0 26.7 jit_solution(6776321217297480238)
XLA Ops:
  0.0 0.0 copy-start
  0.0 1.2 %high.1 = (f32[968,128]{1,0:T(8,128)S(1)}, f32[8,8,128]{2,1,0:T(8,128)S(1)}, f32[8,128]{1,0:T(8,128)S(1)}) custom-call(f32[1920,128]{1,0:T(8,128)} %bitcast.1, f32[8]{0:T(128)} %kappa.1), custom_call_target="tpu_custom_call" | custom-call | bytes 3690000 | tf_op jit(solution)/shard_map/high/pallas_call | solution.py:587
  1.2 0.0 copy-start.1
  1.2 0.0 copy-start.2
  1.2 0.0 copy-start.3
  1.2 3.0 %collective-permute-start.4 = (f32[968,128]{1,0:T(8,128)S(1)}, f32[968,128]{1,0:T(8,128)S(1)}, u32[]{:S(2)}, u32[]{:S(2)}) collective-permute-start(f32[968,128]{1,0:T(8,128)S(1)} %get-tuple-element.26.high), channel_id=1, source_target_pairs={{0,1},{1,2},{2,3},{3,7},{5,4},{6,5},{7,6},{4,0},{8,9},{9,10},{10,1... | collective-permute-start | bytes 1486856 | tf_op jit(solution)/shard_map/ppermute | solution.py:628
  4.3 0.0 copy-done
  4.3 0.0 collective-permute-start.3
  4.3 0.4 %edges.1 = (f32[64,128]{1,0:T(8,128)S(1)}, f32[64,128]{1,0:T(8,128)S(1)}, f32[160,128]{1,0:T(8,128)S(1)}) custom-call(f32[968,128]{1,0:T(8,128)S(1)} %get-tuple-element.26.high, f32[968,128]{1,0:T(8,128)S(1)} %low.1), custom_call_target="tpu_custom_call" | custom-call | bytes 1476000 | tf_op jit(solution)/shard_map/edges/pallas_call | solution.py:587
  4.8 1.6 %collective-permute-start = (f32[160,128]{1,0:T(8,128)S(1)}, f32[160,128]{1,0:T(8,128)S(1)}, u32[]{:S(2)}, u32[]{:S(2)}) collective-permute-start(f32[160,128]{1,0:T(8,128)S(1)} %get-tuple-element.31), channel_id=1, source_target_pairs={{0,16},{4,20},{8,24},{12,28},{16,0},{20,4},{24,8},{28,12},{1,17},{... | collective-permute-start | bytes 245768 | tf_op jit(solution)/shard_map/ppermute | solution.py:615
  6.3 0.0 collective-permute-start.1
  6.3 1.5 %collective-permute-start.2 = (f32[64,128]{1,0:T(8,128)S(1)}, f32[64,128]{1,0:T(8,128)S(1)}, u32[]{:S(2)}, u32[]{:S(2)}) collective-permute-start(f32[64,128]{1,0:T(8,128)S(1)} %get-tuple-element.33), channel_id=1, source_target_pairs={{4,8},{12,16},{20,24},{28,0},{8,4},{16,12},{24,20},{0,28},{5,9},{1... | collective-permute-start | bytes 98312 | tf_op jit(solution)/shard_map/ppermute | solution.py:614
  7.9 0.0 copy-done.1
  7.9 0.0 copy-done.2
  7.9 0.0 copy-done.3
  7.9 2.0 %first.1 = (f32[5,8,64,128]{3,2,1,0:T(8,128)S(1)}, f32[5,8,48,128]{3,2,1,0:T(8,128)S(1)}) custom-call(f32[968,128]{1,0:T(8,128)S(1)} %get-tuple-element.26.high, f32[968,128]{1,0:T(8,128)S(1)} %low.1, f32[5,8,4,128]{3,2,1,0:T(4,128)S(1)} %copy-done.3, f32[128,256]{1,0:T(8,128)S(1)} %copy-done.2, f32[3,48,128]{2,1,0:T(8,128)S(1)} %copy-done.1, ...), custom_call_target="tpu_custom_call" | custom-call | bytes 7380000 | tf_op jit(solution)/shard_map/first/pallas_call | solution.py:587
  9.9 0.0 collective-permute-done.1.inner
  9.9 0.7 %collective-permute-done.2.outer = f32[64,128]{1,0:T(8,128)S(1)} collective-permute-done((f32[64,128]{1,0:T(8,128)S(1)}, f32[64,128]{1,0:T(8,128)S(1)}, u32[]{:S(2)}, u32[]{:S(2)}) %collective-permute-start.2) | collective-permute-done | bytes 32800 | tf_op jit(solution)/shard_map/ppermute | solution.py:614
  10.6 0.0 collective-permute-done.polar
  10.6 1.1 %first_halo.1 = (f32[5,8,48,128]{3,2,1,0:T(8,128)S(1)}, f32[960,128]{1,0:T(8,128)S(1)}, f32[960,128]{1,0:T(8,128)S(1)}) custom-call(f32[5,8,48,128]{3,2,1,0:T(8,128)S(1)} %get-tuple-element.30.given, f32[5,8,64,128]{3,2,1,0:T(8,128)S(1)} %get-tuple-element.29.padded.start, ...), custom_call_target="tpu_custom_call", output_to_operand_aliasing={{0}: (0, {})} | custom-call | bytes 4428000 | tf_op jit(solution)/shard_map/first_halo/pallas_call | solution.py:587
  11.8 0.0 collective-permute-start.8
  11.8 2.0 %collective-permute-start.9 = (f32[960,128]{1,0:T(8,128)S(1)}, f32[960,128]{1,0:T(8,128)S(1)}, u32[]{:S(2)}, u32[]{:S(2)}) collective-permute-start(f32[960,128]{1,0:T(8,128)S(1)} %get-tuple-element.44), channel_id=1, source_target_pairs={{0,1},{1,2},{2,3},{3,7},{5,4},{6,5},{7,6},{4,0},{8,9},{9,10},{10,1... | collective-permute-start | bytes 1474568 | tf_op jit(solution)/shard_map/ppermute | solution.py:654
  13.8 2.1 %collective-permute-done.4.below = f32[968,128]{1,0:T(8,128)S(1)} collective-permute-done((f32[968,128]{1,0:T(8,128)S(1)}, f32[968,128]{1,0:T(8,128)S(1)}, u32[]{:S(2)}, u32[]{:S(2)}) %collective-permute-start.4) | collective-permute-done | bytes 495648 | tf_op jit(solution)/shard_map/ppermute | solution.py:628
  16.0 0.3 %section_low.1 = (f32[5,4,48,128]{3,2,1,0:T(8,128)S(1)}, f32[5,4,48,128]{3,2,1,0:T(8,128)S(1)}) custom-call(f32[5,8,64,128]{3,2,1,0:T(8,128)S(1)} %get-tuple-element.29.padded.start, f32[5,8,48,128]{3,2,1,0:T(8,128)S(1)} %get-tuple-element.34.rate, f32[968,128]{1,0:T(8,128)S(1)} %collective-permute-done.4.below, f32[8,8,128]{2,1,0:T(8,128)S(1)} %get-tuple-element.28.kap.kappa), custom_call_target="tpu_custom_call" | custom-call | bytes 1476000 | tf_op jit(solution)/shard_map/section_low/pallas_call | solution.py:587
  16.2 0.0 collective-permute-done.3.above
  16.2 0.7 %section_high.1 = (f32[5,8,48,128]{3,2,1,0:T(8,128)S(1)}, f32[5,8,64,128]{3,2,1,0:T(8,128)S(1)}, f32[64,128]{1,0:T(8,128)S(1)}, f32[64,128]{1,0:T(8,128)S(1)}, f32[160,128]{1,0:T(8,128)S(1)}) custom-call(f32[5,8,64,128]{3,2,1,0:T(8,128)S(1)} %get-tuple-element.29.padded.start, f32[5,8,48,128]{3,2,1,0:T(8,128)S(1)} %get-tuple-element.34.rate, ...), custom_call_target="tpu_custom_call" | custom-call | bytes 1845000 | tf_op jit(solution)/shard_map/section_high/pallas_call | solution.py:587
  17.0 1.8 %collective-permute-start.5 = (f32[160,128]{1,0:T(8,128)S(1)}, f32[160,128]{1,0:T(8,128)S(1)}, u32[]{:S(2)}, u32[]{:S(2)}) collective-permute-start(f32[160,128]{1,0:T(8,128)S(1)} %get-tuple-element.40), channel_id=1, source_target_pairs={{0,16},{4,20},{8,24},{12,28},{16,0},{20,4},{24,8},{28,12},{1,17},{... | collective-permute-start | bytes 245768 | tf_op jit(solution)/shard_map/ppermute | solution.py:615
  18.7 0.0 collective-permute-start.6
  18.7 1.2 %collective-permute-start.7 = (f32[64,128]{1,0:T(8,128)S(1)}, f32[64,128]{1,0:T(8,128)S(1)}, u32[]{:S(2)}, u32[]{:S(2)}) collective-permute-start(f32[64,128]{1,0:T(8,128)S(1)} %get-tuple-element.42), channel_id=1, source_target_pairs={{4,8},{12,16},{20,24},{28,0},{8,4},{16,12},{24,20},{0,28},{5,9},{1... | collective-permute-start | bytes 98312 | tf_op jit(solution)/shard_map/ppermute | solution.py:614
  19.9 2.5 %second.1 = (f32[5,8,48,128]{3,2,1,0:T(8,128)S(1)}, f32[960,128]{1,0:T(8,128)S(1)}, f32[960,128]{1,0:T(8,128)S(1)}) custom-call(f32[5,8,64,128]{3,2,1,0:T(8,128)S(1)} %get-tuple-element.37.padded, f32[128,256]{1,0:T(8,128)S(1)} %copy-done.2, f32[3,48,128]{2,1,0:T(8,128)S(1)} %copy-done.1, f32[8,8,128]{2,1,0:T(8,128)S(1)} %get-tuple-element.28.kap.kappa, ...), custom_call_target="tpu_custom_call" | custom-call | bytes 9225000 | tf_op jit(solution)/shard_map/second/pallas_call | solution.py:587
  22.4 0.0 collective-permute-done.6.inner
  22.4 0.6 %collective-permute-done.7.outer = f32[64,128]{1,0:T(8,128)S(1)} collective-permute-done((f32[64,128]{1,0:T(8,128)S(1)}, f32[64,128]{1,0:T(8,128)S(1)}, u32[]{:S(2)}, u32[]{:S(2)}) %collective-permute-start.7) | collective-permute-done | bytes 32800 | tf_op jit(solution)/shard_map/ppermute | solution.py:614
  23.0 0.0 collective-permute-done.5.polar
  23.0 0.6 %second_halo.1.both = f32[5,8,48,128]{3,2,1,0:T(8,128)S(1)} custom-call(f32[5,8,48,128]{3,2,1,0:T(8,128)S(1)} %get-tuple-element.39.given, f32[5,8,64,128]{3,2,1,0:T(8,128)S(1)} %get-tuple-element.37.padded, f32[160,128]{1,0:T(8,128)S(1)} %collective-permute-done.5.polar, f32[64,128]{1,0:T(8,128)S(1)} %collective-permute-done.6.inner, ...), custom_call_target="tpu_custom_call" | custom-call | bytes 3690000 | tf_op jit(solution)/shard_map/second_halo/pallas_call | solution.py:587
  23.6 0.9 %end.1.given = f32[5,8,48,128]{3,2,1,0:T(8,128)} custom-call(f32[5,8,64,128]{3,2,1,0:T(8,128)S(1)} %get-tuple-element.37.padded, f32[5,8,48,128]{3,2,1,0:T(8,128)S(1)} %second_halo.1.both, f32[8,8,128]{2,1,0:T(8,128)S(1)} %get-tuple-element.28.kap.kappa), custom_call_target="tpu_custom_call" | custom-call | bytes 1845000 | tf_op jit(solution)/shard_map/end/pallas_call | solution.py:587
  24.5 1.2 %collective-permute-done.8.above = f32[960,128]{1,0:T(8,128)S(1)} collective-permute-done((f32[960,128]{1,0:T(8,128)S(1)}, f32[960,128]{1,0:T(8,128)S(1)}, u32[]{:S(2)}, u32[]{:S(2)}) %collective-permute-start.8) | collective-permute-done | bytes 491552 | tf_op jit(solution)/shard_map/ppermute | solution.py:655
  25.7 0.0 collective-permute-done.9.below
  25.7 1.0 %last.1 = f32[5,8,48,128]{3,2,1,0:T(8,128)} custom-call(f32[5,8,64,128]{3,2,1,0:T(8,128)S(1)} %get-tuple-element.37.padded, f32[5,8,48,128]{3,2,1,0:T(8,128)S(1)} %second_halo.1.both, f32[960,128]{1,0:T(8,128)S(1)} %collective-permute-done.8.above, f32[960,128]{1,0:T(8,128)S(1)} %collective-permute-done.9.below, ...), custom_call_target="tpu_custom_call", output_to_operand_aliasing={{}: (7, {})} | custom-call | bytes 3690000 | tf_op jit(solution)/shard_map/last/pallas_call | solution.py:587
  (1 shorter events, 0.0 us)
Async XLA Ops:
  0.0 4.3 %copy-start = (f32[5,8,48,128]{3,2,1,0:T(8,128)S(1)}, f32[5,8,48,128]{3,2,1,0:T(8,128)}, u32[]{:S(2)}) copy-start(f32[5,8,48,128]{3,2,1,0:T(8,128)} %param.5) | copy-start | bytes 2949124
  1.2 6.7 %copy-start.1 = (f32[3,48,128]{2,1,0:T(8,128)S(1)}, f32[3,48,128]{2,1,0:T(8,128)}, u32[]{:S(2)}) copy-start(f32[3,48,128]{2,1,0:T(8,128)} %constant.5.clone.geo) | copy-start | bytes 221188
  1.2 6.7 %copy-start.2 = (f32[128,256]{1,0:T(8,128)S(1)}, f32[128,256]{1,0:T(8,128)}, u32[]{:S(2)}) copy-start(f32[128,256]{1,0:T(8,128)} %constant.4.clone.matrix) | copy-start | bytes 393220
  1.2 6.6 %copy-start.3 = (f32[5,8,4,128]{3,2,1,0:T(4,128)S(1)}, f32[5,8,4,128]{3,2,1,0:T(4,128)}, u32[]{:S(2)}) copy-start(f32[5,8,4,128]{3,2,1,0:T(4,128)} %beyond.1) | copy-start | bytes 245764
  1.2 14.7 %collective-permute-start.4 = (f32[968,128]{1,0:T(8,128)S(1)}, f32[968,128]{1,0:T(8,128)S(1)}, u32[]{:S(2)}, u32[]{:S(2)}) collective-permute-start(f32[968,128]{1,0:T(8,128)S(1)} %get-tuple-element.26.high), channel_id=1, source_target_pairs={{0,1},{1,2},{2,3},{3,7},{5,4},{6,5},{7,6},{4,0},{8,9},{9,10},{10,1... | collective-permute-start | bytes 1486856 | tf_op jit(solution)/shard_map/ppermute | solution.py:628
  4.3 11.9 %collective-permute-start.3 = (f32[968,128]{1,0:T(8,128)S(1)}, f32[968,128]{1,0:T(8,128)S(1)}, u32[]{:S(2)}, u32[]{:S(2)}) collective-permute-start(f32[968,128]{1,0:T(8,128)S(1)} %low.1), channel_id=1, source_target_pairs={{1,0},{2,1},{3,2},{7,3},{4,5},{5,6},{6,7},{0,4},{9,8},{10,9},{11,1... | collective-permute-start | bytes 1486856 | tf_op jit(solution)/shard_map/ppermute | solution.py:630
  4.8 5.9 %collective-permute-start = (f32[160,128]{1,0:T(8,128)S(1)}, f32[160,128]{1,0:T(8,128)S(1)}, u32[]{:S(2)}, u32[]{:S(2)}) collective-permute-start(f32[160,128]{1,0:T(8,128)S(1)} %get-tuple-element.31), channel_id=1, source_target_pairs={{0,16},{4,20},{8,24},{12,28},{16,0},{20,4},{24,8},{28,12},{1,17},{... | collective-permute-start | bytes 245768 | tf_op jit(solution)/shard_map/ppermute | solution.py:615
  6.3 3.6 %collective-permute-start.1 = (f32[64,128]{1,0:T(8,128)S(1)}, f32[64,128]{1,0:T(8,128)S(1)}, u32[]{:S(2)}, u32[]{:S(2)}) collective-permute-start(f32[64,128]{1,0:T(8,128)S(1)} %get-tuple-element.32), channel_id=1, source_target_pairs={{0,4},{8,12},{16,20},{24,28},{4,0},{12,8},{20,16},{28,24},{1,5},{9... | collective-permute-start | bytes 98312 | tf_op jit(solution)/shard_map/ppermute | solution.py:613
  6.3 4.3 %collective-permute-start.2 = (f32[64,128]{1,0:T(8,128)S(1)}, f32[64,128]{1,0:T(8,128)S(1)}, u32[]{:S(2)}, u32[]{:S(2)}) collective-permute-start(f32[64,128]{1,0:T(8,128)S(1)} %get-tuple-element.33), channel_id=1, source_target_pairs={{4,8},{12,16},{20,24},{28,0},{8,4},{16,12},{24,20},{0,28},{5,9},{1... | collective-permute-start | bytes 98312 | tf_op jit(solution)/shard_map/ppermute | solution.py:614
  11.8 13.9 %collective-permute-start.8 = (f32[960,128]{1,0:T(8,128)S(1)}, f32[960,128]{1,0:T(8,128)S(1)}, u32[]{:S(2)}, u32[]{:S(2)}) collective-permute-start(f32[960,128]{1,0:T(8,128)S(1)} %get-tuple-element.43), channel_id=1, source_target_pairs={{1,0},{2,1},{3,2},{7,3},{4,5},{5,6},{6,7},{0,4},{9,8},{10,9},{11,1... | collective-permute-start | bytes 1474568 | tf_op jit(solution)/shard_map/ppermute | solution.py:655
  11.8 13.9 %collective-permute-start.9 = (f32[960,128]{1,0:T(8,128)S(1)}, f32[960,128]{1,0:T(8,128)S(1)}, u32[]{:S(2)}, u32[]{:S(2)}) collective-permute-start(f32[960,128]{1,0:T(8,128)S(1)} %get-tuple-element.44), channel_id=1, source_target_pairs={{0,1},{1,2},{2,3},{3,7},{5,4},{6,5},{7,6},{4,0},{8,9},{9,10},{10,1... | collective-permute-start | bytes 1474568 | tf_op jit(solution)/shard_map/ppermute | solution.py:654
  17.0 6.0 %collective-permute-start.5 = (f32[160,128]{1,0:T(8,128)S(1)}, f32[160,128]{1,0:T(8,128)S(1)}, u32[]{:S(2)}, u32[]{:S(2)}) collective-permute-start(f32[160,128]{1,0:T(8,128)S(1)} %get-tuple-element.40), channel_id=1, source_target_pairs={{0,16},{4,20},{8,24},{12,28},{16,0},{20,4},{24,8},{28,12},{1,17},{... | collective-permute-start | bytes 245768 | tf_op jit(solution)/shard_map/ppermute | solution.py:615
  18.7 3.6 %collective-permute-start.6 = (f32[64,128]{1,0:T(8,128)S(1)}, f32[64,128]{1,0:T(8,128)S(1)}, u32[]{:S(2)}, u32[]{:S(2)}) collective-permute-start(f32[64,128]{1,0:T(8,128)S(1)} %get-tuple-element.41), channel_id=1, source_target_pairs={{0,4},{8,12},{16,20},{24,28},{4,0},{12,8},{20,16},{28,24},{1,5},{9... | collective-permute-start | bytes 98312 | tf_op jit(solution)/shard_map/ppermute | solution.py:613
  18.7 4.2 %collective-permute-start.7 = (f32[64,128]{1,0:T(8,128)S(1)}, f32[64,128]{1,0:T(8,128)S(1)}, u32[]{:S(2)}, u32[]{:S(2)}) collective-permute-start(f32[64,128]{1,0:T(8,128)S(1)} %get-tuple-element.42), channel_id=1, source_target_pairs={{4,8},{12,16},{20,24},{28,0},{8,4},{16,12},{24,20},{0,28},{5,9},{1... | collective-permute-start | bytes 98312 | tf_op jit(solution)/shard_map/ppermute | solution.py:614
